TPU v7x, 32 devices: a whole 2x2x4 slice. The times are simulated.
32 devices in a mesh: dp: 16 (over z, y, core), space: 2 (over x).
Axes of the slice: x: 2, y: 2, z: 4, core: 2. Of those that a mesh axis runs over, the one named last changes fastest.
Arguments:
- occupancy: int32 [16, 5, 32, 128], P('dp', None, 'space'), may hold values from 0 to 8191
- state_labels: int32 [16, 2, 8], P('dp', 'space'), may hold values 0 or 1
- lift_weight: bfloat16 [13, 32], replicated, may hold values from -1.75 to 1.75
- temporal_weight: bfloat16 [3, 3, 5, 32, 64], replicated, may hold values from -0.21875 to 0.21875
- middle_weight: bfloat16 [3, 3, 64, 128], replicated, may hold values from -0.375 to 0.375
- deeper_weight: bfloat16 [3, 3, 128, 256], replicated, may hold values from -0.25 to 0.25
- deepest_weight: bfloat16 [3, 3, 256, 512], replicated, may hold values from -0.1875 to 0.1875
- head_weight: bfloat16 [512], replicated, may hold values from -0.25 to 0.25
Outputs:
- temporal_grad: float32 [3, 3, 5, 32, 64], replicated
- middle_grad: float32 [3, 3, 64, 128], replicated
- deeper_grad: float32 [3, 3, 128, 256], replicated
- deepest_grad: float32 [3, 3, 256, 512], replicated
- head_grad: float32 [512], replicated
All inputs are finite; a program needn't handle non-finite values. No bound on the sum of `state_labels` on one device may be relied on, other than what follows from the above.
Results may differ from a plain program's by a relative error of at most 0.015.
Values may be sent and summed in bfloat16 or wider, within the bound.
No kernel may reach another device: no remote copies, remote signals or barrier semaphores. Data moves between devices by JAX's collectives and lax.ppermute only.
A program may use at most 64 MiB of HBM per device.

v0:
```python
import jax
import jax.numpy as jnp
from jax import lax
from jax.sharding import PartitionSpec as P


def from_behind(block, axis, distance):
    devices = range(lax.axis_size(axis))
    route = [(i - distance, i) for i in devices if i - distance in devices]
    return lax.ppermute(block, axis, route)


def conv_layer(feature_map, weight):
    upper_row = from_behind(feature_map[:, :, -1:, :], "space", 1)
    padded = jnp.concatenate([upper_row, feature_map], axis=2)
    padded = jnp.pad(padded, ((0, 0), (0, 0), (0, 0), (1, 0)))
    accumulated = lax.conv_general_dilated(
        padded,
        weight,
        (2, 2),
        "VALID",
        dimension_numbers=("NCHW", "HWIO", "NCHW"),
        preferred_element_type=jnp.float32,
    )
    gate = jax.nn.sigmoid(accumulated)
    slope = gate * (1.0 + accumulated * (1.0 - gate))
    return ((accumulated * gate).astype(jnp.bfloat16), slope, padded)


def weight_grad(padded, delta):
    return lax.conv_general_dilated(
        padded,
        delta,
        (1, 1),
        "VALID",
        rhs_dilation=(2, 2),
        dimension_numbers=("CNHW", "IOHW", "HWNC"),
        preferred_element_type=jnp.float32,
    )


def input_grad(delta, weight):
    flipped = weight[::-1, ::-1]
    accumulated = lax.conv_general_dilated(
        delta,
        flipped,
        (1, 1),
        ((2, 2), (2, 2)),
        lhs_dilation=(2, 2),
        dimension_numbers=("NCHW", "HWOI", "NCHW"),
        preferred_element_type=jnp.float32,
    )
    lower_row = from_behind(accumulated[:, :, 0:1, 1:], "space", -1)
    local_part = accumulated[:, :, 1:, 1:]
    return jnp.concatenate([local_part[:, :, :-1], local_part[:, :, -1:] + lower_row], axis=2)


def local(
    occupancy,
    state_labels,
    lift_weight,
    temporal_weight,
    middle_weight,
    deeper_weight,
    deepest_weight,
    head_weight,
):
    samples_here = occupancy.shape[0]
    frames = occupancy.shape[1]
    heights = lift_weight.shape[0]
    lift_width = lift_weight.shape[1]
    shifts = jnp.arange(heights, dtype=jnp.int32)
    height_bits = jnp.bitwise_and(
        jnp.right_shift(occupancy[:, :, None], shifts[None, None, :, None, None]), 1
    ).astype(jnp.bfloat16)
    lifted = jnp.einsum(
        "stcrw,ck->stkrw", height_bits, lift_weight, preferred_element_type=jnp.float32
    )
    lifted = jnp.maximum(lifted, 0.0).astype(jnp.bfloat16)
    lifted = lifted.reshape(samples_here, frames * lift_width, lifted.shape[3], lifted.shape[4])
    first_kernel = temporal_weight.reshape(3, 3, frames * lift_width, temporal_weight.shape[4])
    first_map, first_slope, lifted_padded = conv_layer(lifted, first_kernel)
    second_map, second_slope, first_padded = conv_layer(first_map, middle_weight)
    third_map, third_slope, second_padded = conv_layer(second_map, deeper_weight)
    fourth_map, fourth_slope, third_padded = conv_layer(third_map, deepest_weight)
    batch_total = state_labels.shape[0] * lax.axis_size("dp")
    logits = jnp.einsum("sorw,o->srw", fourth_map, head_weight, preferred_element_type=jnp.float32)
    logit_grad = (jax.nn.sigmoid(logits) - state_labels.astype(jnp.float32)) / batch_total
    head_float = head_weight.astype(jnp.float32)
    head_grad = jnp.einsum("sorw,srw->o", fourth_map.astype(jnp.float32), logit_grad)
    fourth_delta = (logit_grad[:, None] * head_float[None, :, None, None] * fourth_slope).astype(
        jnp.bfloat16
    )
    deepest_grad = weight_grad(third_padded, fourth_delta)
    third_delta = (input_grad(fourth_delta, deepest_weight) * third_slope).astype(jnp.bfloat16)
    deeper_grad = weight_grad(second_padded, third_delta)
    second_delta = (input_grad(third_delta, deeper_weight) * second_slope).astype(jnp.bfloat16)
    middle_grad = weight_grad(first_padded, second_delta)
    first_delta = (input_grad(second_delta, middle_weight) * first_slope).astype(jnp.bfloat16)
    temporal_grad = weight_grad(lifted_padded, first_delta).reshape(temporal_weight.shape)
    reduced = lax.psum(
        (temporal_grad, middle_grad, deeper_grad, deepest_grad, head_grad), ("dp", "space")
    )
    return (reduced[0], reduced[1], reduced[2], reduced[3], reduced[4])


def solution(mesh):
    return jax.shard_map(
        local,
        mesh=mesh,
        in_specs=(
            P("dp", None, "space", None),
            P("dp", "space", None),
            P(),
            P(),
            P(),
            P(),
            P(),
            P(),
        ),
        out_specs=(P(), P(), P(), P(), P()),
        check_vma=False,
    )
```

profile of v0, /device:TPU:0, one launch (start us, length us, event | category | flops | bytes accessed | tf_op | source)
XLA Modules:
  0.0 273.4 jit_solution(2235157991737551507)
XLA Ops:
  7.2 0.0 copy-start
  7.2 0.0 all-reduce.3.cloned.1.call-start
  7.2 1.3 fusion.9
  8.5 0.3 copy.145
  8.8 2.8 %copy.146 = bf16[1,160,16,128]{1,0,3,2:T(2,128)(2,1)} copy(bf16[1,160,16,128]{3,2,1,0:T(8,128)(2,1)S(1)} %bitcast.167) | data formatting | bytes 1310720 | tf_op jit(solution)/shard_map/reshape | solution.py:80
  11.7 1.0 slice.81
  12.7 4.8 %collective-permute-start = (bf16[1,160,1,128]{1,0,3,2:T(2,128)(2,1)S(1)}, bf16[1,160,1,128]{1,0,3,2:T(2,128)(2,1)S(1)}, u32[]{:S(2)}, u32[]{:S(2)}) collective-permute-start(bf16[1,160,1,128]{1,0,3,2:T(2,128)(2,1)S(1)} %slice.81), channel_id=1, source_target_pairs={{0,1},{2,3},{4,5},{6,7},{8,9},{10,11},{12,13},{14,15},{16,17},{18,... | collective-permute-start | bytes 122888 | tf_op jit(solution)/shard_map/ppermute | solution.py:10
  17.6 2.7 %collective-permute-done = bf16[1,160,1,128]{1,0,3,2:T(2,128)(2,1)S(1)} collective-permute-done((bf16[1,160,1,128]{1,0,3,2:T(2,128)(2,1)S(1)}, bf16[1,160,1,128]{1,0,3,2:T(2,128)(2,1)S(1)}, u32[]{:S(2)}, u32[]{:S(2)}) %collective-permute-start) | collective-permute-done | bytes 40992 | tf_op jit(solution)/shard_map/ppermute | solution.py:10
  20.3 6.2 %pad_maximum_fusion = bf16[1,160,17,128]{1,0,3,2:T(2,128)(2,1)} fusion(bf16[1,160,16,128]{1,0,3,2:T(2,128)(2,1)} %copy.146, bf16[1,160,1,128]{1,0,3,2:T(2,128)(2,1)S(1)} %collective-permute-done), kind=kLoop, calls=%fused_computation.2 | loop fusion | flops 348160 | bytes 1392640 | tf_op jit(solution)/shard_map/concatenate | solution.py:15
  26.5 5.9 %copy.148 = bf16[1,160,17,128]{3,1,2,0:T(8,128)(2,1)} copy(bf16[1,160,17,128]{1,0,3,2:T(2,128)(2,1)} %pad_maximum_fusion) | data formatting | bytes 1392640 | tf_op jit(solution)/shard_map/concatenate | solution.py:15
  32.5 1.7 copy.200
  34.1 1.5 pad.8.clone
  35.6 3.4 %reshape.106 = bf16[160,17,1,8,18]{0,4,3,1,2:T(8,128)(2,1)} reshape(bf16[160,17,1,144]{0,3,1,2:T(8,128)(2,1)} %pad.8.clone) | data formatting | bytes 1566720 | tf_op jit(solution)/shard_map/conv_general_dilated | solution.py:17
  39.0 1.8 copy.151
  40.9 1.6 add_multiply_fusion
  42.5 4.4 %collective-permute-start.1 = (bf16[1,64,1,64]{1,0,3,2:T(2,128)(2,1)S(1)}, bf16[1,64,1,64]{1,0,3,2:T(2,128)(2,1)S(1)}, u32[]{:S(2)}, u32[]{:S(2)}) collective-permute-start(bf16[1,64,1,64]{1,0,3,2:T(2,128)(2,1)S(1)} %slice_bitcast_fusion.1), channel_id=1, source_target_pairs={{0,1},{2,3},{4,5},{6,7},{8,9},{10,11},{12,13},{14,15},{16,17},{18,... | collective-permute-start | bytes 24584 | tf_op jit(solution)/shard_map/ppermute | solution.py:10
  47.0 0.2 copy.231
  47.2 1.3 collective-permute-done.1
  48.5 0.5 pad_maximum_fusion.1
  49.0 0.2 copy.156
  49.1 0.2 copy.201
  49.3 0.1 pad.10.clone
  49.4 0.1 reshape.113
  49.5 0.1 copy.159
  49.6 1.9 add_multiply_fusion.1
  51.5 4.2 %collective-permute-start.2 = (bf16[1,128,1,32]{1,0,3,2:T(2,128)(2,1)S(1)}, bf16[1,128,1,32]{1,0,3,2:T(2,128)(2,1)S(1)}, u32[]{:S(2)}, u32[]{:S(2)}) collective-permute-start(bf16[1,128,1,32]{1,0,3,2:T(2,128)(2,1)S(1)} %slice_bitcast_fusion.3), channel_id=1, source_target_pairs={{0,1},{2,3},{4,5},{6,7},{8,9},{10,11},{12,13},{14,15},{16,17},{18,... | collective-permute-start | bytes 24584 | tf_op jit(solution)/shard_map/ppermute | solution.py:10
  55.8 0.1 copy.232
  55.9 1.3 collective-permute-done.2
  57.2 0.1 pad_maximum_fusion.2
  57.3 0.5 copy-done.8
  57.9 0.2 add_multiply_fusion.2
  58.2 4.2 %collective-permute-start.3 = (bf16[1,256,1,16]{1,0,3,2:T(2,128)(2,1)S(1)}, bf16[1,256,1,16]{1,0,3,2:T(2,128)(2,1)S(1)}, u32[]{:S(2)}, u32[]{:S(2)}) collective-permute-start(bf16[1,256,1,16]{1,0,3,2:T(2,128)(2,1)S(1)} %slice_bitcast_fusion.2), channel_id=1, source_target_pairs={{0,1},{2,3},{4,5},{6,7},{8,9},{10,11},{12,13},{14,15},{16,17},{18,... | collective-permute-start | bytes 24584 | tf_op jit(solution)/shard_map/ppermute | solution.py:10
  62.5 1.0 copy.184
  63.5 0.7 slice.110
  64.4 0.1 pad_maximum_fusion.3
  64.6 0.4 multiply_convert_fusion.3
  65.2 0.1 fusion.19
  65.3 0.1 fusion.61
  65.4 0.4 copy-done.12
  65.8 0.8 fusion.64
  66.7 1.5 collective-permute-start.4
  68.1 3.1 %fusion.62 = f32[3,3,256,512]{3,2,1,0:T(8,128)} fusion(bf16[1,512,1,8]{1,3,2,0:T(8,128)(2,1)S(1)} %fusion.61, bf16[1,256,2,16]{1,0,3,2:T(2,128)(2,1)S(1)} %bitcast.181, bf16[1,256,1,16]{1,0,3,2:T(2,128)(2,1)S(1)} %collective-permute-done.3), kind=kOutput, calls=%fused_computation.103 | convolution fusion | flops 18137088 | bytes 4751360 | tf_op jit(solution)/shard_map/conv_general_dilated | solution.py:31
  71.2 1.1 collective-permute-done.4
  72.3 0.4 fusion.87
  72.8 1.4 collective-permute-start.5
  74.2 1.5 fusion.85
  75.7 2.9 %collective-permute-done.5 = f32[1,128,1,32]{1,0,3,2:T(1,128)S(1)} collective-permute-done((f32[1,128,1,32]{1,0,3,2:T(1,128)S(1)}, f32[1,128,1,32]{1,0,3,2:T(1,128)S(1)}, u32[]{:S(2)}, u32[]{:S(2)}) %collective-permute-start.5) | collective-permute-done | bytes 16416 | tf_op jit(solution)/shard_map/ppermute | solution.py:10
  78.7 0.1 fusion.49
  78.9 0.3 convolution_select_fusion
  79.3 0.1 copy.183
  79.5 1.4 collective-permute-start.6
  80.9 2.5 fusion.93
  83.4 2.0 collective-permute-done.6
  85.4 0.1 fusion.24
  85.5 5.6 %fusion.25 = f32[3,3,160,64]{3,2,1,0:T(8,128)} fusion(bf16[1,160,17,128]{1,0,3,2:T(2,128)(2,1)S(1)} %copy-done.1, bf16[1,64,8,64]{1,3,2,0:T(8,128)(2,1)S(1)} %fusion.24), kind=kOutput, calls=%fused_computation.40 | convolution fusion | flops 93880320 | bytes 1130496 | tf_op jit(solution)/shard_map/conv_general_dilated | solution.py:31
  91.1 0.0 all-reduce.3.cloned.1.call-update
  91.2 0.6 copy-done.13
  91.8 0.1 fusion.66
  91.9 41.6 %psum.39 = f32[512]{0:T(512)} all-reduce(f32[512]{0:T(512)S(1)} %bitcast.187), channel_id=1, replica_groups=mesh['dp'=16,'space'=2] {'dp','space'}, use_global_device_ids=true, to_apply=%region_4.5 | all-reduce | flops 512 | bytes 4096 | tf_op jit(solution)/shard_map/psum | solution.py:101
  133.5 123.2 %all-reduce.3.cloned.1.call-done = (f32[3,3,5,32,64]{4,3,2,1,0:T(8,128)}, f32[3,3,64,128]{3,2,1,0:T(8,128)}, f32[3,3,128,256]{3,2,1,0:T(8,128)}, f32[3,3,256,512]{3,2,1,0:T(8,128)}) async-done(((f32[3,3,5,32,64]{4,3,2,1,0:T(8,128)}, f32[3,3,64,128]{3,2,1,0:T(8,128)}, f32[3,3,128,256]{3,2,1,0:T(8,128)}, f32[3,3,256,512]{3,2,1,0:T(8,128)}), (f32[3,3,5,32,64]{4,3,2,1,0:T(8,128)}, f32[3,3,64,128]{3,2,1,0:T(8,128)}, ...) | async-done | bytes 6561808 | tf_op jit(solution)/shard_map/psum | solution.py:101
  256.7 2.1 copy.241
  258.8 1.7 copy.242
  260.5 1.0 copy.243
  261.6 5.0 %copy.244 = f32[3,3,256,512]{3,2,1,0:T(8,128)} copy(f32[3,3,256,512]{3,2,1,0:T(8,128)} %get-tuple-element.22) | data formatting | bytes 9437184
  (93 shorter events, 0.9 us)
Async XLA Ops:
  7.2 57.4 %copy-start = (bf16[3,3,256,512]{3,2,1,0:T(8,128)(2,1)S(1)}, bf16[3,3,256,512]{3,2,1,0:T(8,128)(2,1)}, u32[]{:S(2)}) copy-start(bf16[3,3,256,512]{3,2,1,0:T(8,128)(2,1)} %param.14) | copy-start | bytes 7077892
  7.2 249.5 %all-reduce.3.cloned.1.call-start = ((), (), s32[]{:S(2)}) async-start(), calls=%async_computation | async-start | bytes 13860864 | tf_op jit(solution)/shard_map/psum | solution.py:101
  12.7 7.6 %collective-permute-start = (bf16[1,160,1,128]{1,0,3,2:T(2,128)(2,1)S(1)}, bf16[1,160,1,128]{1,0,3,2:T(2,128)(2,1)S(1)}, u32[]{:S(2)}, u32[]{:S(2)}) collective-permute-start(bf16[1,160,1,128]{1,0,3,2:T(2,128)(2,1)S(1)} %slice.81), channel_id=1, source_target_pairs={{0,1},{2,3},{4,5},{6,7},{8,9},{10,11},{12,13},{14,15},{16,17},{18,... | collective-permute-start | bytes 122888 | tf_op jit(solution)/shard_map/ppermute | solution.py:10
  39.0 1.8 copy-start.15
  39.0 1.8 copy-start.17
  42.4 7.1 %copy-start.18 = (pred[8,5]{0,1:T(8,128)(4,1)S(1)}, pred[8,5]{0,1:T(8,128)(4,1)}, u32[]{:S(2)}) copy-start(pred[8,5]{0,1:T(8,128)(4,1)} %constant.40) | copy-start | bytes 124
  42.5 6.0 %collective-permute-start.1 = (bf16[1,64,1,64]{1,0,3,2:T(2,128)(2,1)S(1)}, bf16[1,64,1,64]{1,0,3,2:T(2,128)(2,1)S(1)}, u32[]{:S(2)}, u32[]{:S(2)}) collective-permute-start(bf16[1,64,1,64]{1,0,3,2:T(2,128)(2,1)S(1)} %slice_bitcast_fusion.1), channel_id=1, source_target_pairs={{0,1},{2,3},{4,5},{6,7},{8,9},{10,11},{12,13},{14,15},{16,17},{18,... | collective-permute-start | bytes 24584 | tf_op jit(solution)/shard_map/ppermute | solution.py:10
  49.0 9.2 %copy-start.3 = (bf16[1,64,9,64]{1,0,3,2:T(2,128)(2,1)}, bf16[1,64,9,64]{1,0,3,2:T(2,128)(2,1)S(1)}, u32[]{:S(2)}) copy-start(bf16[1,64,9,64]{1,0,3,2:T(2,128)(2,1)S(1)} %pad_maximum_fusion.1) | copy-start | bytes 221188
  49.0 8.9 %copy-start.19 = (pred[8,3]{0,1:T(4,128)(4,1)S(1)}, pred[8,3]{0,1:T(4,128)(4,1)}, u32[]{:S(2)}) copy-start(pred[8,3]{0,1:T(4,128)(4,1)} %constant.39) | copy-start | bytes 76
  49.4 13.1 %copy-start.10 = (bf16[512]{0:T(512)(128)(2,1)S(1)}, bf16[512]{0:T(512)(128)(2,1)}, u32[]{:S(2)}) copy-start(bf16[512]{0:T(512)(128)(2,1)} %param.15) | copy-start | bytes 3076
  49.5 8.4 %copy-start.5 = (bf16[3,3,128,256]{3,2,1,0:T(8,128)(2,1)S(1)}, bf16[3,3,128,256]{3,2,1,0:T(8,128)(2,1)}, u32[]{:S(2)}) copy-start(bf16[3,3,128,256]{3,2,1,0:T(8,128)(2,1)} %param.13) | copy-start | bytes 1769476
  51.5 13.1 %copy-start.14 = (pred[8,2]{0,1:T(4,128)(4,1)S(1)}, pred[8,2]{0,1:T(4,128)(4,1)}, u32[]{:S(2)}) copy-start(pred[8,2]{0,1:T(4,128)(4,1)} %constant.38) | copy-start | bytes 52
  51.5 5.7 %collective-permute-start.2 = (bf16[1,128,1,32]{1,0,3,2:T(2,128)(2,1)S(1)}, bf16[1,128,1,32]{1,0,3,2:T(2,128)(2,1)S(1)}, u32[]{:S(2)}, u32[]{:S(2)}) collective-permute-start(bf16[1,128,1,32]{1,0,3,2:T(2,128)(2,1)S(1)} %slice_bitcast_fusion.3), channel_id=1, source_target_pairs={{0,1},{2,3},{4,5},{6,7},{8,9},{10,11},{12,13},{14,15},{16,17},{18,... | collective-permute-start | bytes 24584 | tf_op jit(solution)/shard_map/ppermute | solution.py:10
  57.2 0.6 copy-start.8
  57.8 6.4 %copy-start.7 = (f32[4,8,5,128]{3,1,2,0:T(8,128)S(1)}, f32[4,8,5,128]{3,1,2,0:T(8,128)}, u32[]{:S(2)}) copy-start(f32[4,8,5,128]{3,1,2,0:T(8,128)} %get-tuple-element.11) | copy-start | bytes 245764
  58.2 6.2 %collective-permute-start.3 = (bf16[1,256,1,16]{1,0,3,2:T(2,128)(2,1)S(1)}, bf16[1,256,1,16]{1,0,3,2:T(2,128)(2,1)S(1)}, u32[]{:S(2)}, u32[]{:S(2)}) collective-permute-start(bf16[1,256,1,16]{1,0,3,2:T(2,128)(2,1)S(1)} %slice_bitcast_fusion.2), channel_id=1, source_target_pairs={{0,1},{2,3},{4,5},{6,7},{8,9},{10,11},{12,13},{14,15},{16,17},{18,... | collective-permute-start | bytes 24584 | tf_op jit(solution)/shard_map/ppermute | solution.py:10
  63.5 1.7 copy-start.16
  65.3 0.5 copy-start.12
  66.6 7.6 %copy-start.9 = (bf16[1,128,1,32]{1,0,3,2:T(2,128)(2,1)S(1)}, bf16[1,128,1,32]{1,0,3,2:T(2,128)(2,1)}, u32[]{:S(2)}) copy-start(bf16[1,128,1,32]{1,0,3,2:T(2,128)(2,1)} %copy-done.8) | copy-start | bytes 24580
  66.7 5.6 %collective-permute-start.4 = (f32[1,256,1,16]{1,0,3,2:T(1,128)S(1)}, f32[1,256,1,16]{1,0,3,2:T(1,128)S(1)}, u32[]{:S(2)}, u32[]{:S(2)}) collective-permute-start(f32[1,256,1,16]{1,0,3,2:T(1,128)S(1)} %get-tuple-element.14), channel_id=1, source_target_pairs={{1,0},{3,2},{5,4},{7,6},{9,8},{11,10},{13,12},{15,14},{17,16},{19,... | collective-permute-start | bytes 49160 | tf_op jit(solution)/shard_map/ppermute | solution.py:10
  72.8 6.1 %copy-start.6 = (bf16[3,3,64,128]{3,2,1,0:T(8,128)(2,1)S(1)}, bf16[3,3,64,128]{3,2,1,0:T(8,128)(2,1)}, u32[]{:S(2)}) copy-start(bf16[3,3,64,128]{3,2,1,0:T(8,128)(2,1)} %param.12) | copy-start | bytes 442372
  72.8 6.1 %copy-start.11 = (pred[8,10]{0,1:T(8,128)(4,1)S(1)}, pred[8,10]{0,1:T(8,128)(4,1)}, u32[]{:S(2)}) copy-start(pred[8,10]{0,1:T(8,128)(4,1)} %constant.37) | copy-start | bytes 244
  72.8 5.9 %collective-permute-start.5 = (f32[1,128,1,32]{1,0,3,2:T(1,128)S(1)}, f32[1,128,1,32]{1,0,3,2:T(1,128)S(1)}, u32[]{:S(2)}, u32[]{:S(2)}) collective-permute-start(f32[1,128,1,32]{1,0,3,2:T(1,128)S(1)} %slice.103), channel_id=1, source_target_pairs={{1,0},{3,2},{5,4},{7,6},{9,8},{11,10},{13,12},{15,14},{17,16},{19,... | collective-permute-start | bytes 49160 | tf_op jit(solution)/shard_map/ppermute | solution.py:10
  79.5 6.0 %copy-start.4 = (f32[8,1,64,64]{3,0,2,1:T(8,128)S(1)}, f32[8,1,64,64]{3,0,2,1:T(8,128)}, u32[]{:S(2)}) copy-start(f32[8,1,64,64]{3,0,2,1:T(8,128)} %slice.110) | copy-start | bytes 393220
  79.5 6.0 %copy-start.1 = (bf16[1,160,17,128]{1,0,3,2:T(2,128)(2,1)S(1)}, bf16[1,160,17,128]{1,0,3,2:T(2,128)(2,1)}, u32[]{:S(2)}) copy-start(bf16[1,160,17,128]{1,0,3,2:T(2,128)(2,1)} %pad_maximum_fusion) | copy-start | bytes 2088964
  79.5 5.9 %collective-permute-start.6 = (f32[1,64,1,64]{1,3,2,0:T(8,128)S(1)}, f32[1,64,1,64]{1,3,2,0:T(8,128)S(1)}, u32[]{:S(2)}, u32[]{:S(2)}) collective-permute-start(f32[1,64,1,64]{1,3,2,0:T(8,128)S(1)} %slice.109), channel_id=1, source_target_pairs={{1,0},{3,2},{5,4},{7,6},{9,8},{11,10},{13,12},{15,14},{17,16},{19,... | collective-permute-start | bytes 49160 | tf_op jit(solution)/shard_map/ppermute | solution.py:10
  91.1 0.7 copy-start.13
  256.7 3.8 %copy-start.2 = (f32[3,3,128,256]{3,2,1,0:T(8,128)S(1)}, f32[3,3,128,256]{3,2,1,0:T(8,128)}, u32[]{:S(2)}) copy-start(f32[3,3,128,256]{3,2,1,0:T(8,128)} %get-tuple-element.21) | copy-start | bytes 3538948
Sparse Core Ops, SparseCore 0:
  91.3 165.3 all-reduce.2
where the time goes:
time: 274 us; the launch traced here: 273 us
  waiting for transfers between devices  135 us (49%)
  blocking collectives  41.6 us (15%)
  local copies, waits for them, and re-layouts  33.2 us (12%)
  starting transfers between devices  22 us (8%)
  matrix products  20 us (7%)
  between operations  14.8 us (5%)
  other arithmetic  7.19 us (3%)
    psum x1, waiting for transfers between devices, local(): lax.psum((temporal_grad, middle_grad, deeper_grad, deepest_grad, head_gra...  123 us
    psum x1, blocking collectives, local(): lax.psum((temporal_grad, middle_grad, deeper_grad, deepest_grad, head_gra...  41.6 us
    ppermute x7, starting transfers between devices, from_behind(): return lax.ppermute(block, axis, route)  22 us
    unnamed x54, local copies, waits for them, and re-layouts  13.6 us
    conv_general_dilated x4, matrix products, weight_grad(): lax.conv_general_dilated(padded, delta, (1, 1), 'VALID', rhs_dilation=(2,...  12.7 us
    ppermute x7, waiting for transfers between devices, from_behind(): return lax.ppermute(block, axis, route)  11.4 us
    concatenate x6, local copies, waits for them, and re-layouts, conv_layer(): padded = jnp.concatenate([upper_row, feature_map], axis=2)  7.66 us
    concatenate x4, other arithmetic, conv_layer(): padded = jnp.concatenate([upper_row, feature_map], axis=2)  6.89 us
  transfers between devices with their start and end apart: 8, of which 7 were waited for; matrix products, arithmetic and copies ran while one was open for 3% of the time, Pallas kernels for 0%

commit v1 on v0

v1 whole, which is shorter than its diff:
```python
import functools

import jax
import jax.numpy as jnp
from jax import lax
from jax.experimental import pallas as pl
from jax.experimental.pallas import tpu as pltpu
from jax.sharding import PartitionSpec as P

BLOCK = 8
UP_ROWS = 3
DOWN_ROWS = 5
MIB = 1 << 20


def f32_dot(left, right, contract):
    return lax.dot_general(
        left, right, ((contract[0], contract[1]), ((), ())), preferred_element_type=jnp.float32
    )


def dot_nn(left, right):
    return f32_dot(left, right, ((1,), (0,)))


def dot_nt(left, right):
    return f32_dot(left, right, ((1,), (1,)))


def dot_tn(left, right):
    return f32_dot(left, right, ((0,), (0,)))


def rounded(value):
    return value.astype(jnp.bfloat16).astype(jnp.float32)


def silu_and_slope(pre):
    gate = jax.nn.sigmoid(pre)
    return rounded(pre * gate), gate * (1.0 + pre * (1.0 - gate))


def shift_block(value, step):
    shape = value.shape
    flat = value.reshape(-1, shape[-1])
    moved = pltpu.roll(flat, step % flat.shape[0], 0)
    index = lax.broadcasted_iota(jnp.int32, flat.shape, 0) % BLOCK
    edge = 0 if step > 0 else BLOCK - 1
    return jnp.where(index == edge, 0.0, moved).reshape(shape)


def fill_map(ref, value, offset):
    n, rows, phases, _, channels = value.shape
    split = value.reshape(n, rows, phases // 2, 2, BLOCK, channels)
    for row in range(rows):
        pair, parity = divmod(row + offset, 2)
        ref[:, pair, parity, pl.ds(0, phases // 2), 1] = split[:, row, :, 0]
        ref[:, pair, parity, pl.ds(1, phases // 2), 0] = split[:, row, :, 1]
        ref[:, pair, parity, 0, 0] = shift_block(split[:, row, phases // 2 - 1, 1], 1)


def map_tap(ref, row_tap, col_tap, out_rows, out_phases):
    cells = ref[
        :,
        pl.ds(row_tap // 2, out_rows),
        row_tap % 2,
        pl.ds(col_tap // 2, out_phases),
        col_tap % 2,
    ]
    return cells.reshape(-1, cells.shape[-1]).astype(jnp.bfloat16)


def fill_delta(ref, value):
    rows, phases = value.shape[1:3]
    ref[:, pl.ds(0, rows), pl.ds(0, phases)] = value
    ref[:, pl.ds(0, rows), phases] = shift_block(value[:, :, 0], -1)


def delta_parts(ref, weight_ref, row_parity, col_parity, rows, phases):
    taps = (((1, 0),), ((2, 0), (0, 1)))
    total = None
    for row_tap, row_step in taps[row_parity]:
        for col_tap, col_step in taps[col_parity]:
            cells = ref[:, pl.ds(row_step, rows), pl.ds(col_step, phases)]
            lead = cells.shape[:-1]
            flat = cells.reshape(-1, cells.shape[-1]).astype(jnp.bfloat16)
            part = dot_nt(flat, weight_ref[3 * row_tap + col_tap])
            total = part if total is None else total + part
    return total.reshape(*lead, total.shape[-1])


def early_kernel(
    up_ref,
    own_ref,
    down_ref,
    lift_ref,
    first_w_ref,
    second_w_ref,
    label_ref,
    send_ref,
    lifted_ref,
    first_ref,
    first_slope_ref,
    second_slope_ref,
    bits_ref,
):
    frames, band, cols = own_ref.shape
    phases = cols // BLOCK
    rows = UP_ROWS + band + DOWN_ROWS
    first_rows = (rows - 2) // 2
    second_rows = (first_rows - 1) // 2
    height = lax.broadcasted_iota(jnp.int32, (16, cols), 0)
    bits_ref[...] = jnp.zeros(bits_ref.shape, jnp.bfloat16)
    for row in range(rows):
        for frame in range(frames):
            if row < UP_ROWS:
                line = up_ref[frame, pl.ds(row, 1)]
            elif row < UP_ROWS + band:
                line = own_ref[frame, pl.ds(row - UP_ROWS, 1)]
            else:
                line = down_ref[frame, pl.ds(row - UP_ROWS - band, 1)]
            bit = jnp.bitwise_and(jnp.right_shift(jnp.broadcast_to(line, height.shape), height), 1)
            bits_ref[pl.ds(row * 128 + frame * 16, 16)] = bit.astype(jnp.float32).astype(
                jnp.bfloat16
            )
    place = lax.broadcasted_iota(jnp.int32, (cols, cols), 0)
    column = lax.broadcasted_iota(jnp.int32, (cols, cols), 1)
    order = jnp.where(column == (place % BLOCK) * phases + place // BLOCK, 1.0, 0.0)
    spread = dot_nt(order.astype(jnp.bfloat16), bits_ref[...]).astype(jnp.bfloat16)
    stacked = jnp.concatenate(
        [spread[:, row * 128 : row * 128 + 128] for row in range(rows)], axis=0
    )
    lifted = rounded(jnp.maximum(dot_nn(stacked, lift_ref[...]), 0.0))
    fill_map(lifted_ref, lifted.reshape(1, rows, phases, BLOCK, lifted.shape[-1]), 0)

    phases //= 2
    pre = None
    for tap in range(9):
        cells = map_tap(lifted_ref, tap // 3, tap % 3, first_rows, phases)
        part = dot_nn(cells, first_w_ref[tap])
        pre = part if pre is None else pre + part
    value, slope = silu_and_slope(pre)
    shape = (1, first_rows, phases, BLOCK, value.shape[-1])
    fill_map(first_ref, value.reshape(shape), 0)
    first_slope_ref[...] = slope.reshape(shape)[:, 1 : 1 + band // 2]

    phases //= 2
    pre = None
    for tap in range(9):
        cells = map_tap(first_ref, tap // 3, tap % 3, second_rows, phases)
        part = dot_nn(cells, second_w_ref[tap])
        pre = part if pre is None else pre + part
    value, slope = silu_and_slope(pre)
    second_slope_ref[...] = slope.reshape(1, second_rows, phases, BLOCK, slope.shape[-1])
    sent = band // 4 * phases * BLOCK
    send_ref[pl.ds(0, sent)] = value[:sent].astype(jnp.bfloat16)
    send_ref[pl.ds(sent, 16)] = label_ref[...]


def deep_kernel(
    batch,
    bands,
    got_ref,
    third_w_ref,
    fourth_w_ref,
    fourth_wt_ref,
    head_ref,
    third_delta_ref,
    third_taps_ref,
    fourth_taps_ref,
    fourth_flat_ref,
    head_grad_ref,
    second_ref,
    third_ref,
    third_slope_ref,
    fourth_delta_ref,
):
    samples = got_ref.shape[0] // bands
    channels = got_ref.shape[2]
    rows, phases = 4 * bands, 4
    cells = got_ref.shape[1] - 16
    second_ref[:, 0, 0] = jnp.zeros(second_ref.shape[:1] + second_ref.shape[3:], jnp.float32)
    second = got_ref[:, pl.ds(0, cells)].astype(jnp.float32)
    fill_map(second_ref, second.reshape(samples, rows, phases, BLOCK, channels), 1)
    labels = got_ref[:, pl.ds(cells, 16)].astype(jnp.float32)[:, :BLOCK].reshape(-1, channels)

    rows, phases = rows // 2, phases // 2
    for tap in range(9):
        third_taps_ref[:, pl.ds(tap * channels, channels)] = map_tap(
            second_ref, tap // 3, tap % 3, rows, phases
        )
    value, slope = silu_and_slope(dot_nn(third_taps_ref[...], third_w_ref[...]))
    channels = value.shape[-1]
    third_ref[:, 0, 0] = jnp.zeros(third_ref.shape[:1] + third_ref.shape[3:], jnp.float32)
    fill_map(third_ref, value.reshape(samples, rows, phases, BLOCK, channels), 1)
    third_slope_ref[...] = slope.reshape(third_slope_ref.shape)

    rows, phases = rows // 2, phases // 2
    for tap in range(9):
        fourth_taps_ref[:, pl.ds(tap * channels, channels)] = map_tap(
            third_ref, tap // 3, tap % 3, rows, phases
        )
    value, slope = silu_and_slope(dot_nn(fourth_taps_ref[...], fourth_w_ref[...]))
    head = head_ref[...]
    logits = jnp.sum(value * head, axis=1, keepdims=True)
    logit_grad = (jax.nn.sigmoid(logits) - labels[:, :1]) / batch

    @pl.when(pl.program_id(0) == 0)
    def _():
        head_grad_ref[...] = jnp.zeros(head_grad_ref.shape, jnp.float32)

    head_grad_ref[...] += jnp.sum(value * logit_grad, axis=0, keepdims=True)
    delta = rounded(logit_grad * head * slope)
    fourth_flat_ref[...] = delta.astype(jnp.bfloat16)
    fourth_delta_ref[:, rows] = jnp.zeros(
        fourth_delta_ref.shape[:1] + fourth_delta_ref.shape[2:], jnp.float32
    )
    fill_delta(fourth_delta_ref, delta.reshape(samples, rows, phases, BLOCK, delta.shape[-1]))
    for row_parity in range(2):
        for col_parity in range(2):
            part = delta_parts(
                fourth_delta_ref, fourth_wt_ref, row_parity, col_parity, rows, phases
            )
            part = rounded(part * third_slope_ref[:, :, row_parity, :, col_parity])
            for row in range(rows):
                third_delta_ref[:, 2 * row + row_parity, col_parity] = part[:, row, 0]
    third_delta_ref[:, 2 * rows] = jnp.zeros(
        third_delta_ref.shape[:1] + third_delta_ref.shape[2:], jnp.float32
    )


def late_kernel(
    place_ref,
    third_delta_ref,
    third_wt_ref,
    second_wt_ref,
    lifted_ref,
    first_ref,
    first_slope_ref,
    second_slope_ref,
    out_ref,
    third_ref,
    second_ref,
    first_delta_ref,
):
    row_from = 2 * place_ref[1]
    fill_delta(third_ref, third_delta_ref[:, pl.ds(row_from, 3)])
    band_rows, phases = 4, 2
    for row_parity in range(2):
        rows = 3 - row_parity
        for col_parity in range(2):
            part = delta_parts(third_ref, third_wt_ref, row_parity, col_parity, rows, phases)
            for row in range(rows):
                for phase in range(phases):
                    at = (slice(None), 2 * row + row_parity, 2 * phase + col_parity)
                    second_ref[at] = rounded(part[:, row, phase] * second_slope_ref[at])
    phases = 4
    second_ref[:, :, phases] = shift_block(second_ref[:, :, 0], -1)
    for row_parity in range(2):
        for col_parity in range(2):
            part = delta_parts(
                second_ref, second_wt_ref, row_parity, col_parity, band_rows, phases
            )
            for row in range(band_rows):
                for phase in range(phases):
                    at = (slice(None), 2 * row + row_parity, 2 * phase + col_parity)
                    first_delta_ref[at] = rounded(part[:, row, phase] * first_slope_ref[at])
    delta = second_ref[:, pl.ds(0, band_rows), pl.ds(0, phases)]
    delta = delta.reshape(-1, delta.shape[-1]).astype(jnp.bfloat16)
    depth = first_ref.shape[-1]
    base = 9 * lifted_ref.shape[-1] // 2
    for tap in range(9):
        cells = map_tap(first_ref, tap // 3, tap % 3, band_rows, phases)
        out_ref[pl.ds(base + tap * depth, depth)] = dot_tn(cells, delta)
    delta = first_delta_ref[...]
    delta = delta.reshape(-1, delta.shape[-1]).astype(jnp.bfloat16)
    parts = []
    for tap in range(9):
        cells = map_tap(lifted_ref, 2 + tap // 3, tap % 3, 2 * band_rows, 2 * phases)
        parts.append(dot_tn(cells, delta))
    whole = jnp.concatenate(parts, axis=0)
    out_ref[pl.ds(0, base)] = jnp.concatenate([whole[:base], whole[base:]], axis=1)


def grads_kernel(third_taps_ref, third_delta_ref, fourth_taps_ref, fourth_flat_ref, out3, out4):
    @pl.when(pl.program_id(1) == 0)
    def _():
        out3[...] = jnp.zeros(out3.shape, jnp.float32)
        out4[...] = jnp.zeros(out4.shape, jnp.float32)

    out4[...] += dot_tn(fourth_taps_ref[...], fourth_flat_ref[...])
    delta = third_delta_ref[:, pl.ds(0, third_delta_ref.shape[1] - 1)]
    delta = delta.reshape(-1, delta.shape[-1]).astype(jnp.bfloat16)
    out3[...] += dot_tn(third_taps_ref[...], delta)


def cost(flops, size):
    return pl.CostEstimate(flops=flops, bytes_accessed=size, transcendentals=0)


def step(shift):
    devices = range(lax.axis_size("space"))
    return [(i, i + shift) for i in devices if i + shift in devices]


def local(
    occupancy,
    state_labels,
    lift_weight,
    temporal_weight,
    middle_weight,
    deeper_weight,
    deepest_weight,
    head_weight,
):
    bands = lax.axis_size("space")
    samples = lax.axis_size("dp")
    _, frames, band, cols = occupancy.shape
    heights, lift_width = lift_weight.shape
    lift_all = frames * lift_width
    one, two = middle_weight.shape[2:]
    three, four = deepest_weight.shape[2:]
    f32 = jnp.float32

    own = occupancy[0]
    up = lax.ppermute(own[:, band - UP_ROWS :], "space", step(1))
    down = lax.ppermute(own[:, :DOWN_ROWS], "space", step(-1))
    label = jnp.zeros((16, two), jnp.bfloat16)
    label = label.at[:BLOCK].set(
        jnp.broadcast_to(state_labels.reshape(BLOCK, 1), (BLOCK, two)).astype(jnp.bfloat16)
    )
    lift = jnp.pad(lift_weight, ((0, 16 - heights), (0, 0)))
    lift = jnp.einsum("ab,ck->acbk", jnp.eye(frames, dtype=lift.dtype), lift)
    lift = jnp.pad(lift.reshape(frames * 16, lift_all), ((0, 128 - frames * 16), (0, 0)))
    first_w = temporal_weight.reshape(9, lift_all, one)
    second_w = middle_weight.reshape(9, one, two)
    third_w = deeper_weight.reshape(9, two, three)
    fourth_w = deepest_weight.reshape(9, three, four)
    head = head_weight.astype(f32).reshape(1, four)

    rows = UP_ROWS + band + DOWN_ROWS
    first_rows = (rows - 2) // 2
    second_rows = (first_rows - 1) // 2
    vmem = pl.BlockSpec(memory_space=pltpu.VMEM)
    sent = band // 4 * 4 * BLOCK + 16
    payload, lifted, first, first_slope, second_slope = pl.pallas_call(
        early_kernel,
        out_shape=(
            jax.ShapeDtypeStruct((sent, two), jnp.bfloat16),
            jax.ShapeDtypeStruct((1, rows // 2, 2, cols // 16 + 1, 2, BLOCK, lift_all), f32),
            jax.ShapeDtypeStruct((1, first_rows // 2 + 1, 2, cols // 32 + 1, 2, BLOCK, one), f32),
            jax.ShapeDtypeStruct((1, band // 2, cols // 16, BLOCK, one), f32),
            jax.ShapeDtypeStruct((1, second_rows, cols // 32, BLOCK, two), f32),
        ),
        in_specs=[vmem] * 7,
        out_specs=(vmem,) * 5,
        scratch_shapes=[pltpu.VMEM((rows * 128, cols), jnp.bfloat16)],
        compiler_params=pltpu.CompilerParams(vmem_limit_bytes=32 * MIB),
        cost_estimate=cost(200_000_000, 4_000_000),
        name="early",
    )(up, own, down, lift, first_w, second_w, label)

    gathered = lax.all_gather(payload, ("dp", "space"), axis=0, tiled=False)

    chunk = max(1, min(samples, 32 // bands))
    steps = samples // chunk
    third_cells = 2 * bands * 2 * BLOCK
    fourth_cells = bands * BLOCK
    full = lambda *shape: pl.BlockSpec(shape, lambda i: (0,) * len(shape))
    third_delta, third_taps, fourth_taps, fourth_flat, head_grad = pl.pallas_call(
        functools.partial(deep_kernel, samples, bands),
        grid=(steps,),
        out_shape=(
            jax.ShapeDtypeStruct((samples, 2 * bands + 1, 2, BLOCK, three), f32),
            jax.ShapeDtypeStruct((samples * third_cells, 9 * two), jnp.bfloat16),
            jax.ShapeDtypeStruct((samples * fourth_cells, 9 * three), jnp.bfloat16),
            jax.ShapeDtypeStruct((samples * fourth_cells, four), jnp.bfloat16),
            jax.ShapeDtypeStruct((1, four), f32),
        ),
        in_specs=[
            pl.BlockSpec((chunk * bands, sent, two), lambda i: (i, 0, 0)),
            full(9 * two, three),
            full(9 * three, four),
            full(9, three, four),
            full(1, four),
        ],
        out_specs=(
            pl.BlockSpec((chunk, 2 * bands + 1, 2, BLOCK, three), lambda i: (i, 0, 0, 0, 0)),
            pl.BlockSpec((chunk * third_cells, 9 * two), lambda i: (i, 0)),
            pl.BlockSpec((chunk * fourth_cells, 9 * three), lambda i: (i, 0)),
            pl.BlockSpec((chunk * fourth_cells, four), lambda i: (i, 0)),
            full(1, four),
        ),
        scratch_shapes=[
            pltpu.VMEM((chunk, 2 * bands + 1, 2, 3, 2, BLOCK, two), f32),
            pltpu.VMEM((chunk, bands + 1, 2, 2, 2, BLOCK, three), f32),
            pltpu.VMEM((chunk, bands, 2, 1, 2, BLOCK, three), f32),
            pltpu.VMEM((chunk, bands + 1, 2, BLOCK, four), f32),
        ],
        compiler_params=pltpu.CompilerParams(vmem_limit_bytes=56 * MIB),
        cost_estimate=cost(2_000_000_000, 12_000_000),
        name="deep",
    )(gathered, third_w.reshape(9 * two, three), fourth_w.reshape(9 * three, four), fourth_w, head)

    place = jnp.stack([lax.axis_index("dp"), lax.axis_index("space")]).astype(jnp.int32)
    whole = lambda *shape: pl.BlockSpec(shape, lambda i, place: (0,) * len(shape))
    half = 9 * lift_all // 2
    partial = pl.pallas_call(
        late_kernel,
        grid_spec=pltpu.PrefetchScalarGridSpec(
            num_scalar_prefetch=1,
            grid=(1,),
            in_specs=[
                pl.BlockSpec(
                    (1, 2 * bands + 1, 2, BLOCK, three), lambda i, place: (place[0], 0, 0, 0, 0)
                ),
                whole(*third_w.shape),
                whole(*second_w.shape),
                whole(*lifted.shape),
                whole(*first.shape),
                whole(*first_slope.shape),
                whole(*second_slope.shape),
            ],
            out_specs=whole(half + 9 * one, two),
            scratch_shapes=[
                pltpu.VMEM((1, 3, 3, BLOCK, three), f32),
                pltpu.VMEM((1, 5, 5, BLOCK, two), f32),
                pltpu.VMEM((1, band // 2, cols // 16, BLOCK, one), f32),
            ],
        ),
        out_shape=jax.ShapeDtypeStruct((half + 9 * one, two), f32),
        compiler_params=pltpu.CompilerParams(vmem_limit_bytes=32 * MIB),
        cost_estimate=cost(200_000_000, 6_000_000),
        name="late",
    )(place, third_delta, third_w, second_w, lifted, first, first_slope, second_slope)

    summed = lax.psum(partial, ("dp", "space"))

    deeper_grad, deepest_grad = pl.pallas_call(
        grads_kernel,
        grid=(9, steps),
        out_shape=(
            jax.ShapeDtypeStruct((9 * two, three), f32),
            jax.ShapeDtypeStruct((9 * three, four), f32),
        ),
        in_specs=[
            pl.BlockSpec((chunk * third_cells, two), lambda t, i: (i, t)),
            pl.BlockSpec((chunk, 2 * bands + 1, 2, BLOCK, three), lambda t, i: (i, 0, 0, 0, 0)),
            pl.BlockSpec((chunk * fourth_cells, three), lambda t, i: (i, t)),
            pl.BlockSpec((chunk * fourth_cells, four), lambda t, i: (i, 0)),
        ],
        out_specs=(
            pl.BlockSpec((two, three), lambda t, i: (t, 0)),
            pl.BlockSpec((three, four), lambda t, i: (t, 0)),
        ),
        compiler_params=pltpu.CompilerParams(vmem_limit_bytes=32 * MIB),
        cost_estimate=cost(1_300_000_000, 10_000_000),
        name="grads",
    )(third_taps, third_delta, fourth_taps, fourth_flat)

    temporal = jnp.concatenate([summed[:half, :one], summed[:half, one:]], axis=0)
    return (
        temporal.reshape(temporal_weight.shape),
        summed[half:].reshape(middle_weight.shape),
        deeper_grad.reshape(deeper_weight.shape),
        deepest_grad.reshape(deepest_weight.shape),
        head_grad.reshape(four),
    )


def solution(mesh):
    return jax.shard_map(
        local,
        mesh=mesh,
        in_specs=(
            P("dp", None, "space", None),
            P("dp", "space", None),
            P(),
            P(),
            P(),
            P(),
            P(),
            P(),
        ),
        out_specs=(P(), P(), P(), P(), P()),
        check_vma=False,
    )
```

time: 274 us -> 233 us (0.85)
  blocking collectives: 41.6 us -> 0 us
  waiting for transfers between devices: 135 us -> 174 us
  Pallas kernels: 0 us -> 20.4 us
  matrix products: 20 us -> 0 us
  local copies, waits for them, and re-layouts: 33.2 us -> 13.6 us
  starting transfers between devices: 22 us -> 6.19 us
  other arithmetic: 7.19 us -> 3 us
    all_gather x0 -> x1, waiting for transfers between devices: none -> 53.2 us  [local(): gathered = lax.all_gather(payload, ('dp', 'space'), axis=0, tiled=False)]
    psum x1 -> x0, blocking collectives: 41.6 us -> none  [local(): lax.psum((temporal_grad, middle_grad, deeper_grad, deepest_grad, head_gra...]
    pallas_call x0 -> x4, Pallas kernels: none -> 20.4 us  [the longest x1 7.91 us: local(): pl.pallas_call(functools.partial(deep_kernel, samples, bands), grid=(step...]
    conv_general_dilated x11 -> x0, matrix products: 18.4 us -> none  [the longest x4 12.7 us: weight_grad(): lax.conv_general_dilated(padded, delta, (1, 1), 'VALID', rhs_dilation=(2,...]
    ppermute x7 -> x2, starting transfers between devices: 22 us -> 6.11 us  [the longest x1 4.83 us: local(): up = lax.ppermute(own[:, band - UP_ROWS:], 'space', step(1))]
    ppermute x7 -> x2, waiting for transfers between devices: 11.4 us -> 2.76 us  [the longest x1 2.76 us: local(): down = lax.ppermute(own[:, :DOWN_ROWS], 'space', step(-1))]
    concatenate x6 -> x0, local copies, waits for them, and re-layouts: 7.66 us -> none  [conv_layer(): padded = jnp.concatenate([upper_row, feature_map], axis=2)]
    concatenate x4 -> x1, other arithmetic: 6.89 us -> 0.92 us  [local(): jnp.concatenate([summed[:half, :one], summed[:half, one:]], axis=0)]
  transfers between devices with their start and end apart: 8 -> 4, of which waited for: 7 -> 3; matrix products, arithmetic and copies ran while one was open for 3% -> 2% of each run, Pallas kernels for 0% -> 3%
where the time goes in v1:
time: 233 us; the launch traced here: 232 us
  waiting for transfers between devices  174 us (75%)
  Pallas kernels  20.4 us (9%)
  between operations  14.2 us (6%)
  local copies, waits for them, and re-layouts  13.6 us (6%)
  starting transfers between devices  6.19 us (3%)
  other arithmetic  3 us (1%)
    psum x1, waiting for transfers between devices, local(): summed = lax.psum(partial, ('dp', 'space'))  118 us
    all_gather x1, waiting for transfers between devices, local(): gathered = lax.all_gather(payload, ('dp', 'space'), axis=0, tiled=False)  53.2 us
    unnamed x28, local copies, waits for them, and re-layouts  8.1 us
    pallas_call x1, Pallas kernels, local(): pl.pallas_call(functools.partial(deep_kernel, samples, bands), grid=(step...  7.91 us
    pallas_call x1, Pallas kernels, local(): pl.pallas_call(grads_kernel, grid=(9, steps), out_shape=(jax.ShapeDtypeSt...  6.2 us
    ppermute x1, starting transfers between devices, local(): up = lax.ppermute(own[:, band - UP_ROWS:], 'space', step(1))  4.83 us
  transfers between devices with their start and end apart: 4, of which 3 were waited for; matrix products, arithmetic and copies ran while one was open for 2% of the time, Pallas kernels for 3%

profile of v1, /device:TPU:0, one launch (start us, length us, event | category | flops | bytes accessed | tf_op | source)
XLA Modules:
  0.0 231.6 jit_solution(15434932591568359705)
XLA Ops:
  7.2 0.0 all-gather.3.cloned.1.call-start
  7.2 0.7 slice.36
  7.9 4.8 %collective-permute-start = (s32[5,3,128]{2,1,0:T(4,128)S(1)}, s32[5,3,128]{2,1,0:T(4,128)S(1)}, u32[]{:S(2)}, u32[]{:S(2)}) collective-permute-start(s32[5,3,128]{2,1,0:T(4,128)S(1)} %slice.36), channel_id=1, source_target_pairs={{0,1},{2,3},{4,5},{6,7},{8,9},{10,11},{12,13},{14,15},{16,17},{18,... | collective-permute-start | bytes 23048 | tf_op jit(solution)/shard_map/ppermute | solution.py:326
  12.8 0.7 slice.37
  13.5 1.3 collective-permute-start.1
  14.8 0.7 pad.11
  15.5 0.1 multiply_bitcast_fusion
  15.6 0.7 convert_bitcast_fusion
  16.3 0.1 reshape.72
  16.4 0.0 collective-permute-done.up_ref
  16.4 2.8 %collective-permute-done.1.down_ref = s32[5,5,128]{2,1,0:T(8,128)S(1)} collective-permute-done((s32[5,5,128]{2,1,0:T(8,128)S(1)}, s32[5,5,128]{2,1,0:T(8,128)S(1)}, u32[]{:S(2)}, u32[]{:S(2)}) %collective-permute-start.1) | collective-permute-done | bytes 12832 | tf_op jit(solution)/shard_map/ppermute | solution.py:327
  19.2 0.1 scatter.8.label_ref
  19.3 0.0 copy-start.8
  19.3 0.9 copy-done.8
  20.2 0.0 copy-start.12
  20.2 0.8 copy-done.12
  20.9 0.0 copy-start.13
  20.9 1.0 copy-done.13
  21.9 3.6 %early.1 = (bf16[144,128]{1,0:T(8,128)(2,1)}, f32[1,12,2,9,2,8,160]{6,5,4,3,2,1,0:T(8,128)S(1)}, f32[1,6,2,5,2,8,64]{6,5,4,3,2,1,0:T(8,128)S(1)}, f32[1,8,8,8,64...) custom-call(s32[5,3,128]{2,1,0:T(4,128)S(1)} %collective-permute-done.up_ref, s32[5,16,128]{2,1,0:T(8,128)S(1)} %bitcast.26, ...), custom_call_target="tpu_custom_call" | custom-call | flops 200000000 | bytes 4000000 | tf_op jit(solution)/shard_map/early/pallas_call | solution.py:346
  25.6 0.0 copy-start.2
  25.6 1.8 copy-done.2
  27.4 0.0 copy-start.10
  27.4 0.6 copy-done.10
  28.0 0.0 all-gather.3.cloned.1.call-update
  28.0 0.0 all-reduce.5.cloned.1.call-start
  28.1 1.3 reshape.84
  29.3 0.1 pad_add_fusion.place_ref
  29.4 53.2 %all-gather.3.cloned.1.call-done = bf16[4608,128]{1,0:T(8,128)(2,1)} async-done(((bf16[144,128]{1,0:T(8,128)(2,1)}), bf16[4608,128]{1,0:T(8,128)(2,1)}) %all-gather.3.cloned.1.call-update) | async-done | bytes 1179664 | tf_op jit(solution)/shard_map/all_gather | solution.py:363
  82.6 0.0 copy-start.3
  82.6 0.0 copy-start.6
  82.6 0.0 copy-start.9
  82.6 0.0 copy-start.11
  82.6 7.9 %deep.1 = (f32[16,5,2,8,256]{4,3,2,1,0:T(8,128)}, bf16[1024,1152]{1,0:T(8,128)(2,1)}, bf16[256,2304]{1,0:T(8,128)(2,1)}, bf16[256,512]{1,0:T(8,128)(2,1)}, f32[1,512]{1,0:T(1,128)}) custom-call(bf16[32,144,128]{2,1,0:T(8,128)(2,1)} %bitcast.34, bf16[1152,256]{1,0:T(8,128)(2,1)} %bitcast.20, bf16[2304,512]{1,0:T(8,128)(2,1)} %bitcast.32, ...), custom_call_target="tpu_custom_call" | custom-call | flops 2000000000 | bytes 12000000 | tf_op jit(solution)/shard_map/deep/pallas_call | solution.py:370
  90.5 0.0 copy-done.3
  90.6 0.0 copy-done.6
  90.6 0.0 copy-done.9
  90.6 0.0 copy-done.11
  90.6 0.0 copy-start
  90.6 1.3 copy-done
  91.9 0.0 copy-start.1
  91.9 0.0 copy-start.5
  91.9 0.0 copy-start.7
  91.9 2.6 %late.1 = f32[1296,128]{1,0:T(8,128)} custom-call(s32[2]{0:T(128)S(1)} %pad_add_fusion.place_ref, f32[16,5,2,8,256]{4,3,2,1,0:T(8,128)S(1)} %copy-done, bf16[9,128,256]{2,1,0:T(8,128)(2,1)S(1)} %bitcast.21, bf16[9,64,128]{2,1,0:T(8,128)(2,1)S(1)} %bitcast.23, f32[1,12,2,9,2,8,160]{6,5,4,3,2,1,0:T(8,128)S(1)} %copy-done.3, ...), custom_call_target="tpu_custom_call" | custom-call | flops 200000000 | bytes 6000000 | tf_op jit(solution)/shard_map/late/pallas_call | solution.py:408
  94.5 0.0 all-reduce.5.cloned.1.call-update
  94.5 0.0 copy-done.1
  94.6 0.0 copy-done.5
  94.6 0.0 copy-done.7
  94.6 0.0 copy-start.4
  94.6 1.7 copy-done.4
  96.2 6.2 %grads.1 = (f32[1152,256]{1,0:T(8,128)}, f32[2304,512]{1,0:T(8,128)}) custom-call(bf16[1024,1152]{1,0:T(8,128)(2,1)S(1)} %copy-done.4, f32[16,5,2,8,256]{4,3,2,1,0:T(8,128)S(1)} %copy-done.1, bf16[256,2304]{1,0:T(8,128)(2,1)S(1)} %copy-done.5, bf16[256,512]{1,0:T(8,128)(2,1)S(1)} %copy-done.7), custom_call_target="tpu_custom_call" | custom-call | flops 1300000000 | bytes 10000000 | tf_op jit(solution)/shard_map/grads/pallas_call | solution.py:439
  102.4 118.3 %all-reduce.5.cloned.1.call-done = f32[1296,128]{1,0:T(8,128)} async-done(((f32[1296,128]{1,0:T(8,128)}), f32[1296,128]{1,0:T(8,128)}) %all-reduce.5.cloned.1.call-update) | async-done | bytes 663568 | tf_op jit(solution)/shard_map/psum | solution.py:437
  220.7 1.4 fusion.1
  222.1 0.9 pad_maximum_fusion
  223.0 1.7 slice.40
  (3 shorter events, 0.0 us)
Async XLA Ops:
  7.2 75.5 %all-gather.3.cloned.1.call-start = ((), (), s32[]{:S(2)}) async-start(), calls=%async_computation.1 | async-start | bytes 1216512 | tf_op jit(solution)/shard_map/all_gather | solution.py:363
  7.9 8.5 %collective-permute-start = (s32[5,3,128]{2,1,0:T(4,128)S(1)}, s32[5,3,128]{2,1,0:T(4,128)S(1)}, u32[]{:S(2)}, u32[]{:S(2)}) collective-permute-start(s32[5,3,128]{2,1,0:T(4,128)S(1)} %slice.36), channel_id=1, source_target_pairs={{0,1},{2,3},{4,5},{6,7},{8,9},{10,11},{12,13},{14,15},{16,17},{18,... | collective-permute-start | bytes 23048 | tf_op jit(solution)/shard_map/ppermute | solution.py:326
  13.5 5.7 %collective-permute-start.1 = (s32[5,5,128]{2,1,0:T(8,128)S(1)}, s32[5,5,128]{2,1,0:T(8,128)S(1)}, u32[]{:S(2)}, u32[]{:S(2)}) collective-permute-start(s32[5,5,128]{2,1,0:T(8,128)S(1)} %slice.37), channel_id=1, source_target_pairs={{1,0},{3,2},{5,4},{7,6},{9,8},{11,10},{13,12},{15,14},{17,16},{19,... | collective-permute-start | bytes 38408 | tf_op jit(solution)/shard_map/ppermute | solution.py:327
  19.3 0.9 copy-start.8
  20.2 0.8 copy-start.12
  20.9 1.0 copy-start.13
  25.6 1.8 copy-start.2
  27.4 0.6 copy-start.10
  28.0 192.7 %all-reduce.5.cloned.1.call-start = ((), (), s32[]{:S(2)}) async-start(), calls=%async_computation | async-start | bytes 1327104 | tf_op jit(solution)/shard_map/psum | solution.py:437
  82.6 7.9 %copy-start.3 = (f32[1,12,2,9,2,8,160]{6,5,4,3,2,1,0:T(8,128)S(1)}, f32[1,12,2,9,2,8,160]{6,5,4,3,2,1,0:T(8,128)}, u32[]{:S(2)}) copy-start(f32[1,12,2,9,2,8,160]{6,5,4,3,2,1,0:T(8,128)} %copy-done.2) | copy-start | bytes 6635524
  82.6 7.9 %copy-start.6 = (bf16[3,3,128,256]{3,2,1,0:T(8,128)(2,1)S(1)}, bf16[3,3,128,256]{3,2,1,0:T(8,128)(2,1)}, u32[]{:S(2)}) copy-start(bf16[3,3,128,256]{3,2,1,0:T(8,128)(2,1)} %param.15) | copy-start | bytes 1769476
  82.6 7.9 %copy-start.9 = (bf16[3,3,64,128]{3,2,1,0:T(8,128)(2,1)S(1)}, bf16[3,3,64,128]{3,2,1,0:T(8,128)(2,1)}, u32[]{:S(2)}) copy-start(bf16[3,3,64,128]{3,2,1,0:T(8,128)(2,1)} %param.14) | copy-start | bytes 442372
  82.6 7.9 %copy-start.11 = (f32[1,5,4,8,128]{4,3,2,1,0:T(8,128)S(1)}, f32[1,5,4,8,128]{4,3,2,1,0:T(8,128)}, u32[]{:S(2)}) copy-start(f32[1,5,4,8,128]{4,3,2,1,0:T(8,128)} %copy-done.10) | copy-start | bytes 245764
  90.6 1.3 copy-start
  91.9 2.7 %copy-start.1 = (f32[16,5,2,8,256]{4,3,2,1,0:T(8,128)S(1)}, f32[16,5,2,8,256]{4,3,2,1,0:T(8,128)}, u32[]{:S(2)}) copy-start(f32[16,5,2,8,256]{4,3,2,1,0:T(8,128)} %get-tuple-element.30.third_delta_ref) | copy-start | bytes 3932164
  91.9 2.7 %copy-start.5 = (bf16[256,2304]{1,0:T(8,128)(2,1)S(1)}, bf16[256,2304]{1,0:T(8,128)(2,1)}, u32[]{:S(2)}) copy-start(bf16[256,2304]{1,0:T(8,128)(2,1)} %get-tuple-element.36.fourth_taps_ref) | copy-start | bytes 3538948
  91.9 2.7 %copy-start.7 = (bf16[256,512]{1,0:T(8,128)(2,1)S(1)}, bf16[256,512]{1,0:T(8,128)(2,1)}, u32[]{:S(2)}) copy-start(bf16[256,512]{1,0:T(8,128)(2,1)} %get-tuple-element.37.fourth_flat_ref) | copy-start | bytes 786436
  94.6 1.7 copy-start.4
Sparse Core Ops, SparseCore 0:
  28.1 54.4 all-gather.2
  94.7 126.0 all-reduce.4

commit v2 on v1

v2 whole, which is shorter than its diff:
```python
import functools

import jax
import jax.numpy as jnp
from jax import lax
from jax.experimental import pallas as pl
from jax.experimental.pallas import tpu as pltpu
from jax.sharding import PartitionSpec as P

BLOCK = 8
MIB = 1 << 20


def f32_dot(left, right, contract):
    return lax.dot_general(
        left, right, ((contract[0], contract[1]), ((), ())), preferred_element_type=jnp.float32
    )


def dot_nn(left, right):
    return f32_dot(left, right, ((1,), (0,)))


def dot_nt(left, right):
    return f32_dot(left, right, ((1,), (1,)))


def dot_tn(left, right):
    return f32_dot(left, right, ((0,), (0,)))


def rounded(value):
    return value.astype(jnp.bfloat16).astype(jnp.float32)


def silu_and_slope(pre):
    gate = jax.nn.sigmoid(pre)
    return rounded(pre * gate), gate * (1.0 + pre * (1.0 - gate))


def zero_row(ref):
    ref[:, 0, 0] = jnp.zeros(ref.shape[:1] + ref.shape[3:], ref.dtype)


def last_row_zero(ref):
    ref[:, ref.shape[1] - 1] = jnp.zeros(ref.shape[:1] + ref.shape[2:], ref.dtype)


def shift_block(value, step):
    shape = value.shape
    flat = value.reshape(-1, shape[-1])
    moved = pltpu.roll(flat, step % flat.shape[0], 0)
    index = lax.broadcasted_iota(jnp.int32, flat.shape, 0) % BLOCK
    edge = 0 if step > 0 else BLOCK - 1
    return jnp.where(index == edge, 0.0, moved).reshape(shape)


def fill_map(ref, value, offset):
    n, rows, phases, _, channels = value.shape
    split = value.reshape(n, rows, phases // 2, 2, BLOCK, channels)
    for row in range(rows):
        pair, parity = divmod(row + offset, 2)
        ref[:, pair, parity, pl.ds(0, phases // 2), 1] = split[:, row, :, 0]
        ref[:, pair, parity, pl.ds(1, phases // 2), 0] = split[:, row, :, 1]
        ref[:, pair, parity, 0, 0] = shift_block(split[:, row, phases // 2 - 1, 1], 1)


def map_tap(ref, row_tap, col_tap, out_rows, out_phases):
    cells = ref[
        :,
        pl.ds(row_tap // 2, out_rows),
        row_tap % 2,
        pl.ds(col_tap // 2, out_phases),
        col_tap % 2,
    ]
    return cells.reshape(-1, cells.shape[-1]).astype(jnp.bfloat16)


def fill_delta(ref, value):
    rows, phases = value.shape[1:3]
    ref[:, pl.ds(0, rows), pl.ds(0, phases)] = value
    ref[:, pl.ds(0, rows), phases] = shift_block(value[:, :, 0], -1)


def delta_parts(ref, weight_ref, row_parity, col_parity, rows, phases):
    taps = (((1, 0),), ((2, 0), (0, 1)))
    total = None
    for row_tap, row_step in taps[row_parity]:
        for col_tap, col_step in taps[col_parity]:
            cells = ref[:, pl.ds(row_step, rows), pl.ds(col_step, phases)]
            lead = cells.shape[:-1]
            flat = cells.reshape(-1, cells.shape[-1]).astype(jnp.bfloat16)
            part = dot_nt(flat, weight_ref[3 * row_tap + col_tap])
            total = part if total is None else total + part
    return total.reshape(*lead, total.shape[-1])


def early_kernel(
    frames,
    slot_ref,
    got_ref,
    lift_ref,
    first_w_ref,
    second_w_ref,
    send_ref,
    even_ref,
    odd_ref,
    first_ref,
    first_slope_ref,
    second_slope_ref,
    bits_ref,
):
    bands, lines, cols = got_ref.shape
    band = (lines - BLOCK) // frames
    phases = cols // BLOCK
    row_cells = cols // 2
    height = lax.broadcasted_iota(jnp.int32, (16, cols), 0)
    place = lax.broadcasted_iota(jnp.int32, (cols, cols), 0)
    column = lax.broadcasted_iota(jnp.int32, (cols, cols), 1)
    order = jnp.where(column == (place % BLOCK) * phases + place // BLOCK, 1.0, 0.0)
    order = order.astype(jnp.bfloat16)
    sent = (band // 4) * bands * (phases // 4) * BLOCK
    lane16 = lax.broadcasted_iota(jnp.int32, (16, send_ref.shape[1]), 1)
    bits_ref[...] = jnp.zeros(bits_ref.shape, jnp.bfloat16)
    odd_ref[pl.ds(0, row_cells)] = jnp.zeros((row_cells, odd_ref.shape[1]), jnp.bfloat16)
    for index in range(bands):
        slot = slot_ref[index]
        for row in range(band):
            for frame in range(frames):
                line = jnp.broadcast_to(got_ref[slot, pl.ds(frame * band + row, 1)], height.shape)
                bit = jnp.bitwise_and(jnp.right_shift(line, height), 1)
                bits_ref[pl.ds(row * 128 + frame * 16, 16)] = bit.astype(jnp.float32).astype(
                    jnp.bfloat16
                )
        line = jnp.broadcast_to(got_ref[slot, pl.ds(frames * band, 1)], height.shape)
        bits_ref[pl.ds(frames * 16, 16)] = line.astype(jnp.float32).astype(jnp.bfloat16)
        spread = dot_nt(order, bits_ref[...])
        label = jnp.where(lane16 == index, spread[:16, frames * 16 : frames * 16 + 1], 0.0)
        labels = label if index == 0 else labels + label
        spread = spread.astype(jnp.bfloat16)
        stacked = jnp.concatenate(
            [spread[:, row * 128 : row * 128 + 128] for row in range(band)], axis=0
        )
        lifted = jnp.maximum(dot_nn(stacked, lift_ref[...]), 0.0)
        lifted = lifted.reshape(band // 2, 2, phases // 2, 2, BLOCK, lifted.shape[-1])
        for parity, ref in ((0, even_ref), (1, odd_ref)):
            here = lifted[:, parity, :, 0]
            right = lifted[:, parity, :, 1]
            left = jnp.concatenate([shift_block(right[:, -1], 1)[:, None], right[:, :-1]], axis=1)
            taps = [part.reshape(-1, part.shape[-1]) for part in (left, here, right)]
            lane = lax.broadcasted_iota(jnp.int32, (taps[0].shape[0], 128), 1)
            tail = jnp.where(lane < 32, taps[0][:, 128:], taps[1][:, 128:])
            tail = jnp.where(lane < 64, tail, taps[2][:, 128:])
            cells = jnp.concatenate([part[:, :128] for part in taps] + [tail], axis=1)
            at = (index * (band // 2) + parity) * row_cells
            ref[pl.ds(at, cells.shape[0])] = cells.astype(jnp.bfloat16)

    send_ref[pl.ds(sent, 16)] = labels.astype(jnp.bfloat16)
    rows, phases = bands * band // 2, phases // 2
    cells = rows * row_cells
    pre = dot_nn(odd_ref[pl.ds(0, cells)], first_w_ref[0])
    pre += dot_nn(even_ref[...], first_w_ref[1])
    pre += dot_nn(odd_ref[pl.ds(row_cells, cells)], first_w_ref[2])
    value, slope = silu_and_slope(pre)
    shape = (1, rows, phases, BLOCK, value.shape[-1])
    zero_row(first_ref)
    fill_map(first_ref, value.reshape(shape), 1)
    first_slope_ref[...] = slope.reshape(shape)

    rows, phases = rows // 2, phases // 2
    pre = None
    for tap in range(9):
        cells = map_tap(first_ref, tap // 3, tap % 3, rows, phases)
        part = dot_nn(cells, second_w_ref[tap])
        pre = part if pre is None else pre + part
    value, slope = silu_and_slope(pre)
    second_slope_ref[...] = slope.reshape(second_slope_ref.shape)
    send_ref[pl.ds(0, value.shape[0])] = value.astype(jnp.bfloat16)


def deep_kernel(
    batch,
    bands,
    slot_ref,
    got_ref,
    third_w_ref,
    fourth_w_ref,
    fourth_wt_ref,
    head_ref,
    third_delta_ref,
    fourth_taps_ref,
    fourth_flat_ref,
    head_grad_ref,
    third_grad_ref,
    second_ref,
    third_taps_ref,
    third_ref,
    third_slope_ref,
    fourth_delta_ref,
):
    samples = second_ref.shape[0]
    channels = got_ref.shape[2]
    rows, phases = 4 * bands, 4
    cells = rows * phases * BLOCK
    zero_row(second_ref)
    labels = []
    for sample in range(samples):
        slot = slot_ref[pl.program_id(0) * samples + sample]
        second = got_ref[slot, pl.ds(0, cells)].astype(jnp.float32)
        fill_map(
            second_ref.at[pl.ds(sample, 1)],
            second.reshape(1, rows, phases, BLOCK, channels),
            1,
        )
        label = got_ref[slot, pl.ds(cells, 16)].astype(jnp.float32)
        labels += [label[:BLOCK, index : index + 1] for index in range(bands)]
    labels = jnp.concatenate(labels, axis=0)

    rows, phases = rows // 2, phases // 2
    for tap in range(9):
        third_taps_ref[:, pl.ds(tap * channels, channels)] = map_tap(
            second_ref, tap // 3, tap % 3, rows, phases
        )
    value, slope = silu_and_slope(dot_nn(third_taps_ref[...], third_w_ref[...]))
    channels = value.shape[-1]
    zero_row(third_ref)
    fill_map(third_ref, value.reshape(samples, rows, phases, BLOCK, channels), 1)
    third_slope_ref[...] = slope.reshape(third_slope_ref.shape)

    rows, phases = rows // 2, phases // 2
    for tap in range(9):
        fourth_taps_ref[:, pl.ds(tap * channels, channels)] = map_tap(
            third_ref, tap // 3, tap % 3, rows, phases
        )
    value, slope = silu_and_slope(dot_nn(fourth_taps_ref[...], fourth_w_ref[...]))
    head = head_ref[...]
    logits = jnp.sum(value * head, axis=1, keepdims=True)
    logit_grad = (jax.nn.sigmoid(logits) - labels) / batch

    @pl.when(pl.program_id(0) == 0)
    def _():
        head_grad_ref[...] = jnp.zeros(head_grad_ref.shape, jnp.float32)
        third_grad_ref[...] = jnp.zeros(third_grad_ref.shape, jnp.float32)

    head_grad_ref[...] += jnp.sum(value * logit_grad, axis=0, keepdims=True)
    delta = rounded(logit_grad * head * slope)
    fourth_flat_ref[...] = delta.astype(jnp.bfloat16)
    last_row_zero(fourth_delta_ref)
    fill_delta(fourth_delta_ref, delta.reshape(samples, rows, phases, BLOCK, delta.shape[-1]))
    for row_parity in range(2):
        for col_parity in range(2):
            part = delta_parts(
                fourth_delta_ref, fourth_wt_ref, row_parity, col_parity, rows, phases
            )
            part = rounded(part * third_slope_ref[:, :, row_parity, :, col_parity])
            for row in range(rows):
                third_delta_ref[:, 2 * row + row_parity, col_parity] = part[:, row, 0]
    last_row_zero(third_delta_ref)
    delta = third_delta_ref[:, pl.ds(0, 2 * rows)]
    delta = delta.reshape(-1, delta.shape[-1]).astype(jnp.bfloat16)
    third_grad_ref[...] += dot_tn(third_taps_ref[...], delta)


def late_kernel(
    place_ref,
    third_delta_ref,
    third_wt_ref,
    second_wt_ref,
    even_ref,
    odd_ref,
    first_ref,
    first_slope_ref,
    second_slope_ref,
    out_ref,
    third_ref,
    second_ref,
    first_delta_ref,
):
    rows, phases = third_delta_ref.shape[1] - 1, third_delta_ref.shape[2]
    fill_delta(third_ref, third_delta_ref[...])
    last_row_zero(second_ref)
    for row_parity in range(2):
        for col_parity in range(2):
            part = delta_parts(third_ref, third_wt_ref, row_parity, col_parity, rows, phases)
            for row in range(rows):
                for phase in range(phases):
                    at = (slice(None), 2 * row + row_parity, 2 * phase + col_parity)
                    second_ref[at] = rounded(part[:, row, phase] * second_slope_ref[at])
    rows, phases = 2 * rows, 2 * phases
    second_ref[:, :, phases] = shift_block(second_ref[:, :, 0], -1)
    for row_parity in range(2):
        for col_parity in range(2):
            part = delta_parts(second_ref, second_wt_ref, row_parity, col_parity, rows, phases)
            for row in range(rows):
                for phase in range(phases):
                    at = (slice(None), 2 * row + row_parity, 2 * phase + col_parity)
                    first_delta_ref[at] = rounded(part[:, row, phase] * first_slope_ref[at])
    delta = second_ref[:, pl.ds(0, rows), pl.ds(0, phases)]
    delta = delta.reshape(-1, delta.shape[-1]).astype(jnp.bfloat16)
    depth = first_ref.shape[-1]
    base = out_ref.shape[0] - 9 * depth
    for tap in range(9):
        cells = map_tap(first_ref, tap // 3, tap % 3, rows, phases)
        out_ref[pl.ds(base + tap * depth, depth)] = dot_tn(cells, delta)
    delta = first_delta_ref[...]
    delta = delta.reshape(-1, delta.shape[-1]).astype(jnp.bfloat16)
    cells = delta.shape[0]
    row_cells = cells // (2 * rows)
    taps = (odd_ref[pl.ds(0, cells)], even_ref[...], odd_ref[pl.ds(row_cells, cells)])
    for tap in range(3):
        part = dot_tn(delta, taps[tap])
        for piece in range(part.shape[1] // 128):
            at = (tap * (part.shape[1] // 128) + piece) * depth
            out_ref[pl.ds(at, depth)] = part[:, piece * 128 : piece * 128 + 128]


def grads_kernel(fourth_taps_ref, fourth_flat_ref, out_ref):
    @pl.when(pl.program_id(1) == 0)
    def _():
        out_ref[...] = jnp.zeros(out_ref.shape, jnp.float32)

    out_ref[...] += dot_tn(fourth_taps_ref[...], fourth_flat_ref[...])


def finish_kernel(got_ref, temporal_ref, middle_ref):
    depth = temporal_ref.shape[2]
    base = 12 * depth
    middle_ref[...] = got_ref[pl.ds(base, middle_ref.shape[0])].astype(jnp.float32)
    for tap in range(3):
        parts = [
            got_ref[pl.ds((4 * tap + piece) * depth, depth)].astype(jnp.float32).T
            for piece in range(4)
        ]
        for col_tap in range(3):
            rest = temporal_ref.shape[1] - 128
            temporal_ref[3 * tap + col_tap, pl.ds(0, 128)] = parts[col_tap]
            temporal_ref[3 * tap + col_tap, pl.ds(128, rest)] = parts[3][
                col_tap * rest : col_tap * rest + rest
            ]


def cost(flops, size):
    return pl.CostEstimate(flops=flops, bytes_accessed=size, transcendentals=0)


def doubled(value, axis, bits):
    order = [0]
    for bit in bits:
        route = [(i, i ^ bit) for i in range(lax.axis_size(axis))]
        value = jnp.concatenate([value, lax.ppermute(value, axis, route)], axis=0)
        order = order + [m ^ bit for m in order]
    return value, order


def slots(axis, order):
    place = [order.index(i) for i in range(len(order))]
    table = jnp.asarray([[place[i ^ me] for i in range(len(order))] for me in range(len(order))])
    return lax.dynamic_index_in_dim(table.astype(jnp.int32), lax.axis_index(axis), 0, False)


def bits_of(size, descending):
    bits = [1 << k for k in range(size.bit_length() - 1)]
    return bits[::-1] if descending else bits


def summed_over_dp(partial, samples):
    rows, lanes = partial.shape
    share = -(-rows // (8 * samples)) * 8
    sent = jnp.pad(partial.astype(jnp.bfloat16), ((0, share * samples - rows), (0, 0)))
    sent = sent.reshape(samples, share, lanes)
    got = lax.all_to_all(sent, "dp", 0, 0)
    total = jnp.sum(got.astype(jnp.float32), axis=0).astype(jnp.bfloat16)
    sent = jnp.broadcast_to(total[None], got.shape)
    got = lax.all_to_all(sent, "dp", 0, 0)
    return got.reshape(samples * share, lanes)


def local(
    occupancy,
    state_labels,
    lift_weight,
    temporal_weight,
    middle_weight,
    deeper_weight,
    deepest_weight,
    head_weight,
):
    bands = lax.axis_size("space")
    samples = lax.axis_size("dp")
    _, frames, band, cols = occupancy.shape
    heights, lift_width = lift_weight.shape
    lift_all = frames * lift_width
    one, two = middle_weight.shape[2:]
    three, four = deepest_weight.shape[2:]
    f32 = jnp.float32
    phases = cols // BLOCK

    zero = jnp.zeros((), jnp.int32)
    label = lax.pad(state_labels[0], zero, ((0, BLOCK - 1, 0), (0, phases - 1, phases - 1)))
    lines = jnp.concatenate([occupancy.reshape(frames * band, cols), label], axis=0)
    lines, order = doubled(lines[None], "space", bits_of(bands, False))
    band_slots = slots("space", order)
    rest = lift_all - 128
    lift = jnp.pad(lift_weight, ((0, 16 - heights), (0, 0)))
    lift = jnp.einsum("ab,ck->acbk", jnp.eye(frames, dtype=lift.dtype), lift)
    lift = lift.reshape(frames * 16, lift_all)
    lift = jnp.concatenate([lift] + [lift[:, 128:]] * 2, axis=1)
    lift = jnp.pad(lift, ((0, 128 - frames * 16), (0, 128 - 3 * rest)))
    first_w = temporal_weight.reshape(3, 3, lift_all, one)
    first_w = jnp.concatenate(
        [
            first_w[:, :, :128].reshape(3, 384, one),
            first_w[:, :, 128:].reshape(3, 3 * rest, one),
            jnp.zeros((3, 128 - 3 * rest, one), first_w.dtype),
        ],
        axis=1,
    )
    second_w = middle_weight.reshape(9, one, two)
    third_w = deeper_weight.reshape(9, two, three)
    fourth_w = deepest_weight.reshape(9, three, four)
    head = head_weight.astype(f32).reshape(1, four)

    rows = bands * band
    vmem = pl.BlockSpec(memory_space=pltpu.VMEM)
    smem = pl.BlockSpec(memory_space=pltpu.SMEM)
    sent = rows // 4 * phases // 4 * BLOCK + 16
    payload, even, odd, first, first_slope, second_slope = pl.pallas_call(
        functools.partial(early_kernel, frames),
        out_shape=(
            jax.ShapeDtypeStruct((sent, two), jnp.bfloat16),
            jax.ShapeDtypeStruct((rows // 2 * cols // 2, 512), jnp.bfloat16),
            jax.ShapeDtypeStruct(((rows // 2 + 1) * cols // 2, 512), jnp.bfloat16),
            jax.ShapeDtypeStruct((1, rows // 4 + 1, 2, phases // 4 + 1, 2, BLOCK, one), f32),
            jax.ShapeDtypeStruct((1, rows // 2, phases // 2, BLOCK, one), f32),
            jax.ShapeDtypeStruct((1, rows // 4, phases // 4, BLOCK, two), f32),
        ),
        in_specs=[smem] + [vmem] * 4,
        out_specs=(vmem,) * 6,
        scratch_shapes=[pltpu.VMEM((band * 128, cols), jnp.bfloat16)],
        compiler_params=pltpu.CompilerParams(vmem_limit_bytes=56 * MIB),
        cost_estimate=cost(200_000_000, 4_000_000),
        name="early",
    )(band_slots, lines, lift, first_w, second_w)

    gathered, order = doubled(payload[None], "dp", bits_of(samples, True))
    sample_slots = slots("dp", order)

    chunk = max(1, min(samples, 32 // bands))
    steps = samples // chunk
    third_cells = 2 * bands * 2 * BLOCK
    fourth_cells = bands * BLOCK
    full = lambda *shape: pl.BlockSpec(shape, lambda i, slot: (0,) * len(shape))
    third_delta, fourth_taps, fourth_flat, head_grad, deeper_grad = pl.pallas_call(
        functools.partial(deep_kernel, samples, bands),
        grid_spec=pltpu.PrefetchScalarGridSpec(
            num_scalar_prefetch=1,
            grid=(steps,),
            in_specs=[
                full(samples, sent, two),
                full(9 * two, three),
                full(9 * three, four),
                full(9, three, four),
                full(1, four),
            ],
            out_specs=(
                pl.BlockSpec(
                    (chunk, 2 * bands + 1, 2, BLOCK, three), lambda i, slot: (i, 0, 0, 0, 0)
                ),
                pl.BlockSpec((chunk * fourth_cells, 9 * three), lambda i, slot: (i, 0)),
                pl.BlockSpec((chunk * fourth_cells, four), lambda i, slot: (i, 0)),
                full(1, four),
                full(9 * two, three),
            ),
            scratch_shapes=[
                pltpu.VMEM((chunk, 2 * bands + 1, 2, 3, 2, BLOCK, two), f32),
                pltpu.VMEM((chunk * third_cells, 9 * two), jnp.bfloat16),
                pltpu.VMEM((chunk, bands + 1, 2, 2, 2, BLOCK, three), f32),
                pltpu.VMEM((chunk, bands, 2, 1, 2, BLOCK, three), f32),
                pltpu.VMEM((chunk, bands + 1, 2, BLOCK, four), f32),
            ],
        ),
        out_shape=(
            jax.ShapeDtypeStruct((samples, 2 * bands + 1, 2, BLOCK, three), f32),
            jax.ShapeDtypeStruct((samples * fourth_cells, 9 * three), jnp.bfloat16),
            jax.ShapeDtypeStruct((samples * fourth_cells, four), jnp.bfloat16),
            jax.ShapeDtypeStruct((1, four), f32),
            jax.ShapeDtypeStruct((9 * two, three), f32),
        ),
        compiler_params=pltpu.CompilerParams(vmem_limit_bytes=56 * MIB),
        cost_estimate=cost(2_000_000_000, 12_000_000),
        name="deep",
    )(
        sample_slots,
        gathered,
        third_w.reshape(9 * two, three),
        fourth_w.reshape(9 * three, four),
        fourth_w,
        head,
    )

    place = lax.axis_index("dp").astype(jnp.int32).reshape(1)
    whole = lambda *shape: pl.BlockSpec(shape, lambda i, place: (0,) * len(shape))
    partial = pl.pallas_call(
        late_kernel,
        grid_spec=pltpu.PrefetchScalarGridSpec(
            num_scalar_prefetch=1,
            grid=(1,),
            in_specs=[
                pl.BlockSpec(
                    (1, 2 * bands + 1, 2, BLOCK, three), lambda i, place: (place[0], 0, 0, 0, 0)
                ),
                whole(*third_w.shape),
                whole(*second_w.shape),
                whole(*even.shape),
                whole(*odd.shape),
                whole(*first.shape),
                whole(*first_slope.shape),
                whole(*second_slope.shape),
            ],
            out_specs=whole(21 * one, two),
            scratch_shapes=[
                pltpu.VMEM((1, 2 * bands + 1, 3, BLOCK, three), f32),
                pltpu.VMEM((1, 4 * bands + 1, 5, BLOCK, two), f32),
                pltpu.VMEM(first_slope.shape, f32),
            ],
        ),
        out_shape=jax.ShapeDtypeStruct((21 * one, two), f32),
        compiler_params=pltpu.CompilerParams(vmem_limit_bytes=60 * MIB),
        cost_estimate=cost(200_000_000, 6_000_000),
        name="late",
    )(place, third_delta, third_w, second_w, even, odd, first, first_slope, second_slope)

    summed = summed_over_dp(partial, samples)

    deepest_grad = pl.pallas_call(
        grads_kernel,
        grid=(9, steps),
        out_shape=jax.ShapeDtypeStruct((9 * three, four), f32),
        in_specs=[
            pl.BlockSpec((chunk * fourth_cells, three), lambda t, i: (i, t)),
            pl.BlockSpec((chunk * fourth_cells, four), lambda t, i: (i, 0)),
        ],
        out_specs=pl.BlockSpec((three, four), lambda t, i: (t, 0)),
        compiler_params=pltpu.CompilerParams(vmem_limit_bytes=32 * MIB),
        cost_estimate=cost(600_000_000, 6_000_000),
        name="grads",
    )(fourth_taps, fourth_flat)
    temporal_grad, middle_grad = pl.pallas_call(
        finish_kernel,
        out_shape=(
            jax.ShapeDtypeStruct((9, lift_all, one), f32),
            jax.ShapeDtypeStruct((9 * one, two), f32),
        ),
        in_specs=[vmem],
        out_specs=(vmem, vmem),
        cost_estimate=cost(1_000_000, 1_500_000),
        name="finish",
    )(summed)
    return (
        temporal_grad.reshape(temporal_weight.shape),
        middle_grad.reshape(middle_weight.shape),
        deeper_grad.reshape(deeper_weight.shape),
        deepest_grad.reshape(deepest_weight.shape),
        head_grad.reshape(four),
    )


def solution(mesh):
    return jax.shard_map(
        local,
        mesh=mesh,
        in_specs=(
            P("dp", None, "space", None),
            P("dp", "space", None),
            P(),
            P(),
            P(),
            P(),
            P(),
            P(),
        ),
        out_specs=(P(), P(), P(), P(), P()),
        check_vma=False,
    )
```

time: 233 us -> 92.5 us (0.40)
  waiting for transfers between devices: 174 us -> 18.2 us
  blocking collectives: 0 us -> 17.9 us
  between operations: 14.2 us -> 0.79 us
  Pallas kernels: 20.4 us -> 27.1 us
  starting transfers between devices: 6.19 us -> 12.1 us
  local copies, waits for them, and re-layouts: 13.6 us -> 8.03 us
  other arithmetic: 3 us -> 7.66 us
    psum x1 -> x0, waiting for transfers between devices: 118 us -> none  [local(): summed = lax.psum(partial, ('dp', 'space'))]
    all_gather x1 -> x0, waiting for transfers between devices: 53.2 us -> none  [local(): gathered = lax.all_gather(payload, ('dp', 'space'), axis=0, tiled=False)]
    all_to_all x0 -> x1, blocking collectives: none -> 17.9 us  [summed_over_dp(): got = lax.all_to_all(sent, 'dp', 0, 0)]
    ppermute x2 -> x5, waiting for transfers between devices: 2.76 us -> 11.9 us  [doubled(): value = jnp.concatenate([value, lax.ppermute(value, axis, route)], axis=0)]
    all_to_all x0 -> x1, waiting for transfers between devices: none -> 6.31 us  [summed_over_dp(): got = lax.all_to_all(sent, 'dp', 0, 0)]
    unnamed x28 -> x18, local copies, waits for them, and re-layouts: 8.1 us -> 1.83 us
    pallas_call x3 -> x4, Pallas kernels: 17.7 us -> 22.7 us  [the longest x1 9.67 us: local(): pl.pallas_call(functools.partial(deep_kernel, samples, bands), grid_spec=...]
    concatenate x1 -> x6, other arithmetic: 0.92 us -> 5 us  [the longest x4 3.39 us: doubled(): value = jnp.concatenate([value, lax.ppermute(value, axis, route)], axis=0)]
  transfers between devices with their start and end apart: 4 -> 6, of which waited for: 3 -> 5; matrix products, arithmetic and copies ran while one was open for 2% -> 8% of each run, Pallas kernels for 3% -> 6%
where the time goes in v2:
time: 92.5 us; the launch traced here: 91.8 us
  Pallas kernels  27.1 us (29%)
  waiting for transfers between devices  18.2 us (20%)
  blocking collectives  17.9 us (19%)
  starting transfers between devices  12.1 us (13%)
  local copies, waits for them, and re-layouts  8.03 us (9%)
  other arithmetic  7.66 us (8%)
    all_to_all x1, blocking collectives, summed_over_dp(): got = lax.all_to_all(sent, 'dp', 0, 0)  17.9 us
    ppermute x5, waiting for transfers between devices, doubled(): value = jnp.concatenate([value, lax.ppermute(value, axis, route)], axis=0)  11.9 us
    pallas_call x1, Pallas kernels, local(): pl.pallas_call(functools.partial(deep_kernel, samples, bands), grid_spec=...  9.67 us
    ppermute x5, starting transfers between devices, doubled(): value = jnp.concatenate([value, lax.ppermute(value, axis, route)], axis=0)  8.57 us
    all_to_all x1, waiting for transfers between devices, summed_over_dp(): got = lax.all_to_all(sent, 'dp', 0, 0)  6.31 us
    pallas_call x1, Pallas kernels, local(): pl.pallas_call(functools.partial(early_kernel, frames), out_shape=(jax.Sh...  5.65 us
    pallas_call x1, Pallas kernels, local(): pl.pallas_call(grads_kernel, grid=(9, steps), out_shape=jax.ShapeDtypeStr...  5.3 us
    pallas_call x1, Pallas kernels, local(): pl.pallas_call(late_kernel, grid_spec=pltpu.PrefetchScalarGridSpec(num_sc...  4.38 us
  transfers between devices with their start and end apart: 6, of which 5 were waited for; matrix products, arithmetic and copies ran while one was open for 8% of the time, Pallas kernels for 6%

profile of v2, /device:TPU:0, one launch (start us, length us, event | category | flops | bytes accessed | tf_op | source)
XLA Modules:
  0.0 91.8 jit_solution(10696492027474585110)
XLA Ops:
  0.6 0.0 copy-start.6
  0.6 0.7 pad.15
  1.4 0.8 add_bitcast_fusion
  2.2 2.9 %collective-permute-start = (s32[1,88,128]{2,1,0:T(8,128)S(1)}, s32[1,88,128]{2,1,0:T(8,128)S(1)}, u32[]{:S(2)}, u32[]{:S(2)}) collective-permute-start(s32[1,88,128]{2,1,0:T(8,128)S(1)} %add_bitcast_fusion), channel_id=1, source_target_pairs={{0,1},{1,0},{2,3},{3,2},{4,5},{5,4},{6,7},{7,6},{8,9},{9,8},{10,11... | collective-permute-start | bytes 135176 | tf_op jit(solution)/shard_map/ppermute | solution.py:350
  5.1 0.9 slice.14
  6.0 1.0 %slice.13 = bf16[3,3,128,64]{3,2,1,0:T(8,128)(2,1)S(1)} slice(bf16[3,3,160,64]{3,2,1,0:T(8,128)(2,1)} %bitcast.40), slice={[0:3], [0:3], [0:128], [0:64]} | slice | bytes 294912 | tf_op jit(solution)/shard_map/slice | solution.py:412
  7.0 0.7 pad.16
  7.7 0.1 multiply_bitcast_fusion
  7.8 0.1 reshape.66
  7.9 0.7 fusion.8.lift_ref
  8.6 0.1 pad.30.clone
  8.7 0.0 copy-start.5
  8.7 0.9 maximum_maximum_fusion.first_w_ref
  9.6 0.0 copy-done.6
  9.6 0.5 dynamic-slice_bitcast_fusion.slot_ref
  10.1 0.0 collective-permute-done
  10.1 0.6 pad_add_fusion.got_ref
  10.8 5.7 %early.1 = (bf16[272,128]{1,0:T(8,128)(2,1)}, bf16[1024,512]{1,0:T(8,128)(2,1)}, bf16[1088,512]{1,0:T(8,128)(2,1)}, f32[1,9,2,5,2,8,64]{6,5,4,3,2,1,0:T(8,128)},...) custom-call(s32[2]{0:T(128)} %dynamic-slice_bitcast_fusion.slot_ref, s32[2,88,128]{2,1,0:T(8,128)} %pad_add_fusion.got_ref, ...), custom_call_target="tpu_custom_call" | custom-call | flops 200000000 | bytes 4000000 | tf_op jit(solution)/shard_map/early/pallas_call | solution.py:427
  16.4 0.0 copy-start.3
  16.4 2.6 %collective-permute-start.1 = (bf16[1,272,128]{2,1,0:T(8,128)(2,1)}, bf16[1,272,128]{2,1,0:T(8,128)(2,1)S(1)}, u32[]{:S(2)}, u32[]{:S(2)}) collective-permute-start(bf16[1,272,128]{2,1,0:T(8,128)(2,1)} %bitcast.33), channel_id=1, source_target_pairs={{0,16},{2,18},{4,20},{6,22},{8,24},{10,26},{12,28},{14,30},{16,0},... | collective-permute-start | bytes 208904 | tf_op jit(solution)/shard_map/ppermute | solution.py:350
  19.0 3.2 %collective-permute-done.1 = bf16[1,272,128]{2,1,0:T(8,128)(2,1)S(1)} collective-permute-done((bf16[1,272,128]{2,1,0:T(8,128)(2,1)}, bf16[1,272,128]{2,1,0:T(8,128)(2,1)S(1)}, u32[]{:S(2)}, u32[]{:S(2)}) %collective-permute-start.1) | collective-permute-done | bytes 69664 | tf_op jit(solution)/shard_map/ppermute | solution.py:350
  22.2 0.9 pad_maximum_fusion.2
  23.1 1.4 %collective-permute-start.2 = (bf16[2,272,128]{2,1,0:T(8,128)(2,1)S(1)}, bf16[2,272,128]{2,1,0:T(8,128)(2,1)S(1)}, u32[]{:S(2)}, u32[]{:S(2)}) collective-permute-start(bf16[2,272,128]{2,1,0:T(8,128)(2,1)S(1)} %pad_maximum_fusion.2), channel_id=1, source_target_pairs={{0,8},{2,10},{4,12},{6,14},{8,0},{10,2},{12,4},{14,6},{16,24},{18,... | collective-permute-start | bytes 417800 | tf_op jit(solution)/shard_map/ppermute | solution.py:350
  24.5 3.8 %collective-permute-done.2 = bf16[2,272,128]{2,1,0:T(8,128)(2,1)S(1)} collective-permute-done((bf16[2,272,128]{2,1,0:T(8,128)(2,1)S(1)}, bf16[2,272,128]{2,1,0:T(8,128)(2,1)S(1)}, u32[]{:S(2)}, u32[]{:S(2)}) %collective-permute-start.2) | collective-permute-done | bytes 139296 | tf_op jit(solution)/shard_map/ppermute | solution.py:350
  28.2 0.9 pad_maximum_fusion.1
  29.1 1.6 %collective-permute-start.3 = (bf16[4,272,128]{2,1,0:T(8,128)(2,1)S(1)}, bf16[4,272,128]{2,1,0:T(8,128)(2,1)S(1)}, u32[]{:S(2)}, u32[]{:S(2)}) collective-permute-start(bf16[4,272,128]{2,1,0:T(8,128)(2,1)S(1)} %pad_maximum_fusion.1), channel_id=1, source_target_pairs={{0,4},{2,6},{4,0},{6,2},{8,12},{10,14},{12,8},{14,10},{16,20},{18,... | collective-permute-start | bytes 835592 | tf_op jit(solution)/shard_map/ppermute | solution.py:350
  30.7 0.0 copy-done.5
  30.7 0.6 reshape.82
  31.3 1.3 %dynamic-slice_bitcast_fusion.1.slot_ref = s32[16]{0:T(128)} fusion(s32[16,16]{1,0:T(8,128)} %constant.30.clone, s32[]{:T(128)S(6)} %select_n.8), kind=kLoop, calls=%fused_computation.26 | loop fusion | bytes 132 | tf_op jit(solution)/shard_map/jit(dynamic_index_in_dim)/squeeze | solution.py:358
  32.6 3.1 %collective-permute-done.3 = bf16[4,272,128]{2,1,0:T(8,128)(2,1)S(1)} collective-permute-done((bf16[4,272,128]{2,1,0:T(8,128)(2,1)S(1)}, bf16[4,272,128]{2,1,0:T(8,128)(2,1)S(1)}, u32[]{:S(2)}, u32[]{:S(2)}) %collective-permute-start.3) | collective-permute-done | bytes 278560 | tf_op jit(solution)/shard_map/ppermute | solution.py:350
  35.8 0.9 %pad_maximum_fusion = bf16[8,272,128]{2,1,0:T(8,128)(2,1)S(1)} fusion(bf16[4,272,128]{2,1,0:T(8,128)(2,1)S(1)} %collective-permute-done.3, bf16[2,272,128]{2,1,0:T(8,128)(2,1)S(1)} %collective-permute-done.2, bf16[1,272,128]{2,1,0:T(8,128)(2,1)S(1)} %collective-permute-done.1, bf16[1,272,128]{2,1,0:T(8,128)(2,1)} %bitcast.36), kind=kLoop, calls=%fused_computation | loop fusion | flops 835584 | bytes 1114112 | tf_op jit(solution)/shard_map/concatenate | solution.py:350
  36.7 0.1 collective-permute-start.4
  36.8 0.0 copy-done.3
  36.9 1.8 %collective-permute-done.4 = bf16[8,272,128]{2,1,0:T(8,128)(2,1)S(1)} collective-permute-done((bf16[8,272,128]{2,1,0:T(8,128)(2,1)S(1)}, bf16[8,272,128]{2,1,0:T(8,128)(2,1)S(1)}, u32[]{:S(2)}, u32[]{:S(2)}) %collective-permute-start.4) | collective-permute-done | bytes 557088 | tf_op jit(solution)/shard_map/ppermute | solution.py:350
  38.7 0.1 constant_dynamic-update-slice_fusion.got_ref
  38.8 0.0 copy-start.4
  38.8 1.0 %copy-done.4 = bf16[16,272,128]{2,1,0:T(8,128)(2,1)} copy-done((bf16[16,272,128]{2,1,0:T(8,128)(2,1)}, bf16[16,272,128]{2,1,0:T(8,128)(2,1)S(1)}, u32[]{:S(2)}) %copy-start.4) | copy-done | bytes 1114136
  39.8 9.7 %deep.1 = (f32[16,5,2,8,256]{4,3,2,1,0:T(8,128)}, bf16[256,2304]{1,0:T(8,128)(2,1)}, bf16[256,512]{1,0:T(8,128)(2,1)}, f32[1,512]{1,0:T(1,128)}, f32[1152,256]{1,0:T(8,128)}) custom-call(s32[16]{0:T(128)} %dynamic-slice_bitcast_fusion.1.slot_ref, bf16[16,272,128]{2,1,0:T(8,128)(2,1)} %copy-done.4, bf16[1152,256]{1,0:T(8,128)(2,1)} %bitcast.37, ...), custom_call_target="tpu_custom_call" | custom-call | flops 2000000000 | bytes 12000000 | tf_op jit(solution)/shard_map/deep/pallas_call | solution.py:453
  49.5 4.4 %late.1 = f32[1344,128]{1,0:T(8,128)} custom-call(s32[1]{0:T(128)} %bitcast.place_ref, f32[16,5,2,8,256]{4,3,2,1,0:T(8,128)} %get-tuple-element.19.third_delta_ref, bf16[9,128,256]{2,1,0:T(8,128)(2,1)} %bitcast.38, bf16[9,64,128]{2,1,0:T(8,128)(2,1)} %bitcast.43, bf16[1024,512]{1,0:T(8,128)(2,1)} %get-tuple-element.20.even_ref, ...), custom_call_target="tpu_custom_call" | custom-call | flops 200000000 | bytes 6000000 | tf_op jit(solution)/shard_map/late/pallas_call | solution.py:503
  53.9 1.1 %convert_element_type.7 = bf16[1344,128]{1,0:T(8,128)(2,1)S(1)} convert(f32[1344,128]{1,0:T(8,128)} %late.1) | non-fusion elementwise | flops 172032 | bytes 1032192 | tf_op jit(solution)/shard_map/convert_element_type | solution.py:369
  55.0 0.0 copy-start
  55.0 0.0 copy-start.1
  55.0 17.9 %all_to_all.10 = bf16[16,88,128]{2,1,0:T(8,128)(2,1)S(1)} all-to-all(bf16[16,88,128]{2,1,0:T(8,128)(2,1)S(1)} %bitcast.31), channel_id=1, replica_groups=mesh['dp'=16,'space'=2] {'dp'}, dimensions={0} | all-to-all | bytes 720896 | tf_op jit(solution)/shard_map/all_to_all | solution.py:371
  72.9 0.1 reduce_sum.12
  73.0 0.8 broadcast_in_dim.18
  73.8 3.5 %all-to-all-start.1 = ((bf16[16,88,128]{2,1,0:T(8,128)(2,1)}), bf16[16,88,128]{2,1,0:T(8,128)(2,1)S(1)}, u32[]{:S(2)}, u32[]{:S(2)}) async-start(bf16[16,88,128]{2,1,0:T(8,128)(2,1)} %broadcast_in_dim.18), calls=%async_computation.1 | async-start | bytes 720896 | tf_op jit(solution)/shard_map/all_to_all | solution.py:374
  77.3 0.0 copy-done
  77.3 0.0 copy-done.1
  77.4 5.3 %grads.1 = f32[2304,512]{1,0:T(8,128)} custom-call(bf16[256,2304]{1,0:T(8,128)(2,1)S(1)} %copy-done, bf16[256,512]{1,0:T(8,128)(2,1)S(1)} %copy-done.1), custom_call_target="tpu_custom_call" | custom-call | flops 600000000 | bytes 6000000 | tf_op jit(solution)/shard_map/grads/pallas_call | solution.py:535
  82.7 6.3 %all-to-all-done.1 = bf16[16,88,128]{2,1,0:T(8,128)(2,1)S(1)} async-done(((bf16[16,88,128]{2,1,0:T(8,128)(2,1)}), bf16[16,88,128]{2,1,0:T(8,128)(2,1)S(1)}, u32[]{:S(2)}, u32[]{:S(2)}) %all-to-all-start.1) | async-done | bytes 360480 | tf_op jit(solution)/shard_map/all_to_all | solution.py:374
  89.0 0.0 copy-start.2
  89.0 0.7 copy-done.2
  89.7 2.1 %finish.1 = (f32[9,160,64]{2,1,0:T(8,128)}, f32[576,128]{1,0:T(8,128)}) custom-call(bf16[1408,128]{1,0:T(8,128)(2,1)} %bitcast.30), custom_call_target="tpu_custom_call" | custom-call | flops 1000000 | bytes 1500000 | tf_op jit(solution)/shard_map/finish/pallas_call | solution.py:548
  (8 shorter events, 0.1 us)
Async XLA Ops:
  0.6 9.0 %copy-start.6 = (s32[2,2]{1,0:T(2,128)S(1)}, s32[2,2]{1,0:T(2,128)}, u32[]{:S(2)}) copy-start(s32[2,2]{1,0:T(2,128)} %constant.29.clone) | copy-start | bytes 52
  2.2 8.0 %collective-permute-start = (s32[1,88,128]{2,1,0:T(8,128)S(1)}, s32[1,88,128]{2,1,0:T(8,128)S(1)}, u32[]{:S(2)}, u32[]{:S(2)}) collective-permute-start(s32[1,88,128]{2,1,0:T(8,128)S(1)} %add_bitcast_fusion), channel_id=1, source_target_pairs={{0,1},{1,0},{2,3},{3,2},{4,5},{5,4},{6,7},{7,6},{8,9},{9,8},{10,11... | collective-permute-start | bytes 135176 | tf_op jit(solution)/shard_map/ppermute | solution.py:350
  8.7 22.0 %copy-start.5 = (bf16[512]{0:T(512)(128)(2,1)S(1)}, bf16[512]{0:T(512)(128)(2,1)}, u32[]{:S(2)}) copy-start(bf16[512]{0:T(512)(128)(2,1)} %param.17) | copy-start | bytes 3076
  16.4 20.4 %copy-start.3 = (bf16[272,128]{1,0:T(8,128)(2,1)S(1)}, bf16[272,128]{1,0:T(8,128)(2,1)}, u32[]{:S(2)}) copy-start(bf16[272,128]{1,0:T(8,128)(2,1)} %get-tuple-element.18) | copy-start | bytes 208900
  16.4 5.8 %collective-permute-start.1 = (bf16[1,272,128]{2,1,0:T(8,128)(2,1)}, bf16[1,272,128]{2,1,0:T(8,128)(2,1)S(1)}, u32[]{:S(2)}, u32[]{:S(2)}) collective-permute-start(bf16[1,272,128]{2,1,0:T(8,128)(2,1)} %bitcast.33), channel_id=1, source_target_pairs={{0,16},{2,18},{4,20},{6,22},{8,24},{10,26},{12,28},{14,30},{16,0},... | collective-permute-start | bytes 208904 | tf_op jit(solution)/shard_map/ppermute | solution.py:350
  23.1 5.1 %collective-permute-start.2 = (bf16[2,272,128]{2,1,0:T(8,128)(2,1)S(1)}, bf16[2,272,128]{2,1,0:T(8,128)(2,1)S(1)}, u32[]{:S(2)}, u32[]{:S(2)}) collective-permute-start(bf16[2,272,128]{2,1,0:T(8,128)(2,1)S(1)} %pad_maximum_fusion.2), channel_id=1, source_target_pairs={{0,8},{2,10},{4,12},{6,14},{8,0},{10,2},{12,4},{14,6},{16,24},{18,... | collective-permute-start | bytes 417800 | tf_op jit(solution)/shard_map/ppermute | solution.py:350
  29.1 6.6 %collective-permute-start.3 = (bf16[4,272,128]{2,1,0:T(8,128)(2,1)S(1)}, bf16[4,272,128]{2,1,0:T(8,128)(2,1)S(1)}, u32[]{:S(2)}, u32[]{:S(2)}) collective-permute-start(bf16[4,272,128]{2,1,0:T(8,128)(2,1)S(1)} %pad_maximum_fusion.1), channel_id=1, source_target_pairs={{0,4},{2,6},{4,0},{6,2},{8,12},{10,14},{12,8},{14,10},{16,20},{18,... | collective-permute-start | bytes 835592 | tf_op jit(solution)/shard_map/ppermute | solution.py:350
  36.7 2.0 %collective-permute-start.4 = (bf16[8,272,128]{2,1,0:T(8,128)(2,1)S(1)}, bf16[8,272,128]{2,1,0:T(8,128)(2,1)S(1)}, u32[]{:S(2)}, u32[]{:S(2)}) collective-permute-start(bf16[8,272,128]{2,1,0:T(8,128)(2,1)S(1)} %pad_maximum_fusion), channel_id=1, source_target_pairs={{0,2},{2,0},{4,6},{6,4},{8,10},{10,8},{12,14},{14,12},{16,18},{18,... | collective-permute-start | bytes 1671176 | tf_op jit(solution)/shard_map/ppermute | solution.py:350
  38.8 1.0 %copy-start.4 = (bf16[16,272,128]{2,1,0:T(8,128)(2,1)}, bf16[16,272,128]{2,1,0:T(8,128)(2,1)S(1)}, u32[]{:S(2)}) copy-start(bf16[16,272,128]{2,1,0:T(8,128)(2,1)S(1)} %constant_dynamic-update-slice_fusion.got_ref) | copy-start | bytes 3342340
  55.0 22.3 %copy-start = (bf16[256,2304]{1,0:T(8,128)(2,1)S(1)}, bf16[256,2304]{1,0:T(8,128)(2,1)}, u32[]{:S(2)}) copy-start(bf16[256,2304]{1,0:T(8,128)(2,1)} %get-tuple-element.28.fourth_taps_ref) | copy-start | bytes 3538948
  55.0 22.3 %copy-start.1 = (bf16[256,512]{1,0:T(8,128)(2,1)S(1)}, bf16[256,512]{1,0:T(8,128)(2,1)}, u32[]{:S(2)}) copy-start(bf16[256,512]{1,0:T(8,128)(2,1)} %get-tuple-element.29.fourth_flat_ref) | copy-start | bytes 786436
  73.8 15.2 %all-to-all-start.1 = ((bf16[16,88,128]{2,1,0:T(8,128)(2,1)}), bf16[16,88,128]{2,1,0:T(8,128)(2,1)S(1)}, u32[]{:S(2)}, u32[]{:S(2)}) async-start(bf16[16,88,128]{2,1,0:T(8,128)(2,1)} %broadcast_in_dim.18), calls=%async_computation.1 | async-start | bytes 720896 | tf_op jit(solution)/shard_map/all_to_all | solution.py:374
  89.0 0.7 copy-start.2

commit v3 on v2

v3 whole, which is shorter than its diff:
```python
import functools

import jax
import jax.numpy as jnp
from jax import lax
from jax.experimental import pallas as pl
from jax.experimental.pallas import tpu as pltpu
from jax.sharding import PartitionSpec as P

BLOCK = 8
MIB = 1 << 20


def f32_dot(left, right, contract):
    return lax.dot_general(
        left, right, ((contract[0], contract[1]), ((), ())), preferred_element_type=jnp.float32
    )


def dot_nn(left, right):
    return f32_dot(left, right, ((1,), (0,)))


def dot_nt(left, right):
    return f32_dot(left, right, ((1,), (1,)))


def dot_tn(left, right):
    return f32_dot(left, right, ((0,), (0,)))


def rounded(value):
    return value.astype(jnp.bfloat16).astype(jnp.float32)


def silu_and_slope(pre):
    gate = jax.nn.sigmoid(pre)
    return rounded(pre * gate), gate * (1.0 + pre * (1.0 - gate))


def zero_row(ref):
    ref[:, 0, 0] = jnp.zeros(ref.shape[:1] + ref.shape[3:], ref.dtype)


def last_row_zero(ref):
    ref[:, ref.shape[1] - 1] = jnp.zeros(ref.shape[:1] + ref.shape[2:], ref.dtype)


def shift_block(value, step):
    shape = value.shape
    flat = value.reshape(-1, shape[-1])
    moved = pltpu.roll(flat, step % flat.shape[0], 0)
    index = lax.broadcasted_iota(jnp.int32, flat.shape, 0) % BLOCK
    edge = 0 if step > 0 else BLOCK - 1
    return jnp.where(index == edge, 0.0, moved).reshape(shape)


def fill_map(ref, value, offset):
    n, rows, phases, _, channels = value.shape
    split = value.reshape(n, rows, phases // 2, 2, BLOCK, channels)
    for row in range(rows):
        pair, parity = divmod(row + offset, 2)
        ref[:, pair, parity, pl.ds(0, phases // 2), 1] = split[:, row, :, 0]
        ref[:, pair, parity, pl.ds(1, phases // 2), 0] = split[:, row, :, 1]
        ref[:, pair, parity, 0, 0] = shift_block(split[:, row, phases // 2 - 1, 1], 1)


def map_tap(ref, row_tap, col_tap, out_rows, out_phases):
    cells = ref[
        :,
        pl.ds(row_tap // 2, out_rows),
        row_tap % 2,
        pl.ds(col_tap // 2, out_phases),
        col_tap % 2,
    ]
    return cells.reshape(-1, cells.shape[-1]).astype(jnp.bfloat16)


def fill_delta(ref, value):
    rows, phases = value.shape[1:3]
    ref[:, pl.ds(0, rows), pl.ds(0, phases)] = value
    ref[:, pl.ds(0, rows), phases] = shift_block(value[:, :, 0], -1)


def delta_parts(ref, weight_ref, row_parity, col_parity, rows, phases):
    taps = (((1, 0),), ((2, 0), (0, 1)))
    total = None
    for row_tap, row_step in taps[row_parity]:
        for col_tap, col_step in taps[col_parity]:
            cells = ref[:, pl.ds(row_step, rows), pl.ds(col_step, phases)]
            lead = cells.shape[:-1]
            flat = cells.reshape(-1, cells.shape[-1]).astype(jnp.bfloat16)
            part = dot_nn(flat, weight_ref[3 * row_tap + col_tap])
            total = part if total is None else total + part
    return total.reshape(*lead, total.shape[-1])


def early_kernel(frames, pieces, *refs):
    got_refs = refs[:pieces]
    label_refs = refs[pieces : 2 * pieces]
    (
        lift_ref,
        first_w_ref,
        second_w_ref,
        send_ref,
        even_ref,
        odd_ref,
        first_ref,
        first_slope_ref,
        second_slope_ref,
        bits_ref,
        lift_all_ref,
        first_all_ref,
    ) = refs[2 * pieces :]
    me = lax.axis_index("space")
    bands = 1 << (pieces - 1)
    _, _, band, cols = got_refs[0].shape
    phases = cols // BLOCK
    row_cells = cols // 2
    heights, width = lift_ref.shape
    rest = first_w_ref.shape[1] - 128

    tall = jnp.concatenate(
        [lift_ref[...].astype(jnp.float32), jnp.zeros((16 - heights, width), jnp.float32)], axis=0
    )
    tall = jnp.concatenate([tall] * (256 // width), axis=1)
    tall = jnp.concatenate([tall] * 8, axis=0)
    frame_of_row = lax.broadcasted_iota(jnp.int32, tall.shape, 0) // 16
    lane = lax.broadcasted_iota(jnp.int32, tall.shape, 1)
    frame_of_lane = jnp.minimum(lane // width, frames - 1)
    keep = (frame_of_row == frame_of_lane) & (lane < 128 + 3 * rest)
    lift_all_ref[...] = jnp.where(keep, tall, 0.0).astype(jnp.bfloat16)
    first_all_ref[...] = jnp.zeros(first_all_ref.shape, jnp.bfloat16)
    for tap in range(9):
        row_tap, col_tap = divmod(tap, 3)
        first_all_ref[row_tap, pl.ds(col_tap * 128, 128)] = first_w_ref[tap, pl.ds(0, 128)]
        first_all_ref[row_tap, pl.ds(384 + col_tap * rest, rest)] = first_w_ref[
            tap, pl.ds(128, rest)
        ]

    height = lax.broadcasted_iota(jnp.int32, (16, cols), 0)
    place = lax.broadcasted_iota(jnp.int32, (cols, cols), 0)
    column = lax.broadcasted_iota(jnp.int32, (cols, cols), 1)
    order = jnp.where(column == (place % BLOCK) * phases + place // BLOCK, 1.0, 0.0)
    order = order.astype(jnp.bfloat16)
    sent = (band // 4) * bands * (phases // 4) * BLOCK
    label_lane = lax.broadcasted_iota(jnp.int32, (16, send_ref.shape[1]), 1)
    label_row = lax.broadcasted_iota(jnp.int32, (16, BLOCK), 0)
    label_column = lax.broadcasted_iota(jnp.int32, (16, BLOCK), 1)
    labels = jnp.zeros((16, send_ref.shape[1]), jnp.float32)
    bits_ref[...] = jnp.zeros(bits_ref.shape, jnp.bfloat16)
    odd_ref[pl.ds(0, row_cells)] = jnp.zeros((row_cells, odd_ref.shape[1]), jnp.bfloat16)
    for slot in range(bands):
        index = me ^ slot
        piece = slot.bit_length()
        inner = slot - (1 << (piece - 1)) if slot else 0
        got_ref, label_ref = got_refs[piece], label_refs[piece]
        for row in range(band):
            for frame in range(frames):
                line = jnp.broadcast_to(got_ref[inner, frame, pl.ds(row, 1)], height.shape)
                bit = jnp.bitwise_and(jnp.right_shift(line, height), 1)
                bits_ref[pl.ds(row * 128 + frame * 16, 16)] = bit.astype(jnp.float32).astype(
                    jnp.bfloat16
                )
        label = jnp.broadcast_to(label_ref[inner].astype(jnp.float32), label_row.shape)
        label = jnp.sum(
            jnp.where(label_row == label_column, label, 0.0), axis=1, keepdims=True
        )
        labels += jnp.where(label_lane == index, label, 0.0)
        spread = dot_nt(order, bits_ref[...]).astype(jnp.bfloat16)
        stacked = jnp.concatenate(
            [spread[:, row * 128 : row * 128 + 128] for row in range(band)], axis=0
        )
        lifted = jnp.maximum(dot_nn(stacked, lift_all_ref[...]), 0.0)
        lifted = lifted.reshape(band // 2, 2, phases // 2, 2, BLOCK, lifted.shape[-1])
        for parity, ref in ((0, even_ref), (1, odd_ref)):
            here = lifted[:, parity, :, 0]
            right = lifted[:, parity, :, 1]
            left = jnp.concatenate([shift_block(right[:, -1], 1)[:, None], right[:, :-1]], axis=1)
            taps = [part.reshape(-1, part.shape[-1]) for part in (left, here, right)]
            lane = lax.broadcasted_iota(jnp.int32, (taps[0].shape[0], 128), 1)
            tail = jnp.where(lane < rest, taps[0][:, 128:], taps[1][:, 128:])
            tail = jnp.where(lane < 2 * rest, tail, taps[2][:, 128:])
            cells = jnp.concatenate([part[:, :128] for part in taps] + [tail], axis=1)
            at = pl.multiple_of((index * (band // 2) + parity) * row_cells, row_cells)
            ref[pl.ds(at, cells.shape[0])] = cells.astype(jnp.bfloat16)

    send_ref[pl.ds(sent, 16)] = labels.astype(jnp.bfloat16)
    rows, phases = bands * band // 2, phases // 2
    cells = rows * row_cells
    pre = dot_nn(odd_ref[pl.ds(0, cells)], first_all_ref[0])
    pre += dot_nn(even_ref[...], first_all_ref[1])
    pre += dot_nn(odd_ref[pl.ds(row_cells, cells)], first_all_ref[2])
    value, slope = silu_and_slope(pre)
    shape = (1, rows, phases, BLOCK, value.shape[-1])
    zero_row(first_ref)
    fill_map(first_ref, value.reshape(shape), 1)
    first_slope_ref[...] = slope.reshape(shape)

    rows, phases = rows // 2, phases // 2
    pre = None
    for tap in range(9):
        cells = map_tap(first_ref, tap // 3, tap % 3, rows, phases)
        part = dot_nn(cells, second_w_ref[tap])
        pre = part if pre is None else pre + part
    value, slope = silu_and_slope(pre)
    second_slope_ref[...] = slope.reshape(second_slope_ref.shape)
    send_ref[pl.ds(0, value.shape[0])] = value.astype(jnp.bfloat16)


def transpose_kernel(second_w_ref, third_w_ref, fourth_w_ref, second_ref, third_ref, fourth_ref):
    for tap in range(9):
        second_ref[tap] = second_w_ref[tap].T
        third_ref[tap] = third_w_ref[tap].T
        fourth_ref[tap] = fourth_w_ref[tap].T


def take_samples(near_ref, far_ref, second_ref, label_ref, bands):
    half = near_ref.shape[0]
    width = half.bit_length()
    chunk, channels = second_ref.shape[0], second_ref.shape[-1]
    rows, phases = 4 * bands, 4
    cells = rows * phases * BLOCK
    me = lax.axis_index("dp")
    for slot in range(2 * half):
        reverse = sum(((slot >> k) & 1) << (width - 1 - k) for k in range(width))
        sample = me ^ reverse
        ref = near_ref if slot < half else far_ref

        def take(ref=ref, inner=slot % half, place=sample % chunk):
            second = ref[inner, pl.ds(0, cells)].astype(jnp.float32)
            fill_map(
                second_ref.at[pl.ds(place, 1)],
                second.reshape(1, rows, phases, BLOCK, channels),
                1,
            )
            if label_ref is not None:
                label = ref[inner, pl.ds(cells, 16)].astype(jnp.float32)[:BLOCK]
                for index in range(bands):
                    label_ref[place, index] = jnp.broadcast_to(
                        label[:, index : index + 1], label.shape
                    )

        if chunk == 2 * half:
            take()
        else:
            pl.when(sample // chunk == pl.program_id(0))(take)


def third_taps(second_ref, taps_ref, rows, phases):
    channels = second_ref.shape[-1]
    for tap in range(9):
        taps_ref[:, pl.ds(tap * channels, channels)] = map_tap(
            second_ref, tap // 3, tap % 3, rows, phases
        )


def deep_kernel(
    batch,
    bands,
    near_ref,
    far_ref,
    third_w_ref,
    fourth_w_ref,
    fourth_wt_ref,
    head_ref,
    third_delta_ref,
    fourth_taps_ref,
    fourth_flat_ref,
    head_grad_ref,
    second_ref,
    label_ref,
    third_taps_ref,
    third_ref,
    third_slope_ref,
    fourth_delta_ref,
):
    samples = second_ref.shape[0]
    zero_row(second_ref)
    take_samples(near_ref, far_ref, second_ref, label_ref, bands)
    labels = label_ref[...].reshape(-1, label_ref.shape[-1])[:, :1]

    rows, phases = 2 * bands, 2
    third_taps(second_ref, third_taps_ref, rows, phases)
    value, slope = silu_and_slope(dot_nn(third_taps_ref[...], third_w_ref[...]))
    channels = value.shape[-1]
    zero_row(third_ref)
    fill_map(third_ref, value.reshape(samples, rows, phases, BLOCK, channels), 1)
    third_slope_ref[...] = slope.reshape(third_slope_ref.shape)

    rows, phases = rows // 2, phases // 2
    for tap in range(9):
        fourth_taps_ref[:, pl.ds(tap * channels, channels)] = map_tap(
            third_ref, tap // 3, tap % 3, rows, phases
        )
    value, slope = silu_and_slope(dot_nn(fourth_taps_ref[...], fourth_w_ref[...]))
    head = head_ref[...].astype(jnp.float32)
    logits = jnp.sum(value * head, axis=1, keepdims=True)
    logit_grad = (jax.nn.sigmoid(logits) - labels) / batch

    @pl.when(pl.program_id(0) == 0)
    def _():
        head_grad_ref[...] = jnp.zeros(head_grad_ref.shape, jnp.float32)

    head_grad_ref[...] += jnp.sum(value * logit_grad, axis=0, keepdims=True)
    delta = rounded(logit_grad * head * slope)
    fourth_flat_ref[...] = delta.astype(jnp.bfloat16)
    last_row_zero(fourth_delta_ref)
    fill_delta(fourth_delta_ref, delta.reshape(samples, rows, phases, BLOCK, delta.shape[-1]))
    for row_parity in range(2):
        for col_parity in range(2):
            part = delta_parts(
                fourth_delta_ref, fourth_wt_ref, row_parity, col_parity, rows, phases
            )
            part = rounded(part * third_slope_ref[:, :, row_parity, :, col_parity])
            for row in range(rows):
                third_delta_ref[:, 2 * row + row_parity, col_parity] = part[:, row, 0]
    last_row_zero(third_delta_ref)


def late_kernel(
    third_delta_ref,
    third_wt_ref,
    second_wt_ref,
    even_ref,
    odd_ref,
    first_ref,
    first_slope_ref,
    second_slope_ref,
    out_ref,
    third_ref,
    second_ref,
    first_delta_ref,
):
    sample = lax.axis_index("dp")
    rows, phases = third_delta_ref.shape[1] - 1, third_delta_ref.shape[2]
    fill_delta(third_ref, third_delta_ref[pl.ds(sample, 1)])
    last_row_zero(second_ref)
    for row_parity in range(2):
        for col_parity in range(2):
            part = delta_parts(third_ref, third_wt_ref, row_parity, col_parity, rows, phases)
            for row in range(rows):
                for phase in range(phases):
                    at = (slice(None), 2 * row + row_parity, 2 * phase + col_parity)
                    second_ref[at] = rounded(part[:, row, phase] * second_slope_ref[at])
    rows, phases = 2 * rows, 2 * phases

    @pl.when(lax.axis_index("space") != 0)
    def _():
        delta = second_ref[:, pl.ds(0, rows), pl.ds(0, phases)]
        delta = delta.reshape(-1, delta.shape[-1]).astype(jnp.bfloat16)
        depth = first_ref.shape[-1]
        for tap in range(9):
            cells = map_tap(first_ref, tap // 3, tap % 3, rows, phases)
            out_ref[pl.ds(tap * depth, depth)] = dot_tn(cells, delta).astype(jnp.bfloat16)
        left = out_ref.shape[0] - 9 * depth
        out_ref[pl.ds(9 * depth, left)] = jnp.zeros((left, out_ref.shape[1]), jnp.bfloat16)

    @pl.when(lax.axis_index("space") == 0)
    def _():
        second_ref[:, :, phases] = shift_block(second_ref[:, :, 0], -1)
        for row_parity in range(2):
            for col_parity in range(2):
                part = delta_parts(
                    second_ref, second_wt_ref, row_parity, col_parity, rows, phases
                )
                for row in range(rows):
                    for phase in range(phases):
                        at = (slice(None), 2 * row + row_parity, 2 * phase + col_parity)
                        first_delta_ref[at] = rounded(part[:, row, phase] * first_slope_ref[at])
        delta = first_delta_ref[...]
        delta = delta.reshape(-1, delta.shape[-1]).astype(jnp.bfloat16)
        cells, depth = delta.shape
        row_cells = cells // (2 * rows)
        taps = (odd_ref[pl.ds(0, cells)], even_ref[...], odd_ref[pl.ds(row_cells, cells)])
        for tap in range(3):
            part = dot_tn(delta, taps[tap]).astype(jnp.bfloat16)
            for piece in range(4):
                out_ref[pl.ds((4 * tap + piece) * depth, depth)] = part[
                    :, piece * 128 : piece * 128 + 128
                ]


def third_grad_kernel(
    bands, near_ref, far_ref, delta_ref, out_ref, second_ref, third_taps_ref
):
    zero_row(second_ref)
    take_samples(near_ref, far_ref, second_ref, None, bands)
    third_taps(second_ref, third_taps_ref, 2 * bands, 2)
    delta = delta_ref[:, pl.ds(0, 2 * bands)]
    delta = delta.reshape(-1, delta.shape[-1]).astype(jnp.bfloat16)

    @pl.when(pl.program_id(0) == 0)
    def _():
        out_ref[...] = jnp.zeros(out_ref.shape, jnp.float32)

    out_ref[...] += dot_tn(third_taps_ref[...], delta)


def fourth_grad_kernel(fourth_taps_ref, fourth_flat_ref, out_ref):
    @pl.when(pl.program_id(1) == 0)
    def _():
        out_ref[...] = jnp.zeros(out_ref.shape, jnp.float32)

    out_ref[...] += dot_tn(fourth_taps_ref[...], fourth_flat_ref[...])


def sum_kernel(got_ref, out_ref):
    total = got_ref[0].astype(jnp.float32)
    for index in range(1, got_ref.shape[0]):
        total += got_ref[index].astype(jnp.float32)
    total = total.astype(jnp.bfloat16)
    for index in range(out_ref.shape[0]):
        out_ref[index] = total


def finish_kernel(got_ref, temporal_ref, middle_ref, flat_ref):
    samples, _, share, lanes = got_ref.shape
    depth = temporal_ref.shape[2]
    for sample in range(samples):
        flat_ref[pl.ds(sample * share, share)] = got_ref[sample, 0].astype(jnp.float32)
        rows = min(share, middle_ref.shape[0] - sample * share)
        if rows > 0:
            middle_ref[pl.ds(sample * share, rows)] = got_ref[sample, 1].astype(jnp.float32)[:rows]
    rest = temporal_ref.shape[1] - 128
    for tap in range(3):
        parts = [flat_ref[pl.ds((4 * tap + piece) * depth, depth)].T for piece in range(4)]
        for col_tap in range(3):
            temporal_ref[3 * tap + col_tap, pl.ds(0, 128)] = parts[col_tap]
            temporal_ref[3 * tap + col_tap, pl.ds(128, rest)] = parts[3][
                col_tap * rest : col_tap * rest + rest
            ]


def cost(flops, size):
    return pl.CostEstimate(flops=flops, bytes_accessed=size, transcendentals=0)


def swapped(value, axis, bit):
    return lax.ppermute(value, axis, [(i, i ^ bit) for i in range(lax.axis_size(axis))])


def band_pieces(value, bands):
    pieces = [value]
    bit = 1
    while bit < bands:
        whole = pieces[0] if bit == 1 else jnp.concatenate(pieces, axis=0)
        pieces.append(swapped(whole, "space", bit))
        bit *= 2
    return pieces


def gathered_halves(value, samples):
    half = samples // 2
    near = jnp.zeros((half,) + value.shape[1:], value.dtype)
    near = lax.dynamic_update_slice(near, value, (0, 0, 0))
    count = 1
    while count < half:
        part = swapped(near[:count], "dp", half // count)
        near = lax.dynamic_update_slice(near, part, (count, 0, 0))
        count *= 2
    return near, swapped(near, "dp", 1)


def local(
    occupancy,
    state_labels,
    lift_weight,
    temporal_weight,
    middle_weight,
    deeper_weight,
    deepest_weight,
    head_weight,
):
    bands = lax.axis_size("space")
    samples = lax.axis_size("dp")
    _, frames, band, cols = occupancy.shape
    lift_all = frames * lift_weight.shape[1]
    one, two = middle_weight.shape[2:]
    three, four = deepest_weight.shape[2:]
    f32, bf16 = jnp.float32, jnp.bfloat16
    shaped = jax.ShapeDtypeStruct
    phases = cols // BLOCK
    rows = bands * band
    small = samples * bands <= 32
    vmem = pl.BlockSpec(memory_space=pltpu.VMEM)

    def grant(size):
        return pltpu.CompilerParams(vmem_limit_bytes=(size if small else 60) * MIB)

    lines = band_pieces(occupancy, bands)
    labels = band_pieces(state_labels, bands)
    first_w = temporal_weight.reshape(9, lift_all, one)
    second_w = middle_weight.reshape(9, one, two)
    third_w = deeper_weight.reshape(9, two, three)
    fourth_w = deepest_weight.reshape(9, three, four)
    head = head_weight.reshape(1, four)

    sent = rows // 4 * phases // 4 * BLOCK + 16
    payload, even, odd, first, first_slope, second_slope = pl.pallas_call(
        functools.partial(early_kernel, frames, len(lines)),
        out_shape=(
            shaped((sent, two), bf16),
            shaped((rows // 2 * cols // 2, 512), bf16),
            shaped(((rows // 2 + 1) * cols // 2, 512), bf16),
            shaped((1, rows // 4 + 1, 2, phases // 4 + 1, 2, BLOCK, one), f32),
            shaped((1, rows // 2, phases // 2, BLOCK, one), f32),
            shaped((1, rows // 4, phases // 4, BLOCK, two), f32),
        ),
        in_specs=[vmem] * (2 * len(lines) + 3),
        out_specs=(vmem,) * 6,
        scratch_shapes=[
            pltpu.VMEM((band * 128, cols), bf16),
            pltpu.VMEM((128, 256), bf16),
            pltpu.VMEM((3, 512, one), bf16),
        ],
        compiler_params=grant(24),
        cost_estimate=cost(200_000_000, 4_000_000),
        name="early",
    )(*lines, *labels, lift_weight, first_w, second_w)

    near, far = gathered_halves(payload[None], samples)

    second_wt, third_wt, fourth_wt = pl.pallas_call(
        transpose_kernel,
        out_shape=(
            shaped((9, two, one), bf16),
            shaped((9, three, two), bf16),
            shaped((9, four, three), bf16),
        ),
        in_specs=[vmem] * 3,
        out_specs=(vmem,) * 3,
        compiler_params=grant(16),
        cost_estimate=cost(10_000_000, 6_000_000),
        name="transpose",
    )(second_w, third_w, fourth_w)

    chunk = max(1, min(samples, 32 // bands))
    steps = samples // chunk
    third_cells = 2 * bands * 2 * BLOCK
    fourth_cells = bands * BLOCK
    full = lambda *shape: pl.BlockSpec(shape, lambda i: (0,) * len(shape))
    delta_block = pl.BlockSpec(
        (chunk, 2 * bands + 1, 2, BLOCK, three), lambda i: (i, 0, 0, 0, 0)
    )
    second_scratch = pltpu.VMEM((chunk, 2 * bands + 1, 2, 3, 2, BLOCK, two), f32)
    third_taps_scratch = pltpu.VMEM((chunk * third_cells, 9 * two), bf16)
    third_delta, fourth_taps, fourth_flat, head_grad = pl.pallas_call(
        functools.partial(deep_kernel, samples, bands),
        grid=(steps,),
        out_shape=(
            shaped((samples, 2 * bands + 1, 2, BLOCK, three), f32),
            shaped((samples * fourth_cells, 9 * three), bf16),
            shaped((samples * fourth_cells, four), bf16),
            shaped((1, four), f32),
        ),
        in_specs=[
            full(*near.shape),
            full(*far.shape),
            full(9 * two, three),
            full(9 * three, four),
            full(9, four, three),
            full(1, four),
        ],
        out_specs=(
            delta_block,
            pl.BlockSpec((chunk * fourth_cells, 9 * three), lambda i: (i, 0)),
            pl.BlockSpec((chunk * fourth_cells, four), lambda i: (i, 0)),
            full(1, four),
        ),
        scratch_shapes=[
            second_scratch,
            pltpu.VMEM((chunk, bands, BLOCK, two), f32),
            third_taps_scratch,
            pltpu.VMEM((chunk, bands + 1, 2, 2, 2, BLOCK, three), f32),
            pltpu.VMEM((chunk, bands, 2, 1, 2, BLOCK, three), f32),
            pltpu.VMEM((chunk, bands + 1, 2, BLOCK, four), f32),
        ],
        compiler_params=grant(40),
        cost_estimate=cost(1_300_000_000, 12_000_000),
        name="deep",
    )(
        near,
        far,
        third_w.reshape(9 * two, three),
        fourth_w.reshape(9 * three, four),
        fourth_wt,
        head,
    )

    share = 12 * one // samples
    partial = pl.pallas_call(
        late_kernel,
        out_shape=shaped((12 * one, two), bf16),
        in_specs=[vmem] * 8,
        out_specs=vmem,
        scratch_shapes=[
            pltpu.VMEM((1, 2 * bands + 1, 3, BLOCK, three), f32),
            pltpu.VMEM((1, 4 * bands + 1, 5, BLOCK, two), f32),
            pltpu.VMEM(first_slope.shape, f32),
        ],
        compiler_params=grant(24),
        cost_estimate=cost(200_000_000, 6_000_000),
        name="late",
    )(third_delta, third_wt, second_wt, even, odd, first, first_slope, second_slope)

    got = lax.all_to_all(partial.reshape(samples, share, two), "dp", 0, 0)
    total = pl.pallas_call(
        sum_kernel,
        out_shape=shaped((samples * bands, share, two), bf16),
        in_specs=[vmem],
        out_specs=vmem,
        cost_estimate=cost(100_000, 600_000),
        name="sum",
    )(got)
    got = lax.all_to_all(total, ("dp", "space"), 0, 0)

    deeper_grad = pl.pallas_call(
        functools.partial(third_grad_kernel, bands),
        grid=(steps,),
        out_shape=shaped((9 * two, three), f32),
        in_specs=[full(*near.shape), full(*far.shape), delta_block],
        out_specs=full(9 * two, three),
        scratch_shapes=[second_scratch, third_taps_scratch],
        compiler_params=grant(24),
        cost_estimate=cost(600_000_000, 6_000_000),
        name="third_grad",
    )(near, far, third_delta)
    deepest_grad = pl.pallas_call(
        fourth_grad_kernel,
        grid=(9, steps),
        out_shape=shaped((9 * three, four), f32),
        in_specs=[
            pl.BlockSpec((chunk * fourth_cells, three), lambda t, i: (i, t)),
            pl.BlockSpec((chunk * fourth_cells, four), lambda t, i: (i, 0)),
        ],
        out_specs=pl.BlockSpec((three, four), lambda t, i: (t, 0)),
        compiler_params=grant(16),
        cost_estimate=cost(600_000_000, 6_000_000),
        name="fourth_grad",
    )(fourth_taps, fourth_flat)
    temporal_grad, middle_grad = pl.pallas_call(
        finish_kernel,
        out_shape=(shaped((9, lift_all, one), f32), shaped((9 * one, two), f32)),
        in_specs=[vmem],
        out_specs=(vmem, vmem),
        scratch_shapes=[pltpu.VMEM((12 * one, two), f32)],
        compiler_params=grant(16),
        cost_estimate=cost(1_000_000, 1_500_000),
        name="finish",
    )(got.reshape(samples, bands, share, two))
    return (
        temporal_grad.reshape(temporal_weight.shape),
        middle_grad.reshape(middle_weight.shape),
        deeper_grad.reshape(deeper_weight.shape),
        deepest_grad.reshape(deepest_weight.shape),
        head_grad.reshape(four),
    )


def solution(mesh):
    return jax.shard_map(
        local,
        mesh=mesh,
        in_specs=(
            P("dp", None, "space", None),
            P("dp", "space", None),
            P(),
            P(),
            P(),
            P(),
            P(),
            P(),
        ),
        out_specs=(P(), P(), P(), P(), P()),
        check_vma=False,
    )
```

time: 92.5 us -> 74.4 us (0.80)
  other arithmetic: 7.66 us -> 0 us
  Pallas kernels: 27.1 us -> 20.6 us
  local copies, waits for them, and re-layouts: 8.03 us -> 5.48 us
  blocking collectives: 17.9 us -> 15.5 us
  waiting for transfers between devices: 18.2 us -> 19.8 us
    pallas_call x5 -> x8, Pallas kernels: 27.1 us -> 20.6 us  [the longest x1 5.29 us: local(): pl.pallas_call(fourth_grad_kernel, grid=(9, steps), out_shape=shaped((9 *...]
    concatenate x6 -> x0, other arithmetic: 5 us -> none  [the longest x4 3.39 us: doubled(): value = jnp.concatenate([value, lax.ppermute(value, axis, route)], axis=0)]
    ppermute x5 -> x6, waiting for transfers between devices: 11.9 us -> 15.6 us  [swapped(): lax.ppermute(value, axis, [(i, i ^ bit) for i in range(lax.axis_size(axis...]
    unnamed x18 -> x20, local copies, waits for them, and re-layouts: 1.83 us -> 5.3 us
    all_to_all x1, blocking collectives: 17.9 us -> 15.5 us  [local(): got = lax.all_to_all(partial.reshape(samples, share, two), 'dp', 0, 0)]
    all_to_all x1, waiting for transfers between devices: 6.31 us -> 4.13 us  [local(): got = lax.all_to_all(total, ('dp', 'space'), 0, 0)]
    slice x3 -> x2, local copies, waits for them, and re-layouts: 1.88 us -> 0.03 us  [gathered_halves(): part = swapped(near[:count], 'dp', half // count)]
    squeeze x2 -> x0, local copies, waits for them, and re-layouts: 1.8 us -> none  [slots(): lax.dynamic_index_in_dim(table.astype(jnp.int32), lax.axis_index(axis), 0...]
  transfers between devices with their start and end apart: 6 -> 7, of which waited for: 5 -> 6; matrix products, arithmetic and copies ran while one was open for 8% -> 0% of each run, Pallas kernels for 6% -> 11%
where the time goes in v3:
time: 74.4 us; the launch traced here: 73.7 us
  Pallas kernels  20.6 us (28%)
  waiting for transfers between devices  19.8 us (27%)
  blocking collectives  15.5 us (21%)
  starting transfers between devices  11.6 us (16%)
  local copies, waits for them, and re-layouts  5.48 us (7%)
  between operations  0.77 us (1%)
    ppermute x6, waiting for transfers between devices, swapped(): lax.ppermute(value, axis, [(i, i ^ bit) for i in range(lax.axis_size(axis...  15.6 us
    all_to_all x1, blocking collectives, local(): got = lax.all_to_all(partial.reshape(samples, share, two), 'dp', 0, 0)  15.5 us
    ppermute x6, starting transfers between devices, swapped(): lax.ppermute(value, axis, [(i, i ^ bit) for i in range(lax.axis_size(axis...  9.03 us
    unnamed x20, local copies, waits for them, and re-layouts  5.3 us
    pallas_call x1, Pallas kernels, local(): pl.pallas_call(fourth_grad_kernel, grid=(9, steps), out_shape=shaped((9 *...  5.29 us
    pallas_call x1, Pallas kernels, local(): pl.pallas_call(functools.partial(deep_kernel, samples, bands), grid=(step...  4.41 us
    all_to_all x1, waiting for transfers between devices, local(): got = lax.all_to_all(total, ('dp', 'space'), 0, 0)  4.13 us
    pallas_call x1, Pallas kernels, local(): pl.pallas_call(functools.partial(early_kernel, frames, len(lines)), out_s...  3.94 us
  transfers between devices with their start and end apart: 7, of which 6 were waited for; matrix products, arithmetic and copies ran while one was open for 0% of the time, Pallas kernels for 11%

profile of v3, /device:TPU:0, one launch (start us, length us, event | category | flops | bytes accessed | tf_op | source)
XLA Modules:
  0.0 73.7 jit_solution(11371783175121640301)
XLA Ops:
  0.6 3.0 %collective-permute-start = (s32[1,5,16,128]{3,2,1,0:T(8,128)}, s32[1,5,16,128]{3,2,1,0:T(8,128)S(1)}, u32[]{:S(2)}, u32[]{:S(2)}) collective-permute-start(s32[1,5,16,128]{3,2,1,0:T(8,128)} %refs_0_.1), channel_id=1, source_target_pairs={{0,1},{1,0},{2,3},{3,2},{4,5},{5,4},{6,7},{7,6},{8,9},{9,8},{10,11... | collective-permute-start | bytes 122888 | tf_op jit(solution)/shard_map/ppermute | solution.py:440
  3.6 0.1 collective-permute-start.1
  3.7 3.6 %collective-permute-done.1.refs_3_ = s32[1,1,8]{2,1,0:T(1,128)S(1)} collective-permute-done((s32[1,1,8]{2,1,0:T(1,128)}, s32[1,1,8]{2,1,0:T(1,128)S(1)}, u32[]{:S(2)}, u32[]{:S(2)}) %collective-permute-start.1) | collective-permute-done | bytes 64 | tf_op jit(solution)/shard_map/ppermute | solution.py:440
  7.3 0.0 collective-permute-done.refs_1_
  7.3 0.0 copy-start.4
  7.3 0.9 %copy-done.4 = bf16[3,3,64,128]{3,2,1,0:T(8,128)(2,1)S(1)} copy-done((bf16[3,3,64,128]{3,2,1,0:T(8,128)(2,1)S(1)}, bf16[3,3,64,128]{3,2,1,0:T(8,128)(2,1)}, u32[]{:S(2)}) %copy-start.4) | copy-done | bytes 147480
  8.2 0.0 copy-start.5
  8.2 1.0 %copy-done.5 = bf16[3,3,5,32,64]{4,3,2,1,0:T(8,128)(2,1)S(1)} copy-done((bf16[3,3,5,32,64]{4,3,2,1,0:T(8,128)(2,1)S(1)}, bf16[3,3,5,32,64]{4,3,2,1,0:T(8,128)(2,1)}, u32[]{:S(2)}) %copy-start.5) | copy-done | bytes 184344
  9.2 0.0 copy-start.6
  9.2 0.8 %copy-done.6 = s32[1,5,16,128]{3,2,1,0:T(8,128)S(1)} copy-done((s32[1,5,16,128]{3,2,1,0:T(8,128)S(1)}, s32[1,5,16,128]{3,2,1,0:T(8,128)}, u32[]{:S(2)}) %copy-start.6) | copy-done | bytes 40984
  10.0 0.0 copy-start.7
  10.0 0.7 copy-done.7
  10.7 0.0 copy-start.8
  10.7 0.7 copy-done.8
  11.3 0.0 copy-start.1
  11.3 3.9 %early.1 = (bf16[272,128]{1,0:T(8,128)(2,1)S(1)}, bf16[1024,512]{1,0:T(8,128)(2,1)S(1)}, bf16[1088,512]{1,0:T(8,128)(2,1)S(1)}, f32[1,9,2,5,2,8,64]{6,5,4,3,2,1,...) custom-call(s32[1,5,16,128]{3,2,1,0:T(8,128)S(1)} %copy-done.6, ...), custom_call_target="tpu_custom_call" | custom-call | flops 200000000 | bytes 4000000 | tf_op jit(solution)/shard_map/early/pallas_call | solution.py:500
  15.3 0.0 copy-start.9
  15.3 0.0 copy-start
  15.3 2.7 %collective-permute-start.2 = (bf16[1,272,128]{2,1,0:T(8,128)(2,1)S(1)}, bf16[1,272,128]{2,1,0:T(8,128)(2,1)S(1)}, u32[]{:S(2)}, u32[]{:S(2)}) collective-permute-start(bf16[1,272,128]{2,1,0:T(8,128)(2,1)S(1)} %bitcast.22), channel_id=1, source_target_pairs={{0,16},{2,18},{4,20},{6,22},{8,24},{10,26},{12,28},{14,30},{16,0},... | collective-permute-start | bytes 208904 | tf_op jit(solution)/shard_map/ppermute | solution.py:440
  18.0 0.1 dynamic_update_slice.12
  18.0 2.5 %collective-permute-done.2 = bf16[1,272,128]{2,1,0:T(8,128)(2,1)S(1)} collective-permute-done((bf16[1,272,128]{2,1,0:T(8,128)(2,1)S(1)}, bf16[1,272,128]{2,1,0:T(8,128)(2,1)S(1)}, u32[]{:S(2)}, u32[]{:S(2)}) %collective-permute-start.2) | collective-permute-done | bytes 69664 | tf_op jit(solution)/shard_map/ppermute | solution.py:440
  20.6 1.6 %collective-permute-start.3 = (bf16[2,272,128]{2,1,0:T(8,128)(2,1)S(1)}, bf16[2,272,128]{2,1,0:T(8,128)(2,1)S(1)}, u32[]{:S(2)}, u32[]{:S(2)}) collective-permute-start(bf16[2,272,128]{2,1,0:T(8,128)(2,1)S(1)} %slice.9), channel_id=1, source_target_pairs={{0,8},{2,10},{4,12},{6,14},{8,0},{10,2},{12,4},{14,6},{16,24},{18,... | collective-permute-start | bytes 417800 | tf_op jit(solution)/shard_map/ppermute | solution.py:440
  22.3 3.5 %collective-permute-done.3 = bf16[2,272,128]{2,1,0:T(8,128)(2,1)S(1)} collective-permute-done((bf16[2,272,128]{2,1,0:T(8,128)(2,1)S(1)}, bf16[2,272,128]{2,1,0:T(8,128)(2,1)S(1)}, u32[]{:S(2)}, u32[]{:S(2)}) %collective-permute-start.3) | collective-permute-done | bytes 139296 | tf_op jit(solution)/shard_map/ppermute | solution.py:440
  25.8 1.6 %collective-permute-start.4 = (bf16[4,272,128]{2,1,0:T(8,128)(2,1)S(1)}, bf16[4,272,128]{2,1,0:T(8,128)(2,1)S(1)}, u32[]{:S(2)}, u32[]{:S(2)}) collective-permute-start(bf16[4,272,128]{2,1,0:T(8,128)(2,1)S(1)} %slice.10), channel_id=1, source_target_pairs={{0,4},{2,6},{4,0},{6,2},{8,12},{10,14},{12,8},{14,10},{16,20},{18,... | collective-permute-start | bytes 835592 | tf_op jit(solution)/shard_map/ppermute | solution.py:440
  27.4 5.0 %collective-permute-done.4 = bf16[4,272,128]{2,1,0:T(8,128)(2,1)S(1)} collective-permute-done((bf16[4,272,128]{2,1,0:T(8,128)(2,1)S(1)}, bf16[4,272,128]{2,1,0:T(8,128)(2,1)S(1)}, u32[]{:S(2)}, u32[]{:S(2)}) %collective-permute-start.4) | collective-permute-done | bytes 278560 | tf_op jit(solution)/shard_map/ppermute | solution.py:440
  32.4 0.1 collective-permute-start.5
  32.5 0.0 copy-done.9
  32.5 0.0 copy-done.1
  32.6 0.0 copy-done
  32.6 0.9 %transpose.1 = (bf16[9,128,64]{2,1,0:T(8,128)(2,1)S(1)}, bf16[9,256,128]{2,1,0:T(8,128)(2,1)S(1)}, bf16[9,512,256]{2,1,0:T(8,128)(2,1)S(1)}) custom-call(bf16[9,64,128]{2,1,0:T(8,128)(2,1)S(1)} %bitcast.21, bf16[9,128,256]{2,1,0:T(8,128)(2,1)S(1)} %bitcast.16, bf16[9,256,512]{2,1,0:T(8,128)(2,1)S(1)} %bitcast.14), custom_call_target="tpu_custom_call" | custom-call | flops 10000000 | bytes 6000000 | tf_op jit(solution)/shard_map/transpose/pallas_call | solution.py:524
  33.5 1.0 %collective-permute-done.5.far_ref = bf16[8,272,128]{2,1,0:T(8,128)(2,1)S(1)} collective-permute-done((bf16[8,272,128]{2,1,0:T(8,128)(2,1)S(1)}, bf16[8,272,128]{2,1,0:T(8,128)(2,1)S(1)}, u32[]{:S(2)}, u32[]{:S(2)}) %collective-permute-start.5) | collective-permute-done | bytes 557088 | tf_op jit(solution)/shard_map/ppermute | solution.py:440
  34.5 4.4 %deep.1 = (f32[16,5,2,8,256]{4,3,2,1,0:T(8,128)S(1)}, bf16[256,2304]{1,0:T(8,128)(2,1)S(1)}, bf16[256,512]{1,0:T(8,128)(2,1)S(1)}, f32[1,512]{1,0:T(1,128)}) custom-call(bf16[8,272,128]{2,1,0:T(8,128)(2,1)S(1)} %constant_dynamic-update-slice_fusion.near_ref, bf16[8,272,128]{2,1,0:T(8,128)(2,1)S(1)} %collective-permute-done.5.far_ref, ...), custom_call_target="tpu_custom_call" | custom-call | flops 1300000000 | bytes 12000000 | tf_op jit(solution)/shard_map/deep/pallas_call | solution.py:548
  38.9 0.0 copy-start.2
  38.9 1.2 %late.1 = bf16[768,128]{1,0:T(8,128)(2,1)S(1)} custom-call(f32[16,5,2,8,256]{4,3,2,1,0:T(8,128)S(1)} %get-tuple-element.22.third_delta_ref.delta_ref, bf16[9,256,128]{2,1,0:T(8,128)(2,1)S(1)} %get-tuple-element.23.third_wt_ref, bf16[9,128,64]{2,1,0:T(8,128)(2,1)S(1)} %get-tuple-element.24.second_wt_ref, bf16[1024,512]{1,0:T(8,128)(2,1)S(1)} %get-tuple-element.25.even_ref, ...), custom_call_target="tpu_custom_call" | custom-call | flops 200000000 | bytes 6000000 | tf_op jit(solution)/shard_map/late/pallas_call | solution.py:592
  40.1 0.0 copy-done.2
  40.1 15.5 %all_to_all.10.got_ref = bf16[16,48,128]{2,1,0:T(8,128)(2,1)} all-to-all(bf16[16,48,128]{2,1,0:T(8,128)(2,1)S(1)} %bitcast.19), channel_id=1, replica_groups=mesh['dp'=16,'space'=2] {'dp'}, dimensions={0} | all-to-all | bytes 393216 | tf_op jit(solution)/shard_map/all_to_all | solution.py:607
  55.6 1.7 %sum.1 = bf16[32,48,128]{2,1,0:T(8,128)(2,1)} custom-call(bf16[16,48,128]{2,1,0:T(8,128)(2,1)} %all_to_all.10.got_ref), custom_call_target="tpu_custom_call" | custom-call | flops 100000 | bytes 600000 | tf_op jit(solution)/shard_map/sum/pallas_call | solution.py:608
  57.3 2.6 %all-to-all-start.1 = ((bf16[32,48,128]{2,1,0:T(8,128)(2,1)}), bf16[32,48,128]{2,1,0:T(8,128)(2,1)S(1)}, u32[]{:S(2)}, u32[]{:S(2)}) async-start(bf16[32,48,128]{2,1,0:T(8,128)(2,1)} %sum.1), calls=%async_computation.1 | async-start | bytes 786432 | tf_op jit(solution)/shard_map/all_to_all | solution.py:616
  59.9 0.0 copy-start.3
  59.9 1.3 %copy-done.3 = bf16[256,2304]{1,0:T(8,128)(2,1)S(1)} copy-done((bf16[256,2304]{1,0:T(8,128)(2,1)S(1)}, bf16[256,2304]{1,0:T(8,128)(2,1)}, u32[]{:S(2)}) %copy-start.3) | copy-done | bytes 1179672
  61.2 5.3 %fourth_grad.1 = f32[2304,512]{1,0:T(8,128)} custom-call(bf16[256,2304]{1,0:T(8,128)(2,1)S(1)} %copy-done.3, bf16[256,512]{1,0:T(8,128)(2,1)S(1)} %get-tuple-element.33.fourth_flat_ref), custom_call_target="tpu_custom_call" | custom-call | flops 600000000 | bytes 6000000 | tf_op jit(solution)/shard_map/fourth_grad/pallas_call | solution.py:629
  66.5 2.1 %third_grad.1 = f32[1152,256]{1,0:T(8,128)} custom-call(bf16[8,272,128]{2,1,0:T(8,128)(2,1)S(1)} %constant_dynamic-update-slice_fusion.near_ref, bf16[8,272,128]{2,1,0:T(8,128)(2,1)S(1)} %collective-permute-done.5.far_ref, f32[16,5,2,8,256]{4,3,2,1,0:T(8,128)S(1)} %get-tuple-element.22.third_delta_ref.delta_ref), custom_call_target="tpu_custom_call" | custom-call | flops 600000000 | bytes 6000000 | tf_op jit(solution)/shard_map/third_grad/pallas_call | solution.py:618
  68.5 4.1 %all-to-all-done.1 = bf16[32,48,128]{2,1,0:T(8,128)(2,1)S(1)} async-done(((bf16[32,48,128]{2,1,0:T(8,128)(2,1)}), bf16[32,48,128]{2,1,0:T(8,128)(2,1)S(1)}, u32[]{:S(2)}, u32[]{:S(2)}) %all-to-all-start.1) | async-done | bytes 393248 | tf_op jit(solution)/shard_map/all_to_all | solution.py:616
  72.6 1.1 %finish.1 = (f32[9,160,64]{2,1,0:T(8,128)}, f32[576,128]{1,0:T(8,128)}) custom-call(bf16[16,2,48,128]{3,2,1,0:T(8,128)(2,1)S(1)} %bitcast.18), custom_call_target="tpu_custom_call" | custom-call | flops 1000000 | bytes 1500000 | tf_op jit(solution)/shard_map/finish/pallas_call | solution.py:642
  (6 shorter events, 0.1 us)
Async XLA Ops:
  0.6 6.7 %collective-permute-start = (s32[1,5,16,128]{3,2,1,0:T(8,128)}, s32[1,5,16,128]{3,2,1,0:T(8,128)S(1)}, u32[]{:S(2)}, u32[]{:S(2)}) collective-permute-start(s32[1,5,16,128]{3,2,1,0:T(8,128)} %refs_0_.1), channel_id=1, source_target_pairs={{0,1},{1,0},{2,3},{3,2},{4,5},{5,4},{6,7},{7,6},{8,9},{9,8},{10,11... | collective-permute-start | bytes 122888 | tf_op jit(solution)/shard_map/ppermute | solution.py:440
  3.6 3.7 %collective-permute-start.1 = (s32[1,1,8]{2,1,0:T(1,128)}, s32[1,1,8]{2,1,0:T(1,128)S(1)}, u32[]{:S(2)}, u32[]{:S(2)}) collective-permute-start(s32[1,1,8]{2,1,0:T(1,128)} %refs_2_.1), channel_id=1, source_target_pairs={{0,1},{1,0},{2,3},{3,2},{4,5},{5,4},{6,7},{7,6},{8,9},{9,8},{10,11... | collective-permute-start | bytes 104 | tf_op jit(solution)/shard_map/ppermute | solution.py:440
  7.3 0.9 %copy-start.4 = (bf16[3,3,64,128]{3,2,1,0:T(8,128)(2,1)S(1)}, bf16[3,3,64,128]{3,2,1,0:T(8,128)(2,1)}, u32[]{:S(2)}) copy-start(bf16[3,3,64,128]{3,2,1,0:T(8,128)(2,1)} %param.12) | copy-start | bytes 442372
  8.2 1.0 %copy-start.5 = (bf16[3,3,5,32,64]{4,3,2,1,0:T(8,128)(2,1)S(1)}, bf16[3,3,5,32,64]{4,3,2,1,0:T(8,128)(2,1)}, u32[]{:S(2)}) copy-start(bf16[3,3,5,32,64]{4,3,2,1,0:T(8,128)(2,1)} %param.11) | copy-start | bytes 552964
  9.2 0.8 %copy-start.6 = (s32[1,5,16,128]{3,2,1,0:T(8,128)S(1)}, s32[1,5,16,128]{3,2,1,0:T(8,128)}, u32[]{:S(2)}) copy-start(s32[1,5,16,128]{3,2,1,0:T(8,128)} %refs_0_.1) | copy-start | bytes 122884
  10.0 0.7 copy-start.7
  10.7 0.7 copy-start.8
  11.3 21.2 %copy-start.1 = (bf16[3,3,128,256]{3,2,1,0:T(8,128)(2,1)S(1)}, bf16[3,3,128,256]{3,2,1,0:T(8,128)(2,1)}, u32[]{:S(2)}) copy-start(bf16[3,3,128,256]{3,2,1,0:T(8,128)(2,1)} %param.13) | copy-start | bytes 1769476
  15.3 17.2 %copy-start.9 = (bf16[512]{0:T(512)(128)(2,1)S(1)}, bf16[512]{0:T(512)(128)(2,1)}, u32[]{:S(2)}) copy-start(bf16[512]{0:T(512)(128)(2,1)} %param.15) | copy-start | bytes 3076
  15.3 17.3 %copy-start = (bf16[3,3,256,512]{3,2,1,0:T(8,128)(2,1)S(1)}, bf16[3,3,256,512]{3,2,1,0:T(8,128)(2,1)}, u32[]{:S(2)}) copy-start(bf16[3,3,256,512]{3,2,1,0:T(8,128)(2,1)} %param.14) | copy-start | bytes 7077892
  15.3 5.3 %collective-permute-start.2 = (bf16[1,272,128]{2,1,0:T(8,128)(2,1)S(1)}, bf16[1,272,128]{2,1,0:T(8,128)(2,1)S(1)}, u32[]{:S(2)}, u32[]{:S(2)}) collective-permute-start(bf16[1,272,128]{2,1,0:T(8,128)(2,1)S(1)} %bitcast.22), channel_id=1, source_target_pairs={{0,16},{2,18},{4,20},{6,22},{8,24},{10,26},{12,28},{14,30},{16,0},... | collective-permute-start | bytes 208904 | tf_op jit(solution)/shard_map/ppermute | solution.py:440
  20.6 5.1 %collective-permute-start.3 = (bf16[2,272,128]{2,1,0:T(8,128)(2,1)S(1)}, bf16[2,272,128]{2,1,0:T(8,128)(2,1)S(1)}, u32[]{:S(2)}, u32[]{:S(2)}) collective-permute-start(bf16[2,272,128]{2,1,0:T(8,128)(2,1)S(1)} %slice.9), channel_id=1, source_target_pairs={{0,8},{2,10},{4,12},{6,14},{8,0},{10,2},{12,4},{14,6},{16,24},{18,... | collective-permute-start | bytes 417800 | tf_op jit(solution)/shard_map/ppermute | solution.py:440
  25.8 6.6 %collective-permute-start.4 = (bf16[4,272,128]{2,1,0:T(8,128)(2,1)S(1)}, bf16[4,272,128]{2,1,0:T(8,128)(2,1)S(1)}, u32[]{:S(2)}, u32[]{:S(2)}) collective-permute-start(bf16[4,272,128]{2,1,0:T(8,128)(2,1)S(1)} %slice.10), channel_id=1, source_target_pairs={{0,4},{2,6},{4,0},{6,2},{8,12},{10,14},{12,8},{14,10},{16,20},{18,... | collective-permute-start | bytes 835592 | tf_op jit(solution)/shard_map/ppermute | solution.py:440
  32.4 2.0 %collective-permute-start.5 = (bf16[8,272,128]{2,1,0:T(8,128)(2,1)S(1)}, bf16[8,272,128]{2,1,0:T(8,128)(2,1)S(1)}, u32[]{:S(2)}, u32[]{:S(2)}) collective-permute-start(bf16[8,272,128]{2,1,0:T(8,128)(2,1)S(1)} %constant_dynamic-update-slice_fusion.near_ref), channel_id=1, source_target_pairs={{0,2},{2,0},{4,6},{6,4},{8,10},{10,8},{12,14},{14,12},{16,18},{18,... | collective-permute-start | bytes 1671176 | tf_op jit(solution)/shard_map/ppermute | solution.py:440
  38.9 1.2 %copy-start.2 = (bf16[256,2304]{1,0:T(8,128)(2,1)}, bf16[256,2304]{1,0:T(8,128)(2,1)S(1)}, u32[]{:S(2)}) copy-start(bf16[256,2304]{1,0:T(8,128)(2,1)S(1)} %get-tuple-element.32.fourth_taps_ref) | copy-start | bytes 3538948
  57.3 15.4 %all-to-all-start.1 = ((bf16[32,48,128]{2,1,0:T(8,128)(2,1)}), bf16[32,48,128]{2,1,0:T(8,128)(2,1)S(1)}, u32[]{:S(2)}, u32[]{:S(2)}) async-start(bf16[32,48,128]{2,1,0:T(8,128)(2,1)} %sum.1), calls=%async_computation.1 | async-start | bytes 786432 | tf_op jit(solution)/shard_map/all_to_all | solution.py:616
  59.9 1.3 %copy-start.3 = (bf16[256,2304]{1,0:T(8,128)(2,1)S(1)}, bf16[256,2304]{1,0:T(8,128)(2,1)}, u32[]{:S(2)}) copy-start(bf16[256,2304]{1,0:T(8,128)(2,1)} %copy-done.2) | copy-start | bytes 3538948

commit v4 on v3

--- a/solution.py
+++ b/solution.py
@@ -95,31 +95,95 @@
     return total.reshape(*lead, total.shape[-1])
 
 
-def early_kernel(frames, pieces, *refs):
-    got_refs = refs[:pieces]
-    label_refs = refs[pieces : 2 * pieces]
-    (
-        lift_ref,
-        first_w_ref,
-        second_w_ref,
-        send_ref,
-        even_ref,
-        odd_ref,
-        first_ref,
-        first_slope_ref,
-        second_slope_ref,
-        bits_ref,
-        lift_all_ref,
-        first_all_ref,
-    ) = refs[2 * pieces :]
+def column_order(cols):
+    place = lax.broadcasted_iota(jnp.int32, (cols, cols), 0)
+    column = lax.broadcasted_iota(jnp.int32, (cols, cols), 1)
+    source = (place % BLOCK) * (cols // BLOCK) + place // BLOCK
+    return jnp.where(column == source, 1.0, 0.0).astype(jnp.bfloat16)
+
+
+def band_cells(got_ref, inner, index, order, lift_ref, bits_ref, even_ref, odd_ref, rest):
+    _, frames, band, cols = got_ref.shape
+    phases, row_cells = cols // BLOCK, cols // 2
+    height = lax.broadcasted_iota(jnp.int32, (16, cols), 0)
+    for row in range(band):
+        for frame in range(frames):
+            line = jnp.broadcast_to(got_ref[inner, frame, pl.ds(row, 1)], height.shape)
+            bit = jnp.bitwise_and(jnp.right_shift(line, height), 1)
+            bits_ref[pl.ds(row * 128 + frame * 16, 16)] = bit.astype(jnp.float32).astype(
+                jnp.bfloat16
+            )
+    spread = dot_nt(order, bits_ref[...]).astype(jnp.bfloat16)
+    stacked = jnp.concatenate(
+        [spread[:, row * 128 : row * 128 + 128] for row in range(band)], axis=0
+    )
+    lifted = jnp.maximum(dot_nn(stacked, lift_ref[...]), 0.0)
+    lifted = lifted.reshape(band // 2, 2, phases // 2, 2, BLOCK, lifted.shape[-1])
+    for parity, ref in ((0, even_ref), (1, odd_ref)):
+        here = lifted[:, parity, :, 0]
+        right = lifted[:, parity, :, 1]
+        left = jnp.concatenate([shift_block(right[:, -1], 1)[:, None], right[:, :-1]], axis=1)
+        taps = [part.reshape(-1, part.shape[-1]) for part in (left, here, right)]
+        lane = lax.broadcasted_iota(jnp.int32, (taps[0].shape[0], 128), 1)
+        tail = jnp.where(lane < rest, taps[0][:, 128:], taps[1][:, 128:])
+        tail = jnp.where(lane < 2 * rest, tail, taps[2][:, 128:])
+        cells = jnp.concatenate([part[:, :128] for part in taps] + [tail], axis=1)
+        if index is None:
+            ref[...] = cells.astype(jnp.bfloat16)
+        else:
+            at = pl.multiple_of((index * (band // 2) + parity) * row_cells, row_cells)
+            ref[pl.ds(at, cells.shape[0])] = cells.astype(jnp.bfloat16)
+
+
+def band_label(label_ref, inner, index, shape):
+    lane = lax.broadcasted_iota(jnp.int32, shape, 1)
+    row = lax.broadcasted_iota(jnp.int32, (shape[0], BLOCK), 0)
+    column = lax.broadcasted_iota(jnp.int32, (shape[0], BLOCK), 1)
+    label = jnp.broadcast_to(label_ref[inner].astype(jnp.float32), row.shape)
+    label = jnp.sum(jnp.where(row == column, label, 0.0), axis=1, keepdims=True)
+    return jnp.where(lane == index, label, 0.0)
+
+
+def own_kernel(
+    got_hbm,
+    label_hbm,
+    lift_hbm,
+    first_w_hbm,
+    second_w_hbm,
+    even_ref,
+    odd_ref,
+    labels_ref,
+    lift_all_ref,
+    first_all_ref,
+    second_w_ref,
+    got_ref,
+    label_ref,
+    lift_ref,
+    first_w_ref,
+    bits_ref,
+    sems,
+):
+    pairs = (
+        (got_hbm, got_ref),
+        (lift_hbm, lift_ref),
+        (label_hbm, label_ref),
+        (first_w_hbm, first_w_ref),
+        (second_w_hbm, second_w_ref),
+    )
+    copies = [
+        pltpu.make_async_copy(source, target, sems.at[k])
+        for k, (source, target) in enumerate(pairs)
+    ]
+    for copy in copies:
+        copy.start()
     me = lax.axis_index("space")
-    bands = 1 << (pieces - 1)
-    _, _, band, cols = got_refs[0].shape
-    phases = cols // BLOCK
-    row_cells = cols // 2
+    _, frames, _, cols = got_ref.shape
     heights, width = lift_ref.shape
     rest = first_w_ref.shape[1] - 128
-
+    bits_ref[...] = jnp.zeros(bits_ref.shape, jnp.bfloat16)
+    first_all_ref[...] = jnp.zeros(first_all_ref.shape, jnp.bfloat16)
+    order = column_order(cols)
+    copies[1].wait()
     tall = jnp.concatenate(
         [lift_ref[...].astype(jnp.float32), jnp.zeros((16 - heights, width), jnp.float32)], axis=0
     )
@@ -130,62 +194,66 @@
     frame_of_lane = jnp.minimum(lane // width, frames - 1)
     keep = (frame_of_row == frame_of_lane) & (lane < 128 + 3 * rest)
     lift_all_ref[...] = jnp.where(keep, tall, 0.0).astype(jnp.bfloat16)
-    first_all_ref[...] = jnp.zeros(first_all_ref.shape, jnp.bfloat16)
+    copies[0].wait()
+    band_cells(got_ref, 0, None, order, lift_all_ref, bits_ref, even_ref, odd_ref, rest)
+    copies[2].wait()
+    labels_ref[...] = band_label(label_ref, 0, me, labels_ref.shape)
+    copies[3].wait()
     for tap in range(9):
         row_tap, col_tap = divmod(tap, 3)
         first_all_ref[row_tap, pl.ds(col_tap * 128, 128)] = first_w_ref[tap, pl.ds(0, 128)]
         first_all_ref[row_tap, pl.ds(384 + col_tap * rest, rest)] = first_w_ref[
             tap, pl.ds(128, rest)
         ]
-
-    height = lax.broadcasted_iota(jnp.int32, (16, cols), 0)
-    place = lax.broadcasted_iota(jnp.int32, (cols, cols), 0)
-    column = lax.broadcasted_iota(jnp.int32, (cols, cols), 1)
-    order = jnp.where(column == (place % BLOCK) * phases + place // BLOCK, 1.0, 0.0)
-    order = order.astype(jnp.bfloat16)
-    sent = (band // 4) * bands * (phases // 4) * BLOCK
-    label_lane = lax.broadcasted_iota(jnp.int32, (16, send_ref.shape[1]), 1)
-    label_row = lax.broadcasted_iota(jnp.int32, (16, BLOCK), 0)
-    label_column = lax.broadcasted_iota(jnp.int32, (16, BLOCK), 1)
-    labels = jnp.zeros((16, send_ref.shape[1]), jnp.float32)
+    copies[4].wait()
+
+
+def early_kernel(pieces, rest, *refs):
+    got_refs = refs[:pieces]
+    label_refs = refs[pieces : 2 * pieces]
+    (
+        labels_ref,
+        lift_all_ref,
+        first_all_ref,
+        second_w_ref,
+        own_even_ref,
+        own_odd_ref,
+        even_ref,
+        odd_ref,
+        send_ref,
+        first_ref,
+        first_slope_ref,
+        second_slope_ref,
+        bits_ref,
+    ) = refs[2 * pieces :]
+    me = lax.axis_index("space")
+    bands = 1 << pieces
+    _, _, band, cols = got_refs[0].shape
+    phases, row_cells = cols // BLOCK, cols // 2
+    order = column_order(cols)
+    labels = labels_ref[...]
+    cells = own_even_ref.shape[0]
+    at = pl.multiple_of(me * cells, cells)
+    even_ref[pl.ds(at, cells)] = own_even_ref[...]
+    odd_ref[pl.ds(pl.multiple_of(at + row_cells, row_cells), cells)] = own_odd_ref[...]
+    odd_ref[pl.ds(0, row_cells)] = jnp.zeros((row_cells, odd_ref.shape[1]), jnp.bfloat16)
     bits_ref[...] = jnp.zeros(bits_ref.shape, jnp.bfloat16)
-    odd_ref[pl.ds(0, row_cells)] = jnp.zeros((row_cells, odd_ref.shape[1]), jnp.bfloat16)
-    for slot in range(bands):
-        index = me ^ slot
-        piece = slot.bit_length()
-        inner = slot - (1 << (piece - 1)) if slot else 0
-        got_ref, label_ref = got_refs[piece], label_refs[piece]
-        for row in range(band):
-            for frame in range(frames):
-                line = jnp.broadcast_to(got_ref[inner, frame, pl.ds(row, 1)], height.shape)
-                bit = jnp.bitwise_and(jnp.right_shift(line, height), 1)
-                bits_ref[pl.ds(row * 128 + frame * 16, 16)] = bit.astype(jnp.float32).astype(
-                    jnp.bfloat16
-                )
-        label = jnp.broadcast_to(label_ref[inner].astype(jnp.float32), label_row.shape)
-        label = jnp.sum(
-            jnp.where(label_row == label_column, label, 0.0), axis=1, keepdims=True
+    for slot in range(1, bands):
+        piece = slot.bit_length() - 1
+        inner = slot - (1 << piece)
+        band_cells(
+            got_refs[piece],
+            inner,
+            me ^ slot,
+            order,
+            lift_all_ref,
+            bits_ref,
+            even_ref,
+            odd_ref,
+            rest,
         )
-        labels += jnp.where(label_lane == index, label, 0.0)
-        spread = dot_nt(order, bits_ref[...]).astype(jnp.bfloat16)
-        stacked = jnp.concatenate(
-            [spread[:, row * 128 : row * 128 + 128] for row in range(band)], axis=0
-        )
-        lifted = jnp.maximum(dot_nn(stacked, lift_all_ref[...]), 0.0)
-        lifted = lifted.reshape(band // 2, 2, phases // 2, 2, BLOCK, lifted.shape[-1])
-        for parity, ref in ((0, even_ref), (1, odd_ref)):
-            here = lifted[:, parity, :, 0]
-            right = lifted[:, parity, :, 1]
-            left = jnp.concatenate([shift_block(right[:, -1], 1)[:, None], right[:, :-1]], axis=1)
-            taps = [part.reshape(-1, part.shape[-1]) for part in (left, here, right)]
-            lane = lax.broadcasted_iota(jnp.int32, (taps[0].shape[0], 128), 1)
-            tail = jnp.where(lane < rest, taps[0][:, 128:], taps[1][:, 128:])
-            tail = jnp.where(lane < 2 * rest, tail, taps[2][:, 128:])
-            cells = jnp.concatenate([part[:, :128] for part in taps] + [tail], axis=1)
-            at = pl.multiple_of((index * (band // 2) + parity) * row_cells, row_cells)
-            ref[pl.ds(at, cells.shape[0])] = cells.astype(jnp.bfloat16)
-
-    send_ref[pl.ds(sent, 16)] = labels.astype(jnp.bfloat16)
+        labels += band_label(label_refs[piece], inner, me ^ slot, labels.shape)
+
     rows, phases = bands * band // 2, phases // 2
     cells = rows * row_cells
     pre = dot_nn(odd_ref[pl.ds(0, cells)], first_all_ref[0])
@@ -205,7 +273,9 @@
         pre = part if pre is None else pre + part
     value, slope = silu_and_slope(pre)
     second_slope_ref[...] = slope.reshape(second_slope_ref.shape)
-    send_ref[pl.ds(0, value.shape[0])] = value.astype(jnp.bfloat16)
+    sent = value.shape[0]
+    send_ref[pl.ds(0, sent)] = value.astype(jnp.bfloat16)
+    send_ref[pl.ds(sent, 16)] = labels.astype(jnp.bfloat16)
 
 
 def transpose_kernel(second_w_ref, third_w_ref, fourth_w_ref, second_ref, third_ref, fourth_ref):
@@ -264,7 +334,7 @@
     fourth_w_ref,
     fourth_wt_ref,
     head_ref,
-    third_delta_ref,
+    third_flat_ref,
     fourth_taps_ref,
     fourth_flat_ref,
     head_grad_ref,
@@ -273,6 +343,7 @@
     third_taps_ref,
     third_ref,
     third_slope_ref,
+    third_delta_ref,
     fourth_delta_ref,
 ):
     samples = second_ref.shape[0]
@@ -315,7 +386,9 @@
             part = rounded(part * third_slope_ref[:, :, row_parity, :, col_parity])
             for row in range(rows):
                 third_delta_ref[:, 2 * row + row_parity, col_parity] = part[:, row, 0]
-    last_row_zero(third_delta_ref)
+    third_flat_ref[...] = (
+        third_delta_ref[...].reshape(third_flat_ref.shape).astype(jnp.bfloat16)
+    )
 
 
 def late_kernel(
@@ -327,14 +400,16 @@
     first_ref,
     first_slope_ref,
     second_slope_ref,
-    out_ref,
-    third_ref,
-    second_ref,
-    first_delta_ref,
+    *refs,
 ):
+    out_refs = refs[:4]
+    third_ref, second_ref, first_delta_ref, flat_ref = refs[4:]
     sample = lax.axis_index("dp")
-    rows, phases = third_delta_ref.shape[1] - 1, third_delta_ref.shape[2]
-    fill_delta(third_ref, third_delta_ref[pl.ds(sample, 1)])
+    _, rows, cells, channels = third_delta_ref.shape
+    phases = cells // BLOCK
+    delta = third_delta_ref[pl.ds(sample, 1)].astype(jnp.float32)
+    fill_delta(third_ref, delta.reshape(1, rows, phases, BLOCK, channels))
+    last_row_zero(third_ref)
     last_row_zero(second_ref)
     for row_parity in range(2):
         for col_parity in range(2):
@@ -344,41 +419,35 @@
                     at = (slice(None), 2 * row + row_parity, 2 * phase + col_parity)
                     second_ref[at] = rounded(part[:, row, phase] * second_slope_ref[at])
     rows, phases = 2 * rows, 2 * phases
-
-    @pl.when(lax.axis_index("space") != 0)
-    def _():
-        delta = second_ref[:, pl.ds(0, rows), pl.ds(0, phases)]
-        delta = delta.reshape(-1, delta.shape[-1]).astype(jnp.bfloat16)
-        depth = first_ref.shape[-1]
-        for tap in range(9):
-            cells = map_tap(first_ref, tap // 3, tap % 3, rows, phases)
-            out_ref[pl.ds(tap * depth, depth)] = dot_tn(cells, delta).astype(jnp.bfloat16)
-        left = out_ref.shape[0] - 9 * depth
-        out_ref[pl.ds(9 * depth, left)] = jnp.zeros((left, out_ref.shape[1]), jnp.bfloat16)
-
-    @pl.when(lax.axis_index("space") == 0)
-    def _():
-        second_ref[:, :, phases] = shift_block(second_ref[:, :, 0], -1)
-        for row_parity in range(2):
-            for col_parity in range(2):
-                part = delta_parts(
-                    second_ref, second_wt_ref, row_parity, col_parity, rows, phases
-                )
-                for row in range(rows):
-                    for phase in range(phases):
-                        at = (slice(None), 2 * row + row_parity, 2 * phase + col_parity)
-                        first_delta_ref[at] = rounded(part[:, row, phase] * first_slope_ref[at])
-        delta = first_delta_ref[...]
-        delta = delta.reshape(-1, delta.shape[-1]).astype(jnp.bfloat16)
-        cells, depth = delta.shape
-        row_cells = cells // (2 * rows)
-        taps = (odd_ref[pl.ds(0, cells)], even_ref[...], odd_ref[pl.ds(row_cells, cells)])
-        for tap in range(3):
-            part = dot_tn(delta, taps[tap]).astype(jnp.bfloat16)
-            for piece in range(4):
-                out_ref[pl.ds((4 * tap + piece) * depth, depth)] = part[
-                    :, piece * 128 : piece * 128 + 128
-                ]
+    second_ref[:, :, phases] = shift_block(second_ref[:, :, 0], -1)
+    for row_parity in range(2):
+        for col_parity in range(2):
+            part = delta_parts(second_ref, second_wt_ref, row_parity, col_parity, rows, phases)
+            for row in range(rows):
+                for phase in range(phases):
+                    at = (slice(None), 2 * row + row_parity, 2 * phase + col_parity)
+                    first_delta_ref[at] = rounded(part[:, row, phase] * first_slope_ref[at])
+    delta = second_ref[:, pl.ds(0, rows), pl.ds(0, phases)]
+    delta = delta.reshape(-1, delta.shape[-1]).astype(jnp.bfloat16)
+    depth = first_ref.shape[-1]
+    for tap in range(9):
+        cells = map_tap(first_ref, tap // 3, tap % 3, rows, phases)
+        flat_ref[pl.ds((12 + tap) * depth, depth)] = dot_tn(cells, delta)
+    delta = first_delta_ref[...]
+    delta = delta.reshape(-1, delta.shape[-1]).astype(jnp.bfloat16)
+    cells = delta.shape[0]
+    row_cells = cells // (2 * rows)
+    taps = (odd_ref[pl.ds(0, cells)], even_ref[...], odd_ref[pl.ds(row_cells, cells)])
+    for tap in range(3):
+        part = dot_tn(delta, taps[tap])
+        for piece in range(4):
+            flat_ref[pl.ds((4 * tap + piece) * depth, depth)] = part[
+                :, piece * 128 : piece * 128 + 128
+            ]
+    share = out_refs[0].shape[0]
+    for slot in range(4):
+        at = pl.multiple_of(((sample % 4) ^ slot) * share, share)
+        out_refs[slot][...] = flat_ref[pl.ds(at, share)].astype(jnp.bfloat16)
 
 
 def third_grad_kernel(
@@ -387,8 +456,7 @@
     zero_row(second_ref)
     take_samples(near_ref, far_ref, second_ref, None, bands)
     third_taps(second_ref, third_taps_ref, 2 * bands, 2)
-    delta = delta_ref[:, pl.ds(0, 2 * bands)]
-    delta = delta.reshape(-1, delta.shape[-1]).astype(jnp.bfloat16)
+    delta = delta_ref[...].reshape(-1, delta_ref.shape[-1])
 
     @pl.when(pl.program_id(0) == 0)
     def _():
@@ -405,23 +473,16 @@
     out_ref[...] += dot_tn(fourth_taps_ref[...], fourth_flat_ref[...])
 
 
-def sum_kernel(got_ref, out_ref):
-    total = got_ref[0].astype(jnp.float32)
-    for index in range(1, got_ref.shape[0]):
-        total += got_ref[index].astype(jnp.float32)
-    total = total.astype(jnp.bfloat16)
-    for index in range(out_ref.shape[0]):
-        out_ref[index] = total
-
-
-def finish_kernel(got_ref, temporal_ref, middle_ref, flat_ref):
-    samples, _, share, lanes = got_ref.shape
+def finish_kernel(*refs):
+    got_refs = refs[:4]
+    temporal_ref, middle_ref, flat_ref = refs[4:]
+    me = lax.axis_index("dp") % 4
+    share = got_refs[0].shape[0]
+    for slot in range(4):
+        at = pl.multiple_of((me ^ slot) * share, share)
+        flat_ref[pl.ds(at, share)] = got_refs[slot][...].astype(jnp.float32)
     depth = temporal_ref.shape[2]
-    for sample in range(samples):
-        flat_ref[pl.ds(sample * share, share)] = got_ref[sample, 0].astype(jnp.float32)
-        rows = min(share, middle_ref.shape[0] - sample * share)
-        if rows > 0:
-            middle_ref[pl.ds(sample * share, rows)] = got_ref[sample, 1].astype(jnp.float32)[:rows]
+    middle_ref[...] = flat_ref[pl.ds(12 * depth, 9 * depth)]
     rest = temporal_ref.shape[1] - 128
     for tap in range(3):
         parts = [flat_ref[pl.ds((4 * tap + piece) * depth, depth)].T for piece in range(4)]
@@ -452,14 +513,28 @@
 
 def gathered_halves(value, samples):
     half = samples // 2
+    quarter = half // 2
     near = jnp.zeros((half,) + value.shape[1:], value.dtype)
     near = lax.dynamic_update_slice(near, value, (0, 0, 0))
-    count = 1
-    while count < half:
-        part = swapped(near[:count], "dp", half // count)
-        near = lax.dynamic_update_slice(near, part, (count, 0, 0))
+    last, count, others = value, 1, []
+    while count < quarter:
+        part = near[:count] if count > 1 else value
+        got = swapped(part, "dp", half // count)
+        others.append((swapped(last, "dp", 2), quarter + (count // 2 if count > 1 else 0)))
+        near = lax.dynamic_update_slice(near, got, (count, 0, 0))
+        last = got
         count *= 2
+    others.append((swapped(last, "dp", 2), quarter + (count // 2 if count > 1 else 0)))
+    for part, at in others:
+        near = lax.dynamic_update_slice(near, part, (at, 0, 0))
     return near, swapped(near, "dp", 1)
+
+
+def added(*parts):
+    total = parts[0].astype(jnp.float32)
+    for part in parts[1:]:
+        total = total + part.astype(jnp.float32)
+    return total.astype(jnp.bfloat16)
 
 
 def local(
@@ -497,27 +572,57 @@
     head = head_weight.reshape(1, four)
 
     sent = rows // 4 * phases // 4 * BLOCK + 16
-    payload, even, odd, first, first_slope, second_slope = pl.pallas_call(
-        functools.partial(early_kernel, frames, len(lines)),
+    hbm = pl.BlockSpec(memory_space=pltpu.HBM)
+    even_shape = shaped((rows // 2 * cols // 2, 512), bf16)
+    odd_shape = shaped(((rows // 2 + 1) * cols // 2, 512), bf16)
+    bits_scratch = pltpu.VMEM((band * 128, cols), bf16)
+    own_cells = shaped((band // 2 * cols // 2, 512), bf16)
+    own_args = [
+        pltpu.with_memory_space_constraint(value, pltpu.HBM)
+        for value in (occupancy, state_labels, lift_weight, first_w, second_w)
+    ]
+    own_even, own_odd, own_labels, lift_all_w, first_all, second_w2 = pl.pallas_call(
+        own_kernel,
         out_shape=(
+            own_cells,
+            own_cells,
+            shaped((16, two), f32),
+            shaped((128, 256), bf16),
+            shaped((3, 512, one), bf16),
+            shaped(second_w.shape, bf16),
+        ),
+        in_specs=[hbm] * 5,
+        out_specs=(vmem,) * 6,
+        scratch_shapes=[
+            pltpu.VMEM(occupancy.shape, occupancy.dtype),
+            pltpu.VMEM(state_labels.shape, state_labels.dtype),
+            pltpu.VMEM(lift_weight.shape, bf16),
+            pltpu.VMEM(first_w.shape, bf16),
+            bits_scratch,
+            pltpu.SemaphoreType.DMA((5,)),
+        ],
+        compiler_params=grant(16),
+        cost_estimate=cost(100_000_000, 4_000_000),
+        name="own_band",
+    )(*own_args)
+    pieces = len(lines) - 1
+    even, odd, payload, first, first_slope, second_slope = pl.pallas_call(
+        functools.partial(early_kernel, pieces, lift_all - 128),
+        out_shape=(
+            even_shape,
+            odd_shape,
             shaped((sent, two), bf16),
-            shaped((rows // 2 * cols // 2, 512), bf16),
-            shaped(((rows // 2 + 1) * cols // 2, 512), bf16),
             shaped((1, rows // 4 + 1, 2, phases // 4 + 1, 2, BLOCK, one), f32),
             shaped((1, rows // 2, phases // 2, BLOCK, one), f32),
             shaped((1, rows // 4, phases // 4, BLOCK, two), f32),
         ),
-        in_specs=[vmem] * (2 * len(lines) + 3),
+        in_specs=[vmem] * (2 * pieces + 6),
         out_specs=(vmem,) * 6,
-        scratch_shapes=[
-            pltpu.VMEM((band * 128, cols), bf16),
-            pltpu.VMEM((128, 256), bf16),
-            pltpu.VMEM((3, 512, one), bf16),
-        ],
+        scratch_shapes=[bits_scratch],
         compiler_params=grant(24),
-        cost_estimate=cost(200_000_000, 4_000_000),
+        cost_estimate=cost(150_000_000, 4_000_000),
         name="early",
-    )(*lines, *labels, lift_weight, first_w, second_w)
+    )(*lines[1:], *labels[1:], own_labels, lift_all_w, first_all, second_w2, own_even, own_odd)
 
     near, far = gathered_halves(payload[None], samples)
 
@@ -541,7 +646,7 @@
     fourth_cells = bands * BLOCK
     full = lambda *shape: pl.BlockSpec(shape, lambda i: (0,) * len(shape))
     delta_block = pl.BlockSpec(
-        (chunk, 2 * bands + 1, 2, BLOCK, three), lambda i: (i, 0, 0, 0, 0)
+        (chunk, 2 * bands, 2 * BLOCK, three), lambda i: (i, 0, 0, 0)
     )
     second_scratch = pltpu.VMEM((chunk, 2 * bands + 1, 2, 3, 2, BLOCK, two), f32)
     third_taps_scratch = pltpu.VMEM((chunk * third_cells, 9 * two), bf16)
@@ -549,7 +654,7 @@
         functools.partial(deep_kernel, samples, bands),
         grid=(steps,),
         out_shape=(
-            shaped((samples, 2 * bands + 1, 2, BLOCK, three), f32),
+            shaped((samples, 2 * bands, 2 * BLOCK, three), bf16),
             shaped((samples * fourth_cells, 9 * three), bf16),
             shaped((samples * fourth_cells, four), bf16),
             shaped((1, four), f32),
@@ -574,6 +679,7 @@
             third_taps_scratch,
             pltpu.VMEM((chunk, bands + 1, 2, 2, 2, BLOCK, three), f32),
             pltpu.VMEM((chunk, bands, 2, 1, 2, BLOCK, three), f32),
+            pltpu.VMEM((chunk, 2 * bands, 2, BLOCK, three), f32),
             pltpu.VMEM((chunk, bands + 1, 2, BLOCK, four), f32),
         ],
         compiler_params=grant(40),
@@ -588,33 +694,25 @@
         head,
     )
 
-    share = 12 * one // samples
-    partial = pl.pallas_call(
+    share = 21 * one // 4
+    quarters = pl.pallas_call(
         late_kernel,
-        out_shape=shaped((12 * one, two), bf16),
+        out_shape=(shaped((share, two), bf16),) * 4,
         in_specs=[vmem] * 8,
-        out_specs=vmem,
+        out_specs=(vmem,) * 4,
         scratch_shapes=[
             pltpu.VMEM((1, 2 * bands + 1, 3, BLOCK, three), f32),
             pltpu.VMEM((1, 4 * bands + 1, 5, BLOCK, two), f32),
             pltpu.VMEM(first_slope.shape, f32),
+            pltpu.VMEM((21 * one, two), f32),
         ],
         compiler_params=grant(24),
         cost_estimate=cost(200_000_000, 6_000_000),
         name="late",
     )(third_delta, third_wt, second_wt, even, odd, first, first_slope, second_slope)
 
-    got = lax.all_to_all(partial.reshape(samples, share, two), "dp", 0, 0)
-    total = pl.pallas_call(
-        sum_kernel,
-        out_shape=shaped((samples * bands, share, two), bf16),
-        in_specs=[vmem],
-        out_specs=vmem,
-        cost_estimate=cost(100_000, 600_000),
-        name="sum",
-    )(got)
-    got = lax.all_to_all(total, ("dp", "space"), 0, 0)
-
+    mine, near3, far3, delta3 = lax.optimization_barrier((quarters[0], near, far, third_delta))
+    got = [swapped(quarters[slot], "dp", slot) for slot in (1, 2, 3)]
     deeper_grad = pl.pallas_call(
         functools.partial(third_grad_kernel, bands),
         grid=(steps,),
@@ -625,30 +723,43 @@
         compiler_params=grant(24),
         cost_estimate=cost(600_000_000, 6_000_000),
         name="third_grad",
-    )(near, far, third_delta)
+    )(near3, far3, delta3)
+    got[2], deeper_grad = lax.optimization_barrier((got[2], deeper_grad))
+    total = added(mine, *got)
+    bit = 4
+    while 2 * bit < samples:
+        total = added(total, swapped(total, "dp", bit))
+        bit *= 2
+    total, fourth_taps, fourth_flat = lax.optimization_barrier((total, fourth_taps, fourth_flat))
+    other = swapped(total, "dp", bit) if bit < samples else jnp.zeros_like(total)
     deepest_grad = pl.pallas_call(
         fourth_grad_kernel,
-        grid=(9, steps),
+        grid=(3, steps),
         out_shape=shaped((9 * three, four), f32),
         in_specs=[
-            pl.BlockSpec((chunk * fourth_cells, three), lambda t, i: (i, t)),
+            pl.BlockSpec((chunk * fourth_cells, 3 * three), lambda t, i: (i, t)),
             pl.BlockSpec((chunk * fourth_cells, four), lambda t, i: (i, 0)),
         ],
-        out_specs=pl.BlockSpec((three, four), lambda t, i: (t, 0)),
+        out_specs=pl.BlockSpec((3 * three, four), lambda t, i: (t, 0)),
         compiler_params=grant(16),
         cost_estimate=cost(600_000_000, 6_000_000),
         name="fourth_grad",
     )(fourth_taps, fourth_flat)
+    other, deepest_grad = lax.optimization_barrier((other, deepest_grad))
+    total = added(total, other)
+    beside = swapped(total, "dp", 2)
+    core = swapped(total, "dp", 1)
+    across = swapped(beside, "dp", 1)
     temporal_grad, middle_grad = pl.pallas_call(
         finish_kernel,
         out_shape=(shaped((9, lift_all, one), f32), shaped((9 * one, two), f32)),
-        in_specs=[vmem],
+        in_specs=[vmem] * 4,
         out_specs=(vmem, vmem),
-        scratch_shapes=[pltpu.VMEM((12 * one, two), f32)],
+        scratch_shapes=[pltpu.VMEM((21 * one, two), f32)],
         compiler_params=grant(16),
         cost_estimate=cost(1_000_000, 1_500_000),
         name="finish",
-    )(got.reshape(samples, bands, share, two))
+    )(total, core, beside, across)
     return (
         temporal_grad.reshape(temporal_weight.shape),
         middle_grad.reshape(middle_weight.shape),

time: 74.4 us -> 57.9 us (0.78)
  blocking collectives: 15.5 us -> 0 us
  starting transfers between devices: 11.6 us -> 19.3 us
  local copies, waits for them, and re-layouts: 5.48 us -> 0.18 us
  Pallas kernels: 20.6 us -> 17.4 us
    all_to_all x1 -> x0, blocking collectives: 15.5 us -> none  [local(): got = lax.all_to_all(partial.reshape(samples, share, two), 'dp', 0, 0)]
    ppermute x6 -> x16, starting transfers between devices: 9.03 us -> 19.3 us  [swapped(): lax.ppermute(value, axis, [(i, i ^ bit) for i in range(lax.axis_size(axis...]
    unnamed x20 -> x8, local copies, waits for them, and re-layouts: 5.3 us -> 0.02 us
    ppermute x6 -> x16, waiting for transfers between devices: 15.6 us -> 20 us  [swapped(): lax.ppermute(value, axis, [(i, i ^ bit) for i in range(lax.axis_size(axis...]
    all_to_all x1 -> x0, waiting for transfers between devices: 4.13 us -> none  [local(): got = lax.all_to_all(total, ('dp', 'space'), 0, 0)]
    pallas_call x4, Pallas kernels: 12.2 us -> 8.82 us  [the longest x1 3.15 us: local(): pl.pallas_call(fourth_grad_kernel, grid=(3, steps), out_shape=shaped((9 *...]
    all_to_all x1 -> x0, starting transfers between devices: 2.6 us -> none  [local(): got = lax.all_to_all(total, ('dp', 'space'), 0, 0)]
  transfers between devices with their start and end apart: 7 -> 16, of which waited for: 6 -> 11; matrix products, arithmetic and copies ran while one was open for 0% -> 0% of each run, Pallas kernels for 11% -> 14%
where the time goes in v4:
time: 57.9 us; the launch traced here: 57.7 us
  waiting for transfers between devices  20 us (35%)
  starting transfers between devices  19.3 us (33%)
  Pallas kernels  17.4 us (30%)
  between operations  0.8 us (1%)
    ppermute x16, waiting for transfers between devices, swapped(): lax.ppermute(value, axis, [(i, i ^ bit) for i in range(lax.axis_size(axis...  20 us
    ppermute x16, starting transfers between devices, swapped(): lax.ppermute(value, axis, [(i, i ^ bit) for i in range(lax.axis_size(axis...  19.3 us
    pallas_call x1, Pallas kernels, local(): pl.pallas_call(functools.partial(deep_kernel, samples, bands), grid=(step...  4.36 us
    pallas_call x1, Pallas kernels, local(): pl.pallas_call(fourth_grad_kernel, grid=(3, steps), out_shape=shaped((9 *...  3.15 us
    pallas_call x1, Pallas kernels, local(): pl.pallas_call(functools.partial(early_kernel, pieces, lift_all - 128), o...  2.73 us
    pallas_call x1, Pallas kernels, local(): pl.pallas_call(functools.partial(third_grad_kernel, bands), grid=(steps,)...  2.07 us
    pallas_call x1, Pallas kernels, local(): pl.pallas_call(own_kernel, out_shape=(own_cells, own_cells, shaped((16, t...  1.67 us
    pallas_call x1, Pallas kernels, local(): pl.pallas_call(late_kernel, out_shape=(shaped((share, two), bf16),) * 4,...  1.28 us
  transfers between devices with their start and end apart: 16, of which 11 were waited for; matrix products, arithmetic and copies ran while one was open for 0% of the time, Pallas kernels for 14%

profile of v4, /device:TPU:0, one launch (start us, length us, event | category | flops | bytes accessed | tf_op | source)
XLA Modules:
  0.0 57.7 jit_solution(7776515882420335385)
XLA Ops:
  0.6 0.0 copy-start.2
  0.6 0.0 copy-start.3
  0.7 0.0 copy-start.1
  0.7 0.0 copy-start
  0.7 3.0 %collective-permute-start = (s32[1,5,16,128]{3,2,1,0:T(8,128)}, s32[1,5,16,128]{3,2,1,0:T(8,128)S(1)}, u32[]{:S(2)}, u32[]{:S(2)}) collective-permute-start(s32[1,5,16,128]{3,2,1,0:T(8,128)} %got_hbm.1), channel_id=1, source_target_pairs={{0,1},{1,0},{2,3},{3,2},{4,5},{5,4},{6,7},{7,6},{8,9},{9,8},{10,11... | collective-permute-start | bytes 122888 | tf_op jit(solution)/shard_map/ppermute | solution.py:501
  3.7 0.1 collective-permute-start.1
  3.8 1.7 %own_band.1 = (bf16[512,512]{1,0:T(8,128)(2,1)S(1)}, bf16[512,512]{1,0:T(8,128)(2,1)S(1)}, f32[16,128]{1,0:T(8,128)S(1)}, bf16[128,256]{1,0:T(8,128)(2,1)S(1)}, ...) custom-call(s32[1,5,16,128]{3,2,1,0:T(8,128)} %got_hbm.1, s32[1,1,8]{2,1,0:T(1,128)} %label_hbm.1, ...), custom_call_target="tpu_custom_call" | custom-call | flops 100000000 | bytes 4000000 | tf_op jit(solution)/shard_map/own_band/pallas_call | solution.py:584
  5.4 1.9 %collective-permute-done.1.refs_1_ = s32[1,1,8]{2,1,0:T(1,128)S(1)} collective-permute-done((s32[1,1,8]{2,1,0:T(1,128)}, s32[1,1,8]{2,1,0:T(1,128)S(1)}, u32[]{:S(2)}, u32[]{:S(2)}) %collective-permute-start.1) | collective-permute-done | bytes 64 | tf_op jit(solution)/shard_map/ppermute | solution.py:501
  7.4 0.0 collective-permute-done.refs_0_
  7.4 2.7 %early.1 = (bf16[1024,512]{1,0:T(8,128)(2,1)S(1)}, bf16[1088,512]{1,0:T(8,128)(2,1)S(1)}, bf16[272,128]{1,0:T(8,128)(2,1)S(1)}, f32[1,9,2,5,2,8,64]{6,5,4,3,2,1,...) custom-call(s32[1,5,16,128]{3,2,1,0:T(8,128)S(1)} %collective-permute-done.refs_0_, ...), custom_call_target="tpu_custom_call" | custom-call | flops 150000000 | bytes 4000000 | tf_op jit(solution)/shard_map/early/pallas_call | solution.py:609
  10.1 2.7 %collective-permute-start.2 = (bf16[1,272,128]{2,1,0:T(8,128)(2,1)S(1)}, bf16[1,272,128]{2,1,0:T(8,128)(2,1)S(1)}, u32[]{:S(2)}, u32[]{:S(2)}) collective-permute-start(bf16[1,272,128]{2,1,0:T(8,128)(2,1)S(1)} %bitcast.18), channel_id=1, source_target_pairs={{0,16},{2,18},{4,20},{6,22},{8,24},{10,26},{12,28},{14,30},{16,0},... | collective-permute-start | bytes 208904 | tf_op jit(solution)/shard_map/ppermute | solution.py:501
  12.7 0.1 dynamic_update_slice.18
  12.8 2.5 %collective-permute-done.2 = bf16[1,272,128]{2,1,0:T(8,128)(2,1)S(1)} collective-permute-done((bf16[1,272,128]{2,1,0:T(8,128)(2,1)S(1)}, bf16[1,272,128]{2,1,0:T(8,128)(2,1)S(1)}, u32[]{:S(2)}, u32[]{:S(2)}) %collective-permute-start.2) | collective-permute-done | bytes 69664 | tf_op jit(solution)/shard_map/ppermute | solution.py:501
  15.4 1.6 %collective-permute-start.3 = (bf16[2,272,128]{2,1,0:T(8,128)(2,1)S(1)}, bf16[2,272,128]{2,1,0:T(8,128)(2,1)S(1)}, u32[]{:S(2)}, u32[]{:S(2)}) collective-permute-start(bf16[2,272,128]{2,1,0:T(8,128)(2,1)S(1)} %slice.4), channel_id=1, source_target_pairs={{0,8},{2,10},{4,12},{6,14},{8,0},{10,2},{12,4},{14,6},{16,24},{18,... | collective-permute-start | bytes 417800 | tf_op jit(solution)/shard_map/ppermute | solution.py:501
  17.0 1.5 %collective-permute-start.4 = (bf16[1,272,128]{2,1,0:T(8,128)(2,1)S(1)}, bf16[1,272,128]{2,1,0:T(8,128)(2,1)S(1)}, u32[]{:S(2)}, u32[]{:S(2)}) collective-permute-start(bf16[1,272,128]{2,1,0:T(8,128)(2,1)S(1)} %bitcast.20), channel_id=1, source_target_pairs={{0,4},{2,6},{4,0},{6,2},{8,12},{10,14},{12,8},{14,10},{16,20},{18,... | collective-permute-start | bytes 208904 | tf_op jit(solution)/shard_map/ppermute | solution.py:501
  18.6 0.5 collective-permute-start.5
  19.1 1.5 %collective-permute-done.3 = bf16[2,272,128]{2,1,0:T(8,128)(2,1)S(1)} collective-permute-done((bf16[2,272,128]{2,1,0:T(8,128)(2,1)S(1)}, bf16[2,272,128]{2,1,0:T(8,128)(2,1)S(1)}, u32[]{:S(2)}, u32[]{:S(2)}) %collective-permute-start.3) | collective-permute-done | bytes 139296 | tf_op jit(solution)/shard_map/ppermute | solution.py:501
  20.5 1.5 %collective-permute-start.6 = (bf16[2,272,128]{2,1,0:T(8,128)(2,1)S(1)}, bf16[2,272,128]{2,1,0:T(8,128)(2,1)S(1)}, u32[]{:S(2)}, u32[]{:S(2)}) collective-permute-start(bf16[2,272,128]{2,1,0:T(8,128)(2,1)S(1)} %collective-permute-done.3), channel_id=1, source_target_pairs={{0,4},{2,6},{4,0},{6,2},{8,12},{10,14},{12,8},{14,10},{16,20},{18,... | collective-permute-start | bytes 417800 | tf_op jit(solution)/shard_map/ppermute | solution.py:501
  22.1 0.0 collective-permute-done.4
  22.1 0.8 %collective-permute-done.5 = bf16[1,272,128]{2,1,0:T(8,128)(2,1)S(1)} collective-permute-done((bf16[1,272,128]{2,1,0:T(8,128)(2,1)S(1)}, bf16[1,272,128]{2,1,0:T(8,128)(2,1)S(1)}, u32[]{:S(2)}, u32[]{:S(2)}) %collective-permute-start.5) | collective-permute-done | bytes 69664 | tf_op jit(solution)/shard_map/ppermute | solution.py:501
  22.9 2.7 %collective-permute-done.6 = bf16[2,272,128]{2,1,0:T(8,128)(2,1)S(1)} collective-permute-done((bf16[2,272,128]{2,1,0:T(8,128)(2,1)S(1)}, bf16[2,272,128]{2,1,0:T(8,128)(2,1)S(1)}, u32[]{:S(2)}, u32[]{:S(2)}) %collective-permute-start.6) | collective-permute-done | bytes 139296 | tf_op jit(solution)/shard_map/ppermute | solution.py:501
  25.6 0.1 collective-permute-start.7
  25.7 0.0 copy-done.3
  25.7 0.0 copy-done.2
  25.7 0.0 copy-done.1
  25.7 0.0 copy-done
  25.7 0.9 %transpose.1 = (bf16[9,128,64]{2,1,0:T(8,128)(2,1)S(1)}, bf16[9,256,128]{2,1,0:T(8,128)(2,1)S(1)}, bf16[9,512,256]{2,1,0:T(8,128)(2,1)S(1)}) custom-call(bf16[9,64,128]{2,1,0:T(8,128)(2,1)S(1)} %bitcast.17, bf16[9,128,256]{2,1,0:T(8,128)(2,1)S(1)} %bitcast.14, bf16[9,256,512]{2,1,0:T(8,128)(2,1)S(1)} %bitcast.12), custom_call_target="tpu_custom_call" | custom-call | flops 10000000 | bytes 6000000 | tf_op jit(solution)/shard_map/transpose/pallas_call | solution.py:629
  26.6 1.0 %collective-permute-done.7.far_ref = bf16[8,272,128]{2,1,0:T(8,128)(2,1)S(1)} collective-permute-done((bf16[8,272,128]{2,1,0:T(8,128)(2,1)S(1)}, bf16[8,272,128]{2,1,0:T(8,128)(2,1)S(1)}, u32[]{:S(2)}, u32[]{:S(2)}) %collective-permute-start.7) | collective-permute-done | bytes 557088 | tf_op jit(solution)/shard_map/ppermute | solution.py:501
  27.6 4.4 %deep.1 = (bf16[16,4,16,256]{3,2,1,0:T(8,128)(2,1)S(1)}, bf16[256,2304]{1,0:T(8,128)(2,1)S(1)}, bf16[256,512]{1,0:T(8,128)(2,1)S(1)}, f32[1,512]{1,0:T(1,128)}) custom-call(bf16[8,272,128]{2,1,0:T(8,128)(2,1)S(1)} %constant_dynamic-update-slice_fusion.near_ref, bf16[8,272,128]{2,1,0:T(8,128)(2,1)S(1)} %collective-permute-done.7.far_ref, ...), custom_call_target="tpu_custom_call" | custom-call | flops 1300000000 | bytes 12000000 | tf_op jit(solution)/shard_map/deep/pallas_call | solution.py:653
  32.0 1.3 %late.1 = (bf16[336,128]{1,0:T(8,128)(2,1)S(1)}, bf16[336,128]{1,0:T(8,128)(2,1)S(1)}, bf16[336,128]{1,0:T(8,128)(2,1)S(1)}, bf16[336,128]{1,0:T(8,128)(2,1)S(1)}) custom-call(bf16[16,4,16,256]{3,2,1,0:T(8,128)(2,1)S(1)} %get-tuple-element.64.third_delta_ref.delta_ref, bf16[9,256,128]{2,1,0:T(8,128)(2,1)S(1)} %get-tuple-element.50.third_wt_ref, ...), custom_call_target="tpu_custom_call" | custom-call | flops 200000000 | bytes 6000000 | tf_op jit(solution)/shard_map/late/pallas_call | solution.py:698
  33.3 1.3 %collective-permute-start.10 = (bf16[336,128]{1,0:T(8,128)(2,1)S(1)}, bf16[336,128]{1,0:T(8,128)(2,1)S(1)}, u32[]{:S(2)}, u32[]{:S(2)}) collective-permute-start(bf16[336,128]{1,0:T(8,128)(2,1)S(1)} %get-tuple-element.61), channel_id=1, source_target_pairs={{0,6},{2,4},{4,2},{6,0},{8,14},{10,12},{12,10},{14,8},{16,22},{18,... | collective-permute-start | bytes 258056 | tf_op jit(solution)/shard_map/ppermute | solution.py:501
  34.6 0.4 collective-permute-start.8
  35.0 0.5 collective-permute-start.9
  35.5 2.1 %third_grad.1 = f32[1152,256]{1,0:T(8,128)} custom-call(bf16[8,272,128]{2,1,0:T(8,128)(2,1)S(1)} %constant_dynamic-update-slice_fusion.near_ref, bf16[8,272,128]{2,1,0:T(8,128)(2,1)S(1)} %collective-permute-done.7.far_ref, bf16[16,4,16,256]{3,2,1,0:T(8,128)(2,1)S(1)} %get-tuple-element.64.third_delta_ref.delta_ref), custom_call_target="tpu_custom_call" | custom-call | flops 600000000 | bytes 6000000 | tf_op jit(solution)/shard_map/third_grad/pallas_call | solution.py:716
  37.5 0.3 collective-permute-done.10
  37.8 0.0 collective-permute-done.8
  37.8 2.2 %collective-permute-done.9 = bf16[336,128]{1,0:T(8,128)(2,1)S(1)} collective-permute-done((bf16[336,128]{1,0:T(8,128)(2,1)S(1)}, bf16[336,128]{1,0:T(8,128)(2,1)S(1)}, u32[]{:S(2)}, u32[]{:S(2)}) %collective-permute-start.9) | collective-permute-done | bytes 86048 | tf_op jit(solution)/shard_map/ppermute | solution.py:501
  40.0 0.1 add_convert_fusion.2
  40.1 1.6 %collective-permute-start.11 = (bf16[336,128]{1,0:T(8,128)(2,1)S(1)}, bf16[336,128]{1,0:T(8,128)(2,1)S(1)}, u32[]{:S(2)}, u32[]{:S(2)}) collective-permute-start(bf16[336,128]{1,0:T(8,128)(2,1)S(1)} %add_convert_fusion.2), channel_id=1, source_target_pairs={{0,8},{2,10},{4,12},{6,14},{8,0},{10,2},{12,4},{14,6},{16,24},{18,... | collective-permute-start | bytes 258056 | tf_op jit(solution)/shard_map/ppermute | solution.py:501
  41.7 2.9 %collective-permute-done.11 = bf16[336,128]{1,0:T(8,128)(2,1)S(1)} collective-permute-done((bf16[336,128]{1,0:T(8,128)(2,1)S(1)}, bf16[336,128]{1,0:T(8,128)(2,1)S(1)}, u32[]{:S(2)}, u32[]{:S(2)}) %collective-permute-start.11) | collective-permute-done | bytes 86048 | tf_op jit(solution)/shard_map/ppermute | solution.py:501
  44.6 2.9 %collective-permute-start.12 = (bf16[336,128]{1,0:T(8,128)(2,1)S(1)}, bf16[336,128]{1,0:T(8,128)(2,1)S(1)}, u32[]{:S(2)}, u32[]{:S(2)}) collective-permute-start(bf16[336,128]{1,0:T(8,128)(2,1)S(1)} %add_convert_fusion.1), channel_id=1, source_target_pairs={{0,16},{2,18},{4,20},{6,22},{8,24},{10,26},{12,28},{14,30},{16,0},... | collective-permute-start | bytes 258056 | tf_op jit(solution)/shard_map/ppermute | solution.py:501
  47.5 3.1 %fourth_grad.1 = f32[2304,512]{1,0:T(8,128)} custom-call(bf16[256,2304]{1,0:T(8,128)(2,1)S(1)} %get-tuple-element.69.fourth_taps_ref, bf16[256,512]{1,0:T(8,128)(2,1)S(1)} %get-tuple-element.70.fourth_flat_ref), custom_call_target="tpu_custom_call" | custom-call | flops 600000000 | bytes 6000000 | tf_op jit(solution)/shard_map/fourth_grad/pallas_call | solution.py:735
  50.6 0.0 collective-permute-done.12
  50.7 1.6 %collective-permute-start.14 = (bf16[336,128]{1,0:T(8,128)(2,1)S(1)}, bf16[336,128]{1,0:T(8,128)(2,1)S(1)}, u32[]{:S(2)}, u32[]{:S(2)}) collective-permute-start(bf16[336,128]{1,0:T(8,128)(2,1)S(1)} %add_convert_fusion.refs_0_), channel_id=1, source_target_pairs={{0,4},{2,6},{4,0},{6,2},{8,12},{10,14},{12,8},{14,10},{16,20},{18,... | collective-permute-start | bytes 258056 | tf_op jit(solution)/shard_map/ppermute | solution.py:501
  52.3 0.0 collective-permute-start.13
  52.3 2.9 %collective-permute-done.14.refs_2_ = bf16[336,128]{1,0:T(8,128)(2,1)S(1)} collective-permute-done((bf16[336,128]{1,0:T(8,128)(2,1)S(1)}, bf16[336,128]{1,0:T(8,128)(2,1)S(1)}, u32[]{:S(2)}, u32[]{:S(2)}) %collective-permute-start.14) | collective-permute-done | bytes 86048 | tf_op jit(solution)/shard_map/ppermute | solution.py:501
  55.2 0.0 collective-permute-start.15
  55.2 0.0 collective-permute-done.13.refs_1_
  55.2 1.3 %collective-permute-done.15.refs_3_ = bf16[336,128]{1,0:T(8,128)(2,1)S(1)} collective-permute-done((bf16[336,128]{1,0:T(8,128)(2,1)S(1)}, bf16[336,128]{1,0:T(8,128)(2,1)S(1)}, u32[]{:S(2)}, u32[]{:S(2)}) %collective-permute-start.15) | collective-permute-done | bytes 86048 | tf_op jit(solution)/shard_map/ppermute | solution.py:501
  56.5 1.2 %finish.1 = (f32[9,160,64]{2,1,0:T(8,128)}, f32[576,128]{1,0:T(8,128)}) custom-call(bf16[336,128]{1,0:T(8,128)(2,1)S(1)} %add_convert_fusion.refs_0_, bf16[336,128]{1,0:T(8,128)(2,1)S(1)} %collective-permute-done.13.refs_1_, bf16[336,128]{1,0:T(8,128)(2,1)S(1)} %collective-permute-done.14.refs_2_, bf16[336,128]{1,0:T(8,128)(2,1)S(1)} %collective-permute-done.15.refs_3_), custom_call_target="tpu_custom_call" | custom-call | flops 1000000 | bytes 1500000 | tf_op jit(solution)/shard_map/finish/pallas_call | solution.py:753
  (9 shorter events, 0.1 us)
Async XLA Ops:
  0.6 25.1 %copy-start.2 = (bf16[3,3,64,128]{3,2,1,0:T(8,128)(2,1)S(1)}, bf16[3,3,64,128]{3,2,1,0:T(8,128)(2,1)}, u32[]{:S(2)}) copy-start(bf16[3,3,64,128]{3,2,1,0:T(8,128)(2,1)} %param.12) | copy-start | bytes 442372
  0.6 25.0 %copy-start.3 = (bf16[512]{0:T(512)(128)(2,1)S(1)}, bf16[512]{0:T(512)(128)(2,1)}, u32[]{:S(2)}) copy-start(bf16[512]{0:T(512)(128)(2,1)} %param.15) | copy-start | bytes 3076
  0.7 25.1 %copy-start.1 = (bf16[3,3,128,256]{3,2,1,0:T(8,128)(2,1)S(1)}, bf16[3,3,128,256]{3,2,1,0:T(8,128)(2,1)}, u32[]{:S(2)}) copy-start(bf16[3,3,128,256]{3,2,1,0:T(8,128)(2,1)} %param.13) | copy-start | bytes 1769476
  0.7 25.1 %copy-start = (bf16[3,3,256,512]{3,2,1,0:T(8,128)(2,1)S(1)}, bf16[3,3,256,512]{3,2,1,0:T(8,128)(2,1)}, u32[]{:S(2)}) copy-start(bf16[3,3,256,512]{3,2,1,0:T(8,128)(2,1)} %param.14) | copy-start | bytes 7077892
  0.7 6.7 %collective-permute-start = (s32[1,5,16,128]{3,2,1,0:T(8,128)}, s32[1,5,16,128]{3,2,1,0:T(8,128)S(1)}, u32[]{:S(2)}, u32[]{:S(2)}) collective-permute-start(s32[1,5,16,128]{3,2,1,0:T(8,128)} %got_hbm.1), channel_id=1, source_target_pairs={{0,1},{1,0},{2,3},{3,2},{4,5},{5,4},{6,7},{7,6},{8,9},{9,8},{10,11... | collective-permute-start | bytes 122888 | tf_op jit(solution)/shard_map/ppermute | solution.py:501
  3.7 3.7 %collective-permute-start.1 = (s32[1,1,8]{2,1,0:T(1,128)}, s32[1,1,8]{2,1,0:T(1,128)S(1)}, u32[]{:S(2)}, u32[]{:S(2)}) collective-permute-start(s32[1,1,8]{2,1,0:T(1,128)} %label_hbm.1), channel_id=1, source_target_pairs={{0,1},{1,0},{2,3},{3,2},{4,5},{5,4},{6,7},{7,6},{8,9},{9,8},{10,11... | collective-permute-start | bytes 104 | tf_op jit(solution)/shard_map/ppermute | solution.py:501
  10.1 5.3 %collective-permute-start.2 = (bf16[1,272,128]{2,1,0:T(8,128)(2,1)S(1)}, bf16[1,272,128]{2,1,0:T(8,128)(2,1)S(1)}, u32[]{:S(2)}, u32[]{:S(2)}) collective-permute-start(bf16[1,272,128]{2,1,0:T(8,128)(2,1)S(1)} %bitcast.18), channel_id=1, source_target_pairs={{0,16},{2,18},{4,20},{6,22},{8,24},{10,26},{12,28},{14,30},{16,0},... | collective-permute-start | bytes 208904 | tf_op jit(solution)/shard_map/ppermute | solution.py:501
  15.4 5.1 %collective-permute-start.3 = (bf16[2,272,128]{2,1,0:T(8,128)(2,1)S(1)}, bf16[2,272,128]{2,1,0:T(8,128)(2,1)S(1)}, u32[]{:S(2)}, u32[]{:S(2)}) collective-permute-start(bf16[2,272,128]{2,1,0:T(8,128)(2,1)S(1)} %slice.4), channel_id=1, source_target_pairs={{0,8},{2,10},{4,12},{6,14},{8,0},{10,2},{12,4},{14,6},{16,24},{18,... | collective-permute-start | bytes 417800 | tf_op jit(solution)/shard_map/ppermute | solution.py:501
  17.0 5.0 %collective-permute-start.4 = (bf16[1,272,128]{2,1,0:T(8,128)(2,1)S(1)}, bf16[1,272,128]{2,1,0:T(8,128)(2,1)S(1)}, u32[]{:S(2)}, u32[]{:S(2)}) collective-permute-start(bf16[1,272,128]{2,1,0:T(8,128)(2,1)S(1)} %bitcast.20), channel_id=1, source_target_pairs={{0,4},{2,6},{4,0},{6,2},{8,12},{10,14},{12,8},{14,10},{16,20},{18,... | collective-permute-start | bytes 208904 | tf_op jit(solution)/shard_map/ppermute | solution.py:501
  18.6 4.3 %collective-permute-start.5 = (bf16[1,272,128]{2,1,0:T(8,128)(2,1)S(1)}, bf16[1,272,128]{2,1,0:T(8,128)(2,1)S(1)}, u32[]{:S(2)}, u32[]{:S(2)}) collective-permute-start(bf16[1,272,128]{2,1,0:T(8,128)(2,1)S(1)} %collective-permute-done.2), channel_id=1, source_target_pairs={{0,4},{2,6},{4,0},{6,2},{8,12},{10,14},{12,8},{14,10},{16,20},{18,... | collective-permute-start | bytes 208904 | tf_op jit(solution)/shard_map/ppermute | solution.py:501
  20.5 5.1 %collective-permute-start.6 = (bf16[2,272,128]{2,1,0:T(8,128)(2,1)S(1)}, bf16[2,272,128]{2,1,0:T(8,128)(2,1)S(1)}, u32[]{:S(2)}, u32[]{:S(2)}) collective-permute-start(bf16[2,272,128]{2,1,0:T(8,128)(2,1)S(1)} %collective-permute-done.3), channel_id=1, source_target_pairs={{0,4},{2,6},{4,0},{6,2},{8,12},{10,14},{12,8},{14,10},{16,20},{18,... | collective-permute-start | bytes 417800 | tf_op jit(solution)/shard_map/ppermute | solution.py:501
  25.6 2.0 %collective-permute-start.7 = (bf16[8,272,128]{2,1,0:T(8,128)(2,1)S(1)}, bf16[8,272,128]{2,1,0:T(8,128)(2,1)S(1)}, u32[]{:S(2)}, u32[]{:S(2)}) collective-permute-start(bf16[8,272,128]{2,1,0:T(8,128)(2,1)S(1)} %constant_dynamic-update-slice_fusion.near_ref), channel_id=1, source_target_pairs={{0,2},{2,0},{4,6},{6,4},{8,10},{10,8},{12,14},{14,12},{16,18},{18,... | collective-permute-start | bytes 1671176 | tf_op jit(solution)/shard_map/ppermute | solution.py:501
  33.3 4.6 %collective-permute-start.10 = (bf16[336,128]{1,0:T(8,128)(2,1)S(1)}, bf16[336,128]{1,0:T(8,128)(2,1)S(1)}, u32[]{:S(2)}, u32[]{:S(2)}) collective-permute-start(bf16[336,128]{1,0:T(8,128)(2,1)S(1)} %get-tuple-element.61), channel_id=1, source_target_pairs={{0,6},{2,4},{4,2},{6,0},{8,14},{10,12},{12,10},{14,8},{16,22},{18,... | collective-permute-start | bytes 258056 | tf_op jit(solution)/shard_map/ppermute | solution.py:501
  34.6 3.2 %collective-permute-start.8 = (bf16[336,128]{1,0:T(8,128)(2,1)S(1)}, bf16[336,128]{1,0:T(8,128)(2,1)S(1)}, u32[]{:S(2)}, u32[]{:S(2)}) collective-permute-start(bf16[336,128]{1,0:T(8,128)(2,1)S(1)} %get-tuple-element.59), channel_id=1, source_target_pairs={{0,2},{2,0},{4,6},{6,4},{8,10},{10,8},{12,14},{14,12},{16,18},{18,... | collective-permute-start | bytes 258056 | tf_op jit(solution)/shard_map/ppermute | solution.py:501
  35.0 5.0 %collective-permute-start.9 = (bf16[336,128]{1,0:T(8,128)(2,1)S(1)}, bf16[336,128]{1,0:T(8,128)(2,1)S(1)}, u32[]{:S(2)}, u32[]{:S(2)}) collective-permute-start(bf16[336,128]{1,0:T(8,128)(2,1)S(1)} %get-tuple-element.60), channel_id=1, source_target_pairs={{0,4},{2,6},{4,0},{6,2},{8,12},{10,14},{12,8},{14,10},{16,20},{18,... | collective-permute-start | bytes 258056 | tf_op jit(solution)/shard_map/ppermute | solution.py:501
  40.1 4.6 %collective-permute-start.11 = (bf16[336,128]{1,0:T(8,128)(2,1)S(1)}, bf16[336,128]{1,0:T(8,128)(2,1)S(1)}, u32[]{:S(2)}, u32[]{:S(2)}) collective-permute-start(bf16[336,128]{1,0:T(8,128)(2,1)S(1)} %add_convert_fusion.2), channel_id=1, source_target_pairs={{0,8},{2,10},{4,12},{6,14},{8,0},{10,2},{12,4},{14,6},{16,24},{18,... | collective-permute-start | bytes 258056 | tf_op jit(solution)/shard_map/ppermute | solution.py:501
  44.6 6.0 %collective-permute-start.12 = (bf16[336,128]{1,0:T(8,128)(2,1)S(1)}, bf16[336,128]{1,0:T(8,128)(2,1)S(1)}, u32[]{:S(2)}, u32[]{:S(2)}) collective-permute-start(bf16[336,128]{1,0:T(8,128)(2,1)S(1)} %add_convert_fusion.1), channel_id=1, source_target_pairs={{0,16},{2,18},{4,20},{6,22},{8,24},{10,26},{12,28},{14,30},{16,0},... | collective-permute-start | bytes 258056 | tf_op jit(solution)/shard_map/ppermute | solution.py:501
  50.7 4.6 %collective-permute-start.14 = (bf16[336,128]{1,0:T(8,128)(2,1)S(1)}, bf16[336,128]{1,0:T(8,128)(2,1)S(1)}, u32[]{:S(2)}, u32[]{:S(2)}) collective-permute-start(bf16[336,128]{1,0:T(8,128)(2,1)S(1)} %add_convert_fusion.refs_0_), channel_id=1, source_target_pairs={{0,4},{2,6},{4,0},{6,2},{8,12},{10,14},{12,8},{14,10},{16,20},{18,... | collective-permute-start | bytes 258056 | tf_op jit(solution)/shard_map/ppermute | solution.py:501
  52.3 2.9 %collective-permute-start.13 = (bf16[336,128]{1,0:T(8,128)(2,1)S(1)}, bf16[336,128]{1,0:T(8,128)(2,1)S(1)}, u32[]{:S(2)}, u32[]{:S(2)}) collective-permute-start(bf16[336,128]{1,0:T(8,128)(2,1)S(1)} %add_convert_fusion.refs_0_), channel_id=1, source_target_pairs={{0,2},{2,0},{4,6},{6,4},{8,10},{10,8},{12,14},{14,12},{16,18},{18,... | collective-permute-start | bytes 258056 | tf_op jit(solution)/shard_map/ppermute | solution.py:501
  55.2 1.3 %collective-permute-start.15 = (bf16[336,128]{1,0:T(8,128)(2,1)S(1)}, bf16[336,128]{1,0:T(8,128)(2,1)S(1)}, u32[]{:S(2)}, u32[]{:S(2)}) collective-permute-start(bf16[336,128]{1,0:T(8,128)(2,1)S(1)} %collective-permute-done.14.refs_2_), channel_id=1, source_target_pairs={{0,2},{2,0},{4,6},{6,4},{8,10},{10,8},{12,14},{14,12},{16,18},{18,... | collective-permute-start | bytes 258056 | tf_op jit(solution)/shard_map/ppermute | solution.py:501

commit v5 on v4

--- a/solution.py
+++ b/solution.py
@@ -150,14 +150,21 @@
     lift_hbm,
     first_w_hbm,
     second_w_hbm,
+    third_w_hbm,
+    fourth_w_hbm,
     even_ref,
     odd_ref,
     labels_ref,
     lift_all_ref,
     first_all_ref,
     second_w_ref,
+    third_w_ref,
+    fourth_w_ref,
+    second_wt_ref,
+    third_wt_ref,
+    fourth_wt_ref,
+    label_ref,
     got_ref,
-    label_ref,
     lift_ref,
     first_w_ref,
     bits_ref,
@@ -169,6 +176,8 @@
         (label_hbm, label_ref),
         (first_w_hbm, first_w_ref),
         (second_w_hbm, second_w_ref),
+        (third_w_hbm, third_w_ref),
+        (fourth_w_hbm, fourth_w_ref),
     )
     copies = [
         pltpu.make_async_copy(source, target, sems.at[k])
@@ -205,7 +214,12 @@
         first_all_ref[row_tap, pl.ds(384 + col_tap * rest, rest)] = first_w_ref[
             tap, pl.ds(128, rest)
         ]
-    copies[4].wait()
+    pairs = ((second_w_ref, second_wt_ref), (third_w_ref, third_wt_ref))
+    pairs += ((fourth_w_ref, fourth_wt_ref),)
+    for k, (source, target) in enumerate(pairs):
+        copies[4 + k].wait()
+        for tap in range(9):
+            target[tap] = source[tap].T
 
 
 def early_kernel(pieces, rest, *refs):
@@ -278,19 +292,10 @@
     send_ref[pl.ds(sent, 16)] = labels.astype(jnp.bfloat16)
 
 
-def transpose_kernel(second_w_ref, third_w_ref, fourth_w_ref, second_ref, third_ref, fourth_ref):
-    for tap in range(9):
-        second_ref[tap] = second_w_ref[tap].T
-        third_ref[tap] = third_w_ref[tap].T
-        fourth_ref[tap] = fourth_w_ref[tap].T
-
-
 def take_samples(near_ref, far_ref, second_ref, label_ref, bands):
     half = near_ref.shape[0]
     width = half.bit_length()
-    chunk, channels = second_ref.shape[0], second_ref.shape[-1]
-    rows, phases = 4 * bands, 4
-    cells = rows * phases * BLOCK
+    chunk = second_ref.shape[0]
     me = lax.axis_index("dp")
     for slot in range(2 * half):
         reverse = sum(((slot >> k) & 1) << (width - 1 - k) for k in range(width))
@@ -298,18 +303,7 @@
         ref = near_ref if slot < half else far_ref
 
         def take(ref=ref, inner=slot % half, place=sample % chunk):
-            second = ref[inner, pl.ds(0, cells)].astype(jnp.float32)
-            fill_map(
-                second_ref.at[pl.ds(place, 1)],
-                second.reshape(1, rows, phases, BLOCK, channels),
-                1,
-            )
-            if label_ref is not None:
-                label = ref[inner, pl.ds(cells, 16)].astype(jnp.float32)[:BLOCK]
-                for index in range(bands):
-                    label_ref[place, index] = jnp.broadcast_to(
-                        label[:, index : index + 1], label.shape
-                    )
+            put_sample(ref, inner, second_ref, label_ref, place, bands)
 
         if chunk == 2 * half:
             take()
@@ -325,19 +319,29 @@
         )
 
 
-def deep_kernel(
+def put_sample(ref, inner, second_ref, label_ref, place, bands):
+    rows, phases = 4 * bands, 4
+    cells = rows * phases * BLOCK
+    second = ref[inner, pl.ds(0, cells)].astype(jnp.float32)
+    fill_map(
+        second_ref.at[pl.ds(place, 1)],
+        second.reshape(1, rows, phases, BLOCK, second.shape[-1]),
+        1,
+    )
+    if label_ref is not None:
+        label = ref[inner, pl.ds(cells, 16)].astype(jnp.float32)[:BLOCK]
+        for index in range(bands):
+            label_ref[place, index] = jnp.broadcast_to(label[:, index : index + 1], label.shape)
+
+
+def deep_layers(
     batch,
     bands,
-    near_ref,
-    far_ref,
     third_w_ref,
     fourth_w_ref,
     fourth_wt_ref,
     head_ref,
-    third_flat_ref,
     fourth_taps_ref,
-    fourth_flat_ref,
-    head_grad_ref,
     second_ref,
     label_ref,
     third_taps_ref,
@@ -347,10 +351,6 @@
     fourth_delta_ref,
 ):
     samples = second_ref.shape[0]
-    zero_row(second_ref)
-    take_samples(near_ref, far_ref, second_ref, label_ref, bands)
-    labels = label_ref[...].reshape(-1, label_ref.shape[-1])[:, :1]
-
     rows, phases = 2 * bands, 2
     third_taps(second_ref, third_taps_ref, rows, phases)
     value, slope = silu_and_slope(dot_nn(third_taps_ref[...], third_w_ref[...]))
@@ -366,16 +366,10 @@
         )
     value, slope = silu_and_slope(dot_nn(fourth_taps_ref[...], fourth_w_ref[...]))
     head = head_ref[...].astype(jnp.float32)
+    labels = label_ref[...].reshape(-1, label_ref.shape[-1])[:, :1]
     logits = jnp.sum(value * head, axis=1, keepdims=True)
     logit_grad = (jax.nn.sigmoid(logits) - labels) / batch
-
-    @pl.when(pl.program_id(0) == 0)
-    def _():
-        head_grad_ref[...] = jnp.zeros(head_grad_ref.shape, jnp.float32)
-
-    head_grad_ref[...] += jnp.sum(value * logit_grad, axis=0, keepdims=True)
     delta = rounded(logit_grad * head * slope)
-    fourth_flat_ref[...] = delta.astype(jnp.bfloat16)
     last_row_zero(fourth_delta_ref)
     fill_delta(fourth_delta_ref, delta.reshape(samples, rows, phases, BLOCK, delta.shape[-1]))
     for row_parity in range(2):
@@ -386,13 +380,69 @@
             part = rounded(part * third_slope_ref[:, :, row_parity, :, col_parity])
             for row in range(rows):
                 third_delta_ref[:, 2 * row + row_parity, col_parity] = part[:, row, 0]
-    third_flat_ref[...] = (
-        third_delta_ref[...].reshape(third_flat_ref.shape).astype(jnp.bfloat16)
-    )
-
-
-def late_kernel(
+    return value, logit_grad, delta
+
+
+def deep_kernel(
+    batch,
+    bands,
+    near_ref,
+    far_ref,
+    third_w_ref,
+    fourth_w_ref,
+    fourth_wt_ref,
+    head_ref,
+    fourth_taps_ref,
+    fourth_flat_ref,
+    head_grad_ref,
+    third_grad_ref,
+    second_ref,
+    label_ref,
+    third_taps_ref,
+    third_ref,
+    third_slope_ref,
     third_delta_ref,
+    fourth_delta_ref,
+):
+    zero_row(second_ref)
+    take_samples(near_ref, far_ref, second_ref, label_ref, bands)
+    value, logit_grad, delta = deep_layers(
+        batch,
+        bands,
+        third_w_ref,
+        fourth_w_ref,
+        fourth_wt_ref,
+        head_ref,
+        fourth_taps_ref,
+        second_ref,
+        label_ref,
+        third_taps_ref,
+        third_ref,
+        third_slope_ref,
+        third_delta_ref,
+        fourth_delta_ref,
+    )
+
+    @pl.when(pl.program_id(0) == 0)
+    def _():
+        head_grad_ref[...] = jnp.zeros(head_grad_ref.shape, jnp.float32)
+        third_grad_ref[...] = jnp.zeros(third_grad_ref.shape, jnp.float32)
+
+    head_grad_ref[...] += jnp.sum(value * logit_grad, axis=0, keepdims=True)
+    fourth_flat_ref[...] = delta.astype(jnp.bfloat16)
+    delta = third_delta_ref[...]
+    delta = delta.reshape(-1, delta.shape[-1]).astype(jnp.bfloat16)
+    third_grad_ref[...] += dot_tn(third_taps_ref[...], delta)
+
+
+def local_kernel(
+    batch,
+    bands,
+    payload_ref,
+    third_w_ref,
+    fourth_w_ref,
+    fourth_wt_ref,
+    head_ref,
     third_wt_ref,
     second_wt_ref,
     even_ref,
@@ -403,12 +453,26 @@
     *refs,
 ):
     out_refs = refs[:4]
-    third_ref, second_ref, first_delta_ref, flat_ref = refs[4:]
+    third_ref, second_ref, first_delta_ref, flat_ref, second_map_ref, label_ref = refs[4:10]
+    fourth_taps_ref = refs[10]
+    third_delta_ref = refs[14]
+    zero_row(second_map_ref)
+    put_sample(payload_ref, 0, second_map_ref, label_ref, 0, bands)
+    deep_layers(
+        batch,
+        bands,
+        third_w_ref,
+        fourth_w_ref,
+        fourth_wt_ref,
+        head_ref,
+        fourth_taps_ref,
+        second_map_ref,
+        label_ref,
+        *refs[11:16],
+    )
     sample = lax.axis_index("dp")
-    _, rows, cells, channels = third_delta_ref.shape
-    phases = cells // BLOCK
-    delta = third_delta_ref[pl.ds(sample, 1)].astype(jnp.float32)
-    fill_delta(third_ref, delta.reshape(1, rows, phases, BLOCK, channels))
+    _, rows, phases, _, _ = third_delta_ref.shape
+    fill_delta(third_ref, third_delta_ref[...])
     last_row_zero(third_ref)
     last_row_zero(second_ref)
     for row_parity in range(2):
@@ -450,21 +514,6 @@
         out_refs[slot][...] = flat_ref[pl.ds(at, share)].astype(jnp.bfloat16)
 
 
-def third_grad_kernel(
-    bands, near_ref, far_ref, delta_ref, out_ref, second_ref, third_taps_ref
-):
-    zero_row(second_ref)
-    take_samples(near_ref, far_ref, second_ref, None, bands)
-    third_taps(second_ref, third_taps_ref, 2 * bands, 2)
-    delta = delta_ref[...].reshape(-1, delta_ref.shape[-1])
-
-    @pl.when(pl.program_id(0) == 0)
-    def _():
-        out_ref[...] = jnp.zeros(out_ref.shape, jnp.float32)
-
-    out_ref[...] += dot_tn(third_taps_ref[...], delta)
-
-
 def fourth_grad_kernel(fourth_taps_ref, fourth_flat_ref, out_ref):
     @pl.when(pl.program_id(1) == 0)
     def _():
@@ -511,23 +560,51 @@
     return pieces
 
 
-def gathered_halves(value, samples):
-    half = samples // 2
-    quarter = half // 2
-    near = jnp.zeros((half,) + value.shape[1:], value.dtype)
-    near = lax.dynamic_update_slice(near, value, (0, 0, 0))
-    last, count, others = value, 1, []
+def put(buffer, part, at):
+    return lax.dynamic_update_slice(buffer, part, (at,) + (0,) * (buffer.ndim - 1))
+
+
+def gather_and_sum(payload, local_quarters, samples):
+    tie = lax.optimization_barrier
+    half, quarter = samples // 2, samples // 4
+    near = put(jnp.zeros((half,) + payload.shape[1:], payload.dtype), payload, 0)
+    last, last_at, count, bit = payload, 0, 1, 4
+    quarters, total = None, None
     while count < quarter:
-        part = near[:count] if count > 1 else value
-        got = swapped(part, "dp", half // count)
-        others.append((swapped(last, "dp", 2), quarter + (count // 2 if count > 1 else 0)))
-        near = lax.dynamic_update_slice(near, got, (count, 0, 0))
-        last = got
+        got = swapped(near[:count] if count > 1 else payload, "dp", half // count)
+        beside = swapped(last, "dp", 2)
+        if quarters is None:
+            quarters = local_quarters()
+            got, *quarters = tie((got, *quarters))
+        elif total is None:
+            parts = [swapped(quarters[slot], "dp", slot) for slot in (1, 2, 3)]
+            got, *parts = tie((got, *parts))
+            total = added(quarters[0], *parts)
+        else:
+            got, other = tie((got, swapped(total, "dp", bit)))
+            total = added(total, other)
+            bit *= 2
+        near = put(near, beside, quarter + last_at)
+        near = put(near, got, count)
+        last, last_at = got, count
         count *= 2
-    others.append((swapped(last, "dp", 2), quarter + (count // 2 if count > 1 else 0)))
-    for part, at in others:
-        near = lax.dynamic_update_slice(near, part, (at, 0, 0))
-    return near, swapped(near, "dp", 1)
+    far = jnp.zeros_like(near)
+    early = swapped(near[: quarter + last_at], "dp", 1)
+    beside = swapped(last, "dp", 2)
+    if quarters is None:
+        quarters = local_quarters()
+    if total is None:
+        total = added(
+            quarters[0], *[swapped(quarters[slot], "dp", slot) for slot in (1, 2, 3)]
+        )
+    elif bit < samples:
+        beside, other = tie((beside, swapped(total, "dp", bit)))
+        total = added(total, other)
+        bit *= 2
+    near = put(near, beside, quarter + last_at)
+    far = put(far, early, 0)
+    far = put(far, swapped(beside, "dp", 1), quarter + last_at)
+    return near, far, total, bit
 
 
 def added(*parts):
@@ -564,7 +641,6 @@
         return pltpu.CompilerParams(vmem_limit_bytes=(size if small else 60) * MIB)
 
     lines = band_pieces(occupancy, bands)
-    labels = band_pieces(state_labels, bands)
     first_w = temporal_weight.reshape(9, lift_all, one)
     second_w = middle_weight.reshape(9, one, two)
     third_w = deeper_weight.reshape(9, two, three)
@@ -579,9 +655,30 @@
     own_cells = shaped((band // 2 * cols // 2, 512), bf16)
     own_args = [
         pltpu.with_memory_space_constraint(value, pltpu.HBM)
-        for value in (occupancy, state_labels, lift_weight, first_w, second_w)
+        for value in (
+            occupancy,
+            state_labels,
+            lift_weight,
+            first_w,
+            second_w,
+            third_w,
+            fourth_w,
+        )
     ]
-    own_even, own_odd, own_labels, lift_all_w, first_all, second_w2 = pl.pallas_call(
+    (
+        own_even,
+        own_odd,
+        own_labels,
+        lift_all_w,
+        first_all,
+        second_w2,
+        third_w2,
+        fourth_w2,
+        second_wt,
+        third_wt,
+        fourth_wt,
+        labels,
+    ) = pl.pallas_call(
         own_kernel,
         out_shape=(
             own_cells,
@@ -590,21 +687,27 @@
             shaped((128, 256), bf16),
             shaped((3, 512, one), bf16),
             shaped(second_w.shape, bf16),
+            shaped(third_w.shape, bf16),
+            shaped(fourth_w.shape, bf16),
+            shaped((9, two, one), bf16),
+            shaped((9, three, two), bf16),
+            shaped((9, four, three), bf16),
+            shaped(state_labels.shape, state_labels.dtype),
         ),
-        in_specs=[hbm] * 5,
-        out_specs=(vmem,) * 6,
+        in_specs=[hbm] * 7,
+        out_specs=(vmem,) * 12,
         scratch_shapes=[
             pltpu.VMEM(occupancy.shape, occupancy.dtype),
-            pltpu.VMEM(state_labels.shape, state_labels.dtype),
             pltpu.VMEM(lift_weight.shape, bf16),
             pltpu.VMEM(first_w.shape, bf16),
             bits_scratch,
-            pltpu.SemaphoreType.DMA((5,)),
+            pltpu.SemaphoreType.DMA((7,)),
         ],
-        compiler_params=grant(16),
-        cost_estimate=cost(100_000_000, 4_000_000),
+        compiler_params=grant(24),
+        cost_estimate=cost(100_000_000, 10_000_000),
         name="own_band",
     )(*own_args)
+    labels = band_pieces(labels, bands)
     pieces = len(lines) - 1
     even, odd, payload, first, first_slope, second_slope = pl.pallas_call(
         functools.partial(early_kernel, pieces, lift_all - 128),
@@ -624,40 +727,68 @@
         name="early",
     )(*lines[1:], *labels[1:], own_labels, lift_all_w, first_all, second_w2, own_even, own_odd)
 
-    near, far = gathered_halves(payload[None], samples)
-
-    second_wt, third_wt, fourth_wt = pl.pallas_call(
-        transpose_kernel,
-        out_shape=(
-            shaped((9, two, one), bf16),
-            shaped((9, three, two), bf16),
-            shaped((9, four, three), bf16),
-        ),
-        in_specs=[vmem] * 3,
-        out_specs=(vmem,) * 3,
-        compiler_params=grant(16),
-        cost_estimate=cost(10_000_000, 6_000_000),
-        name="transpose",
-    )(second_w, third_w, fourth_w)
+    payload = payload[None]
+    deep_weights = (
+        third_w2.reshape(9 * two, three),
+        fourth_w2.reshape(9 * three, four),
+        fourth_wt,
+        head,
+    )
+
+    third_cells = 2 * bands * 2 * BLOCK
+    fourth_cells = bands * BLOCK
+
+    def second_scratch(count):
+        return pltpu.VMEM((count, 2 * bands + 1, 2, 3, 2, BLOCK, two), f32)
+
+    def third_taps_scratch(count):
+        return pltpu.VMEM((count * third_cells, 9 * two), bf16)
+
+    def deep_scratch(count):
+        return [
+            third_taps_scratch(count),
+            pltpu.VMEM((count, bands + 1, 2, 2, 2, BLOCK, three), f32),
+            pltpu.VMEM((count, bands, 2, 1, 2, BLOCK, three), f32),
+            pltpu.VMEM((count, 2 * bands, 2, BLOCK, three), f32),
+            pltpu.VMEM((count, bands + 1, 2, BLOCK, four), f32),
+        ]
+
+    share = 21 * one // 4
+    local_call = pl.pallas_call(
+        functools.partial(local_kernel, samples, bands),
+        out_shape=(shaped((share, two), bf16),) * 4,
+        in_specs=[vmem] * 12,
+        out_specs=(vmem,) * 4,
+        scratch_shapes=[
+            pltpu.VMEM((1, 2 * bands + 1, 3, BLOCK, three), f32),
+            pltpu.VMEM((1, 4 * bands + 1, 5, BLOCK, two), f32),
+            pltpu.VMEM(first_slope.shape, f32),
+            pltpu.VMEM((21 * one, two), f32),
+            second_scratch(1),
+            pltpu.VMEM((1, bands, BLOCK, two), f32),
+            pltpu.VMEM((fourth_cells, 9 * three), bf16),
+        ]
+        + deep_scratch(1),
+        compiler_params=grant(24),
+        cost_estimate=cost(300_000_000, 9_000_000),
+        name="local",
+    )
+    maps = (third_wt, second_wt, even, odd, first, first_slope, second_slope)
+    near, far, total, bit = gather_and_sum(
+        payload, lambda: local_call(payload, *deep_weights, *maps), samples
+    )
 
     chunk = max(1, min(samples, 32 // bands))
     steps = samples // chunk
-    third_cells = 2 * bands * 2 * BLOCK
-    fourth_cells = bands * BLOCK
     full = lambda *shape: pl.BlockSpec(shape, lambda i: (0,) * len(shape))
-    delta_block = pl.BlockSpec(
-        (chunk, 2 * bands, 2 * BLOCK, three), lambda i: (i, 0, 0, 0)
-    )
-    second_scratch = pltpu.VMEM((chunk, 2 * bands + 1, 2, 3, 2, BLOCK, two), f32)
-    third_taps_scratch = pltpu.VMEM((chunk * third_cells, 9 * two), bf16)
-    third_delta, fourth_taps, fourth_flat, head_grad = pl.pallas_call(
+    fourth_taps, fourth_flat, head_grad, deeper_grad = pl.pallas_call(
         functools.partial(deep_kernel, samples, bands),
         grid=(steps,),
         out_shape=(
-            shaped((samples, 2 * bands, 2 * BLOCK, three), bf16),
             shaped((samples * fourth_cells, 9 * three), bf16),
             shaped((samples * fourth_cells, four), bf16),
             shaped((1, four), f32),
+            shaped((9 * two, three), f32),
         ),
         in_specs=[
             full(*near.shape),
@@ -668,70 +799,23 @@
             full(1, four),
         ],
         out_specs=(
-            delta_block,
             pl.BlockSpec((chunk * fourth_cells, 9 * three), lambda i: (i, 0)),
             pl.BlockSpec((chunk * fourth_cells, four), lambda i: (i, 0)),
             full(1, four),
+            full(9 * two, three),
         ),
-        scratch_shapes=[
-            second_scratch,
-            pltpu.VMEM((chunk, bands, BLOCK, two), f32),
-            third_taps_scratch,
-            pltpu.VMEM((chunk, bands + 1, 2, 2, 2, BLOCK, three), f32),
-            pltpu.VMEM((chunk, bands, 2, 1, 2, BLOCK, three), f32),
-            pltpu.VMEM((chunk, 2 * bands, 2, BLOCK, three), f32),
-            pltpu.VMEM((chunk, bands + 1, 2, BLOCK, four), f32),
-        ],
+        scratch_shapes=[second_scratch(chunk), pltpu.VMEM((chunk, bands, BLOCK, two), f32)]
+        + deep_scratch(chunk),
         compiler_params=grant(40),
         cost_estimate=cost(1_300_000_000, 12_000_000),
         name="deep",
-    )(
-        near,
-        far,
-        third_w.reshape(9 * two, three),
-        fourth_w.reshape(9 * three, four),
-        fourth_wt,
-        head,
-    )
-
-    share = 21 * one // 4
-    quarters = pl.pallas_call(
-        late_kernel,
-        out_shape=(shaped((share, two), bf16),) * 4,
-        in_specs=[vmem] * 8,
-        out_specs=(vmem,) * 4,
-        scratch_shapes=[
-            pltpu.VMEM((1, 2 * bands + 1, 3, BLOCK, three), f32),
-            pltpu.VMEM((1, 4 * bands + 1, 5, BLOCK, two), f32),
-            pltpu.VMEM(first_slope.shape, f32),
-            pltpu.VMEM((21 * one, two), f32),
-        ],
-        compiler_params=grant(24),
-        cost_estimate=cost(200_000_000, 6_000_000),
-        name="late",
-    )(third_delta, third_wt, second_wt, even, odd, first, first_slope, second_slope)
-
-    mine, near3, far3, delta3 = lax.optimization_barrier((quarters[0], near, far, third_delta))
-    got = [swapped(quarters[slot], "dp", slot) for slot in (1, 2, 3)]
-    deeper_grad = pl.pallas_call(
-        functools.partial(third_grad_kernel, bands),
-        grid=(steps,),
-        out_shape=shaped((9 * two, three), f32),
-        in_specs=[full(*near.shape), full(*far.shape), delta_block],
-        out_specs=full(9 * two, three),
-        scratch_shapes=[second_scratch, third_taps_scratch],
-        compiler_params=grant(24),
-        cost_estimate=cost(600_000_000, 6_000_000),
-        name="third_grad",
-    )(near3, far3, delta3)
-    got[2], deeper_grad = lax.optimization_barrier((got[2], deeper_grad))
-    total = added(mine, *got)
-    bit = 4
-    while 2 * bit < samples:
-        total = added(total, swapped(total, "dp", bit))
-        bit *= 2
-    total, fourth_taps, fourth_flat = lax.optimization_barrier((total, fourth_taps, fourth_flat))
-    other = swapped(total, "dp", bit) if bit < samples else jnp.zeros_like(total)
+    )(near, far, *deep_weights)
+
+    if bit < samples:
+        other, fourth_flat = lax.optimization_barrier((swapped(total, "dp", bit), fourth_flat))
+        total = added(total, other)
+    beside = swapped(total, "dp", 2)
+    core = swapped(total, "dp", 1)
     deepest_grad = pl.pallas_call(
         fourth_grad_kernel,
         grid=(3, steps),
@@ -745,10 +829,7 @@
         cost_estimate=cost(600_000_000, 6_000_000),
         name="fourth_grad",
     )(fourth_taps, fourth_flat)
-    other, deepest_grad = lax.optimization_barrier((other, deepest_grad))
-    total = added(total, other)
-    beside = swapped(total, "dp", 2)
-    core = swapped(total, "dp", 1)
+    beside, deepest_grad = lax.optimization_barrier((beside, deepest_grad))
     across = swapped(beside, "dp", 1)
     temporal_grad, middle_grad = pl.pallas_call(
         finish_kernel,

time: 57.9 us -> 50.8 us (0.88)
  waiting for transfers between devices: 20 us -> 14.1 us
  starting transfers between devices: 19.3 us -> 16.5 us
  Pallas kernels: 17.4 us -> 18.9 us
    ppermute x16 -> x17, waiting for transfers between devices: 20 us -> 14.1 us  [swapped(): lax.ppermute(value, axis, [(i, i ^ bit) for i in range(lax.axis_size(axis...]
    ppermute x16 -> x17, starting transfers between devices: 19.3 us -> 16.5 us  [swapped(): lax.ppermute(value, axis, [(i, i ^ bit) for i in range(lax.axis_size(axis...]
    pallas_call x1, Pallas kernels: 4.36 us -> 6.24 us  [local(): pl.pallas_call(functools.partial(deep_kernel, samples, bands), grid=(step...]
    pallas_call x3 -> x1, Pallas kernels: 4.25 us -> 2.77 us  [local(): local_call(payload, *deep_weights, *maps)]
    pallas_call x1, Pallas kernels: 1.67 us -> 2.82 us  [local(): pl.pallas_call(own_kernel, out_shape=(own_cells, own_cells, shaped((16, t...]
  transfers between devices with their start and end apart: 16 -> 17, of which waited for: 11 -> 8; matrix products, arithmetic and copies ran while one was open for 0% -> 1% of each run, Pallas kernels for 14% -> 30%
where the time goes in v5:
time: 50.8 us; the launch traced here: 50.6 us
  Pallas kernels  18.9 us (37%)
  starting transfers between devices  16.5 us (32%)
  waiting for transfers between devices  14.1 us (28%)
  between operations  0.77 us (2%)
    ppermute x17, starting transfers between devices, swapped(): lax.ppermute(value, axis, [(i, i ^ bit) for i in range(lax.axis_size(axis...  16.5 us
    ppermute x17, waiting for transfers between devices, swapped(): lax.ppermute(value, axis, [(i, i ^ bit) for i in range(lax.axis_size(axis...  14.1 us
    pallas_call x1, Pallas kernels, local(): pl.pallas_call(functools.partial(deep_kernel, samples, bands), grid=(step...  6.24 us
    pallas_call x1, Pallas kernels, local(): pl.pallas_call(fourth_grad_kernel, grid=(3, steps), out_shape=shaped((9 *...  3.15 us
    pallas_call x1, Pallas kernels, local(): pl.pallas_call(own_kernel, out_shape=(own_cells, own_cells, shaped((16, t...  2.82 us
    pallas_call x1, Pallas kernels, local(): local_call(payload, *deep_weights, *maps)  2.77 us
    pallas_call x1, Pallas kernels, local(): pl.pallas_call(functools.partial(early_kernel, pieces, lift_all - 128), o...  2.73 us
    pallas_call x1, Pallas kernels, local(): pl.pallas_call(finish_kernel, out_shape=(shaped((9, lift_all, one), f32),...  1.22 us
  transfers between devices with their start and end apart: 17, of which 8 were waited for; matrix products, arithmetic and copies ran while one was open for 1% of the time, Pallas kernels for 30%

profile of v5, /device:TPU:0, one launch (start us, length us, event | category | flops | bytes accessed | tf_op | source)
XLA Modules:
  0.0 50.6 jit_solution(18421223211464945635)
XLA Ops:
  0.6 3.0 %collective-permute-start = (s32[1,5,16,128]{3,2,1,0:T(8,128)}, s32[1,5,16,128]{3,2,1,0:T(8,128)S(1)}, u32[]{:S(2)}, u32[]{:S(2)}) collective-permute-start(s32[1,5,16,128]{3,2,1,0:T(8,128)} %got_hbm.1), channel_id=1, source_target_pairs={{0,1},{1,0},{2,3},{3,2},{4,5},{5,4},{6,7},{7,6},{8,9},{9,8},{10,11... | collective-permute-start | bytes 122888 | tf_op jit(solution)/shard_map/ppermute | solution.py:550
  3.6 0.0 copy-start
  3.6 2.8 %own_band.1 = (bf16[512,512]{1,0:T(8,128)(2,1)S(1)}, bf16[512,512]{1,0:T(8,128)(2,1)S(1)}, f32[16,128]{1,0:T(8,128)S(1)}, bf16[128,256]{1,0:T(8,128)(2,1)S(1)}, ...) custom-call(s32[1,5,16,128]{3,2,1,0:T(8,128)} %got_hbm.1, ...), custom_call_target="tpu_custom_call" | custom-call | flops 100000000 | bytes 10000000 | tf_op jit(solution)/shard_map/own_band/pallas_call | solution.py:681
  6.5 0.1 collective-permute-start.1
  6.6 3.5 %collective-permute-done.1.refs_1_ = s32[1,1,8]{2,1,0:T(1,128)S(1)} collective-permute-done((s32[1,1,8]{2,1,0:T(1,128)S(1)}, s32[1,1,8]{2,1,0:T(1,128)S(1)}, u32[]{:S(2)}, u32[]{:S(2)}) %collective-permute-start.1) | collective-permute-done | bytes 64 | tf_op jit(solution)/shard_map/ppermute | solution.py:550
  10.1 0.0 collective-permute-done.refs_0_
  10.1 2.7 %early.1 = (bf16[1024,512]{1,0:T(8,128)(2,1)S(1)}, bf16[1088,512]{1,0:T(8,128)(2,1)S(1)}, bf16[272,128]{1,0:T(8,128)(2,1)S(1)}, f32[1,9,2,5,2,8,64]{6,5,4,3,2,1,...) custom-call(s32[1,5,16,128]{3,2,1,0:T(8,128)S(1)} %collective-permute-done.refs_0_, ...), custom_call_target="tpu_custom_call" | custom-call | flops 150000000 | bytes 4000000 | tf_op jit(solution)/shard_map/early/pallas_call | solution.py:712
  12.8 2.7 %collective-permute-start.2 = (bf16[1,272,128]{2,1,0:T(8,128)(2,1)S(1)}, bf16[1,272,128]{2,1,0:T(8,128)(2,1)S(1)}, u32[]{:S(2)}, u32[]{:S(2)}) collective-permute-start(bf16[1,272,128]{2,1,0:T(8,128)(2,1)S(1)} %bitcast.16), channel_id=1, source_target_pairs={{0,16},{2,18},{4,20},{6,22},{8,24},{10,26},{12,28},{14,30},{16,0},... | collective-permute-start | bytes 208904 | tf_op jit(solution)/shard_map/ppermute | solution.py:550
  15.5 1.5 %collective-permute-start.3 = (bf16[1,272,128]{2,1,0:T(8,128)(2,1)S(1)}, bf16[1,272,128]{2,1,0:T(8,128)(2,1)S(1)}, u32[]{:S(2)}, u32[]{:S(2)}) collective-permute-start(bf16[1,272,128]{2,1,0:T(8,128)(2,1)S(1)} %bitcast.17), channel_id=1, source_target_pairs={{0,4},{2,6},{4,0},{6,2},{8,12},{10,14},{12,8},{14,10},{16,20},{18,... | collective-permute-start | bytes 208904 | tf_op jit(solution)/shard_map/ppermute | solution.py:550
  17.0 0.0 copy-done
  17.0 0.1 dynamic_update_slice.22
  17.1 2.8 %local.1 = (bf16[336,128]{1,0:T(8,128)(2,1)S(1)}, bf16[336,128]{1,0:T(8,128)(2,1)S(1)}, bf16[336,128]{1,0:T(8,128)(2,1)S(1)}, bf16[336,128]{1,0:T(8,128)(2,1)S(1)}) custom-call(bf16[1,272,128]{2,1,0:T(8,128)(2,1)S(1)} %bitcast.19, bf16[1152,256]{1,0:T(8,128)(2,1)S(1)} %bitcast.14, bf16[2304,512]{1,0:T(8,128)(2,1)S(1)} %bitcast.12, ...), custom_call_target="tpu_custom_call" | custom-call | flops 300000000 | bytes 9000000 | tf_op jit(solution)/shard_map/local/pallas_call | solution.py:778
  19.8 0.0 collective-permute-done.2
  19.9 0.6 %collective-permute-start.11 = (bf16[1,272,128]{2,1,0:T(8,128)(2,1)S(1)}, bf16[1,272,128]{2,1,0:T(8,128)(2,1)S(1)}, u32[]{:S(2)}, u32[]{:S(2)}) collective-permute-start(bf16[1,272,128]{2,1,0:T(8,128)(2,1)S(1)} %collective-permute-done.2), channel_id=1, source_target_pairs={{0,4},{2,6},{4,0},{6,2},{8,12},{10,14},{12,8},{14,10},{16,20},{18,... | collective-permute-start | bytes 208904 | tf_op jit(solution)/shard_map/ppermute | solution.py:550
  20.4 0.0 collective-permute-done.3
  20.5 1.6 %collective-permute-start.4 = (bf16[2,272,128]{2,1,0:T(8,128)(2,1)S(1)}, bf16[2,272,128]{2,1,0:T(8,128)(2,1)S(1)}, u32[]{:S(2)}, u32[]{:S(2)}) collective-permute-start(bf16[2,272,128]{2,1,0:T(8,128)(2,1)S(1)} %slice.8), channel_id=1, source_target_pairs={{0,8},{2,10},{4,12},{6,14},{8,0},{10,2},{12,4},{14,6},{16,24},{18,... | collective-permute-start | bytes 417800 | tf_op jit(solution)/shard_map/ppermute | solution.py:550
  22.1 0.0 collective-permute-start.5
  22.1 1.5 %collective-permute-start.6 = (bf16[336,128]{1,0:T(8,128)(2,1)S(1)}, bf16[336,128]{1,0:T(8,128)(2,1)S(1)}, u32[]{:S(2)}, u32[]{:S(2)}) collective-permute-start(bf16[336,128]{1,0:T(8,128)(2,1)S(1)} %get-tuple-element.73), channel_id=1, source_target_pairs={{0,4},{2,6},{4,0},{6,2},{8,12},{10,14},{12,8},{14,10},{16,20},{18,... | collective-permute-start | bytes 258056 | tf_op jit(solution)/shard_map/ppermute | solution.py:550
  23.7 0.3 collective-permute-start.7
  24.0 0.2 collective-permute-done.11
  24.2 0.0 collective-permute-done.5
  24.3 3.2 %collective-permute-done.6 = bf16[336,128]{1,0:T(8,128)(2,1)S(1)} collective-permute-done((bf16[336,128]{1,0:T(8,128)(2,1)S(1)}, bf16[336,128]{1,0:T(8,128)(2,1)S(1)}, u32[]{:S(2)}, u32[]{:S(2)}) %collective-permute-start.6) | collective-permute-done | bytes 86048 | tf_op jit(solution)/shard_map/ppermute | solution.py:550
  27.5 1.1 %collective-permute-done.7 = bf16[336,128]{1,0:T(8,128)(2,1)S(1)} collective-permute-done((bf16[336,128]{1,0:T(8,128)(2,1)S(1)}, bf16[336,128]{1,0:T(8,128)(2,1)S(1)}, u32[]{:S(2)}, u32[]{:S(2)}) %collective-permute-start.7) | collective-permute-done | bytes 86048 | tf_op jit(solution)/shard_map/ppermute | solution.py:550
  28.5 0.0 collective-permute-done.4
  28.5 0.1 add_convert_fusion.2
  28.6 0.7 %collective-permute-start.9 = (bf16[336,128]{1,0:T(8,128)(2,1)S(1)}, bf16[336,128]{1,0:T(8,128)(2,1)S(1)}, u32[]{:S(2)}, u32[]{:S(2)}) collective-permute-start(bf16[336,128]{1,0:T(8,128)(2,1)S(1)} %add_convert_fusion.2), channel_id=1, source_target_pairs={{0,8},{2,10},{4,12},{6,14},{8,0},{10,2},{12,4},{14,6},{16,24},{18,... | collective-permute-start | bytes 258056 | tf_op jit(solution)/shard_map/ppermute | solution.py:550
  29.3 1.3 %collective-permute-start.8 = (bf16[2,272,128]{2,1,0:T(8,128)(2,1)S(1)}, bf16[2,272,128]{2,1,0:T(8,128)(2,1)S(1)}, u32[]{:S(2)}, u32[]{:S(2)}) collective-permute-start(bf16[2,272,128]{2,1,0:T(8,128)(2,1)S(1)} %collective-permute-done.4), channel_id=1, source_target_pairs={{0,4},{2,6},{4,0},{6,2},{8,12},{10,14},{12,8},{14,10},{16,20},{18,... | collective-permute-start | bytes 417800 | tf_op jit(solution)/shard_map/ppermute | solution.py:550
  30.7 0.1 collective-permute-start.12
  30.8 2.5 %collective-permute-done.9 = bf16[336,128]{1,0:T(8,128)(2,1)S(1)} collective-permute-done((bf16[336,128]{1,0:T(8,128)(2,1)S(1)}, bf16[336,128]{1,0:T(8,128)(2,1)S(1)}, u32[]{:S(2)}, u32[]{:S(2)}) %collective-permute-start.9) | collective-permute-done | bytes 86048 | tf_op jit(solution)/shard_map/ppermute | solution.py:550
  33.3 1.4 %collective-permute-done.8 = bf16[2,272,128]{2,1,0:T(8,128)(2,1)S(1)} collective-permute-done((bf16[2,272,128]{2,1,0:T(8,128)(2,1)S(1)}, bf16[2,272,128]{2,1,0:T(8,128)(2,1)S(1)}, u32[]{:S(2)}, u32[]{:S(2)}) %collective-permute-start.8) | collective-permute-done | bytes 139296 | tf_op jit(solution)/shard_map/ppermute | solution.py:550
  34.7 0.0 collective-permute-start.13
  34.8 2.2 %collective-permute-start.10 = (bf16[336,128]{1,0:T(8,128)(2,1)S(1)}, bf16[336,128]{1,0:T(8,128)(2,1)S(1)}, u32[]{:S(2)}, u32[]{:S(2)}) collective-permute-start(bf16[336,128]{1,0:T(8,128)(2,1)S(1)} %add_convert_fusion.1), channel_id=1, source_target_pairs={{0,16},{2,18},{4,20},{6,22},{8,24},{10,26},{12,28},{14,30},{16,0},... | collective-permute-start | bytes 258056 | tf_op jit(solution)/shard_map/ppermute | solution.py:550
  37.0 0.0 collective-permute-done.13
  37.1 0.0 collective-permute-done.12
  37.1 0.1 pad_maximum_fusion.far_ref
  37.1 6.2 %deep.1 = (bf16[256,2304]{1,0:T(8,128)(2,1)S(1)}, bf16[256,512]{1,0:T(8,128)(2,1)S(1)}, f32[1,512]{1,0:T(1,128)}, f32[1152,256]{1,0:T(8,128)}) custom-call(bf16[8,272,128]{2,1,0:T(8,128)(2,1)S(1)} %constant_dynamic-update-slice_fusion.near_ref, bf16[8,272,128]{2,1,0:T(8,128)(2,1)S(1)} %pad_maximum_fusion.far_ref, bf16[1152,256]{1,0:T(8,128)(2,1)S(1)} %bitcast.15, ...), custom_call_target="tpu_custom_call" | custom-call | flops 1300000000 | bytes 12000000 | tf_op jit(solution)/shard_map/deep/pallas_call | solution.py:784
  43.4 0.0 collective-permute-done.10
  43.4 0.8 %collective-permute-start.15 = (bf16[336,128]{1,0:T(8,128)(2,1)S(1)}, bf16[336,128]{1,0:T(8,128)(2,1)S(1)}, u32[]{:S(2)}, u32[]{:S(2)}) collective-permute-start(bf16[336,128]{1,0:T(8,128)(2,1)S(1)} %add_convert_fusion.refs_0_), channel_id=1, source_target_pairs={{0,4},{2,6},{4,0},{6,2},{8,12},{10,14},{12,8},{14,10},{16,20},{18,... | collective-permute-start | bytes 258056 | tf_op jit(solution)/shard_map/ppermute | solution.py:550
  44.2 0.0 collective-permute-start.14
  44.2 3.1 %fourth_grad.1 = f32[2304,512]{1,0:T(8,128)} custom-call(bf16[256,2304]{1,0:T(8,128)(2,1)S(1)} %get-tuple-element.83.fourth_taps_ref, bf16[256,512]{1,0:T(8,128)(2,1)S(1)} %get-tuple-element.84.fourth_flat_ref), custom_call_target="tpu_custom_call" | custom-call | flops 600000000 | bytes 6000000 | tf_op jit(solution)/shard_map/fourth_grad/pallas_call | solution.py:819
  47.3 0.8 %collective-permute-done.15.refs_2_ = bf16[336,128]{1,0:T(8,128)(2,1)S(1)} collective-permute-done((bf16[336,128]{1,0:T(8,128)(2,1)S(1)}, bf16[336,128]{1,0:T(8,128)(2,1)S(1)}, u32[]{:S(2)}, u32[]{:S(2)}) %collective-permute-start.15) | collective-permute-done | bytes 86048 | tf_op jit(solution)/shard_map/ppermute | solution.py:550
  48.1 0.0 collective-permute-start.16
  48.1 0.0 collective-permute-done.14.refs_1_
  48.1 1.3 %collective-permute-done.16.refs_3_ = bf16[336,128]{1,0:T(8,128)(2,1)S(1)} collective-permute-done((bf16[336,128]{1,0:T(8,128)(2,1)S(1)}, bf16[336,128]{1,0:T(8,128)(2,1)S(1)}, u32[]{:S(2)}, u32[]{:S(2)}) %collective-permute-start.16) | collective-permute-done | bytes 86048 | tf_op jit(solution)/shard_map/ppermute | solution.py:550
  49.4 1.2 %finish.1 = (f32[9,160,64]{2,1,0:T(8,128)}, f32[576,128]{1,0:T(8,128)}) custom-call(bf16[336,128]{1,0:T(8,128)(2,1)S(1)} %add_convert_fusion.refs_0_, bf16[336,128]{1,0:T(8,128)(2,1)S(1)} %collective-permute-done.14.refs_1_, bf16[336,128]{1,0:T(8,128)(2,1)S(1)} %collective-permute-done.15.refs_2_, bf16[336,128]{1,0:T(8,128)(2,1)S(1)} %collective-permute-done.16.refs_3_), custom_call_target="tpu_custom_call" | custom-call | flops 1000000 | bytes 1500000 | tf_op jit(solution)/shard_map/finish/pallas_call | solution.py:834
  (10 shorter events, 0.2 us)
Async XLA Ops:
  0.6 9.4 %collective-permute-start = (s32[1,5,16,128]{3,2,1,0:T(8,128)}, s32[1,5,16,128]{3,2,1,0:T(8,128)S(1)}, u32[]{:S(2)}, u32[]{:S(2)}) collective-permute-start(s32[1,5,16,128]{3,2,1,0:T(8,128)} %got_hbm.1), channel_id=1, source_target_pairs={{0,1},{1,0},{2,3},{3,2},{4,5},{5,4},{6,7},{7,6},{8,9},{9,8},{10,11... | collective-permute-start | bytes 122888 | tf_op jit(solution)/shard_map/ppermute | solution.py:550
  3.6 13.4 %copy-start = (bf16[512]{0:T(512)(128)(2,1)S(1)}, bf16[512]{0:T(512)(128)(2,1)}, u32[]{:S(2)}) copy-start(bf16[512]{0:T(512)(128)(2,1)} %param.15) | copy-start | bytes 3076
  6.5 3.6 %collective-permute-start.1 = (s32[1,1,8]{2,1,0:T(1,128)S(1)}, s32[1,1,8]{2,1,0:T(1,128)S(1)}, u32[]{:S(2)}, u32[]{:S(2)}) collective-permute-start(s32[1,1,8]{2,1,0:T(1,128)S(1)} %get-tuple-element.48), channel_id=1, source_target_pairs={{0,1},{1,0},{2,3},{3,2},{4,5},{5,4},{6,7},{7,6},{8,9},{9,8},{10,11... | collective-permute-start | bytes 104 | tf_op jit(solution)/shard_map/ppermute | solution.py:550
  12.8 7.0 %collective-permute-start.2 = (bf16[1,272,128]{2,1,0:T(8,128)(2,1)S(1)}, bf16[1,272,128]{2,1,0:T(8,128)(2,1)S(1)}, u32[]{:S(2)}, u32[]{:S(2)}) collective-permute-start(bf16[1,272,128]{2,1,0:T(8,128)(2,1)S(1)} %bitcast.16), channel_id=1, source_target_pairs={{0,16},{2,18},{4,20},{6,22},{8,24},{10,26},{12,28},{14,30},{16,0},... | collective-permute-start | bytes 208904 | tf_op jit(solution)/shard_map/ppermute | solution.py:550
  15.5 5.0 %collective-permute-start.3 = (bf16[1,272,128]{2,1,0:T(8,128)(2,1)S(1)}, bf16[1,272,128]{2,1,0:T(8,128)(2,1)S(1)}, u32[]{:S(2)}, u32[]{:S(2)}) collective-permute-start(bf16[1,272,128]{2,1,0:T(8,128)(2,1)S(1)} %bitcast.17), channel_id=1, source_target_pairs={{0,4},{2,6},{4,0},{6,2},{8,12},{10,14},{12,8},{14,10},{16,20},{18,... | collective-permute-start | bytes 208904 | tf_op jit(solution)/shard_map/ppermute | solution.py:550
  19.9 4.4 %collective-permute-start.11 = (bf16[1,272,128]{2,1,0:T(8,128)(2,1)S(1)}, bf16[1,272,128]{2,1,0:T(8,128)(2,1)S(1)}, u32[]{:S(2)}, u32[]{:S(2)}) collective-permute-start(bf16[1,272,128]{2,1,0:T(8,128)(2,1)S(1)} %collective-permute-done.2), channel_id=1, source_target_pairs={{0,4},{2,6},{4,0},{6,2},{8,12},{10,14},{12,8},{14,10},{16,20},{18,... | collective-permute-start | bytes 208904 | tf_op jit(solution)/shard_map/ppermute | solution.py:550
  20.5 8.0 %collective-permute-start.4 = (bf16[2,272,128]{2,1,0:T(8,128)(2,1)S(1)}, bf16[2,272,128]{2,1,0:T(8,128)(2,1)S(1)}, u32[]{:S(2)}, u32[]{:S(2)}) collective-permute-start(bf16[2,272,128]{2,1,0:T(8,128)(2,1)S(1)} %slice.8), channel_id=1, source_target_pairs={{0,8},{2,10},{4,12},{6,14},{8,0},{10,2},{12,4},{14,6},{16,24},{18,... | collective-permute-start | bytes 417800 | tf_op jit(solution)/shard_map/ppermute | solution.py:550
  22.1 2.1 %collective-permute-start.5 = (bf16[336,128]{1,0:T(8,128)(2,1)S(1)}, bf16[336,128]{1,0:T(8,128)(2,1)S(1)}, u32[]{:S(2)}, u32[]{:S(2)}) collective-permute-start(bf16[336,128]{1,0:T(8,128)(2,1)S(1)} %get-tuple-element.72), channel_id=1, source_target_pairs={{0,2},{2,0},{4,6},{6,4},{8,10},{10,8},{12,14},{14,12},{16,18},{18,... | collective-permute-start | bytes 258056 | tf_op jit(solution)/shard_map/ppermute | solution.py:550
  22.1 5.3 %collective-permute-start.6 = (bf16[336,128]{1,0:T(8,128)(2,1)S(1)}, bf16[336,128]{1,0:T(8,128)(2,1)S(1)}, u32[]{:S(2)}, u32[]{:S(2)}) collective-permute-start(bf16[336,128]{1,0:T(8,128)(2,1)S(1)} %get-tuple-element.73), channel_id=1, source_target_pairs={{0,4},{2,6},{4,0},{6,2},{8,12},{10,14},{12,8},{14,10},{16,20},{18,... | collective-permute-start | bytes 258056 | tf_op jit(solution)/shard_map/ppermute | solution.py:550
  23.7 4.9 %collective-permute-start.7 = (bf16[336,128]{1,0:T(8,128)(2,1)S(1)}, bf16[336,128]{1,0:T(8,128)(2,1)S(1)}, u32[]{:S(2)}, u32[]{:S(2)}) collective-permute-start(bf16[336,128]{1,0:T(8,128)(2,1)S(1)} %get-tuple-element.74), channel_id=1, source_target_pairs={{0,6},{2,4},{4,2},{6,0},{8,14},{10,12},{12,10},{14,8},{16,22},{18,... | collective-permute-start | bytes 258056 | tf_op jit(solution)/shard_map/ppermute | solution.py:550
  28.6 4.7 %collective-permute-start.9 = (bf16[336,128]{1,0:T(8,128)(2,1)S(1)}, bf16[336,128]{1,0:T(8,128)(2,1)S(1)}, u32[]{:S(2)}, u32[]{:S(2)}) collective-permute-start(bf16[336,128]{1,0:T(8,128)(2,1)S(1)} %add_convert_fusion.2), channel_id=1, source_target_pairs={{0,8},{2,10},{4,12},{6,14},{8,0},{10,2},{12,4},{14,6},{16,24},{18,... | collective-permute-start | bytes 258056 | tf_op jit(solution)/shard_map/ppermute | solution.py:550
  29.3 5.5 %collective-permute-start.8 = (bf16[2,272,128]{2,1,0:T(8,128)(2,1)S(1)}, bf16[2,272,128]{2,1,0:T(8,128)(2,1)S(1)}, u32[]{:S(2)}, u32[]{:S(2)}) collective-permute-start(bf16[2,272,128]{2,1,0:T(8,128)(2,1)S(1)} %collective-permute-done.4), channel_id=1, source_target_pairs={{0,4},{2,6},{4,0},{6,2},{8,12},{10,14},{12,8},{14,10},{16,20},{18,... | collective-permute-start | bytes 417800 | tf_op jit(solution)/shard_map/ppermute | solution.py:550
  30.7 6.4 %collective-permute-start.12 = (bf16[6,272,128]{2,1,0:T(8,128)(2,1)S(1)}, bf16[6,272,128]{2,1,0:T(8,128)(2,1)S(1)}, u32[]{:S(2)}, u32[]{:S(2)}) collective-permute-start(bf16[6,272,128]{2,1,0:T(8,128)(2,1)S(1)} %slice.9), channel_id=1, source_target_pairs={{0,2},{2,0},{4,6},{6,4},{8,10},{10,8},{12,14},{14,12},{16,18},{18,... | collective-permute-start | bytes 1253384 | tf_op jit(solution)/shard_map/ppermute | solution.py:550
  34.7 2.3 %collective-permute-start.13 = (bf16[2,272,128]{2,1,0:T(8,128)(2,1)S(1)}, bf16[2,272,128]{2,1,0:T(8,128)(2,1)S(1)}, u32[]{:S(2)}, u32[]{:S(2)}) collective-permute-start(bf16[2,272,128]{2,1,0:T(8,128)(2,1)S(1)} %collective-permute-done.8), channel_id=1, source_target_pairs={{0,2},{2,0},{4,6},{6,4},{8,10},{10,8},{12,14},{14,12},{16,18},{18,... | collective-permute-start | bytes 417800 | tf_op jit(solution)/shard_map/ppermute | solution.py:550
  34.8 8.6 %collective-permute-start.10 = (bf16[336,128]{1,0:T(8,128)(2,1)S(1)}, bf16[336,128]{1,0:T(8,128)(2,1)S(1)}, u32[]{:S(2)}, u32[]{:S(2)}) collective-permute-start(bf16[336,128]{1,0:T(8,128)(2,1)S(1)} %add_convert_fusion.1), channel_id=1, source_target_pairs={{0,16},{2,18},{4,20},{6,22},{8,24},{10,26},{12,28},{14,30},{16,0},... | collective-permute-start | bytes 258056 | tf_op jit(solution)/shard_map/ppermute | solution.py:550
  43.4 4.7 %collective-permute-start.15 = (bf16[336,128]{1,0:T(8,128)(2,1)S(1)}, bf16[336,128]{1,0:T(8,128)(2,1)S(1)}, u32[]{:S(2)}, u32[]{:S(2)}) collective-permute-start(bf16[336,128]{1,0:T(8,128)(2,1)S(1)} %add_convert_fusion.refs_0_), channel_id=1, source_target_pairs={{0,4},{2,6},{4,0},{6,2},{8,12},{10,14},{12,8},{14,10},{16,20},{18,... | collective-permute-start | bytes 258056 | tf_op jit(solution)/shard_map/ppermute | solution.py:550
  44.2 3.9 %collective-permute-start.14 = (bf16[336,128]{1,0:T(8,128)(2,1)S(1)}, bf16[336,128]{1,0:T(8,128)(2,1)S(1)}, u32[]{:S(2)}, u32[]{:S(2)}) collective-permute-start(bf16[336,128]{1,0:T(8,128)(2,1)S(1)} %add_convert_fusion.refs_0_), channel_id=1, source_target_pairs={{0,2},{2,0},{4,6},{6,4},{8,10},{10,8},{12,14},{14,12},{16,18},{18,... | collective-permute-start | bytes 258056 | tf_op jit(solution)/shard_map/ppermute | solution.py:550
  48.1 1.3 %collective-permute-start.16 = (bf16[336,128]{1,0:T(8,128)(2,1)S(1)}, bf16[336,128]{1,0:T(8,128)(2,1)S(1)}, u32[]{:S(2)}, u32[]{:S(2)}) collective-permute-start(bf16[336,128]{1,0:T(8,128)(2,1)S(1)} %collective-permute-done.15.refs_2_), channel_id=1, source_target_pairs={{0,2},{2,0},{4,6},{6,4},{8,10},{10,8},{12,14},{14,12},{16,18},{18,... | collective-permute-start | bytes 258056 | tf_op jit(solution)/shard_map/ppermute | solution.py:550

commit v6 on v5

--- a/solution.py
+++ b/solution.py
@@ -160,11 +160,8 @@
     second_w_ref,
     third_w_ref,
     fourth_w_ref,
-    second_wt_ref,
-    third_wt_ref,
-    fourth_wt_ref,
+    got_ref,
     label_ref,
-    got_ref,
     lift_ref,
     first_w_ref,
     bits_ref,
@@ -206,7 +203,7 @@
     copies[0].wait()
     band_cells(got_ref, 0, None, order, lift_all_ref, bits_ref, even_ref, odd_ref, rest)
     copies[2].wait()
-    labels_ref[...] = band_label(label_ref, 0, me, labels_ref.shape)
+    labels_ref[...] = band_label(label_ref, 0, me, labels_ref.shape).astype(jnp.bfloat16)
     copies[3].wait()
     for tap in range(9):
         row_tap, col_tap = divmod(tap, 3)
@@ -214,19 +211,13 @@
         first_all_ref[row_tap, pl.ds(384 + col_tap * rest, rest)] = first_w_ref[
             tap, pl.ds(128, rest)
         ]
-    pairs = ((second_w_ref, second_wt_ref), (third_w_ref, third_wt_ref))
-    pairs += ((fourth_w_ref, fourth_wt_ref),)
-    for k, (source, target) in enumerate(pairs):
-        copies[4 + k].wait()
-        for tap in range(9):
-            target[tap] = source[tap].T
+    for copy in copies[4:]:
+        copy.wait()
 
 
 def early_kernel(pieces, rest, *refs):
     got_refs = refs[:pieces]
-    label_refs = refs[pieces : 2 * pieces]
     (
-        labels_ref,
         lift_all_ref,
         first_all_ref,
         second_w_ref,
@@ -239,13 +230,12 @@
         first_slope_ref,
         second_slope_ref,
         bits_ref,
-    ) = refs[2 * pieces :]
+    ) = refs[pieces:]
     me = lax.axis_index("space")
     bands = 1 << pieces
     _, _, band, cols = got_refs[0].shape
     phases, row_cells = cols // BLOCK, cols // 2
     order = column_order(cols)
-    labels = labels_ref[...]
     cells = own_even_ref.shape[0]
     at = pl.multiple_of(me * cells, cells)
     even_ref[pl.ds(at, cells)] = own_even_ref[...]
@@ -266,7 +256,6 @@
             odd_ref,
             rest,
         )
-        labels += band_label(label_refs[piece], inner, me ^ slot, labels.shape)
 
     rows, phases = bands * band // 2, phases // 2
     cells = rows * row_cells
@@ -289,23 +278,29 @@
     second_slope_ref[...] = slope.reshape(second_slope_ref.shape)
     sent = value.shape[0]
     send_ref[pl.ds(0, sent)] = value.astype(jnp.bfloat16)
-    send_ref[pl.ds(sent, 16)] = labels.astype(jnp.bfloat16)
-
-
-def take_samples(near_ref, far_ref, second_ref, label_ref, bands):
-    half = near_ref.shape[0]
-    width = half.bit_length()
+    send_ref[pl.ds(sent, 16)] = jnp.zeros((16, send_ref.shape[1]), jnp.bfloat16)
+
+
+def transpose_kernel(weight_ref, out_ref):
+    for tap in range(weight_ref.shape[0]):
+        out_ref[tap] = weight_ref[tap].T
+
+
+def take_samples(slot_refs, second_ref, label_ref, bands):
+    count = sum(ref.shape[0] for ref in slot_refs)
+    width = count.bit_length() - 1
     chunk = second_ref.shape[0]
     me = lax.axis_index("dp")
-    for slot in range(2 * half):
+    where = [(ref, inner) for ref in slot_refs for inner in range(ref.shape[0])]
+    for slot in range(count):
         reverse = sum(((slot >> k) & 1) << (width - 1 - k) for k in range(width))
         sample = me ^ reverse
-        ref = near_ref if slot < half else far_ref
-
-        def take(ref=ref, inner=slot % half, place=sample % chunk):
+        ref, inner = where[slot]
+
+        def take(ref=ref, inner=inner, place=sample % chunk):
             put_sample(ref, inner, second_ref, label_ref, place, bands)
 
-        if chunk == 2 * half:
+        if chunk == count:
             take()
         else:
             pl.when(sample // chunk == pl.program_id(0))(take)
@@ -317,6 +312,19 @@
         taps_ref[:, pl.ds(tap * channels, channels)] = map_tap(
             second_ref, tap // 3, tap % 3, rows, phases
         )
+
+
+def delta_columns(ref, weight_ref, row_parity, col_parity, rows, phases):
+    taps = (((1, 0),), ((2, 0), (0, 1)))
+    total = None
+    for row_tap, row_step in taps[row_parity]:
+        for col_tap, col_step in taps[col_parity]:
+            cells = ref[:, pl.ds(row_step, rows), pl.ds(col_step, phases)]
+            lead = cells.shape[:-1]
+            columns = cells.reshape(-1, cells.shape[-1]).T.astype(jnp.bfloat16)
+            part = dot_nn(weight_ref[3 * row_tap + col_tap], columns)
+            total = part if total is None else total + part
+    return total.T.reshape(*lead, total.shape[0])
 
 
 def put_sample(ref, inner, second_ref, label_ref, place, bands):
@@ -339,7 +347,7 @@
     bands,
     third_w_ref,
     fourth_w_ref,
-    fourth_wt_ref,
+    fourth_parts,
     head_ref,
     fourth_taps_ref,
     second_ref,
@@ -353,7 +361,8 @@
     samples = second_ref.shape[0]
     rows, phases = 2 * bands, 2
     third_taps(second_ref, third_taps_ref, rows, phases)
-    value, slope = silu_and_slope(dot_nn(third_taps_ref[...], third_w_ref[...]))
+    weight = third_w_ref[...].reshape(third_taps_ref.shape[1], -1)
+    value, slope = silu_and_slope(dot_nn(third_taps_ref[...], weight))
     channels = value.shape[-1]
     zero_row(third_ref)
     fill_map(third_ref, value.reshape(samples, rows, phases, BLOCK, channels), 1)
@@ -364,7 +373,8 @@
         fourth_taps_ref[:, pl.ds(tap * channels, channels)] = map_tap(
             third_ref, tap // 3, tap % 3, rows, phases
         )
-    value, slope = silu_and_slope(dot_nn(fourth_taps_ref[...], fourth_w_ref[...]))
+    weight = fourth_w_ref[...].reshape(fourth_taps_ref.shape[1], -1)
+    value, slope = silu_and_slope(dot_nn(fourth_taps_ref[...], weight))
     head = head_ref[...].astype(jnp.float32)
     labels = label_ref[...].reshape(-1, label_ref.shape[-1])[:, :1]
     logits = jnp.sum(value * head, axis=1, keepdims=True)
@@ -374,9 +384,7 @@
     fill_delta(fourth_delta_ref, delta.reshape(samples, rows, phases, BLOCK, delta.shape[-1]))
     for row_parity in range(2):
         for col_parity in range(2):
-            part = delta_parts(
-                fourth_delta_ref, fourth_wt_ref, row_parity, col_parity, rows, phases
-            )
+            part = fourth_parts(fourth_delta_ref, row_parity, col_parity, rows, phases)
             part = rounded(part * third_slope_ref[:, :, row_parity, :, col_parity])
             for row in range(rows):
                 third_delta_ref[:, 2 * row + row_parity, col_parity] = part[:, row, 0]
@@ -386,8 +394,10 @@
 def deep_kernel(
     batch,
     bands,
+    stored,
     near_ref,
     far_ref,
+    last_ref,
     third_w_ref,
     fourth_w_ref,
     fourth_wt_ref,
@@ -395,23 +405,21 @@
     fourth_taps_ref,
     fourth_flat_ref,
     head_grad_ref,
-    third_grad_ref,
-    second_ref,
-    label_ref,
-    third_taps_ref,
-    third_ref,
-    third_slope_ref,
-    third_delta_ref,
-    fourth_delta_ref,
+    *refs,
 ):
+    if stored:
+        third_taps_ref, third_flat_ref, second_ref, label_ref = refs[:4]
+    else:
+        third_grad_ref, second_ref, label_ref, third_taps_ref = refs[:4]
+    third_ref, third_slope_ref, third_delta_ref, fourth_delta_ref = refs[4:]
     zero_row(second_ref)
-    take_samples(near_ref, far_ref, second_ref, label_ref, bands)
+    take_samples((near_ref, far_ref, last_ref), second_ref, label_ref, bands)
     value, logit_grad, delta = deep_layers(
         batch,
         bands,
         third_w_ref,
         fourth_w_ref,
-        fourth_wt_ref,
+        lambda ref, *where: delta_parts(ref, fourth_wt_ref, *where),
         head_ref,
         fourth_taps_ref,
         second_ref,
@@ -426,13 +434,15 @@
     @pl.when(pl.program_id(0) == 0)
     def _():
         head_grad_ref[...] = jnp.zeros(head_grad_ref.shape, jnp.float32)
-        third_grad_ref[...] = jnp.zeros(third_grad_ref.shape, jnp.float32)
 
     head_grad_ref[...] += jnp.sum(value * logit_grad, axis=0, keepdims=True)
     fourth_flat_ref[...] = delta.astype(jnp.bfloat16)
     delta = third_delta_ref[...]
     delta = delta.reshape(-1, delta.shape[-1]).astype(jnp.bfloat16)
-    third_grad_ref[...] += dot_tn(third_taps_ref[...], delta)
+    if stored:
+        third_flat_ref[...] = delta
+    else:
+        third_grad_kernel(third_taps_ref, delta, third_grad_ref)
 
 
 def local_kernel(
@@ -441,10 +451,8 @@
     payload_ref,
     third_w_ref,
     fourth_w_ref,
-    fourth_wt_ref,
     head_ref,
-    third_wt_ref,
-    second_wt_ref,
+    second_w_ref,
     even_ref,
     odd_ref,
     first_ref,
@@ -452,10 +460,10 @@
     second_slope_ref,
     *refs,
 ):
-    out_refs = refs[:4]
-    third_ref, second_ref, first_delta_ref, flat_ref, second_map_ref, label_ref = refs[4:10]
-    fourth_taps_ref = refs[10]
-    third_delta_ref = refs[14]
+    keep_ref, pass_ref = refs[:2]
+    third_ref, second_ref, first_delta_ref, flat_ref, second_map_ref, label_ref = refs[2:8]
+    fourth_taps_ref = refs[8]
+    third_delta_ref = refs[12]
     zero_row(second_map_ref)
     put_sample(payload_ref, 0, second_map_ref, label_ref, 0, bands)
     deep_layers(
@@ -463,12 +471,12 @@
         bands,
         third_w_ref,
         fourth_w_ref,
-        fourth_wt_ref,
+        lambda ref, *where: delta_columns(ref, fourth_w_ref, *where),
         head_ref,
         fourth_taps_ref,
         second_map_ref,
         label_ref,
-        *refs[11:16],
+        *refs[9:14],
     )
     sample = lax.axis_index("dp")
     _, rows, phases, _, _ = third_delta_ref.shape
@@ -477,7 +485,7 @@
     last_row_zero(second_ref)
     for row_parity in range(2):
         for col_parity in range(2):
-            part = delta_parts(third_ref, third_wt_ref, row_parity, col_parity, rows, phases)
+            part = delta_columns(third_ref, third_w_ref, row_parity, col_parity, rows, phases)
             for row in range(rows):
                 for phase in range(phases):
                     at = (slice(None), 2 * row + row_parity, 2 * phase + col_parity)
@@ -486,7 +494,7 @@
     second_ref[:, :, phases] = shift_block(second_ref[:, :, 0], -1)
     for row_parity in range(2):
         for col_parity in range(2):
-            part = delta_parts(second_ref, second_wt_ref, row_parity, col_parity, rows, phases)
+            part = delta_columns(second_ref, second_w_ref, row_parity, col_parity, rows, phases)
             for row in range(rows):
                 for phase in range(phases):
                     at = (slice(None), 2 * row + row_parity, 2 * phase + col_parity)
@@ -508,10 +516,19 @@
             flat_ref[pl.ds((4 * tap + piece) * depth, depth)] = part[
                 :, piece * 128 : piece * 128 + 128
             ]
-    share = out_refs[0].shape[0]
+    share = keep_ref.shape[1]
     for slot in range(4):
         at = pl.multiple_of(((sample % 4) ^ slot) * share, share)
-        out_refs[slot][...] = flat_ref[pl.ds(at, share)].astype(jnp.bfloat16)
+        ref = pass_ref if slot % 2 else keep_ref
+        ref[slot // 2] = flat_ref[pl.ds(at, share)].astype(jnp.bfloat16)
+
+
+def third_grad_kernel(taps_ref, delta_ref, out_ref):
+    @pl.when(pl.program_id(0) == 0)
+    def _():
+        out_ref[...] = jnp.zeros(out_ref.shape, jnp.float32)
+
+    out_ref[...] += dot_tn(delta_ref[...], taps_ref[...]).T
 
 
 def fourth_grad_kernel(fourth_taps_ref, fourth_flat_ref, out_ref):
@@ -564,47 +581,41 @@
     return lax.dynamic_update_slice(buffer, part, (at,) + (0,) * (buffer.ndim - 1))
 
 
-def gather_and_sum(payload, local_quarters, samples):
-    tie = lax.optimization_barrier
+def after(value, *others):
+    return lax.optimization_barrier((value, *others))[0]
+
+
+def gather_and_sum(payload, local_sums, transposed, samples):
     half, quarter = samples // 2, samples // 4
     near = put(jnp.zeros((half,) + payload.shape[1:], payload.dtype), payload, 0)
-    last, last_at, count, bit = payload, 0, 1, 4
-    quarters, total = None, None
+    got = swapped(payload, "dp", quarter * 2) if quarter > 1 else None
+    keep, passed = local_sums()
+    core = swapped(passed, "dp", 1)
+    count, beside_count = 1, 0
     while count < quarter:
-        got = swapped(near[:count] if count > 1 else payload, "dp", half // count)
-        beside = swapped(last, "dp", 2)
-        if quarters is None:
-            quarters = local_quarters()
-            got, *quarters = tie((got, *quarters))
-        elif total is None:
-            parts = [swapped(quarters[slot], "dp", slot) for slot in (1, 2, 3)]
-            got, *parts = tie((got, *parts))
-            total = added(quarters[0], *parts)
-        else:
-            got, other = tie((got, swapped(total, "dp", bit)))
-            total = added(total, other)
-            bit *= 2
-        near = put(near, beside, quarter + last_at)
-        near = put(near, got, count)
-        last, last_at = got, count
+        near = put(near, after(got, keep), count)
         count *= 2
-    far = jnp.zeros_like(near)
-    early = swapped(near[: quarter + last_at], "dp", 1)
-    beside = swapped(last, "dp", 2)
-    if quarters is None:
-        quarters = local_quarters()
-    if total is None:
-        total = added(
-            quarters[0], *[swapped(quarters[slot], "dp", slot) for slot in (1, 2, 3)]
-        )
-    elif bit < samples:
-        beside, other = tie((beside, swapped(total, "dp", bit)))
+        if count < quarter:
+            part = near[beside_count:count]
+            got = swapped(near[:count], "dp", half // count)
+            beside = swapped(part, "dp", 2)
+            near = put(near, beside, quarter + beside_count)
+            beside_count = count
+    weights = transposed(after(keep, core))
+    mine, theirs = added(keep[0], core[0]), added(keep[1], core[1])
+    theirs = after(theirs, weights)
+    total = added(mine, swapped(theirs, "dp", 2))
+    beside = swapped(after(near[beside_count:quarter], theirs), "dp", 2)
+    early = swapped(near[: quarter + beside_count], "dp", 1)
+    bit = 4
+    while 2 * bit < samples:
+        other = swapped(total, "dp", bit)
+        beside = after(beside, total)
         total = added(total, other)
         bit *= 2
-    near = put(near, beside, quarter + last_at)
-    far = put(far, early, 0)
-    far = put(far, swapped(beside, "dp", 1), quarter + last_at)
-    return near, far, total, bit
+    near = put(near, beside, quarter + beside_count)
+    last = swapped(beside, "dp", 1)
+    return near, early, last, total, bit, weights
 
 
 def added(*parts):
@@ -674,30 +685,23 @@
         second_w2,
         third_w2,
         fourth_w2,
-        second_wt,
-        third_wt,
-        fourth_wt,
-        labels,
     ) = pl.pallas_call(
         own_kernel,
         out_shape=(
             own_cells,
             own_cells,
-            shaped((16, two), f32),
+            shaped((16, two), bf16),
             shaped((128, 256), bf16),
             shaped((3, 512, one), bf16),
             shaped(second_w.shape, bf16),
             shaped(third_w.shape, bf16),
             shaped(fourth_w.shape, bf16),
-            shaped((9, two, one), bf16),
-            shaped((9, three, two), bf16),
-            shaped((9, four, three), bf16),
-            shaped(state_labels.shape, state_labels.dtype),
         ),
         in_specs=[hbm] * 7,
-        out_specs=(vmem,) * 12,
+        out_specs=(vmem,) * 8,
         scratch_shapes=[
             pltpu.VMEM(occupancy.shape, occupancy.dtype),
+            pltpu.VMEM(state_labels.shape, state_labels.dtype),
             pltpu.VMEM(lift_weight.shape, bf16),
             pltpu.VMEM(first_w.shape, bf16),
             bits_scratch,
@@ -707,7 +711,6 @@
         cost_estimate=cost(100_000_000, 10_000_000),
         name="own_band",
     )(*own_args)
-    labels = band_pieces(labels, bands)
     pieces = len(lines) - 1
     even, odd, payload, first, first_slope, second_slope = pl.pallas_call(
         functools.partial(early_kernel, pieces, lift_all - 128),
@@ -719,21 +722,20 @@
             shaped((1, rows // 2, phases // 2, BLOCK, one), f32),
             shaped((1, rows // 4, phases // 4, BLOCK, two), f32),
         ),
-        in_specs=[vmem] * (2 * pieces + 6),
+        in_specs=[vmem] * (pieces + 5),
         out_specs=(vmem,) * 6,
         scratch_shapes=[bits_scratch],
         compiler_params=grant(24),
         cost_estimate=cost(150_000_000, 4_000_000),
         name="early",
-    )(*lines[1:], *labels[1:], own_labels, lift_all_w, first_all, second_w2, own_even, own_odd)
-
-    payload = payload[None]
-    deep_weights = (
-        third_w2.reshape(9 * two, three),
-        fourth_w2.reshape(9 * three, four),
-        fourth_wt,
-        head,
-    )
+    )(*lines[1:], lift_all_w, first_all, second_w2, own_even, own_odd)
+
+    labels, bit = own_labels, 1
+    while bit < bands:
+        labels = labels + swapped(labels, "space", bit)
+        bit *= 2
+    payload = put(payload, labels, sent - 16)[None]
+    deep_weights = (third_w2, fourth_w2)
 
     third_cells = 2 * bands * 2 * BLOCK
     fourth_cells = bands * BLOCK
@@ -756,9 +758,9 @@
     share = 21 * one // 4
     local_call = pl.pallas_call(
         functools.partial(local_kernel, samples, bands),
-        out_shape=(shaped((share, two), bf16),) * 4,
-        in_specs=[vmem] * 12,
-        out_specs=(vmem,) * 4,
+        out_shape=(shaped((2, share, two), bf16),) * 2,
+        in_specs=[vmem] * 10,
+        out_specs=(vmem,) * 2,
         scratch_shapes=[
             pltpu.VMEM((1, 2 * bands + 1, 3, BLOCK, three), f32),
             pltpu.VMEM((1, 4 * bands + 1, 5, BLOCK, two), f32),
@@ -773,28 +775,54 @@
         cost_estimate=cost(300_000_000, 9_000_000),
         name="local",
     )
-    maps = (third_wt, second_wt, even, odd, first, first_slope, second_slope)
-    near, far, total, bit = gather_and_sum(
-        payload, lambda: local_call(payload, *deep_weights, *maps), samples
-    )
+    maps = (head, second_w2, even, odd, first, first_slope, second_slope)
+    transpose_call = pl.pallas_call(
+        transpose_kernel,
+        out_shape=shaped((9, four, three), bf16),
+        in_specs=[vmem],
+        out_specs=vmem,
+        compiler_params=grant(16),
+        cost_estimate=cost(10_000_000, 5_000_000),
+        name="transpose",
+    )
+
+    near, far, last, total, bit, fourth_wt = gather_and_sum(
+        payload,
+        lambda: local_call(payload, *deep_weights, *maps),
+        lambda keep: transpose_call(after(fourth_w2, keep)),
+        samples,
+    )
+    near = after(near, total)
 
     chunk = max(1, min(samples, 32 // bands))
     steps = samples // chunk
     full = lambda *shape: pl.BlockSpec(shape, lambda i: (0,) * len(shape))
-    fourth_taps, fourth_flat, head_grad, deeper_grad = pl.pallas_call(
-        functools.partial(deep_kernel, samples, bands),
+    rows_block = pl.BlockSpec((chunk * third_cells, 9 * two), lambda i: (i, 0))
+    flat_block = pl.BlockSpec((chunk * third_cells, three), lambda i: (i, 0))
+    grad_shape = shaped((9 * two, three), f32)
+    if small:
+        third_shapes = (
+            shaped((samples * third_cells, 9 * two), bf16),
+            shaped((samples * third_cells, three), bf16),
+        )
+        third_blocks = (rows_block, flat_block)
+    else:
+        third_shapes, third_blocks = (grad_shape,), (full(9 * two, three),)
+    fourth_taps, fourth_flat, head_grad, *thirds = pl.pallas_call(
+        functools.partial(deep_kernel, samples, bands, small),
         grid=(steps,),
         out_shape=(
             shaped((samples * fourth_cells, 9 * three), bf16),
             shaped((samples * fourth_cells, four), bf16),
             shaped((1, four), f32),
-            shaped((9 * two, three), f32),
+            *third_shapes,
         ),
         in_specs=[
             full(*near.shape),
             full(*far.shape),
-            full(9 * two, three),
-            full(9 * three, four),
+            full(*last.shape),
+            full(9, two, three),
+            full(9, three, four),
             full(9, four, three),
             full(1, four),
         ],
@@ -802,14 +830,14 @@
             pl.BlockSpec((chunk * fourth_cells, 9 * three), lambda i: (i, 0)),
             pl.BlockSpec((chunk * fourth_cells, four), lambda i: (i, 0)),
             full(1, four),
-            full(9 * two, three),
+            *third_blocks,
         ),
         scratch_shapes=[second_scratch(chunk), pltpu.VMEM((chunk, bands, BLOCK, two), f32)]
-        + deep_scratch(chunk),
+        + deep_scratch(chunk)[1 if small else 0 :],
         compiler_params=grant(40),
         cost_estimate=cost(1_300_000_000, 12_000_000),
         name="deep",
-    )(near, far, *deep_weights)
+    )(near, far, last, *deep_weights, fourth_wt, head)
 
     if bit < samples:
         other, fourth_flat = lax.optimization_barrier((swapped(total, "dp", bit), fourth_flat))
@@ -831,6 +859,20 @@
     )(fourth_taps, fourth_flat)
     beside, deepest_grad = lax.optimization_barrier((beside, deepest_grad))
     across = swapped(beside, "dp", 1)
+    if small:
+        deeper_grad = pl.pallas_call(
+            third_grad_kernel,
+            grid=(steps,),
+            out_shape=grad_shape,
+            in_specs=[rows_block, flat_block],
+            out_specs=full(9 * two, three),
+            compiler_params=grant(24),
+            cost_estimate=cost(600_000_000, 4_000_000),
+            name="third_grad",
+        )(*thirds)
+    else:
+        deeper_grad = thirds[0]
+    across, deeper_grad = lax.optimization_barrier((across, deeper_grad))
     temporal_grad, middle_grad = pl.pallas_call(
         finish_kernel,
         out_shape=(shaped((9, lift_all, one), f32), shaped((9 * one, two), f32)),

time: 50.8 us -> 45.6 us (0.90)
  waiting for transfers between devices: 14.1 us -> 10.1 us
  starting transfers between devices: 16.5 us -> 14.4 us
  Pallas kernels: 18.9 us -> 19.9 us
    ppermute x17 -> x15, waiting for transfers between devices: 14.1 us -> 10.1 us  [swapped(): lax.ppermute(value, axis, [(i, i ^ bit) for i in range(lax.axis_size(axis...]
    ppermute x17 -> x15, starting transfers between devices: 16.5 us -> 14.4 us  [swapped(): lax.ppermute(value, axis, [(i, i ^ bit) for i in range(lax.axis_size(axis...]
    pallas_call x1, Pallas kernels: 2.77 us -> 3.6 us  [local(): local_call(payload, *deep_weights, *maps)]
    pallas_call x1 -> x3, Pallas kernels: 6.24 us -> 7.02 us  [the longest x1 4.4 us: local(): pl.pallas_call(functools.partial(deep_kernel, samples, bands, small), gri...]
    pallas_call x1, Pallas kernels: 2.82 us -> 2.15 us  [local(): pl.pallas_call(own_kernel, out_shape=(own_cells, own_cells, shaped((16, t...]
  transfers between devices with their start and end apart: 17 -> 15, of which waited for: 8 -> 7; matrix products, arithmetic and copies ran while one was open for 1% -> 1% of each run, Pallas kernels for 30% -> 41%
where the time goes in v6:
time: 45.6 us; the launch traced here: 45.5 us
  Pallas kernels  19.9 us (44%)
  starting transfers between devices  14.4 us (32%)
  waiting for transfers between devices  10.1 us (22%)
  between operations  0.81 us (2%)
    ppermute x15, starting transfers between devices, swapped(): lax.ppermute(value, axis, [(i, i ^ bit) for i in range(lax.axis_size(axis...  14.4 us
    ppermute x15, waiting for transfers between devices, swapped(): lax.ppermute(value, axis, [(i, i ^ bit) for i in range(lax.axis_size(axis...  10.1 us
    pallas_call x1, Pallas kernels, local(): pl.pallas_call(functools.partial(deep_kernel, samples, bands, small), gri...  4.4 us
    pallas_call x1, Pallas kernels, local(): local_call(payload, *deep_weights, *maps)  3.6 us
    pallas_call x1, Pallas kernels, local(): pl.pallas_call(fourth_grad_kernel, grid=(3, steps), out_shape=shaped((9 *...  3.15 us
    pallas_call x1, Pallas kernels, local(): pl.pallas_call(functools.partial(early_kernel, pieces, lift_all - 128), o...  2.73 us
    pallas_call x1, Pallas kernels, local(): pl.pallas_call(own_kernel, out_shape=(own_cells, own_cells, shaped((16, t...  2.15 us
    pallas_call x1, Pallas kernels, local(): pl.pallas_call(third_grad_kernel, grid=(steps,), out_shape=grad_shape, in...  1.97 us
  transfers between devices with their start and end apart: 15, of which 7 were waited for; matrix products, arithmetic and copies ran while one was open for 1% of the time, Pallas kernels for 41%

profile of v6, /device:TPU:0, one launch (start us, length us, event | category | flops | bytes accessed | tf_op | source)
XLA Modules:
  0.0 45.5 jit_solution(15416405564789170108)
XLA Ops:
  0.6 0.0 copy-start
  0.6 3.0 %collective-permute-start = (s32[1,5,16,128]{3,2,1,0:T(8,128)}, s32[1,5,16,128]{3,2,1,0:T(8,128)S(1)}, u32[]{:S(2)}, u32[]{:S(2)}) collective-permute-start(s32[1,5,16,128]{3,2,1,0:T(8,128)} %got_hbm.1), channel_id=1, source_target_pairs={{0,1},{1,0},{2,3},{3,2},{4,5},{5,4},{6,7},{7,6},{8,9},{9,8},{10,11... | collective-permute-start | bytes 122888 | tf_op jit(solution)/shard_map/ppermute | solution.py:567
  3.6 2.2 %own_band.1 = (bf16[512,512]{1,0:T(8,128)(2,1)S(1)}, bf16[512,512]{1,0:T(8,128)(2,1)S(1)}, bf16[16,128]{1,0:T(8,128)(2,1)S(1)}, bf16[128,256]{1,0:T(8,128)(2,1)S...) custom-call(s32[1,5,16,128]{3,2,1,0:T(8,128)} %got_hbm.1, ...), custom_call_target="tpu_custom_call" | custom-call | flops 100000000 | bytes 10000000 | tf_op jit(solution)/shard_map/own_band/pallas_call | solution.py:688
  5.8 0.1 collective-permute-start.1
  5.9 0.0 copy-done
  5.9 0.0 collective-permute-done.refs_0_
  5.9 2.7 %early.1 = (bf16[1024,512]{1,0:T(8,128)(2,1)S(1)}, bf16[1088,512]{1,0:T(8,128)(2,1)S(1)}, bf16[272,128]{1,0:T(8,128)(2,1)S(1)}, f32[1,9,2,5,2,8,64]{6,5,4,3,2,1,...) custom-call(s32[1,5,16,128]{3,2,1,0:T(8,128)S(1)} %collective-permute-done.refs_0_, ...), custom_call_target="tpu_custom_call" | custom-call | flops 150000000 | bytes 4000000 | tf_op jit(solution)/shard_map/early/pallas_call | solution.py:715
  8.7 0.8 %collective-permute-done.1 = bf16[16,128]{1,0:T(8,128)(2,1)S(1)} collective-permute-done((bf16[16,128]{1,0:T(8,128)(2,1)S(1)}, bf16[16,128]{1,0:T(8,128)(2,1)S(1)}, u32[]{:S(2)}, u32[]{:S(2)}) %collective-permute-start.1) | collective-permute-done | bytes 4128 | tf_op jit(solution)/shard_map/ppermute | solution.py:567
  9.5 2.6 %collective-permute-start.6 = (bf16[1,272,128]{2,1,0:T(8,128)(2,1)S(1)}, bf16[1,272,128]{2,1,0:T(8,128)(2,1)S(1)}, u32[]{:S(2)}, u32[]{:S(2)}) collective-permute-start(bf16[1,272,128]{2,1,0:T(8,128)(2,1)S(1)} %bitcast_dynamic-update-slice_fusion.payload_ref), channel_id=1, source_target_pairs={{0,16},{2,18},{4,20},{6,22},{8,24},{10,26},{12,28},{14,30},{16,0},... | collective-permute-start | bytes 208904 | tf_op jit(solution)/shard_map/ppermute | solution.py:567
  12.1 3.6 %local.1 = (bf16[2,336,128]{2,1,0:T(8,128)(2,1)S(1)}, bf16[2,336,128]{2,1,0:T(8,128)(2,1)S(1)}) custom-call(bf16[1,272,128]{2,1,0:T(8,128)(2,1)S(1)} %bitcast_dynamic-update-slice_fusion.payload_ref, bf16[9,128,256]{2,1,0:T(8,128)(2,1)S(1)} %get-tuple-element.47.third_w_ref, bf16[9,256,512]{2,1,0:T(8,128)(2,1)S(1)} %get-tuple-element.48.fourth_w_ref.weight_ref, ...), custom_call_target="tpu_custom_call" | custom-call | flops 300000000 | bytes 9000000 | tf_op jit(solution)/shard_map/local/pallas_call | solution.py:791
  15.7 0.1 collective-permute-start.2
  15.8 0.7 %transpose.1.fourth_wt_ref = bf16[9,512,256]{2,1,0:T(8,128)(2,1)S(1)} custom-call(bf16[9,256,512]{2,1,0:T(8,128)(2,1)S(1)} %get-tuple-element.48.fourth_w_ref.weight_ref), custom_call_target="tpu_custom_call" | custom-call | flops 10000000 | bytes 5000000 | tf_op jit(solution)/shard_map/transpose/pallas_call | solution.py:792
  16.4 0.1 dynamic_update_slice.20
  16.5 0.0 collective-permute-done.6
  16.6 1.6 %collective-permute-start.8 = (bf16[2,272,128]{2,1,0:T(8,128)(2,1)S(1)}, bf16[2,272,128]{2,1,0:T(8,128)(2,1)S(1)}, u32[]{:S(2)}, u32[]{:S(2)}) collective-permute-start(bf16[2,272,128]{2,1,0:T(8,128)(2,1)S(1)} %slice.28), channel_id=1, source_target_pairs={{0,8},{2,10},{4,12},{6,14},{8,0},{10,2},{12,4},{14,6},{16,24},{18,... | collective-permute-start | bytes 417800 | tf_op jit(solution)/shard_map/ppermute | solution.py:567
  18.2 1.5 %collective-permute-start.7 = (bf16[2,272,128]{2,1,0:T(8,128)(2,1)S(1)}, bf16[2,272,128]{2,1,0:T(8,128)(2,1)S(1)}, u32[]{:S(2)}, u32[]{:S(2)}) collective-permute-start(bf16[2,272,128]{2,1,0:T(8,128)(2,1)S(1)} %slice.28), channel_id=1, source_target_pairs={{0,4},{2,6},{4,0},{6,2},{8,12},{10,14},{12,8},{14,10},{16,20},{18,... | collective-permute-start | bytes 417800 | tf_op jit(solution)/shard_map/ppermute | solution.py:567
  19.7 0.0 collective-permute-done.2
  19.8 0.6 %collective-permute-start.3 = (bf16[336,128]{1,0:T(8,128)(2,1)S(1)}, bf16[336,128]{1,0:T(8,128)(2,1)S(1)}, u32[]{:S(2)}, u32[]{:S(2)}) collective-permute-start(bf16[336,128]{1,0:T(8,128)(2,1)S(1)} %fusion.2), channel_id=1, source_target_pairs={{0,4},{2,6},{4,0},{6,2},{8,12},{10,14},{12,8},{14,10},{16,20},{18,... | collective-permute-start | bytes 258056 | tf_op jit(solution)/shard_map/ppermute | solution.py:567
  20.3 2.4 %collective-permute-done.8 = bf16[2,272,128]{2,1,0:T(8,128)(2,1)S(1)} collective-permute-done((bf16[2,272,128]{2,1,0:T(8,128)(2,1)S(1)}, bf16[2,272,128]{2,1,0:T(8,128)(2,1)S(1)}, u32[]{:S(2)}, u32[]{:S(2)}) %collective-permute-start.8) | collective-permute-done | bytes 139296 | tf_op jit(solution)/shard_map/ppermute | solution.py:567
  22.7 1.5 %collective-permute-start.9 = (bf16[2,272,128]{2,1,0:T(8,128)(2,1)S(1)}, bf16[2,272,128]{2,1,0:T(8,128)(2,1)S(1)}, u32[]{:S(2)}, u32[]{:S(2)}) collective-permute-start(bf16[2,272,128]{2,1,0:T(8,128)(2,1)S(1)} %collective-permute-done.8), channel_id=1, source_target_pairs={{0,4},{2,6},{4,0},{6,2},{8,12},{10,14},{12,8},{14,10},{16,20},{18,... | collective-permute-start | bytes 417800 | tf_op jit(solution)/shard_map/ppermute | solution.py:567
  24.2 0.5 %collective-permute-done.7 = bf16[2,272,128]{2,1,0:T(8,128)(2,1)S(1)} collective-permute-done((bf16[2,272,128]{2,1,0:T(8,128)(2,1)S(1)}, bf16[2,272,128]{2,1,0:T(8,128)(2,1)S(1)}, u32[]{:S(2)}, u32[]{:S(2)}) %collective-permute-start.7) | collective-permute-done | bytes 139296 | tf_op jit(solution)/shard_map/ppermute | solution.py:567
  24.7 1.8 %collective-permute-done.3 = bf16[336,128]{1,0:T(8,128)(2,1)S(1)} collective-permute-done((bf16[336,128]{1,0:T(8,128)(2,1)S(1)}, bf16[336,128]{1,0:T(8,128)(2,1)S(1)}, u32[]{:S(2)}, u32[]{:S(2)}) %collective-permute-start.3) | collective-permute-done | bytes 86048 | tf_op jit(solution)/shard_map/ppermute | solution.py:567
  26.6 0.1 collective-permute-start.4
  26.7 0.1 collective-permute-start.10
  26.8 2.0 %collective-permute-done.9 = bf16[2,272,128]{2,1,0:T(8,128)(2,1)S(1)} collective-permute-done((bf16[2,272,128]{2,1,0:T(8,128)(2,1)S(1)}, bf16[2,272,128]{2,1,0:T(8,128)(2,1)S(1)}, u32[]{:S(2)}, u32[]{:S(2)}) %collective-permute-start.9) | collective-permute-done | bytes 139296 | tf_op jit(solution)/shard_map/ppermute | solution.py:567
  28.8 0.0 collective-permute-start.11
  28.8 2.3 %collective-permute-done.4 = bf16[336,128]{1,0:T(8,128)(2,1)S(1)} collective-permute-done((bf16[336,128]{1,0:T(8,128)(2,1)S(1)}, bf16[336,128]{1,0:T(8,128)(2,1)S(1)}, u32[]{:S(2)}, u32[]{:S(2)}) %collective-permute-start.4) | collective-permute-done | bytes 86048 | tf_op jit(solution)/shard_map/ppermute | solution.py:567
  31.2 1.2 %collective-permute-start.5 = (bf16[336,128]{1,0:T(8,128)(2,1)S(1)}, bf16[336,128]{1,0:T(8,128)(2,1)S(1)}, u32[]{:S(2)}, u32[]{:S(2)}) collective-permute-start(bf16[336,128]{1,0:T(8,128)(2,1)S(1)} %add_convert_fusion.1), channel_id=1, source_target_pairs={{0,16},{2,18},{4,20},{6,22},{8,24},{10,26},{12,28},{14,30},{16,0},... | collective-permute-start | bytes 258056 | tf_op jit(solution)/shard_map/ppermute | solution.py:567
  32.4 0.0 collective-permute-done.11.last_ref
  32.4 0.0 collective-permute-done.10.far_ref
  32.4 4.4 %deep.1 = (bf16[256,2304]{1,0:T(8,128)(2,1)S(1)}, bf16[256,512]{1,0:T(8,128)(2,1)S(1)}, f32[1,512]{1,0:T(1,128)}, bf16[1024,1152]{1,0:T(8,128)(2,1)S(1)}, bf16[1024,256]{1,0:T(8,128)(2,1)S(1)}) custom-call(bf16[8,272,128]{2,1,0:T(8,128)(2,1)S(1)} %constant_dynamic-update-slice_fusion.near_ref, bf16[6,272,128]{2,1,0:T(8,128)(2,1)S(1)} %collective-permute-done.10.far_ref, ...), custom_call_target="tpu_custom_call" | custom-call | flops 1300000000 | bytes 12000000 | tf_op jit(solution)/shard_map/deep/pallas_call | solution.py:811
  36.8 0.2 collective-permute-done.5
  37.0 1.6 %collective-permute-start.13 = (bf16[336,128]{1,0:T(8,128)(2,1)S(1)}, bf16[336,128]{1,0:T(8,128)(2,1)S(1)}, u32[]{:S(2)}, u32[]{:S(2)}) collective-permute-start(bf16[336,128]{1,0:T(8,128)(2,1)S(1)} %add_convert_fusion.refs_0_), channel_id=1, source_target_pairs={{0,4},{2,6},{4,0},{6,2},{8,12},{10,14},{12,8},{14,10},{16,20},{18,... | collective-permute-start | bytes 258056 | tf_op jit(solution)/shard_map/ppermute | solution.py:567
  38.6 3.1 %fourth_grad.1 = f32[2304,512]{1,0:T(8,128)} custom-call(bf16[256,2304]{1,0:T(8,128)(2,1)S(1)} %get-tuple-element.64.fourth_taps_ref, bf16[256,512]{1,0:T(8,128)(2,1)S(1)} %get-tuple-element.65.fourth_flat_ref), custom_call_target="tpu_custom_call" | custom-call | flops 600000000 | bytes 6000000 | tf_op jit(solution)/shard_map/fourth_grad/pallas_call | solution.py:847
  41.8 0.0 collective-permute-done.13.refs_2_
  41.8 0.0 collective-permute-start.14
  41.8 0.5 %collective-permute-start.12 = (bf16[336,128]{1,0:T(8,128)(2,1)S(1)}, bf16[336,128]{1,0:T(8,128)(2,1)S(1)}, u32[]{:S(2)}, u32[]{:S(2)}) collective-permute-start(bf16[336,128]{1,0:T(8,128)(2,1)S(1)} %add_convert_fusion.refs_0_), channel_id=1, source_target_pairs={{0,2},{2,0},{4,6},{6,4},{8,10},{10,8},{12,14},{14,12},{16,18},{18,... | collective-permute-start | bytes 258056 | tf_op jit(solution)/shard_map/ppermute | solution.py:567
  42.3 2.0 %third_grad.1 = f32[1152,256]{1,0:T(8,128)} custom-call(bf16[1024,1152]{1,0:T(8,128)(2,1)S(1)} %get-tuple-element.67.taps_ref, bf16[1024,256]{1,0:T(8,128)(2,1)S(1)} %get-tuple-element.68.delta_ref), custom_call_target="tpu_custom_call" | custom-call | flops 600000000 | bytes 4000000 | tf_op jit(solution)/shard_map/third_grad/pallas_call | solution.py:863
  44.2 0.0 collective-permute-done.14.refs_3_
  44.2 0.0 collective-permute-done.12.refs_1_
  44.2 1.2 %finish.1 = (f32[9,160,64]{2,1,0:T(8,128)}, f32[576,128]{1,0:T(8,128)}) custom-call(bf16[336,128]{1,0:T(8,128)(2,1)S(1)} %add_convert_fusion.refs_0_, bf16[336,128]{1,0:T(8,128)(2,1)S(1)} %collective-permute-done.12.refs_1_, bf16[336,128]{1,0:T(8,128)(2,1)S(1)} %collective-permute-done.13.refs_2_, bf16[336,128]{1,0:T(8,128)(2,1)S(1)} %collective-permute-done.14.refs_3_), custom_call_target="tpu_custom_call" | custom-call | flops 1000000 | bytes 1500000 | tf_op jit(solution)/shard_map/finish/pallas_call | solution.py:876
  (12 shorter events, 0.2 us)
Async XLA Ops:
  0.6 5.3 %copy-start = (bf16[512]{0:T(512)(128)(2,1)S(1)}, bf16[512]{0:T(512)(128)(2,1)}, u32[]{:S(2)}) copy-start(bf16[512]{0:T(512)(128)(2,1)} %param.15) | copy-start | bytes 3076
  0.6 5.3 %collective-permute-start = (s32[1,5,16,128]{3,2,1,0:T(8,128)}, s32[1,5,16,128]{3,2,1,0:T(8,128)S(1)}, u32[]{:S(2)}, u32[]{:S(2)}) collective-permute-start(s32[1,5,16,128]{3,2,1,0:T(8,128)} %got_hbm.1), channel_id=1, source_target_pairs={{0,1},{1,0},{2,3},{3,2},{4,5},{5,4},{6,7},{7,6},{8,9},{9,8},{10,11... | collective-permute-start | bytes 122888 | tf_op jit(solution)/shard_map/ppermute | solution.py:567
  5.8 3.7 %collective-permute-start.1 = (bf16[16,128]{1,0:T(8,128)(2,1)S(1)}, bf16[16,128]{1,0:T(8,128)(2,1)S(1)}, u32[]{:S(2)}, u32[]{:S(2)}) collective-permute-start(bf16[16,128]{1,0:T(8,128)(2,1)S(1)} %get-tuple-element.46), channel_id=1, source_target_pairs={{0,1},{1,0},{2,3},{3,2},{4,5},{5,4},{6,7},{7,6},{8,9},{9,8},{10,11... | collective-permute-start | bytes 12296 | tf_op jit(solution)/shard_map/ppermute | solution.py:567
  9.5 7.0 %collective-permute-start.6 = (bf16[1,272,128]{2,1,0:T(8,128)(2,1)S(1)}, bf16[1,272,128]{2,1,0:T(8,128)(2,1)S(1)}, u32[]{:S(2)}, u32[]{:S(2)}) collective-permute-start(bf16[1,272,128]{2,1,0:T(8,128)(2,1)S(1)} %bitcast_dynamic-update-slice_fusion.payload_ref), channel_id=1, source_target_pairs={{0,16},{2,18},{4,20},{6,22},{8,24},{10,26},{12,28},{14,30},{16,0},... | collective-permute-start | bytes 208904 | tf_op jit(solution)/shard_map/ppermute | solution.py:567
  15.7 4.0 %collective-permute-start.2 = (bf16[2,336,128]{2,1,0:T(8,128)(2,1)S(1)}, bf16[2,336,128]{2,1,0:T(8,128)(2,1)S(1)}, u32[]{:S(2)}, u32[]{:S(2)}) collective-permute-start(bf16[2,336,128]{2,1,0:T(8,128)(2,1)S(1)} %get-tuple-element.55), channel_id=1, source_target_pairs={{0,2},{2,0},{4,6},{6,4},{8,10},{10,8},{12,14},{14,12},{16,18},{18,... | collective-permute-start | bytes 516104 | tf_op jit(solution)/shard_map/ppermute | solution.py:567
  16.6 6.1 %collective-permute-start.8 = (bf16[2,272,128]{2,1,0:T(8,128)(2,1)S(1)}, bf16[2,272,128]{2,1,0:T(8,128)(2,1)S(1)}, u32[]{:S(2)}, u32[]{:S(2)}) collective-permute-start(bf16[2,272,128]{2,1,0:T(8,128)(2,1)S(1)} %slice.28), channel_id=1, source_target_pairs={{0,8},{2,10},{4,12},{6,14},{8,0},{10,2},{12,4},{14,6},{16,24},{18,... | collective-permute-start | bytes 417800 | tf_op jit(solution)/shard_map/ppermute | solution.py:567
  18.2 6.5 %collective-permute-start.7 = (bf16[2,272,128]{2,1,0:T(8,128)(2,1)S(1)}, bf16[2,272,128]{2,1,0:T(8,128)(2,1)S(1)}, u32[]{:S(2)}, u32[]{:S(2)}) collective-permute-start(bf16[2,272,128]{2,1,0:T(8,128)(2,1)S(1)} %slice.28), channel_id=1, source_target_pairs={{0,4},{2,6},{4,0},{6,2},{8,12},{10,14},{12,8},{14,10},{16,20},{18,... | collective-permute-start | bytes 417800 | tf_op jit(solution)/shard_map/ppermute | solution.py:567
  19.8 6.8 %collective-permute-start.3 = (bf16[336,128]{1,0:T(8,128)(2,1)S(1)}, bf16[336,128]{1,0:T(8,128)(2,1)S(1)}, u32[]{:S(2)}, u32[]{:S(2)}) collective-permute-start(bf16[336,128]{1,0:T(8,128)(2,1)S(1)} %fusion.2), channel_id=1, source_target_pairs={{0,4},{2,6},{4,0},{6,2},{8,12},{10,14},{12,8},{14,10},{16,20},{18,... | collective-permute-start | bytes 258056 | tf_op jit(solution)/shard_map/ppermute | solution.py:567
  22.7 6.1 %collective-permute-start.9 = (bf16[2,272,128]{2,1,0:T(8,128)(2,1)S(1)}, bf16[2,272,128]{2,1,0:T(8,128)(2,1)S(1)}, u32[]{:S(2)}, u32[]{:S(2)}) collective-permute-start(bf16[2,272,128]{2,1,0:T(8,128)(2,1)S(1)} %collective-permute-done.8), channel_id=1, source_target_pairs={{0,4},{2,6},{4,0},{6,2},{8,12},{10,14},{12,8},{14,10},{16,20},{18,... | collective-permute-start | bytes 417800 | tf_op jit(solution)/shard_map/ppermute | solution.py:567
  26.6 4.6 %collective-permute-start.4 = (bf16[336,128]{1,0:T(8,128)(2,1)S(1)}, bf16[336,128]{1,0:T(8,128)(2,1)S(1)}, u32[]{:S(2)}, u32[]{:S(2)}) collective-permute-start(bf16[336,128]{1,0:T(8,128)(2,1)S(1)} %fusion), channel_id=1, source_target_pairs={{0,8},{2,10},{4,12},{6,14},{8,0},{10,2},{12,4},{14,6},{16,24},{18,... | collective-permute-start | bytes 258056 | tf_op jit(solution)/shard_map/ppermute | solution.py:567
  26.7 5.6 %collective-permute-start.10 = (bf16[6,272,128]{2,1,0:T(8,128)(2,1)S(1)}, bf16[6,272,128]{2,1,0:T(8,128)(2,1)S(1)}, u32[]{:S(2)}, u32[]{:S(2)}) collective-permute-start(bf16[6,272,128]{2,1,0:T(8,128)(2,1)S(1)} %slice.29), channel_id=1, source_target_pairs={{0,2},{2,0},{4,6},{6,4},{8,10},{10,8},{12,14},{14,12},{16,18},{18,... | collective-permute-start | bytes 1253384 | tf_op jit(solution)/shard_map/ppermute | solution.py:567
  28.8 3.5 %collective-permute-start.11 = (bf16[2,272,128]{2,1,0:T(8,128)(2,1)S(1)}, bf16[2,272,128]{2,1,0:T(8,128)(2,1)S(1)}, u32[]{:S(2)}, u32[]{:S(2)}) collective-permute-start(bf16[2,272,128]{2,1,0:T(8,128)(2,1)S(1)} %collective-permute-done.9), channel_id=1, source_target_pairs={{0,2},{2,0},{4,6},{6,4},{8,10},{10,8},{12,14},{14,12},{16,18},{18,... | collective-permute-start | bytes 417800 | tf_op jit(solution)/shard_map/ppermute | solution.py:567
  31.2 5.8 %collective-permute-start.5 = (bf16[336,128]{1,0:T(8,128)(2,1)S(1)}, bf16[336,128]{1,0:T(8,128)(2,1)S(1)}, u32[]{:S(2)}, u32[]{:S(2)}) collective-permute-start(bf16[336,128]{1,0:T(8,128)(2,1)S(1)} %add_convert_fusion.1), channel_id=1, source_target_pairs={{0,16},{2,18},{4,20},{6,22},{8,24},{10,26},{12,28},{14,30},{16,0},... | collective-permute-start | bytes 258056 | tf_op jit(solution)/shard_map/ppermute | solution.py:567
  37.0 4.7 %collective-permute-start.13 = (bf16[336,128]{1,0:T(8,128)(2,1)S(1)}, bf16[336,128]{1,0:T(8,128)(2,1)S(1)}, u32[]{:S(2)}, u32[]{:S(2)}) collective-permute-start(bf16[336,128]{1,0:T(8,128)(2,1)S(1)} %add_convert_fusion.refs_0_), channel_id=1, source_target_pairs={{0,4},{2,6},{4,0},{6,2},{8,12},{10,14},{12,8},{14,10},{16,20},{18,... | collective-permute-start | bytes 258056 | tf_op jit(solution)/shard_map/ppermute | solution.py:567
  41.8 2.5 %collective-permute-start.14 = (bf16[336,128]{1,0:T(8,128)(2,1)S(1)}, bf16[336,128]{1,0:T(8,128)(2,1)S(1)}, u32[]{:S(2)}, u32[]{:S(2)}) collective-permute-start(bf16[336,128]{1,0:T(8,128)(2,1)S(1)} %collective-permute-done.13.refs_2_), channel_id=1, source_target_pairs={{0,2},{2,0},{4,6},{6,4},{8,10},{10,8},{12,14},{14,12},{16,18},{18,... | collective-permute-start | bytes 258056 | tf_op jit(solution)/shard_map/ppermute | solution.py:567
  41.8 2.5 %collective-permute-start.12 = (bf16[336,128]{1,0:T(8,128)(2,1)S(1)}, bf16[336,128]{1,0:T(8,128)(2,1)S(1)}, u32[]{:S(2)}, u32[]{:S(2)}) collective-permute-start(bf16[336,128]{1,0:T(8,128)(2,1)S(1)} %add_convert_fusion.refs_0_), channel_id=1, source_target_pairs={{0,2},{2,0},{4,6},{6,4},{8,10},{10,8},{12,14},{14,12},{16,18},{18,... | collective-permute-start | bytes 258056 | tf_op jit(solution)/shard_map/ppermute | solution.py:567

commit v7 on v6

--- a/solution.py
+++ b/solution.py
@@ -431,18 +431,15 @@
         fourth_delta_ref,
     )
 
-    @pl.when(pl.program_id(0) == 0)
-    def _():
-        head_grad_ref[...] = jnp.zeros(head_grad_ref.shape, jnp.float32)
-
-    head_grad_ref[...] += jnp.sum(value * logit_grad, axis=0, keepdims=True)
+    head_grad = jnp.sum(value * logit_grad, axis=0, keepdims=True)
+    add_to(head_grad_ref, head_grad, stored)
     fourth_flat_ref[...] = delta.astype(jnp.bfloat16)
     delta = third_delta_ref[...]
     delta = delta.reshape(-1, delta.shape[-1]).astype(jnp.bfloat16)
     if stored:
         third_flat_ref[...] = delta
     else:
-        third_grad_kernel(third_taps_ref, delta, third_grad_ref)
+        third_grad_kernel(third_taps_ref, delta, third_grad_ref, False)
 
 
 def local_kernel(
@@ -523,12 +520,30 @@
         ref[slot // 2] = flat_ref[pl.ds(at, share)].astype(jnp.bfloat16)
 
 
-def third_grad_kernel(taps_ref, delta_ref, out_ref):
-    @pl.when(pl.program_id(0) == 0)
-    def _():
-        out_ref[...] = jnp.zeros(out_ref.shape, jnp.float32)
-
-    out_ref[...] += dot_tn(delta_ref[...], taps_ref[...]).T
+def add_to(ref, value, alone):
+    if alone:
+        ref[...] = value
+    else:
+        first = pl.program_id(0) == 0
+        ref[...] = jnp.where(first, 0.0, ref[...]) + value
+
+
+def third_grad_kernel(taps_ref, delta_ref, out_ref, alone=True):
+    add_to(out_ref, dot_tn(delta_ref[...], taps_ref[...]).T, alone)
+
+
+def fourth_grad_alone_kernel(fourth_taps_ref, fourth_flat_ref, out_hbm, grad_ref, sems):
+    depth = grad_ref.shape[1]
+    copies = []
+    for tap in range(9):
+        grad_ref[tap] = dot_tn(
+            fourth_taps_ref[:, pl.ds(tap * depth, depth)], fourth_flat_ref[...]
+        )
+        copy = pltpu.make_async_copy(grad_ref.at[tap], out_hbm.at[tap], sems.at[tap])
+        copy.start()
+        copies.append(copy)
+    for copy in copies:
+        copy.wait()
 
 
 def fourth_grad_kernel(fourth_taps_ref, fourth_flat_ref, out_ref):
@@ -591,6 +606,9 @@
     got = swapped(payload, "dp", quarter * 2) if quarter > 1 else None
     keep, passed = local_sums()
     core = swapped(passed, "dp", 1)
+    mine, theirs = added(keep[0], core[0]), added(keep[1], core[1])
+    mine_beside = swapped(theirs, "dp", 2)
+    weights = transposed(theirs)
     count, beside_count = 1, 0
     while count < quarter:
         near = put(near, after(got, keep), count)
@@ -598,13 +616,10 @@
         if count < quarter:
             part = near[beside_count:count]
             got = swapped(near[:count], "dp", half // count)
-            beside = swapped(part, "dp", 2)
+            beside = swapped(after(part, theirs), "dp", 2)
             near = put(near, beside, quarter + beside_count)
             beside_count = count
-    weights = transposed(after(keep, core))
-    mine, theirs = added(keep[0], core[0]), added(keep[1], core[1])
-    theirs = after(theirs, weights)
-    total = added(mine, swapped(theirs, "dp", 2))
+    total = added(mine, after(mine_beside, weights))
     beside = swapped(after(near[beside_count:quarter], theirs), "dp", 2)
     early = swapped(near[: quarter + beside_count], "dp", 1)
     bit = 4
@@ -797,40 +812,30 @@
     chunk = max(1, min(samples, 32 // bands))
     steps = samples // chunk
     full = lambda *shape: pl.BlockSpec(shape, lambda i: (0,) * len(shape))
-    rows_block = pl.BlockSpec((chunk * third_cells, 9 * two), lambda i: (i, 0))
-    flat_block = pl.BlockSpec((chunk * third_cells, three), lambda i: (i, 0))
     grad_shape = shaped((9 * two, three), f32)
+    third_shapes = (grad_shape,)
     if small:
         third_shapes = (
             shaped((samples * third_cells, 9 * two), bf16),
             shaped((samples * third_cells, three), bf16),
         )
-        third_blocks = (rows_block, flat_block)
-    else:
-        third_shapes, third_blocks = (grad_shape,), (full(9 * two, three),)
     fourth_taps, fourth_flat, head_grad, *thirds = pl.pallas_call(
         functools.partial(deep_kernel, samples, bands, small),
-        grid=(steps,),
+        **({} if small else {"grid": (steps,)}),
         out_shape=(
             shaped((samples * fourth_cells, 9 * three), bf16),
             shaped((samples * fourth_cells, four), bf16),
             shaped((1, four), f32),
             *third_shapes,
         ),
-        in_specs=[
-            full(*near.shape),
-            full(*far.shape),
-            full(*last.shape),
-            full(9, two, three),
-            full(9, three, four),
-            full(9, four, three),
-            full(1, four),
+        in_specs=[vmem] * 7 if small else [
+            full(*value.shape) for value in (near, far, last, *deep_weights, fourth_wt, head)
         ],
-        out_specs=(
+        out_specs=(vmem,) * 5 if small else (
             pl.BlockSpec((chunk * fourth_cells, 9 * three), lambda i: (i, 0)),
             pl.BlockSpec((chunk * fourth_cells, four), lambda i: (i, 0)),
             full(1, four),
-            *third_blocks,
+            full(9 * two, three),
         ),
         scratch_shapes=[second_scratch(chunk), pltpu.VMEM((chunk, bands, BLOCK, two), f32)]
         + deep_scratch(chunk)[1 if small else 0 :],
@@ -844,28 +849,42 @@
         total = added(total, other)
     beside = swapped(total, "dp", 2)
     core = swapped(total, "dp", 1)
-    deepest_grad = pl.pallas_call(
-        fourth_grad_kernel,
-        grid=(3, steps),
-        out_shape=shaped((9 * three, four), f32),
-        in_specs=[
-            pl.BlockSpec((chunk * fourth_cells, 3 * three), lambda t, i: (i, t)),
-            pl.BlockSpec((chunk * fourth_cells, four), lambda t, i: (i, 0)),
-        ],
-        out_specs=pl.BlockSpec((3 * three, four), lambda t, i: (t, 0)),
-        compiler_params=grant(16),
-        cost_estimate=cost(600_000_000, 6_000_000),
-        name="fourth_grad",
-    )(fourth_taps, fourth_flat)
+    if small:
+        deepest_grad = pl.pallas_call(
+            fourth_grad_alone_kernel,
+            out_shape=shaped((9, three, four), f32),
+            in_specs=[vmem] * 2,
+            out_specs=pl.BlockSpec(memory_space=pl.ANY),
+            scratch_shapes=[
+                pltpu.VMEM((9, three, four), f32),
+                pltpu.SemaphoreType.DMA((9,)),
+            ],
+            compiler_params=grant(16),
+            cost_estimate=cost(600_000_000, 6_000_000),
+            name="fourth_grad",
+        )(fourth_taps, fourth_flat)
+    else:
+        deepest_grad = pl.pallas_call(
+            fourth_grad_kernel,
+            grid=(3, steps),
+            out_shape=shaped((9 * three, four), f32),
+            in_specs=[
+                pl.BlockSpec((chunk * fourth_cells, 3 * three), lambda t, i: (i, t)),
+                pl.BlockSpec((chunk * fourth_cells, four), lambda t, i: (i, 0)),
+            ],
+            out_specs=pl.BlockSpec((3 * three, four), lambda t, i: (t, 0)),
+            compiler_params=grant(16),
+            cost_estimate=cost(600_000_000, 6_000_000),
+            name="fourth_grad",
+        )(fourth_taps, fourth_flat)
     beside, deepest_grad = lax.optimization_barrier((beside, deepest_grad))
     across = swapped(beside, "dp", 1)
     if small:
         deeper_grad = pl.pallas_call(
             third_grad_kernel,
-            grid=(steps,),
             out_shape=grad_shape,
-            in_specs=[rows_block, flat_block],
-            out_specs=full(9 * two, three),
+            in_specs=[vmem] * 2,
+            out_specs=vmem,
             compiler_params=grant(24),
             cost_estimate=cost(600_000_000, 4_000_000),
             name="third_grad",

time: 45.6 us -> 44.5 us (0.976)
  waiting for transfers between devices: 10.1 us -> 7.62 us
  starting transfers between devices: 14.4 us -> 16.3 us
  Pallas kernels: 19.9 us -> 19.2 us
    ppermute x15, waiting for transfers between devices: 10.1 us -> 7.62 us  [swapped(): lax.ppermute(value, axis, [(i, i ^ bit) for i in range(lax.axis_size(axis...]
    ppermute x15, starting transfers between devices: 14.4 us -> 16.3 us  [swapped(): lax.ppermute(value, axis, [(i, i ^ bit) for i in range(lax.axis_size(axis...]
    pallas_call x3, Pallas kernels: 9.51 us -> 8.87 us  [the longest x1 4.4 us: local(): pl.pallas_call(functools.partial(deep_kernel, samples, bands, small), **{...]
  transfers between devices with their start and end apart: 15 -> 15, of which waited for: 7 -> 6; matrix products, arithmetic and copies ran while one was open for 1% -> 1% of each run, Pallas kernels for 41% -> 41%
where the time goes in v7:
time: 44.5 us; the launch traced here: 44.3 us
  Pallas kernels  19.2 us (43%)
  starting transfers between devices  16.3 us (37%)
  waiting for transfers between devices  7.62 us (17%)
  between operations  0.81 us (2%)
    ppermute x15, starting transfers between devices, swapped(): lax.ppermute(value, axis, [(i, i ^ bit) for i in range(lax.axis_size(axis...  16.3 us
    ppermute x15, waiting for transfers between devices, swapped(): lax.ppermute(value, axis, [(i, i ^ bit) for i in range(lax.axis_size(axis...  7.62 us
    pallas_call x1, Pallas kernels, local(): pl.pallas_call(functools.partial(deep_kernel, samples, bands, small), **{...  4.4 us
    pallas_call x1, Pallas kernels, local(): local_call(payload, *deep_weights, *maps)  3.6 us
    pallas_call x1, Pallas kernels, local(): pl.pallas_call(functools.partial(early_kernel, pieces, lift_all - 128), o...  2.73 us
    pallas_call x1, Pallas kernels, local(): pl.pallas_call(fourth_grad_alone_kernel, out_shape=shaped((9, three, four...  2.51 us
    pallas_call x1, Pallas kernels, local(): pl.pallas_call(own_kernel, out_shape=(own_cells, own_cells, shaped((16, t...  2.15 us
    pallas_call x1, Pallas kernels, local(): pl.pallas_call(third_grad_kernel, out_shape=grad_shape, in_specs=[vmem] *...  1.96 us
  transfers between devices with their start and end apart: 15, of which 6 were waited for; matrix products, arithmetic and copies ran while one was open for 1% of the time, Pallas kernels for 41%

profile of v7, /device:TPU:0, one launch (start us, length us, event | category | flops | bytes accessed | tf_op | source)
XLA Modules:
  0.0 44.3 jit_solution(8116891905985879569)
XLA Ops:
  0.6 0.0 copy-start
  0.6 3.0 %collective-permute-start = (s32[1,5,16,128]{3,2,1,0:T(8,128)}, s32[1,5,16,128]{3,2,1,0:T(8,128)S(1)}, u32[]{:S(2)}, u32[]{:S(2)}) collective-permute-start(s32[1,5,16,128]{3,2,1,0:T(8,128)} %got_hbm.1), channel_id=1, source_target_pairs={{0,1},{1,0},{2,3},{3,2},{4,5},{5,4},{6,7},{7,6},{8,9},{9,8},{10,11... | collective-permute-start | bytes 122888 | tf_op jit(solution)/shard_map/ppermute | solution.py:582
  3.6 2.2 %own_band.1 = (bf16[512,512]{1,0:T(8,128)(2,1)S(1)}, bf16[512,512]{1,0:T(8,128)(2,1)S(1)}, bf16[16,128]{1,0:T(8,128)(2,1)S(1)}, bf16[128,256]{1,0:T(8,128)(2,1)S...) custom-call(s32[1,5,16,128]{3,2,1,0:T(8,128)} %got_hbm.1, ...), custom_call_target="tpu_custom_call" | custom-call | flops 100000000 | bytes 10000000 | tf_op jit(solution)/shard_map/own_band/pallas_call | solution.py:703
  5.8 0.1 collective-permute-start.1
  5.9 0.0 copy-done
  5.9 0.0 collective-permute-done.refs_0_
  5.9 2.7 %early.1 = (bf16[1024,512]{1,0:T(8,128)(2,1)S(1)}, bf16[1088,512]{1,0:T(8,128)(2,1)S(1)}, bf16[272,128]{1,0:T(8,128)(2,1)S(1)}, f32[1,9,2,5,2,8,64]{6,5,4,3,2,1,...) custom-call(s32[1,5,16,128]{3,2,1,0:T(8,128)S(1)} %collective-permute-done.refs_0_, ...), custom_call_target="tpu_custom_call" | custom-call | flops 150000000 | bytes 4000000 | tf_op jit(solution)/shard_map/early/pallas_call | solution.py:730
  8.7 0.8 %collective-permute-done.1 = bf16[16,128]{1,0:T(8,128)(2,1)S(1)} collective-permute-done((bf16[16,128]{1,0:T(8,128)(2,1)S(1)}, bf16[16,128]{1,0:T(8,128)(2,1)S(1)}, u32[]{:S(2)}, u32[]{:S(2)}) %collective-permute-start.1) | collective-permute-done | bytes 4128 | tf_op jit(solution)/shard_map/ppermute | solution.py:582
  9.5 2.6 %collective-permute-start.6 = (bf16[1,272,128]{2,1,0:T(8,128)(2,1)S(1)}, bf16[1,272,128]{2,1,0:T(8,128)(2,1)S(1)}, u32[]{:S(2)}, u32[]{:S(2)}) collective-permute-start(bf16[1,272,128]{2,1,0:T(8,128)(2,1)S(1)} %bitcast_dynamic-update-slice_fusion.payload_ref), channel_id=1, source_target_pairs={{0,16},{2,18},{4,20},{6,22},{8,24},{10,26},{12,28},{14,30},{16,0},... | collective-permute-start | bytes 208904 | tf_op jit(solution)/shard_map/ppermute | solution.py:582
  12.1 3.6 %local.1 = (bf16[2,336,128]{2,1,0:T(8,128)(2,1)S(1)}, bf16[2,336,128]{2,1,0:T(8,128)(2,1)S(1)}) custom-call(bf16[1,272,128]{2,1,0:T(8,128)(2,1)S(1)} %bitcast_dynamic-update-slice_fusion.payload_ref, bf16[9,128,256]{2,1,0:T(8,128)(2,1)S(1)} %get-tuple-element.49.third_w_ref, bf16[9,256,512]{2,1,0:T(8,128)(2,1)S(1)} %get-tuple-element.58.fourth_w_ref.weight_ref, ...), custom_call_target="tpu_custom_call" | custom-call | flops 300000000 | bytes 9000000 | tf_op jit(solution)/shard_map/local/pallas_call | solution.py:806
  15.7 0.1 collective-permute-start.2
  15.8 0.1 dynamic_update_slice.20
  15.8 0.0 collective-permute-done.6
  15.9 1.6 %collective-permute-start.8 = (bf16[2,272,128]{2,1,0:T(8,128)(2,1)S(1)}, bf16[2,272,128]{2,1,0:T(8,128)(2,1)S(1)}, u32[]{:S(2)}, u32[]{:S(2)}) collective-permute-start(bf16[2,272,128]{2,1,0:T(8,128)(2,1)S(1)} %slice.28), channel_id=1, source_target_pairs={{0,8},{2,10},{4,12},{6,14},{8,0},{10,2},{12,4},{14,6},{16,24},{18,... | collective-permute-start | bytes 417800 | tf_op jit(solution)/shard_map/ppermute | solution.py:582
  17.5 0.0 collective-permute-done.2
  17.6 1.6 %collective-permute-start.3 = (bf16[336,128]{1,0:T(8,128)(2,1)S(1)}, bf16[336,128]{1,0:T(8,128)(2,1)S(1)}, u32[]{:S(2)}, u32[]{:S(2)}) collective-permute-start(bf16[336,128]{1,0:T(8,128)(2,1)S(1)} %fusion.2), channel_id=1, source_target_pairs={{0,4},{2,6},{4,0},{6,2},{8,12},{10,14},{12,8},{14,10},{16,20},{18,... | collective-permute-start | bytes 258056 | tf_op jit(solution)/shard_map/ppermute | solution.py:582
  19.2 0.5 %collective-permute-start.7 = (bf16[2,272,128]{2,1,0:T(8,128)(2,1)S(1)}, bf16[2,272,128]{2,1,0:T(8,128)(2,1)S(1)}, u32[]{:S(2)}, u32[]{:S(2)}) collective-permute-start(bf16[2,272,128]{2,1,0:T(8,128)(2,1)S(1)} %slice.28), channel_id=1, source_target_pairs={{0,4},{2,6},{4,0},{6,2},{8,12},{10,14},{12,8},{14,10},{16,20},{18,... | collective-permute-start | bytes 417800 | tf_op jit(solution)/shard_map/ppermute | solution.py:582
  19.7 0.7 %transpose.1.fourth_wt_ref = bf16[9,512,256]{2,1,0:T(8,128)(2,1)S(1)} custom-call(bf16[9,256,512]{2,1,0:T(8,128)(2,1)S(1)} %get-tuple-element.58.fourth_w_ref.weight_ref), custom_call_target="tpu_custom_call" | custom-call | flops 10000000 | bytes 5000000 | tf_op jit(solution)/shard_map/transpose/pallas_call | solution.py:807
  20.3 1.7 %collective-permute-done.8 = bf16[2,272,128]{2,1,0:T(8,128)(2,1)S(1)} collective-permute-done((bf16[2,272,128]{2,1,0:T(8,128)(2,1)S(1)}, bf16[2,272,128]{2,1,0:T(8,128)(2,1)S(1)}, u32[]{:S(2)}, u32[]{:S(2)}) %collective-permute-start.8) | collective-permute-done | bytes 139296 | tf_op jit(solution)/shard_map/ppermute | solution.py:582
  22.0 1.5 %collective-permute-start.9 = (bf16[2,272,128]{2,1,0:T(8,128)(2,1)S(1)}, bf16[2,272,128]{2,1,0:T(8,128)(2,1)S(1)}, u32[]{:S(2)}, u32[]{:S(2)}) collective-permute-start(bf16[2,272,128]{2,1,0:T(8,128)(2,1)S(1)} %collective-permute-done.8), channel_id=1, source_target_pairs={{0,4},{2,6},{4,0},{6,2},{8,12},{10,14},{12,8},{14,10},{16,20},{18,... | collective-permute-start | bytes 417800 | tf_op jit(solution)/shard_map/ppermute | solution.py:582
  23.6 0.0 collective-permute-done.3
  23.6 1.6 %collective-permute-start.4 = (bf16[336,128]{1,0:T(8,128)(2,1)S(1)}, bf16[336,128]{1,0:T(8,128)(2,1)S(1)}, u32[]{:S(2)}, u32[]{:S(2)}) collective-permute-start(bf16[336,128]{1,0:T(8,128)(2,1)S(1)} %fusion), channel_id=1, source_target_pairs={{0,8},{2,10},{4,12},{6,14},{8,0},{10,2},{12,4},{14,6},{16,24},{18,... | collective-permute-start | bytes 258056 | tf_op jit(solution)/shard_map/ppermute | solution.py:582
  25.2 0.6 %collective-permute-done.7 = bf16[2,272,128]{2,1,0:T(8,128)(2,1)S(1)} collective-permute-done((bf16[2,272,128]{2,1,0:T(8,128)(2,1)S(1)}, bf16[2,272,128]{2,1,0:T(8,128)(2,1)S(1)}, u32[]{:S(2)}, u32[]{:S(2)}) %collective-permute-start.7) | collective-permute-done | bytes 139296 | tf_op jit(solution)/shard_map/ppermute | solution.py:582
  26.0 0.1 collective-permute-start.10
  26.0 2.2 %collective-permute-done.9 = bf16[2,272,128]{2,1,0:T(8,128)(2,1)S(1)} collective-permute-done((bf16[2,272,128]{2,1,0:T(8,128)(2,1)S(1)}, bf16[2,272,128]{2,1,0:T(8,128)(2,1)S(1)}, u32[]{:S(2)}, u32[]{:S(2)}) %collective-permute-start.9) | collective-permute-done | bytes 139296 | tf_op jit(solution)/shard_map/ppermute | solution.py:582
  28.3 0.0 collective-permute-start.11
  28.3 0.0 collective-permute-done.4
  28.3 1.5 %collective-permute-start.5 = (bf16[336,128]{1,0:T(8,128)(2,1)S(1)}, bf16[336,128]{1,0:T(8,128)(2,1)S(1)}, u32[]{:S(2)}, u32[]{:S(2)}) collective-permute-start(bf16[336,128]{1,0:T(8,128)(2,1)S(1)} %add_convert_fusion.1), channel_id=1, source_target_pairs={{0,16},{2,18},{4,20},{6,22},{8,24},{10,26},{12,28},{14,30},{16,0},... | collective-permute-start | bytes 258056 | tf_op jit(solution)/shard_map/ppermute | solution.py:582
  29.8 0.0 collective-permute-done.11.last_ref
  29.9 0.0 collective-permute-done.10.far_ref
  29.9 4.4 %deep.1 = (bf16[256,2304]{1,0:T(8,128)(2,1)S(1)}, bf16[256,512]{1,0:T(8,128)(2,1)S(1)}, f32[1,512]{1,0:T(1,128)}, bf16[1024,1152]{1,0:T(8,128)(2,1)S(1)}, bf16[1024,256]{1,0:T(8,128)(2,1)S(1)}) custom-call(bf16[8,272,128]{2,1,0:T(8,128)(2,1)S(1)} %constant_dynamic-update-slice_fusion.near_ref, bf16[6,272,128]{2,1,0:T(8,128)(2,1)S(1)} %collective-permute-done.10.far_ref, ...), custom_call_target="tpu_custom_call" | custom-call | flops 1300000000 | bytes 12000000 | tf_op jit(solution)/shard_map/deep/pallas_call | solution.py:822
  34.3 1.8 %collective-permute-done.5 = bf16[336,128]{1,0:T(8,128)(2,1)S(1)} collective-permute-done((bf16[336,128]{1,0:T(8,128)(2,1)S(1)}, bf16[336,128]{1,0:T(8,128)(2,1)S(1)}, u32[]{:S(2)}, u32[]{:S(2)}) %collective-permute-start.5) | collective-permute-done | bytes 86048 | tf_op jit(solution)/shard_map/ppermute | solution.py:582
  36.1 1.6 %collective-permute-start.13 = (bf16[336,128]{1,0:T(8,128)(2,1)S(1)}, bf16[336,128]{1,0:T(8,128)(2,1)S(1)}, u32[]{:S(2)}, u32[]{:S(2)}) collective-permute-start(bf16[336,128]{1,0:T(8,128)(2,1)S(1)} %add_convert_fusion.refs_0_), channel_id=1, source_target_pairs={{0,4},{2,6},{4,0},{6,2},{8,12},{10,14},{12,8},{14,10},{16,20},{18,... | collective-permute-start | bytes 258056 | tf_op jit(solution)/shard_map/ppermute | solution.py:582
  37.7 2.5 %fourth_grad.1 = f32[9,256,512]{2,1,0:T(8,128)} custom-call(bf16[256,2304]{1,0:T(8,128)(2,1)S(1)} %get-tuple-element.68.fourth_taps_ref, bf16[256,512]{1,0:T(8,128)(2,1)S(1)} %get-tuple-element.69.fourth_flat_ref), custom_call_target="tpu_custom_call" | custom-call | flops 600000000 | bytes 6000000 | tf_op jit(solution)/shard_map/fourth_grad/pallas_call | solution.py:853
  40.2 0.4 %collective-permute-done.13.refs_2_ = bf16[336,128]{1,0:T(8,128)(2,1)S(1)} collective-permute-done((bf16[336,128]{1,0:T(8,128)(2,1)S(1)}, bf16[336,128]{1,0:T(8,128)(2,1)S(1)}, u32[]{:S(2)}, u32[]{:S(2)}) %collective-permute-start.13) | collective-permute-done | bytes 86048 | tf_op jit(solution)/shard_map/ppermute | solution.py:582
  40.6 0.0 collective-permute-start.14
  40.6 0.5 %collective-permute-start.12 = (bf16[336,128]{1,0:T(8,128)(2,1)S(1)}, bf16[336,128]{1,0:T(8,128)(2,1)S(1)}, u32[]{:S(2)}, u32[]{:S(2)}) collective-permute-start(bf16[336,128]{1,0:T(8,128)(2,1)S(1)} %add_convert_fusion.refs_0_), channel_id=1, source_target_pairs={{0,2},{2,0},{4,6},{6,4},{8,10},{10,8},{12,14},{14,12},{16,18},{18,... | collective-permute-start | bytes 258056 | tf_op jit(solution)/shard_map/ppermute | solution.py:582
  41.1 2.0 %third_grad.1 = f32[1152,256]{1,0:T(8,128)} custom-call(bf16[1024,1152]{1,0:T(8,128)(2,1)S(1)} %get-tuple-element.71.taps_ref, bf16[1024,256]{1,0:T(8,128)(2,1)S(1)} %get-tuple-element.72.delta_ref), custom_call_target="tpu_custom_call" | custom-call | flops 600000000 | bytes 4000000 | tf_op jit(solution)/shard_map/third_grad/pallas_call | solution.py:883
  43.1 0.0 collective-permute-done.14.refs_3_
  43.1 0.0 collective-permute-done.12.refs_1_
  43.1 1.2 %finish.1 = (f32[9,160,64]{2,1,0:T(8,128)}, f32[576,128]{1,0:T(8,128)}) custom-call(bf16[336,128]{1,0:T(8,128)(2,1)S(1)} %add_convert_fusion.refs_0_, bf16[336,128]{1,0:T(8,128)(2,1)S(1)} %collective-permute-done.12.refs_1_, bf16[336,128]{1,0:T(8,128)(2,1)S(1)} %collective-permute-done.13.refs_2_, bf16[336,128]{1,0:T(8,128)(2,1)S(1)} %collective-permute-done.14.refs_3_), custom_call_target="tpu_custom_call" | custom-call | flops 1000000 | bytes 1500000 | tf_op jit(solution)/shard_map/finish/pallas_call | solution.py:895
  (12 shorter events, 0.2 us)
Async XLA Ops:
  0.6 5.3 %copy-start = (bf16[512]{0:T(512)(128)(2,1)S(1)}, bf16[512]{0:T(512)(128)(2,1)}, u32[]{:S(2)}) copy-start(bf16[512]{0:T(512)(128)(2,1)} %param.15) | copy-start | bytes 3076
  0.6 5.3 %collective-permute-start = (s32[1,5,16,128]{3,2,1,0:T(8,128)}, s32[1,5,16,128]{3,2,1,0:T(8,128)S(1)}, u32[]{:S(2)}, u32[]{:S(2)}) collective-permute-start(s32[1,5,16,128]{3,2,1,0:T(8,128)} %got_hbm.1), channel_id=1, source_target_pairs={{0,1},{1,0},{2,3},{3,2},{4,5},{5,4},{6,7},{7,6},{8,9},{9,8},{10,11... | collective-permute-start | bytes 122888 | tf_op jit(solution)/shard_map/ppermute | solution.py:582
  5.8 3.7 %collective-permute-start.1 = (bf16[16,128]{1,0:T(8,128)(2,1)S(1)}, bf16[16,128]{1,0:T(8,128)(2,1)S(1)}, u32[]{:S(2)}, u32[]{:S(2)}) collective-permute-start(bf16[16,128]{1,0:T(8,128)(2,1)S(1)} %get-tuple-element.48), channel_id=1, source_target_pairs={{0,1},{1,0},{2,3},{3,2},{4,5},{5,4},{6,7},{7,6},{8,9},{9,8},{10,11... | collective-permute-start | bytes 12296 | tf_op jit(solution)/shard_map/ppermute | solution.py:582
  9.5 6.4 %collective-permute-start.6 = (bf16[1,272,128]{2,1,0:T(8,128)(2,1)S(1)}, bf16[1,272,128]{2,1,0:T(8,128)(2,1)S(1)}, u32[]{:S(2)}, u32[]{:S(2)}) collective-permute-start(bf16[1,272,128]{2,1,0:T(8,128)(2,1)S(1)} %bitcast_dynamic-update-slice_fusion.payload_ref), channel_id=1, source_target_pairs={{0,16},{2,18},{4,20},{6,22},{8,24},{10,26},{12,28},{14,30},{16,0},... | collective-permute-start | bytes 208904 | tf_op jit(solution)/shard_map/ppermute | solution.py:582
  15.7 1.9 %collective-permute-start.2 = (bf16[2,336,128]{2,1,0:T(8,128)(2,1)S(1)}, bf16[2,336,128]{2,1,0:T(8,128)(2,1)S(1)}, u32[]{:S(2)}, u32[]{:S(2)}) collective-permute-start(bf16[2,336,128]{2,1,0:T(8,128)(2,1)S(1)} %get-tuple-element.57), channel_id=1, source_target_pairs={{0,2},{2,0},{4,6},{6,4},{8,10},{10,8},{12,14},{14,12},{16,18},{18,... | collective-permute-start | bytes 516104 | tf_op jit(solution)/shard_map/ppermute | solution.py:582
  15.9 6.1 %collective-permute-start.8 = (bf16[2,272,128]{2,1,0:T(8,128)(2,1)S(1)}, bf16[2,272,128]{2,1,0:T(8,128)(2,1)S(1)}, u32[]{:S(2)}, u32[]{:S(2)}) collective-permute-start(bf16[2,272,128]{2,1,0:T(8,128)(2,1)S(1)} %slice.28), channel_id=1, source_target_pairs={{0,8},{2,10},{4,12},{6,14},{8,0},{10,2},{12,4},{14,6},{16,24},{18,... | collective-permute-start | bytes 417800 | tf_op jit(solution)/shard_map/ppermute | solution.py:582
  17.6 6.0 %collective-permute-start.3 = (bf16[336,128]{1,0:T(8,128)(2,1)S(1)}, bf16[336,128]{1,0:T(8,128)(2,1)S(1)}, u32[]{:S(2)}, u32[]{:S(2)}) collective-permute-start(bf16[336,128]{1,0:T(8,128)(2,1)S(1)} %fusion.2), channel_id=1, source_target_pairs={{0,4},{2,6},{4,0},{6,2},{8,12},{10,14},{12,8},{14,10},{16,20},{18,... | collective-permute-start | bytes 258056 | tf_op jit(solution)/shard_map/ppermute | solution.py:582
  19.2 6.7 %collective-permute-start.7 = (bf16[2,272,128]{2,1,0:T(8,128)(2,1)S(1)}, bf16[2,272,128]{2,1,0:T(8,128)(2,1)S(1)}, u32[]{:S(2)}, u32[]{:S(2)}) collective-permute-start(bf16[2,272,128]{2,1,0:T(8,128)(2,1)S(1)} %slice.28), channel_id=1, source_target_pairs={{0,4},{2,6},{4,0},{6,2},{8,12},{10,14},{12,8},{14,10},{16,20},{18,... | collective-permute-start | bytes 417800 | tf_op jit(solution)/shard_map/ppermute | solution.py:582
  22.0 6.2 %collective-permute-start.9 = (bf16[2,272,128]{2,1,0:T(8,128)(2,1)S(1)}, bf16[2,272,128]{2,1,0:T(8,128)(2,1)S(1)}, u32[]{:S(2)}, u32[]{:S(2)}) collective-permute-start(bf16[2,272,128]{2,1,0:T(8,128)(2,1)S(1)} %collective-permute-done.8), channel_id=1, source_target_pairs={{0,4},{2,6},{4,0},{6,2},{8,12},{10,14},{12,8},{14,10},{16,20},{18,... | collective-permute-start | bytes 417800 | tf_op jit(solution)/shard_map/ppermute | solution.py:582
  23.6 4.7 %collective-permute-start.4 = (bf16[336,128]{1,0:T(8,128)(2,1)S(1)}, bf16[336,128]{1,0:T(8,128)(2,1)S(1)}, u32[]{:S(2)}, u32[]{:S(2)}) collective-permute-start(bf16[336,128]{1,0:T(8,128)(2,1)S(1)} %fusion), channel_id=1, source_target_pairs={{0,8},{2,10},{4,12},{6,14},{8,0},{10,2},{12,4},{14,6},{16,24},{18,... | collective-permute-start | bytes 258056 | tf_op jit(solution)/shard_map/ppermute | solution.py:582
  26.0 3.9 %collective-permute-start.10 = (bf16[6,272,128]{2,1,0:T(8,128)(2,1)S(1)}, bf16[6,272,128]{2,1,0:T(8,128)(2,1)S(1)}, u32[]{:S(2)}, u32[]{:S(2)}) collective-permute-start(bf16[6,272,128]{2,1,0:T(8,128)(2,1)S(1)} %slice.29), channel_id=1, source_target_pairs={{0,2},{2,0},{4,6},{6,4},{8,10},{10,8},{12,14},{14,12},{16,18},{18,... | collective-permute-start | bytes 1253384 | tf_op jit(solution)/shard_map/ppermute | solution.py:582
  28.3 1.6 %collective-permute-start.11 = (bf16[2,272,128]{2,1,0:T(8,128)(2,1)S(1)}, bf16[2,272,128]{2,1,0:T(8,128)(2,1)S(1)}, u32[]{:S(2)}, u32[]{:S(2)}) collective-permute-start(bf16[2,272,128]{2,1,0:T(8,128)(2,1)S(1)} %collective-permute-done.9), channel_id=1, source_target_pairs={{0,2},{2,0},{4,6},{6,4},{8,10},{10,8},{12,14},{14,12},{16,18},{18,... | collective-permute-start | bytes 417800 | tf_op jit(solution)/shard_map/ppermute | solution.py:582
  28.3 7.8 %collective-permute-start.5 = (bf16[336,128]{1,0:T(8,128)(2,1)S(1)}, bf16[336,128]{1,0:T(8,128)(2,1)S(1)}, u32[]{:S(2)}, u32[]{:S(2)}) collective-permute-start(bf16[336,128]{1,0:T(8,128)(2,1)S(1)} %add_convert_fusion.1), channel_id=1, source_target_pairs={{0,16},{2,18},{4,20},{6,22},{8,24},{10,26},{12,28},{14,30},{16,0},... | collective-permute-start | bytes 258056 | tf_op jit(solution)/shard_map/ppermute | solution.py:582
  36.1 4.6 %collective-permute-start.13 = (bf16[336,128]{1,0:T(8,128)(2,1)S(1)}, bf16[336,128]{1,0:T(8,128)(2,1)S(1)}, u32[]{:S(2)}, u32[]{:S(2)}) collective-permute-start(bf16[336,128]{1,0:T(8,128)(2,1)S(1)} %add_convert_fusion.refs_0_), channel_id=1, source_target_pairs={{0,4},{2,6},{4,0},{6,2},{8,12},{10,14},{12,8},{14,10},{16,20},{18,... | collective-permute-start | bytes 258056 | tf_op jit(solution)/shard_map/ppermute | solution.py:582
  40.6 2.5 %collective-permute-start.14 = (bf16[336,128]{1,0:T(8,128)(2,1)S(1)}, bf16[336,128]{1,0:T(8,128)(2,1)S(1)}, u32[]{:S(2)}, u32[]{:S(2)}) collective-permute-start(bf16[336,128]{1,0:T(8,128)(2,1)S(1)} %collective-permute-done.13.refs_2_), channel_id=1, source_target_pairs={{0,2},{2,0},{4,6},{6,4},{8,10},{10,8},{12,14},{14,12},{16,18},{18,... | collective-permute-start | bytes 258056 | tf_op jit(solution)/shard_map/ppermute | solution.py:582
  40.6 2.5 %collective-permute-start.12 = (bf16[336,128]{1,0:T(8,128)(2,1)S(1)}, bf16[336,128]{1,0:T(8,128)(2,1)S(1)}, u32[]{:S(2)}, u32[]{:S(2)}) collective-permute-start(bf16[336,128]{1,0:T(8,128)(2,1)S(1)} %add_convert_fusion.refs_0_), channel_id=1, source_target_pairs={{0,2},{2,0},{4,6},{6,4},{8,10},{10,8},{12,14},{14,12},{16,18},{18,... | collective-permute-start | bytes 258056 | tf_op jit(solution)/shard_map/ppermute | solution.py:582

commit v8 on v7

--- a/solution.py
+++ b/solution.py
@@ -8,6 +8,7 @@
 from jax.sharding import PartitionSpec as P
 
 BLOCK = 8
+LABEL_BIT = 13
 MIB = 1 << 20
 
 
@@ -33,9 +34,16 @@
     return value.astype(jnp.bfloat16).astype(jnp.float32)
 
 
+def sigmoid(value):
+    below = 1.0 + jnp.exp(jnp.minimum(-value, 80.0))
+    guess = pl.reciprocal(below, approx=True)
+    return guess * (2.0 - below * guess)
+
+
 def silu_and_slope(pre):
-    gate = jax.nn.sigmoid(pre)
-    return rounded(pre * gate), gate * (1.0 + pre * (1.0 - gate))
+    gate = sigmoid(pre)
+    value = pre * gate
+    return rounded(value), gate + value * (1.0 - gate)
 
 
 def zero_row(ref):
@@ -102,7 +110,9 @@
     return jnp.where(column == source, 1.0, 0.0).astype(jnp.bfloat16)
 
 
-def band_cells(got_ref, inner, index, order, lift_ref, bits_ref, even_ref, odd_ref, rest):
+def band_cells(
+    got_ref, inner, index, label_lane, order, lift_ref, bits_ref, even_ref, odd_ref, rest
+):
     _, frames, band, cols = got_ref.shape
     phases, row_cells = cols // BLOCK, cols // 2
     height = lax.broadcasted_iota(jnp.int32, (16, cols), 0)
@@ -114,6 +124,12 @@
                 jnp.bfloat16
             )
     spread = dot_nt(order, bits_ref[...]).astype(jnp.bfloat16)
+    line = jnp.broadcast_to(got_ref[inner, 0, pl.ds(0, 1)], height.shape)
+    line = jnp.bitwise_and(jnp.right_shift(line, LABEL_BIT), 1).astype(jnp.float32)
+    lane = lax.broadcasted_iota(jnp.int32, line.shape, 1)
+    row = lax.broadcasted_iota(jnp.int32, line.shape, 0)
+    label = jnp.sum(jnp.where(row == lane, line, 0.0), axis=1, keepdims=True)
+    label = jnp.where(lane == label_lane, label, 0.0)
     stacked = jnp.concatenate(
         [spread[:, row * 128 : row * 128 + 128] for row in range(band)], axis=0
     )
@@ -133,48 +149,29 @@
         else:
             at = pl.multiple_of((index * (band // 2) + parity) * row_cells, row_cells)
             ref[pl.ds(at, cells.shape[0])] = cells.astype(jnp.bfloat16)
-
-
-def band_label(label_ref, inner, index, shape):
-    lane = lax.broadcasted_iota(jnp.int32, shape, 1)
-    row = lax.broadcasted_iota(jnp.int32, (shape[0], BLOCK), 0)
-    column = lax.broadcasted_iota(jnp.int32, (shape[0], BLOCK), 1)
-    label = jnp.broadcast_to(label_ref[inner].astype(jnp.float32), row.shape)
-    label = jnp.sum(jnp.where(row == column, label, 0.0), axis=1, keepdims=True)
-    return jnp.where(lane == index, label, 0.0)
+    return label
 
 
 def own_kernel(
-    got_hbm,
-    label_hbm,
+    got_ref,
     lift_hbm,
     first_w_hbm,
     second_w_hbm,
-    third_w_hbm,
-    fourth_w_hbm,
     even_ref,
     odd_ref,
     labels_ref,
     lift_all_ref,
     first_all_ref,
     second_w_ref,
-    third_w_ref,
-    fourth_w_ref,
-    got_ref,
-    label_ref,
     lift_ref,
     first_w_ref,
     bits_ref,
     sems,
 ):
     pairs = (
-        (got_hbm, got_ref),
         (lift_hbm, lift_ref),
-        (label_hbm, label_ref),
         (first_w_hbm, first_w_ref),
         (second_w_hbm, second_w_ref),
-        (third_w_hbm, third_w_ref),
-        (fourth_w_hbm, fourth_w_ref),
     )
     copies = [
         pltpu.make_async_copy(source, target, sems.at[k])
@@ -189,7 +186,7 @@
     bits_ref[...] = jnp.zeros(bits_ref.shape, jnp.bfloat16)
     first_all_ref[...] = jnp.zeros(first_all_ref.shape, jnp.bfloat16)
     order = column_order(cols)
-    copies[1].wait()
+    copies[0].wait()
     tall = jnp.concatenate(
         [lift_ref[...].astype(jnp.float32), jnp.zeros((16 - heights, width), jnp.float32)], axis=0
     )
@@ -200,29 +197,32 @@
     frame_of_lane = jnp.minimum(lane // width, frames - 1)
     keep = (frame_of_row == frame_of_lane) & (lane < 128 + 3 * rest)
     lift_all_ref[...] = jnp.where(keep, tall, 0.0).astype(jnp.bfloat16)
-    copies[0].wait()
-    band_cells(got_ref, 0, None, order, lift_all_ref, bits_ref, even_ref, odd_ref, rest)
-    copies[2].wait()
-    labels_ref[...] = band_label(label_ref, 0, me, labels_ref.shape).astype(jnp.bfloat16)
-    copies[3].wait()
+    labels_ref[...] = band_cells(
+        got_ref, 0, None, me, order, lift_all_ref, bits_ref, even_ref, odd_ref, rest
+    )
+    copies[1].wait()
     for tap in range(9):
         row_tap, col_tap = divmod(tap, 3)
         first_all_ref[row_tap, pl.ds(col_tap * 128, 128)] = first_w_ref[tap, pl.ds(0, 128)]
         first_all_ref[row_tap, pl.ds(384 + col_tap * rest, rest)] = first_w_ref[
             tap, pl.ds(128, rest)
         ]
-    for copy in copies[4:]:
-        copy.wait()
+    copies[2].wait()
 
 
 def early_kernel(pieces, rest, *refs):
     got_refs = refs[:pieces]
     (
+        labels_ref,
         lift_all_ref,
         first_all_ref,
         second_w_ref,
         own_even_ref,
         own_odd_ref,
+        third_w_hbm,
+        fourth_w_hbm,
+        third_w_ref,
+        fourth_w_ref,
         even_ref,
         odd_ref,
         send_ref,
@@ -230,7 +230,14 @@
         first_slope_ref,
         second_slope_ref,
         bits_ref,
+        sems,
     ) = refs[pieces:]
+    copies = [
+        pltpu.make_async_copy(third_w_hbm, third_w_ref, sems.at[0]),
+        pltpu.make_async_copy(fourth_w_hbm, fourth_w_ref, sems.at[1]),
+    ]
+    for copy in copies:
+        copy.start()
     me = lax.axis_index("space")
     bands = 1 << pieces
     _, _, band, cols = got_refs[0].shape
@@ -242,12 +249,14 @@
     odd_ref[pl.ds(pl.multiple_of(at + row_cells, row_cells), cells)] = own_odd_ref[...]
     odd_ref[pl.ds(0, row_cells)] = jnp.zeros((row_cells, odd_ref.shape[1]), jnp.bfloat16)
     bits_ref[...] = jnp.zeros(bits_ref.shape, jnp.bfloat16)
+    labels = labels_ref[...]
     for slot in range(1, bands):
         piece = slot.bit_length() - 1
         inner = slot - (1 << piece)
-        band_cells(
+        labels += band_cells(
             got_refs[piece],
             inner,
+            me ^ slot,
             me ^ slot,
             order,
             lift_all_ref,
@@ -278,7 +287,9 @@
     second_slope_ref[...] = slope.reshape(second_slope_ref.shape)
     sent = value.shape[0]
     send_ref[pl.ds(0, sent)] = value.astype(jnp.bfloat16)
-    send_ref[pl.ds(sent, 16)] = jnp.zeros((16, send_ref.shape[1]), jnp.bfloat16)
+    send_ref[pl.ds(sent, 16)] = labels.astype(jnp.bfloat16)
+    for copy in copies:
+        copy.wait()
 
 
 def transpose_kernel(weight_ref, out_ref):
@@ -378,7 +389,7 @@
     head = head_ref[...].astype(jnp.float32)
     labels = label_ref[...].reshape(-1, label_ref.shape[-1])[:, :1]
     logits = jnp.sum(value * head, axis=1, keepdims=True)
-    logit_grad = (jax.nn.sigmoid(logits) - labels) / batch
+    logit_grad = (sigmoid(logits) - labels) / batch
     delta = rounded(logit_grad * head * slope)
     last_row_zero(fourth_delta_ref)
     fill_delta(fourth_delta_ref, delta.reshape(samples, rows, phases, BLOCK, delta.shape[-1]))
@@ -666,7 +677,12 @@
     def grant(size):
         return pltpu.CompilerParams(vmem_limit_bytes=(size if small else 60) * MIB)
 
-    lines = band_pieces(occupancy, bands)
+    marks = lax.pad(
+        state_labels[:, :, None, :],
+        jnp.zeros((), jnp.int32),
+        ((0, 0, 0), (0, frames - 1, 0), (0, band - 1, 0), (0, cols - BLOCK, 0)),
+    )
+    lines = band_pieces(occupancy + (marks << LABEL_BIT), bands)
     first_w = temporal_weight.reshape(9, lift_all, one)
     second_w = middle_weight.reshape(9, one, two)
     third_w = deeper_weight.reshape(9, two, three)
@@ -682,13 +698,9 @@
     own_args = [
         pltpu.with_memory_space_constraint(value, pltpu.HBM)
         for value in (
-            occupancy,
-            state_labels,
             lift_weight,
             first_w,
             second_w,
-            third_w,
-            fourth_w,
         )
     ]
     (
@@ -698,38 +710,34 @@
         lift_all_w,
         first_all,
         second_w2,
-        third_w2,
-        fourth_w2,
     ) = pl.pallas_call(
         own_kernel,
         out_shape=(
             own_cells,
             own_cells,
-            shaped((16, two), bf16),
+            shaped((16, two), f32),
             shaped((128, 256), bf16),
             shaped((3, 512, one), bf16),
             shaped(second_w.shape, bf16),
-            shaped(third_w.shape, bf16),
-            shaped(fourth_w.shape, bf16),
         ),
-        in_specs=[hbm] * 7,
-        out_specs=(vmem,) * 8,
+        in_specs=[vmem] + [hbm] * 3,
+        out_specs=(vmem,) * 6,
         scratch_shapes=[
-            pltpu.VMEM(occupancy.shape, occupancy.dtype),
-            pltpu.VMEM(state_labels.shape, state_labels.dtype),
             pltpu.VMEM(lift_weight.shape, bf16),
             pltpu.VMEM(first_w.shape, bf16),
             bits_scratch,
-            pltpu.SemaphoreType.DMA((7,)),
+            pltpu.SemaphoreType.DMA((3,)),
         ],
         compiler_params=grant(24),
         cost_estimate=cost(100_000_000, 10_000_000),
         name="own_band",
-    )(*own_args)
+    )(lines[0], *own_args)
     pieces = len(lines) - 1
-    even, odd, payload, first, first_slope, second_slope = pl.pallas_call(
+    third_w2, fourth_w2, even, odd, payload, first, first_slope, second_slope = pl.pallas_call(
         functools.partial(early_kernel, pieces, lift_all - 128),
         out_shape=(
+            shaped(third_w.shape, bf16),
+            shaped(fourth_w.shape, bf16),
             even_shape,
             odd_shape,
             shaped((sent, two), bf16),
@@ -737,19 +745,25 @@
             shaped((1, rows // 2, phases // 2, BLOCK, one), f32),
             shaped((1, rows // 4, phases // 4, BLOCK, two), f32),
         ),
-        in_specs=[vmem] * (pieces + 5),
-        out_specs=(vmem,) * 6,
-        scratch_shapes=[bits_scratch],
+        in_specs=[vmem] * (pieces + 6) + [hbm] * 2,
+        out_specs=(vmem,) * 8,
+        scratch_shapes=[bits_scratch, pltpu.SemaphoreType.DMA((2,))],
         compiler_params=grant(24),
         cost_estimate=cost(150_000_000, 4_000_000),
         name="early",
-    )(*lines[1:], lift_all_w, first_all, second_w2, own_even, own_odd)
-
-    labels, bit = own_labels, 1
-    while bit < bands:
-        labels = labels + swapped(labels, "space", bit)
-        bit *= 2
-    payload = put(payload, labels, sent - 16)[None]
+    )(
+        *lines[1:],
+        own_labels,
+        lift_all_w,
+        first_all,
+        second_w2,
+        own_even,
+        own_odd,
+        pltpu.with_memory_space_constraint(third_w, pltpu.HBM),
+        pltpu.with_memory_space_constraint(fourth_w, pltpu.HBM),
+    )
+
+    payload = payload[None]
     deep_weights = (third_w2, fourth_w2)
 
     third_cells = 2 * bands * 2 * BLOCK

time: 44.5 us -> 46.5 us (1.045)
  Pallas kernels: 19.2 us -> 20.6 us
  waiting for transfers between devices: 7.62 us -> 6.5 us
  other arithmetic: 0.13 us -> 0.9 us
  local copies, waits for them, and re-layouts: 0.2 us -> 0.87 us
    pallas_call x1, Pallas kernels: 2.73 us -> 4.41 us  [local(): pl.pallas_call(functools.partial(early_kernel, pieces, lift_all - 128), o...]
    ppermute x15 -> x14, waiting for transfers between devices: 7.62 us -> 6.5 us  [swapped(): lax.ppermute(value, axis, [(i, i ^ bit) for i in range(lax.axis_size(axis...]
    add x0 -> x1, other arithmetic: none -> 0.79 us  [local(): lines = band_pieces(occupancy + (marks << LABEL_BIT), bands)]
    pallas_call x1, Pallas kernels: 2.15 us -> 1.47 us  [local(): pl.pallas_call(own_kernel, out_shape=(own_cells, own_cells, shaped((16, t...]
    reshape x1, local copies, waits for them, and re-layouts: 0.01 us -> 0.68 us  [local(): head = head_weight.reshape(1, four)]
    ppermute x15 -> x14, starting transfers between devices: 16.3 us -> 16.6 us  [swapped(): lax.ppermute(value, axis, [(i, i ^ bit) for i in range(lax.axis_size(axis...]
  transfers between devices with their start and end apart: 15 -> 14, of which waited for: 6 -> 5; matrix products, arithmetic and copies ran while one was open for 1% -> 2% of each run, Pallas kernels for 41% -> 32%
where the time goes in v8:
time: 46.5 us; the launch traced here: 46.2 us
  Pallas kernels  20.6 us (44%)
  starting transfers between devices  16.6 us (36%)
  waiting for transfers between devices  6.5 us (14%)
  other arithmetic  0.9 us (2%)
  local copies, waits for them, and re-layouts  0.87 us (2%)
  between operations  0.79 us (2%)
    ppermute x14, starting transfers between devices, swapped(): lax.ppermute(value, axis, [(i, i ^ bit) for i in range(lax.axis_size(axis...  16.6 us
    ppermute x14, waiting for transfers between devices, swapped(): lax.ppermute(value, axis, [(i, i ^ bit) for i in range(lax.axis_size(axis...  6.5 us
    pallas_call x1, Pallas kernels, local(): pl.pallas_call(functools.partial(deep_kernel, samples, bands, small), **{...  4.74 us
    pallas_call x1, Pallas kernels, local(): pl.pallas_call(functools.partial(early_kernel, pieces, lift_all - 128), o...  4.41 us
    pallas_call x1, Pallas kernels, local(): local_call(payload, *deep_weights, *maps)  3.63 us
    pallas_call x1, Pallas kernels, local(): pl.pallas_call(fourth_grad_alone_kernel, out_shape=shaped((9, three, four...  2.5 us
    pallas_call x1, Pallas kernels, local(): pl.pallas_call(third_grad_kernel, out_shape=grad_shape, in_specs=[vmem] *...  1.96 us
    pallas_call x1, Pallas kernels, local(): pl.pallas_call(own_kernel, out_shape=(own_cells, own_cells, shaped((16, t...  1.47 us
  transfers between devices with their start and end apart: 14, of which 5 were waited for; matrix products, arithmetic and copies ran while one was open for 2% of the time, Pallas kernels for 32%

profile of v8, /device:TPU:0, one launch (start us, length us, event | category | flops | bytes accessed | tf_op | source)
XLA Modules:
  0.0 46.2 jit_solution(2088687684233041183)
XLA Ops:
  0.6 0.8 %shift-left_add_fusion.got_ref = s32[1,5,16,128]{3,2,1,0:T(8,128)S(1)} fusion(s32[1,5,16,128]{3,2,1,0:T(8,128)} %param.8, s32[1,1,1,8]{3,2,1,0:T(1,128)} %bitcast.27), kind=kLoop, calls=%fused_computation.8 | loop fusion | flops 20480 | bytes 81952 | tf_op jit(solution)/shard_map/add | solution.py:685
  1.4 2.9 %collective-permute-start = (s32[1,5,16,128]{3,2,1,0:T(8,128)S(1)}, s32[1,5,16,128]{3,2,1,0:T(8,128)S(1)}, u32[]{:S(2)}, u32[]{:S(2)}) collective-permute-start(s32[1,5,16,128]{3,2,1,0:T(8,128)S(1)} %shift-left_add_fusion.got_ref), channel_id=1, source_target_pairs={{0,1},{1,0},{2,3},{3,2},{4,5},{5,4},{6,7},{7,6},{8,9},{9,8},{10,11... | collective-permute-start | bytes 122888 | tf_op jit(solution)/shard_map/ppermute | solution.py:593
  4.4 0.7 %reshape.54.head_ref = bf16[1,512]{1,0:T(2,128)(2,1)S(1)} reshape(bf16[512]{0:T(512)(128)(2,1)} %param.15) | data formatting | bytes 2048 | tf_op jit(solution)/shard_map/reshape | solution.py:690
  5.0 1.5 %own_band.1 = (bf16[512,512]{1,0:T(8,128)(2,1)S(1)}, bf16[512,512]{1,0:T(8,128)(2,1)S(1)}, f32[16,128]{1,0:T(8,128)S(1)}, bf16[128,256]{1,0:T(8,128)(2,1)S(1)}, ...) custom-call(s32[1,5,16,128]{3,2,1,0:T(8,128)S(1)} %shift-left_add_fusion.got_ref, ...), custom_call_target="tpu_custom_call" | custom-call | flops 100000000 | bytes 10000000 | tf_op jit(solution)/shard_map/own_band/pallas_call | solution.py:713
  6.5 0.0 collective-permute-done.refs_0_
  6.5 4.4 %early.1 = (bf16[9,128,256]{2,1,0:T(8,128)(2,1)S(1)}, bf16[9,256,512]{2,1,0:T(8,128)(2,1)S(1)}, bf16[1024,512]{1,0:T(8,128)(2,1)S(1)}, bf16[1088,512]{1,0:T(8,12...) custom-call(s32[1,5,16,128]{3,2,1,0:T(8,128)S(1)} %collective-permut, ...), custom_call_target="tpu_custom_call" | custom-call | flops 150000000 | bytes 4000000 | tf_op jit(solution)/shard_map/early/pallas_call | solution.py:736
  10.9 3.0 %collective-permute-start.5 = (bf16[1,272,128]{2,1,0:T(8,128)(2,1)S(1)}, bf16[1,272,128]{2,1,0:T(8,128)(2,1)S(1)}, u32[]{:S(2)}, u32[]{:S(2)}) collective-permute-start(bf16[1,272,128]{2,1,0:T(8,128)(2,1)S(1)} %bitcast.18), channel_id=1, source_target_pairs={{0,16},{2,18},{4,20},{6,22},{8,24},{10,26},{12,28},{14,30},{16,0},... | collective-permute-start | bytes 208904 | tf_op jit(solution)/shard_map/ppermute | solution.py:593
  13.9 3.6 %local.1 = (bf16[2,336,128]{2,1,0:T(8,128)(2,1)S(1)}, bf16[2,336,128]{2,1,0:T(8,128)(2,1)S(1)}) custom-call(bf16[1,272,128]{2,1,0:T(8,128)(2,1)S(1)} %bitcast.19, bf16[9,128,256]{2,1,0:T(8,128)(2,1)S(1)} %get-tuple-element.49.third_w_ref, bf16[9,256,512]{2,1,0:T(8,128)(2,1)S(1)} %get-tuple-element.58.fourth_w_ref.weight_ref, ...), custom_call_target="tpu_custom_call" | custom-call | flops 300000000 | bytes 9000000 | tf_op jit(solution)/shard_map/local/pallas_call | solution.py:820
  17.6 0.1 collective-permute-start.1
  17.7 0.1 dynamic_update_slice.15
  17.7 0.0 collective-permute-done.5
  17.8 1.6 %collective-permute-start.7 = (bf16[2,272,128]{2,1,0:T(8,128)(2,1)S(1)}, bf16[2,272,128]{2,1,0:T(8,128)(2,1)S(1)}, u32[]{:S(2)}, u32[]{:S(2)}) collective-permute-start(bf16[2,272,128]{2,1,0:T(8,128)(2,1)S(1)} %slice.28), channel_id=1, source_target_pairs={{0,8},{2,10},{4,12},{6,14},{8,0},{10,2},{12,4},{14,6},{16,24},{18,... | collective-permute-start | bytes 417800 | tf_op jit(solution)/shard_map/ppermute | solution.py:593
  19.4 0.0 collective-permute-done.1
  19.5 1.6 %collective-permute-start.2 = (bf16[336,128]{1,0:T(8,128)(2,1)S(1)}, bf16[336,128]{1,0:T(8,128)(2,1)S(1)}, u32[]{:S(2)}, u32[]{:S(2)}) collective-permute-start(bf16[336,128]{1,0:T(8,128)(2,1)S(1)} %fusion.2), channel_id=1, source_target_pairs={{0,4},{2,6},{4,0},{6,2},{8,12},{10,14},{12,8},{14,10},{16,20},{18,... | collective-permute-start | bytes 258056 | tf_op jit(solution)/shard_map/ppermute | solution.py:593
  21.0 0.5 %collective-permute-start.6 = (bf16[2,272,128]{2,1,0:T(8,128)(2,1)S(1)}, bf16[2,272,128]{2,1,0:T(8,128)(2,1)S(1)}, u32[]{:S(2)}, u32[]{:S(2)}) collective-permute-start(bf16[2,272,128]{2,1,0:T(8,128)(2,1)S(1)} %slice.28), channel_id=1, source_target_pairs={{0,4},{2,6},{4,0},{6,2},{8,12},{10,14},{12,8},{14,10},{16,20},{18,... | collective-permute-start | bytes 417800 | tf_op jit(solution)/shard_map/ppermute | solution.py:593
  21.6 0.7 %transpose.1.fourth_wt_ref = bf16[9,512,256]{2,1,0:T(8,128)(2,1)S(1)} custom-call(bf16[9,256,512]{2,1,0:T(8,128)(2,1)S(1)} %get-tuple-element.58.fourth_w_ref.weight_ref), custom_call_target="tpu_custom_call" | custom-call | flops 10000000 | bytes 5000000 | tf_op jit(solution)/shard_map/transpose/pallas_call | solution.py:821
  22.2 1.7 %collective-permute-done.7 = bf16[2,272,128]{2,1,0:T(8,128)(2,1)S(1)} collective-permute-done((bf16[2,272,128]{2,1,0:T(8,128)(2,1)S(1)}, bf16[2,272,128]{2,1,0:T(8,128)(2,1)S(1)}, u32[]{:S(2)}, u32[]{:S(2)}) %collective-permute-start.7) | collective-permute-done | bytes 139296 | tf_op jit(solution)/shard_map/ppermute | solution.py:593
  23.9 1.5 %collective-permute-start.8 = (bf16[2,272,128]{2,1,0:T(8,128)(2,1)S(1)}, bf16[2,272,128]{2,1,0:T(8,128)(2,1)S(1)}, u32[]{:S(2)}, u32[]{:S(2)}) collective-permute-start(bf16[2,272,128]{2,1,0:T(8,128)(2,1)S(1)} %collective-permute-done.7), channel_id=1, source_target_pairs={{0,4},{2,6},{4,0},{6,2},{8,12},{10,14},{12,8},{14,10},{16,20},{18,... | collective-permute-start | bytes 417800 | tf_op jit(solution)/shard_map/ppermute | solution.py:593
  25.4 0.0 collective-permute-done.2
  25.5 1.6 %collective-permute-start.3 = (bf16[336,128]{1,0:T(8,128)(2,1)S(1)}, bf16[336,128]{1,0:T(8,128)(2,1)S(1)}, u32[]{:S(2)}, u32[]{:S(2)}) collective-permute-start(bf16[336,128]{1,0:T(8,128)(2,1)S(1)} %fusion), channel_id=1, source_target_pairs={{0,8},{2,10},{4,12},{6,14},{8,0},{10,2},{12,4},{14,6},{16,24},{18,... | collective-permute-start | bytes 258056 | tf_op jit(solution)/shard_map/ppermute | solution.py:593
  27.1 0.6 %collective-permute-done.6 = bf16[2,272,128]{2,1,0:T(8,128)(2,1)S(1)} collective-permute-done((bf16[2,272,128]{2,1,0:T(8,128)(2,1)S(1)}, bf16[2,272,128]{2,1,0:T(8,128)(2,1)S(1)}, u32[]{:S(2)}, u32[]{:S(2)}) %collective-permute-start.6) | collective-permute-done | bytes 139296 | tf_op jit(solution)/shard_map/ppermute | solution.py:593
  27.8 0.1 collective-permute-start.9
  27.9 2.2 %collective-permute-done.8 = bf16[2,272,128]{2,1,0:T(8,128)(2,1)S(1)} collective-permute-done((bf16[2,272,128]{2,1,0:T(8,128)(2,1)S(1)}, bf16[2,272,128]{2,1,0:T(8,128)(2,1)S(1)}, u32[]{:S(2)}, u32[]{:S(2)}) %collective-permute-start.8) | collective-permute-done | bytes 139296 | tf_op jit(solution)/shard_map/ppermute | solution.py:593
  30.1 0.0 collective-permute-start.10
  30.1 0.0 collective-permute-done.3
  30.2 1.5 %collective-permute-start.4 = (bf16[336,128]{1,0:T(8,128)(2,1)S(1)}, bf16[336,128]{1,0:T(8,128)(2,1)S(1)}, u32[]{:S(2)}, u32[]{:S(2)}) collective-permute-start(bf16[336,128]{1,0:T(8,128)(2,1)S(1)} %add_convert_fusion.1), channel_id=1, source_target_pairs={{0,16},{2,18},{4,20},{6,22},{8,24},{10,26},{12,28},{14,30},{16,0},... | collective-permute-start | bytes 258056 | tf_op jit(solution)/shard_map/ppermute | solution.py:593
  31.7 0.0 collective-permute-done.10.last_ref
  31.7 0.0 collective-permute-done.9.far_ref
  31.7 4.7 %deep.1 = (bf16[256,2304]{1,0:T(8,128)(2,1)S(1)}, bf16[256,512]{1,0:T(8,128)(2,1)S(1)}, f32[1,512]{1,0:T(1,128)}, bf16[1024,1152]{1,0:T(8,128)(2,1)S(1)}, bf16[1024,256]{1,0:T(8,128)(2,1)S(1)}) custom-call(bf16[8,272,128]{2,1,0:T(8,128)(2,1)S(1)} %constant_dynamic-update-slice_fusion.near_ref, bf16[6,272,128]{2,1,0:T(8,128)(2,1)S(1)} %collective-permute-done.9.far_ref, ...), custom_call_target="tpu_custom_call" | custom-call | flops 1300000000 | bytes 12000000 | tf_op jit(solution)/shard_map/deep/pallas_call | solution.py:836
  36.5 1.5 %collective-permute-done.4 = bf16[336,128]{1,0:T(8,128)(2,1)S(1)} collective-permute-done((bf16[336,128]{1,0:T(8,128)(2,1)S(1)}, bf16[336,128]{1,0:T(8,128)(2,1)S(1)}, u32[]{:S(2)}, u32[]{:S(2)}) %collective-permute-start.4) | collective-permute-done | bytes 86048 | tf_op jit(solution)/shard_map/ppermute | solution.py:593
  38.0 1.6 %collective-permute-start.12 = (bf16[336,128]{1,0:T(8,128)(2,1)S(1)}, bf16[336,128]{1,0:T(8,128)(2,1)S(1)}, u32[]{:S(2)}, u32[]{:S(2)}) collective-permute-start(bf16[336,128]{1,0:T(8,128)(2,1)S(1)} %add_convert_fusion.refs_0_), channel_id=1, source_target_pairs={{0,4},{2,6},{4,0},{6,2},{8,12},{10,14},{12,8},{14,10},{16,20},{18,... | collective-permute-start | bytes 258056 | tf_op jit(solution)/shard_map/ppermute | solution.py:593
  39.5 2.5 %fourth_grad.1 = f32[9,256,512]{2,1,0:T(8,128)} custom-call(bf16[256,2304]{1,0:T(8,128)(2,1)S(1)} %get-tuple-element.68.fourth_taps_ref, bf16[256,512]{1,0:T(8,128)(2,1)S(1)} %get-tuple-element.69.fourth_flat_ref), custom_call_target="tpu_custom_call" | custom-call | flops 600000000 | bytes 6000000 | tf_op jit(solution)/shard_map/fourth_grad/pallas_call | solution.py:867
  42.1 0.5 collective-permute-done.12.refs_2_
  42.5 0.0 collective-permute-start.13
  42.5 0.5 %collective-permute-start.11 = (bf16[336,128]{1,0:T(8,128)(2,1)S(1)}, bf16[336,128]{1,0:T(8,128)(2,1)S(1)}, u32[]{:S(2)}, u32[]{:S(2)}) collective-permute-start(bf16[336,128]{1,0:T(8,128)(2,1)S(1)} %add_convert_fusion.refs_0_), channel_id=1, source_target_pairs={{0,2},{2,0},{4,6},{6,4},{8,10},{10,8},{12,14},{14,12},{16,18},{18,... | collective-permute-start | bytes 258056 | tf_op jit(solution)/shard_map/ppermute | solution.py:593
  43.0 2.0 %third_grad.1 = f32[1152,256]{1,0:T(8,128)} custom-call(bf16[1024,1152]{1,0:T(8,128)(2,1)S(1)} %get-tuple-element.71.taps_ref, bf16[1024,256]{1,0:T(8,128)(2,1)S(1)} %get-tuple-element.72.delta_ref), custom_call_target="tpu_custom_call" | custom-call | flops 600000000 | bytes 4000000 | tf_op jit(solution)/shard_map/third_grad/pallas_call | solution.py:897
  45.0 0.0 collective-permute-done.13.refs_3_
  45.0 0.0 collective-permute-done.11.refs_1_
  45.0 1.2 %finish.1 = (f32[9,160,64]{2,1,0:T(8,128)}, f32[576,128]{1,0:T(8,128)}) custom-call(bf16[336,128]{1,0:T(8,128)(2,1)S(1)} %add_convert_fusion.refs_0_, bf16[336,128]{1,0:T(8,128)(2,1)S(1)} %collective-permute-done.11.refs_1_, bf16[336,128]{1,0:T(8,128)(2,1)S(1)} %collective-permute-done.12.refs_2_, bf16[336,128]{1,0:T(8,128)(2,1)S(1)} %collective-permute-done.13.refs_3_), custom_call_target="tpu_custom_call" | custom-call | flops 1000000 | bytes 1500000 | tf_op jit(solution)/shard_map/finish/pallas_call | solution.py:909
  (10 shorter events, 0.2 us)
Async XLA Ops:
  1.4 5.1 %collective-permute-start = (s32[1,5,16,128]{3,2,1,0:T(8,128)S(1)}, s32[1,5,16,128]{3,2,1,0:T(8,128)S(1)}, u32[]{:S(2)}, u32[]{:S(2)}) collective-permute-start(s32[1,5,16,128]{3,2,1,0:T(8,128)S(1)} %shift-left_add_fusion.got_ref), channel_id=1, source_target_pairs={{0,1},{1,0},{2,3},{3,2},{4,5},{5,4},{6,7},{7,6},{8,9},{9,8},{10,11... | collective-permute-start | bytes 122888 | tf_op jit(solution)/shard_map/ppermute | solution.py:593
  10.9 6.8 %collective-permute-start.5 = (bf16[1,272,128]{2,1,0:T(8,128)(2,1)S(1)}, bf16[1,272,128]{2,1,0:T(8,128)(2,1)S(1)}, u32[]{:S(2)}, u32[]{:S(2)}) collective-permute-start(bf16[1,272,128]{2,1,0:T(8,128)(2,1)S(1)} %bitcast.18), channel_id=1, source_target_pairs={{0,16},{2,18},{4,20},{6,22},{8,24},{10,26},{12,28},{14,30},{16,0},... | collective-permute-start | bytes 208904 | tf_op jit(solution)/shard_map/ppermute | solution.py:593
  17.6 1.9 %collective-permute-start.1 = (bf16[2,336,128]{2,1,0:T(8,128)(2,1)S(1)}, bf16[2,336,128]{2,1,0:T(8,128)(2,1)S(1)}, u32[]{:S(2)}, u32[]{:S(2)}) collective-permute-start(bf16[2,336,128]{2,1,0:T(8,128)(2,1)S(1)} %get-tuple-element.57), channel_id=1, source_target_pairs={{0,2},{2,0},{4,6},{6,4},{8,10},{10,8},{12,14},{14,12},{16,18},{18,... | collective-permute-start | bytes 516104 | tf_op jit(solution)/shard_map/ppermute | solution.py:593
  17.8 6.1 %collective-permute-start.7 = (bf16[2,272,128]{2,1,0:T(8,128)(2,1)S(1)}, bf16[2,272,128]{2,1,0:T(8,128)(2,1)S(1)}, u32[]{:S(2)}, u32[]{:S(2)}) collective-permute-start(bf16[2,272,128]{2,1,0:T(8,128)(2,1)S(1)} %slice.28), channel_id=1, source_target_pairs={{0,8},{2,10},{4,12},{6,14},{8,0},{10,2},{12,4},{14,6},{16,24},{18,... | collective-permute-start | bytes 417800 | tf_op jit(solution)/shard_map/ppermute | solution.py:593
  19.5 6.0 %collective-permute-start.2 = (bf16[336,128]{1,0:T(8,128)(2,1)S(1)}, bf16[336,128]{1,0:T(8,128)(2,1)S(1)}, u32[]{:S(2)}, u32[]{:S(2)}) collective-permute-start(bf16[336,128]{1,0:T(8,128)(2,1)S(1)} %fusion.2), channel_id=1, source_target_pairs={{0,4},{2,6},{4,0},{6,2},{8,12},{10,14},{12,8},{14,10},{16,20},{18,... | collective-permute-start | bytes 258056 | tf_op jit(solution)/shard_map/ppermute | solution.py:593
  21.0 6.7 %collective-permute-start.6 = (bf16[2,272,128]{2,1,0:T(8,128)(2,1)S(1)}, bf16[2,272,128]{2,1,0:T(8,128)(2,1)S(1)}, u32[]{:S(2)}, u32[]{:S(2)}) collective-permute-start(bf16[2,272,128]{2,1,0:T(8,128)(2,1)S(1)} %slice.28), channel_id=1, source_target_pairs={{0,4},{2,6},{4,0},{6,2},{8,12},{10,14},{12,8},{14,10},{16,20},{18,... | collective-permute-start | bytes 417800 | tf_op jit(solution)/shard_map/ppermute | solution.py:593
  23.9 6.2 %collective-permute-start.8 = (bf16[2,272,128]{2,1,0:T(8,128)(2,1)S(1)}, bf16[2,272,128]{2,1,0:T(8,128)(2,1)S(1)}, u32[]{:S(2)}, u32[]{:S(2)}) collective-permute-start(bf16[2,272,128]{2,1,0:T(8,128)(2,1)S(1)} %collective-permute-done.7), channel_id=1, source_target_pairs={{0,4},{2,6},{4,0},{6,2},{8,12},{10,14},{12,8},{14,10},{16,20},{18,... | collective-permute-start | bytes 417800 | tf_op jit(solution)/shard_map/ppermute | solution.py:593
  25.5 4.7 %collective-permute-start.3 = (bf16[336,128]{1,0:T(8,128)(2,1)S(1)}, bf16[336,128]{1,0:T(8,128)(2,1)S(1)}, u32[]{:S(2)}, u32[]{:S(2)}) collective-permute-start(bf16[336,128]{1,0:T(8,128)(2,1)S(1)} %fusion), channel_id=1, source_target_pairs={{0,8},{2,10},{4,12},{6,14},{8,0},{10,2},{12,4},{14,6},{16,24},{18,... | collective-permute-start | bytes 258056 | tf_op jit(solution)/shard_map/ppermute | solution.py:593
  27.8 3.9 %collective-permute-start.9 = (bf16[6,272,128]{2,1,0:T(8,128)(2,1)S(1)}, bf16[6,272,128]{2,1,0:T(8,128)(2,1)S(1)}, u32[]{:S(2)}, u32[]{:S(2)}) collective-permute-start(bf16[6,272,128]{2,1,0:T(8,128)(2,1)S(1)} %slice.29), channel_id=1, source_target_pairs={{0,2},{2,0},{4,6},{6,4},{8,10},{10,8},{12,14},{14,12},{16,18},{18,... | collective-permute-start | bytes 1253384 | tf_op jit(solution)/shard_map/ppermute | solution.py:593
  30.1 1.6 %collective-permute-start.10 = (bf16[2,272,128]{2,1,0:T(8,128)(2,1)S(1)}, bf16[2,272,128]{2,1,0:T(8,128)(2,1)S(1)}, u32[]{:S(2)}, u32[]{:S(2)}) collective-permute-start(bf16[2,272,128]{2,1,0:T(8,128)(2,1)S(1)} %collective-permute-done.8), channel_id=1, source_target_pairs={{0,2},{2,0},{4,6},{6,4},{8,10},{10,8},{12,14},{14,12},{16,18},{18,... | collective-permute-start | bytes 417800 | tf_op jit(solution)/shard_map/ppermute | solution.py:593
  30.2 7.8 %collective-permute-start.4 = (bf16[336,128]{1,0:T(8,128)(2,1)S(1)}, bf16[336,128]{1,0:T(8,128)(2,1)S(1)}, u32[]{:S(2)}, u32[]{:S(2)}) collective-permute-start(bf16[336,128]{1,0:T(8,128)(2,1)S(1)} %add_convert_fusion.1), channel_id=1, source_target_pairs={{0,16},{2,18},{4,20},{6,22},{8,24},{10,26},{12,28},{14,30},{16,0},... | collective-permute-start | bytes 258056 | tf_op jit(solution)/shard_map/ppermute | solution.py:593
  38.0 4.6 %collective-permute-start.12 = (bf16[336,128]{1,0:T(8,128)(2,1)S(1)}, bf16[336,128]{1,0:T(8,128)(2,1)S(1)}, u32[]{:S(2)}, u32[]{:S(2)}) collective-permute-start(bf16[336,128]{1,0:T(8,128)(2,1)S(1)} %add_convert_fusion.refs_0_), channel_id=1, source_target_pairs={{0,4},{2,6},{4,0},{6,2},{8,12},{10,14},{12,8},{14,10},{16,20},{18,... | collective-permute-start | bytes 258056 | tf_op jit(solution)/shard_map/ppermute | solution.py:593
  42.5 2.5 %collective-permute-start.13 = (bf16[336,128]{1,0:T(8,128)(2,1)S(1)}, bf16[336,128]{1,0:T(8,128)(2,1)S(1)}, u32[]{:S(2)}, u32[]{:S(2)}) collective-permute-start(bf16[336,128]{1,0:T(8,128)(2,1)S(1)} %collective-permute-done.12.refs_2_), channel_id=1, source_target_pairs={{0,2},{2,0},{4,6},{6,4},{8,10},{10,8},{12,14},{14,12},{16,18},{18,... | collective-permute-start | bytes 258056 | tf_op jit(solution)/shard_map/ppermute | solution.py:593
  42.5 2.5 %collective-permute-start.11 = (bf16[336,128]{1,0:T(8,128)(2,1)S(1)}, bf16[336,128]{1,0:T(8,128)(2,1)S(1)}, u32[]{:S(2)}, u32[]{:S(2)}) collective-permute-start(bf16[336,128]{1,0:T(8,128)(2,1)S(1)} %add_convert_fusion.refs_0_), channel_id=1, source_target_pairs={{0,2},{2,0},{4,6},{6,4},{8,10},{10,8},{12,14},{14,12},{16,18},{18,... | collective-permute-start | bytes 258056 | tf_op jit(solution)/shard_map/ppermute | solution.py:593

commit v9 on v7

--- a/solution.py
+++ b/solution.py
@@ -327,6 +327,13 @@
     return total.T.reshape(*lead, total.shape[0])
 
 
+def put_label(ref, inner, label_ref, place, bands):
+    cells = 4 * bands * 4 * BLOCK
+    label = ref[inner, pl.ds(cells, 16)].astype(jnp.float32)[:BLOCK]
+    for index in range(bands):
+        label_ref[place, index] = jnp.broadcast_to(label[:, index : index + 1], label.shape)
+
+
 def put_sample(ref, inner, second_ref, label_ref, place, bands):
     rows, phases = 4 * bands, 4
     cells = rows * phases * BLOCK
@@ -337,9 +344,7 @@
         1,
     )
     if label_ref is not None:
-        label = ref[inner, pl.ds(cells, 16)].astype(jnp.float32)[:BLOCK]
-        for index in range(bands):
-            label_ref[place, index] = jnp.broadcast_to(label[:, index : index + 1], label.shape)
+        put_label(ref, inner, label_ref, place, bands)
 
 
 def deep_layers(
@@ -358,17 +363,49 @@
     third_delta_ref,
     fourth_delta_ref,
 ):
-    samples = second_ref.shape[0]
+    value, slope = third_layer(second_ref, third_w_ref, third_taps_ref, bands)
+    zero_row(third_ref)
+    fill_map(third_ref, value, 1)
+    third_slope_ref[...] = slope.reshape(third_slope_ref.shape)
+    return deeper_layers(
+        batch,
+        bands,
+        fourth_w_ref,
+        fourth_parts,
+        head_ref,
+        fourth_taps_ref,
+        label_ref,
+        third_ref,
+        third_slope_ref,
+        third_delta_ref,
+        fourth_delta_ref,
+    )
+
+
+def third_layer(second_ref, third_w_ref, third_taps_ref, bands):
     rows, phases = 2 * bands, 2
     third_taps(second_ref, third_taps_ref, rows, phases)
     weight = third_w_ref[...].reshape(third_taps_ref.shape[1], -1)
     value, slope = silu_and_slope(dot_nn(third_taps_ref[...], weight))
-    channels = value.shape[-1]
-    zero_row(third_ref)
-    fill_map(third_ref, value.reshape(samples, rows, phases, BLOCK, channels), 1)
-    third_slope_ref[...] = slope.reshape(third_slope_ref.shape)
-
-    rows, phases = rows // 2, phases // 2
+    shape = (second_ref.shape[0], rows, phases, BLOCK, value.shape[-1])
+    return value.reshape(shape), slope.reshape(shape)
+
+
+def deeper_layers(
+    batch,
+    bands,
+    fourth_w_ref,
+    fourth_parts,
+    head_ref,
+    fourth_taps_ref,
+    label_ref,
+    third_ref,
+    third_slope_ref,
+    third_delta_ref,
+    fourth_delta_ref,
+):
+    samples, channels = third_ref.shape[0], third_ref.shape[-1]
+    rows, phases = bands, 1
     for tap in range(9):
         fourth_taps_ref[:, pl.ds(tap * channels, channels)] = map_tap(
             third_ref, tap // 3, tap % 3, rows, phases
@@ -391,10 +428,93 @@
     return value, logit_grad, delta
 
 
+def near_kernel(bands, near_ref, third_w_ref, taps_ref, map_ref, slope_ref, second_ref):
+    zero_row(second_ref)
+    for slot in range(near_ref.shape[0]):
+        put_sample(near_ref, slot, second_ref, None, slot, bands)
+    value, slope = third_layer(second_ref, third_w_ref, taps_ref, bands)
+    map_ref[...] = value
+    slope_ref[...] = slope
+
+
+def far_kernel(
+    batch,
+    bands,
+    near_ref,
+    far_ref,
+    last_ref,
+    near_taps_ref,
+    near_map_ref,
+    near_slope_ref,
+    third_w_ref,
+    fourth_w_ref,
+    fourth_wt_ref,
+    head_ref,
+    fourth_taps_ref,
+    fourth_flat_ref,
+    head_grad_ref,
+    third_taps_ref,
+    third_flat_ref,
+    second_ref,
+    far_taps_ref,
+    label_ref,
+    third_ref,
+    third_slope_ref,
+    third_delta_ref,
+    fourth_delta_ref,
+):
+    half, early = near_ref.shape[0], far_ref.shape[0]
+    zero_row(second_ref)
+    for slot in range(half):
+        ref, inner = (far_ref, slot) if slot < early else (last_ref, slot - early)
+        put_sample(ref, inner, second_ref, None, slot, bands)
+    value, slope = third_layer(second_ref, third_w_ref, far_taps_ref, bands)
+    cells = far_taps_ref.shape[0] // half
+    width = half.bit_length()
+    me = lax.axis_index("dp")
+    zero_row(third_ref)
+    for slot in range(2 * half):
+        place = me ^ sum(((slot >> k) & 1) << (width - 1 - k) for k in range(width))
+        inner = slot % half
+        at = pl.ds(pl.multiple_of(place * cells, cells), cells)
+        one = pl.ds(place, 1)
+        if slot < half:
+            third_taps_ref[at] = near_taps_ref[pl.ds(inner * cells, cells)]
+            fill_map(third_ref.at[one], near_map_ref[pl.ds(inner, 1)], 1)
+            third_slope_ref[one] = near_slope_ref[pl.ds(inner, 1)].reshape(
+                (1,) + third_slope_ref.shape[1:]
+            )
+            put_label(near_ref, inner, label_ref, place, bands)
+        else:
+            third_taps_ref[at] = far_taps_ref[pl.ds(inner * cells, cells)]
+            fill_map(third_ref.at[one], value[inner : inner + 1], 1)
+            third_slope_ref[one] = slope[inner : inner + 1].reshape(
+                (1,) + third_slope_ref.shape[1:]
+            )
+            ref, inner = (far_ref, inner) if inner < early else (last_ref, inner - early)
+            put_label(ref, inner, label_ref, place, bands)
+    value, logit_grad, delta = deeper_layers(
+        batch,
+        bands,
+        fourth_w_ref,
+        lambda ref, *where: delta_parts(ref, fourth_wt_ref, *where),
+        head_ref,
+        fourth_taps_ref,
+        label_ref,
+        third_ref,
+        third_slope_ref,
+        third_delta_ref,
+        fourth_delta_ref,
+    )
+    head_grad_ref[...] = jnp.sum(value * logit_grad, axis=0, keepdims=True)
+    fourth_flat_ref[...] = delta.astype(jnp.bfloat16)
+    delta = third_delta_ref[...]
+    third_flat_ref[...] = delta.reshape(-1, delta.shape[-1]).astype(jnp.bfloat16)
+
+
 def deep_kernel(
     batch,
     bands,
-    stored,
     near_ref,
     far_ref,
     last_ref,
@@ -407,10 +527,7 @@
     head_grad_ref,
     *refs,
 ):
-    if stored:
-        third_taps_ref, third_flat_ref, second_ref, label_ref = refs[:4]
-    else:
-        third_grad_ref, second_ref, label_ref, third_taps_ref = refs[:4]
+    third_grad_ref, second_ref, label_ref, third_taps_ref = refs[:4]
     third_ref, third_slope_ref, third_delta_ref, fourth_delta_ref = refs[4:]
     zero_row(second_ref)
     take_samples((near_ref, far_ref, last_ref), second_ref, label_ref, bands)
@@ -432,14 +549,11 @@
     )
 
     head_grad = jnp.sum(value * logit_grad, axis=0, keepdims=True)
-    add_to(head_grad_ref, head_grad, stored)
+    add_to(head_grad_ref, head_grad)
     fourth_flat_ref[...] = delta.astype(jnp.bfloat16)
     delta = third_delta_ref[...]
     delta = delta.reshape(-1, delta.shape[-1]).astype(jnp.bfloat16)
-    if stored:
-        third_flat_ref[...] = delta
-    else:
-        third_grad_kernel(third_taps_ref, delta, third_grad_ref, False)
+    add_to(third_grad_ref, dot_tn(delta, third_taps_ref[...]).T)
 
 
 def local_kernel(
@@ -520,16 +634,13 @@
         ref[slot // 2] = flat_ref[pl.ds(at, share)].astype(jnp.bfloat16)
 
 
-def add_to(ref, value, alone):
-    if alone:
-        ref[...] = value
-    else:
-        first = pl.program_id(0) == 0
-        ref[...] = jnp.where(first, 0.0, ref[...]) + value
-
-
-def third_grad_kernel(taps_ref, delta_ref, out_ref, alone=True):
-    add_to(out_ref, dot_tn(delta_ref[...], taps_ref[...]).T, alone)
+def add_to(ref, value):
+    first = pl.program_id(0) == 0
+    ref[...] = jnp.where(first, 0.0, ref[...]) + value
+
+
+def third_grad_kernel(taps_ref, delta_ref, out_ref):
+    out_ref[...] = dot_tn(delta_ref[...], taps_ref[...]).T
 
 
 def fourth_grad_alone_kernel(fourth_taps_ref, fourth_flat_ref, out_hbm, grad_ref, sems):
@@ -620,13 +731,12 @@
             near = put(near, beside, quarter + beside_count)
             beside_count = count
     total = added(mine, after(mine_beside, weights))
-    beside = swapped(after(near[beside_count:quarter], theirs), "dp", 2)
+    beside = swapped(after(near[beside_count:quarter], total), "dp", 2)
     early = swapped(near[: quarter + beside_count], "dp", 1)
     bit = 4
     while 2 * bit < samples:
-        other = swapped(total, "dp", bit)
+        total = added(total, swapped(total, "dp", bit))
         beside = after(beside, total)
-        total = added(total, other)
         bit *= 2
     near = put(near, beside, quarter + beside_count)
     last = swapped(beside, "dp", 1)
@@ -813,36 +923,65 @@
     steps = samples // chunk
     full = lambda *shape: pl.BlockSpec(shape, lambda i: (0,) * len(shape))
     grad_shape = shaped((9 * two, three), f32)
-    third_shapes = (grad_shape,)
+    fourth_shapes = (
+        shaped((samples * fourth_cells, 9 * three), bf16),
+        shaped((samples * fourth_cells, four), bf16),
+        shaped((1, four), f32),
+    )
+    label_scratch = pltpu.VMEM((chunk, bands, BLOCK, two), f32)
+    deep_cost = cost(1_300_000_000, 12_000_000)
     if small:
-        third_shapes = (
-            shaped((samples * third_cells, 9 * two), bf16),
-            shaped((samples * third_cells, three), bf16),
+        half = samples // 2
+        half_shapes = (
+            shaped((half * third_cells, 9 * two), bf16),
+            shaped((half, 2 * bands, 2, BLOCK, three), f32),
+            shaped((half, 2 * bands, 2, BLOCK, three), f32),
         )
-    fourth_taps, fourth_flat, head_grad, *thirds = pl.pallas_call(
-        functools.partial(deep_kernel, samples, bands, small),
-        **({} if small else {"grid": (steps,)}),
-        out_shape=(
-            shaped((samples * fourth_cells, 9 * three), bf16),
-            shaped((samples * fourth_cells, four), bf16),
-            shaped((1, four), f32),
-            *third_shapes,
-        ),
-        in_specs=[vmem] * 7 if small else [
-            full(*value.shape) for value in (near, far, last, *deep_weights, fourth_wt, head)
-        ],
-        out_specs=(vmem,) * 5 if small else (
-            pl.BlockSpec((chunk * fourth_cells, 9 * three), lambda i: (i, 0)),
-            pl.BlockSpec((chunk * fourth_cells, four), lambda i: (i, 0)),
-            full(1, four),
-            full(9 * two, three),
-        ),
-        scratch_shapes=[second_scratch(chunk), pltpu.VMEM((chunk, bands, BLOCK, two), f32)]
-        + deep_scratch(chunk)[1 if small else 0 :],
-        compiler_params=grant(40),
-        cost_estimate=cost(1_300_000_000, 12_000_000),
-        name="deep",
-    )(near, far, last, *deep_weights, fourth_wt, head)
+        near_third = pl.pallas_call(
+            functools.partial(near_kernel, bands),
+            out_shape=half_shapes,
+            in_specs=[vmem] * 2,
+            out_specs=(vmem,) * 3,
+            scratch_shapes=[second_scratch(half)],
+            compiler_params=grant(24),
+            cost_estimate=cost(300_000_000, 4_000_000),
+            name="near",
+        )(near, third_w2)
+        fourth_taps, fourth_flat, head_grad, *thirds = pl.pallas_call(
+            functools.partial(far_kernel, samples, bands),
+            out_shape=fourth_shapes
+            + (
+                shaped((samples * third_cells, 9 * two), bf16),
+                shaped((samples * third_cells, three), bf16),
+            ),
+            in_specs=[vmem] * 10,
+            out_specs=(vmem,) * 5,
+            scratch_shapes=[second_scratch(half), third_taps_scratch(half), label_scratch]
+            + deep_scratch(chunk)[1:],
+            compiler_params=grant(40),
+            cost_estimate=deep_cost,
+            name="deep",
+        )(near, far, last, *near_third, *deep_weights, fourth_wt, head)
+        deeper_grad = None
+    else:
+        fourth_taps, fourth_flat, head_grad, deeper_grad = pl.pallas_call(
+            functools.partial(deep_kernel, samples, bands),
+            grid=(steps,),
+            out_shape=fourth_shapes + (grad_shape,),
+            in_specs=[
+                full(*value.shape) for value in (near, far, last, *deep_weights, fourth_wt, head)
+            ],
+            out_specs=(
+                pl.BlockSpec((chunk * fourth_cells, 9 * three), lambda i: (i, 0)),
+                pl.BlockSpec((chunk * fourth_cells, four), lambda i: (i, 0)),
+                full(1, four),
+                full(9 * two, three),
+            ),
+            scratch_shapes=[second_scratch(chunk), label_scratch] + deep_scratch(chunk),
+            compiler_params=grant(40),
+            cost_estimate=deep_cost,
+            name="deep",
+        )(near, far, last, *deep_weights, fourth_wt, head)
 
     if bit < samples:
         other, fourth_flat = lax.optimization_barrier((swapped(total, "dp", bit), fourth_flat))
@@ -889,8 +1028,6 @@
             cost_estimate=cost(600_000_000, 4_000_000),
             name="third_grad",
         )(*thirds)
-    else:
-        deeper_grad = thirds[0]
     across, deeper_grad = lax.optimization_barrier((across, deeper_grad))
     temporal_grad, middle_grad = pl.pallas_call(
         finish_kernel,

time: 44.5 us -> 45 us (1.011)
  waiting for transfers between devices: 7.62 us -> 8.71 us
    ppermute x15, waiting for transfers between devices: 7.62 us -> 8.71 us  [swapped(): lax.ppermute(value, axis, [(i, i ^ bit) for i in range(lax.axis_size(axis...]
    pallas_call x1 -> x2, Pallas kernels: 4.4 us -> 4.11 us  [the longest x1 3.55 us: local(): pl.pallas_call(functools.partial(far_kernel, samples, bands), out_shape=f...]
  transfers between devices with their start and end apart: 15 -> 15, of which waited for: 6 -> 8; matrix products, arithmetic and copies ran while one was open for 1% -> 1% of each run, Pallas kernels for 41% -> 40%
where the time goes in v9:
time: 45 us; the launch traced here: 44.8 us
  Pallas kernels  18.9 us (42%)
  starting transfers between devices  16 us (36%)
  waiting for transfers between devices  8.71 us (19%)
  between operations  0.82 us (2%)
    ppermute x15, starting transfers between devices, swapped(): lax.ppermute(value, axis, [(i, i ^ bit) for i in range(lax.axis_size(axis...  16 us
    ppermute x15, waiting for transfers between devices, swapped(): lax.ppermute(value, axis, [(i, i ^ bit) for i in range(lax.axis_size(axis...  8.71 us
    pallas_call x1, Pallas kernels, local(): local_call(payload, *deep_weights, *maps)  3.6 us
    pallas_call x1, Pallas kernels, local(): pl.pallas_call(functools.partial(far_kernel, samples, bands), out_shape=f...  3.55 us
    pallas_call x1, Pallas kernels, local(): pl.pallas_call(functools.partial(early_kernel, pieces, lift_all - 128), o...  2.73 us
    pallas_call x1, Pallas kernels, local(): pl.pallas_call(fourth_grad_alone_kernel, out_shape=shaped((9, three, four...  2.51 us
    pallas_call x1, Pallas kernels, local(): pl.pallas_call(own_kernel, out_shape=(own_cells, own_cells, shaped((16, t...  2.15 us
    pallas_call x1, Pallas kernels, local(): pl.pallas_call(third_grad_kernel, out_shape=grad_shape, in_specs=[vmem] *...  1.96 us
  transfers between devices with their start and end apart: 15, of which 8 were waited for; matrix products, arithmetic and copies ran while one was open for 1% of the time, Pallas kernels for 40%

profile of v9, /device:TPU:0, one launch (start us, length us, event | category | flops | bytes accessed | tf_op | source)
XLA Modules:
  0.0 44.8 jit_solution(18110981551812416024)
XLA Ops:
  0.6 0.0 copy-start
  0.6 3.0 %collective-permute-start = (s32[1,5,16,128]{3,2,1,0:T(8,128)}, s32[1,5,16,128]{3,2,1,0:T(8,128)S(1)}, u32[]{:S(2)}, u32[]{:S(2)}) collective-permute-start(s32[1,5,16,128]{3,2,1,0:T(8,128)} %got_hbm.1), channel_id=1, source_target_pairs={{0,1},{1,0},{2,3},{3,2},{4,5},{5,4},{6,7},{7,6},{8,9},{9,8},{10,11... | collective-permute-start | bytes 122888 | tf_op jit(solution)/shard_map/ppermute | solution.py:693
  3.6 2.2 %own_band.1 = (bf16[512,512]{1,0:T(8,128)(2,1)S(1)}, bf16[512,512]{1,0:T(8,128)(2,1)S(1)}, bf16[16,128]{1,0:T(8,128)(2,1)S(1)}, bf16[128,256]{1,0:T(8,128)(2,1)S...) custom-call(s32[1,5,16,128]{3,2,1,0:T(8,128)} %got_hbm.1, ...), custom_call_target="tpu_custom_call" | custom-call | flops 100000000 | bytes 10000000 | tf_op jit(solution)/shard_map/own_band/pallas_call | solution.py:813
  5.8 0.1 collective-permute-start.1
  5.9 0.0 copy-done
  5.9 0.0 collective-permute-done.refs_0_
  5.9 2.7 %early.1 = (bf16[1024,512]{1,0:T(8,128)(2,1)S(1)}, bf16[1088,512]{1,0:T(8,128)(2,1)S(1)}, bf16[272,128]{1,0:T(8,128)(2,1)S(1)}, f32[1,9,2,5,2,8,64]{6,5,4,3,2,1,...) custom-call(s32[1,5,16,128]{3,2,1,0:T(8,128)S(1)} %collective-permute-done.refs_0_, ...), custom_call_target="tpu_custom_call" | custom-call | flops 150000000 | bytes 4000000 | tf_op jit(solution)/shard_map/early/pallas_call | solution.py:840
  8.7 0.8 %collective-permute-done.1 = bf16[16,128]{1,0:T(8,128)(2,1)S(1)} collective-permute-done((bf16[16,128]{1,0:T(8,128)(2,1)S(1)}, bf16[16,128]{1,0:T(8,128)(2,1)S(1)}, u32[]{:S(2)}, u32[]{:S(2)}) %collective-permute-start.1) | collective-permute-done | bytes 4128 | tf_op jit(solution)/shard_map/ppermute | solution.py:693
  9.5 2.6 %collective-permute-start.6 = (bf16[1,272,128]{2,1,0:T(8,128)(2,1)S(1)}, bf16[1,272,128]{2,1,0:T(8,128)(2,1)S(1)}, u32[]{:S(2)}, u32[]{:S(2)}) collective-permute-start(bf16[1,272,128]{2,1,0:T(8,128)(2,1)S(1)} %bitcast_dynamic-update-slice_fusion.payload_ref), channel_id=1, source_target_pairs={{0,16},{2,18},{4,20},{6,22},{8,24},{10,26},{12,28},{14,30},{16,0},... | collective-permute-start | bytes 208904 | tf_op jit(solution)/shard_map/ppermute | solution.py:693
  12.1 3.6 %local.1 = (bf16[2,336,128]{2,1,0:T(8,128)(2,1)S(1)}, bf16[2,336,128]{2,1,0:T(8,128)(2,1)S(1)}) custom-call(bf16[1,272,128]{2,1,0:T(8,128)(2,1)S(1)} %bitcast_dynamic-update-slice_fusion.payload_ref, bf16[9,128,256]{2,1,0:T(8,128)(2,1)S(1)} %get-tuple-element.52.third_w_ref, bf16[9,256,512]{2,1,0:T(8,128)(2,1)S(1)} %get-tuple-element.61.fourth_w_ref.weight_ref, ...), custom_call_target="tpu_custom_call" | custom-call | flops 300000000 | bytes 9000000 | tf_op jit(solution)/shard_map/local/pallas_call | solution.py:916
  15.7 0.1 collective-permute-start.2
  15.8 0.1 dynamic_update_slice.20
  15.8 0.0 collective-permute-done.6
  15.9 1.6 %collective-permute-start.8 = (bf16[2,272,128]{2,1,0:T(8,128)(2,1)S(1)}, bf16[2,272,128]{2,1,0:T(8,128)(2,1)S(1)}, u32[]{:S(2)}, u32[]{:S(2)}) collective-permute-start(bf16[2,272,128]{2,1,0:T(8,128)(2,1)S(1)} %slice.28), channel_id=1, source_target_pairs={{0,8},{2,10},{4,12},{6,14},{8,0},{10,2},{12,4},{14,6},{16,24},{18,... | collective-permute-start | bytes 417800 | tf_op jit(solution)/shard_map/ppermute | solution.py:693
  17.5 0.0 collective-permute-done.2
  17.6 1.6 %collective-permute-start.3 = (bf16[336,128]{1,0:T(8,128)(2,1)S(1)}, bf16[336,128]{1,0:T(8,128)(2,1)S(1)}, u32[]{:S(2)}, u32[]{:S(2)}) collective-permute-start(bf16[336,128]{1,0:T(8,128)(2,1)S(1)} %fusion.2), channel_id=1, source_target_pairs={{0,4},{2,6},{4,0},{6,2},{8,12},{10,14},{12,8},{14,10},{16,20},{18,... | collective-permute-start | bytes 258056 | tf_op jit(solution)/shard_map/ppermute | solution.py:693
  19.2 0.5 %collective-permute-start.7 = (bf16[2,272,128]{2,1,0:T(8,128)(2,1)S(1)}, bf16[2,272,128]{2,1,0:T(8,128)(2,1)S(1)}, u32[]{:S(2)}, u32[]{:S(2)}) collective-permute-start(bf16[2,272,128]{2,1,0:T(8,128)(2,1)S(1)} %slice.28), channel_id=1, source_target_pairs={{0,4},{2,6},{4,0},{6,2},{8,12},{10,14},{12,8},{14,10},{16,20},{18,... | collective-permute-start | bytes 417800 | tf_op jit(solution)/shard_map/ppermute | solution.py:693
  19.7 0.7 %transpose.1.fourth_wt_ref = bf16[9,512,256]{2,1,0:T(8,128)(2,1)S(1)} custom-call(bf16[9,256,512]{2,1,0:T(8,128)(2,1)S(1)} %get-tuple-element.61.fourth_w_ref.weight_ref), custom_call_target="tpu_custom_call" | custom-call | flops 10000000 | bytes 5000000 | tf_op jit(solution)/shard_map/transpose/pallas_call | solution.py:917
  20.3 1.7 %collective-permute-done.8 = bf16[2,272,128]{2,1,0:T(8,128)(2,1)S(1)} collective-permute-done((bf16[2,272,128]{2,1,0:T(8,128)(2,1)S(1)}, bf16[2,272,128]{2,1,0:T(8,128)(2,1)S(1)}, u32[]{:S(2)}, u32[]{:S(2)}) %collective-permute-start.8) | collective-permute-done | bytes 139296 | tf_op jit(solution)/shard_map/ppermute | solution.py:693
  22.0 0.9 %collective-permute-done.3 = bf16[336,128]{1,0:T(8,128)(2,1)S(1)} collective-permute-done((bf16[336,128]{1,0:T(8,128)(2,1)S(1)}, bf16[336,128]{1,0:T(8,128)(2,1)S(1)}, u32[]{:S(2)}, u32[]{:S(2)}) %collective-permute-start.3) | collective-permute-done | bytes 86048 | tf_op jit(solution)/shard_map/ppermute | solution.py:693
  22.9 1.2 %collective-permute-start.4 = (bf16[336,128]{1,0:T(8,128)(2,1)S(1)}, bf16[336,128]{1,0:T(8,128)(2,1)S(1)}, u32[]{:S(2)}, u32[]{:S(2)}) collective-permute-start(bf16[336,128]{1,0:T(8,128)(2,1)S(1)} %fusion), channel_id=1, source_target_pairs={{0,8},{2,10},{4,12},{6,14},{8,0},{10,2},{12,4},{14,6},{16,24},{18,... | collective-permute-start | bytes 258056 | tf_op jit(solution)/shard_map/ppermute | solution.py:693
  24.1 1.2 %collective-permute-done.7 = bf16[2,272,128]{2,1,0:T(8,128)(2,1)S(1)} collective-permute-done((bf16[2,272,128]{2,1,0:T(8,128)(2,1)S(1)}, bf16[2,272,128]{2,1,0:T(8,128)(2,1)S(1)}, u32[]{:S(2)}, u32[]{:S(2)}) %collective-permute-start.7) | collective-permute-done | bytes 139296 | tf_op jit(solution)/shard_map/ppermute | solution.py:693
  25.4 0.1 collective-permute-start.10
  25.4 1.6 %collective-permute-start.9 = (bf16[2,272,128]{2,1,0:T(8,128)(2,1)S(1)}, bf16[2,272,128]{2,1,0:T(8,128)(2,1)S(1)}, u32[]{:S(2)}, u32[]{:S(2)}) collective-permute-start(bf16[2,272,128]{2,1,0:T(8,128)(2,1)S(1)} %collective-permute-done.8), channel_id=1, source_target_pairs={{0,4},{2,6},{4,0},{6,2},{8,12},{10,14},{12,8},{14,10},{16,20},{18,... | collective-permute-start | bytes 417800 | tf_op jit(solution)/shard_map/ppermute | solution.py:693
  27.0 0.5 %collective-permute-done.4 = bf16[336,128]{1,0:T(8,128)(2,1)S(1)} collective-permute-done((bf16[336,128]{1,0:T(8,128)(2,1)S(1)}, bf16[336,128]{1,0:T(8,128)(2,1)S(1)}, u32[]{:S(2)}, u32[]{:S(2)}) %collective-permute-start.4) | collective-permute-done | bytes 86048 | tf_op jit(solution)/shard_map/ppermute | solution.py:693
  27.5 1.6 %collective-permute-start.5 = (bf16[336,128]{1,0:T(8,128)(2,1)S(1)}, bf16[336,128]{1,0:T(8,128)(2,1)S(1)}, u32[]{:S(2)}, u32[]{:S(2)}) collective-permute-start(bf16[336,128]{1,0:T(8,128)(2,1)S(1)} %add_convert_fusion.1), channel_id=1, source_target_pairs={{0,16},{2,18},{4,20},{6,22},{8,24},{10,26},{12,28},{14,30},{16,0},... | collective-permute-start | bytes 258056 | tf_op jit(solution)/shard_map/ppermute | solution.py:693
  29.1 2.4 %collective-permute-done.9 = bf16[2,272,128]{2,1,0:T(8,128)(2,1)S(1)} collective-permute-done((bf16[2,272,128]{2,1,0:T(8,128)(2,1)S(1)}, bf16[2,272,128]{2,1,0:T(8,128)(2,1)S(1)}, u32[]{:S(2)}, u32[]{:S(2)}) %collective-permute-start.9) | collective-permute-done | bytes 139296 | tf_op jit(solution)/shard_map/ppermute | solution.py:693
  31.5 0.0 collective-permute-start.11
  31.6 0.6 %near.1 = (bf16[512,1152]{1,0:T(8,128)(2,1)S(1)}, f32[8,4,2,8,256]{4,3,2,1,0:T(8,128)S(1)}, f32[8,4,2,8,256]{4,3,2,1,0:T(8,128)S(1)}) custom-call(bf16[8,272,128]{2,1,0:T(8,128)(2,1)S(1)} %constant_dynamic-update-slice_fusion.near_ref, bf16[9,128,256]{2,1,0:T(8,128)(2,1)S(1)} %get-tuple-element.52.third_w_ref), custom_call_target="tpu_custom_call" | custom-call | flops 300000000 | bytes 4000000 | tf_op jit(solution)/shard_map/near/pallas_call | solution.py:940
  32.1 0.8 %collective-permute-done.11.last_ref = bf16[2,272,128]{2,1,0:T(8,128)(2,1)S(1)} collective-permute-done((bf16[2,272,128]{2,1,0:T(8,128)(2,1)S(1)}, bf16[2,272,128]{2,1,0:T(8,128)(2,1)S(1)}, u32[]{:S(2)}, u32[]{:S(2)}) %collective-permute-start.11) | collective-permute-done | bytes 139296 | tf_op jit(solution)/shard_map/ppermute | solution.py:693
  32.9 0.0 collective-permute-done.10.far_ref
  32.9 3.5 %deep.1 = (bf16[256,2304]{1,0:T(8,128)(2,1)S(1)}, bf16[256,512]{1,0:T(8,128)(2,1)S(1)}, f32[1,512]{1,0:T(1,128)}, bf16[1024,1152]{1,0:T(8,128)(2,1)S(1)}, bf16[1024,256]{1,0:T(8,128)(2,1)S(1)}) custom-call(bf16[8,272,128]{2,1,0:T(8,128)(2,1)S(1)} %constant_dynamic-update-slice_fusion.near_ref, bf16[6,272,128]{2,1,0:T(8,128)(2,1)S(1)} %collective-permute-done.10.far_ref, ...), custom_call_target="tpu_custom_call" | custom-call | flops 1300000000 | bytes 12000000 | tf_op jit(solution)/shard_map/deep/pallas_call | solution.py:950
  36.4 0.0 collective-permute-done.5
  36.5 1.6 %collective-permute-start.13 = (bf16[336,128]{1,0:T(8,128)(2,1)S(1)}, bf16[336,128]{1,0:T(8,128)(2,1)S(1)}, u32[]{:S(2)}, u32[]{:S(2)}) collective-permute-start(bf16[336,128]{1,0:T(8,128)(2,1)S(1)} %add_convert_fusion.refs_0_), channel_id=1, source_target_pairs={{0,4},{2,6},{4,0},{6,2},{8,12},{10,14},{12,8},{14,10},{16,20},{18,... | collective-permute-start | bytes 258056 | tf_op jit(solution)/shard_map/ppermute | solution.py:693
  38.1 2.5 %fourth_grad.1 = f32[9,256,512]{2,1,0:T(8,128)} custom-call(bf16[256,2304]{1,0:T(8,128)(2,1)S(1)} %get-tuple-element.74.fourth_taps_ref, bf16[256,512]{1,0:T(8,128)(2,1)S(1)} %get-tuple-element.75.fourth_flat_ref), custom_call_target="tpu_custom_call" | custom-call | flops 600000000 | bytes 6000000 | tf_op jit(solution)/shard_map/fourth_grad/pallas_call | solution.py:992
  40.6 0.5 %collective-permute-done.13.refs_2_ = bf16[336,128]{1,0:T(8,128)(2,1)S(1)} collective-permute-done((bf16[336,128]{1,0:T(8,128)(2,1)S(1)}, bf16[336,128]{1,0:T(8,128)(2,1)S(1)}, u32[]{:S(2)}, u32[]{:S(2)}) %collective-permute-start.13) | collective-permute-done | bytes 86048 | tf_op jit(solution)/shard_map/ppermute | solution.py:693
  41.1 0.0 collective-permute-start.14
  41.1 0.5 %collective-permute-start.12 = (bf16[336,128]{1,0:T(8,128)(2,1)S(1)}, bf16[336,128]{1,0:T(8,128)(2,1)S(1)}, u32[]{:S(2)}, u32[]{:S(2)}) collective-permute-start(bf16[336,128]{1,0:T(8,128)(2,1)S(1)} %add_convert_fusion.refs_0_), channel_id=1, source_target_pairs={{0,2},{2,0},{4,6},{6,4},{8,10},{10,8},{12,14},{14,12},{16,18},{18,... | collective-permute-start | bytes 258056 | tf_op jit(solution)/shard_map/ppermute | solution.py:693
  41.6 2.0 %third_grad.1 = f32[1152,256]{1,0:T(8,128)} custom-call(bf16[1024,1152]{1,0:T(8,128)(2,1)S(1)} %get-tuple-element.77.taps_ref, bf16[1024,256]{1,0:T(8,128)(2,1)S(1)} %get-tuple-element.78.delta_ref), custom_call_target="tpu_custom_call" | custom-call | flops 600000000 | bytes 4000000 | tf_op jit(solution)/shard_map/third_grad/pallas_call | solution.py:1022
  43.6 0.0 collective-permute-done.14.refs_3_
  43.6 0.0 collective-permute-done.12.refs_1_
  43.6 1.2 %finish.1 = (f32[9,160,64]{2,1,0:T(8,128)}, f32[576,128]{1,0:T(8,128)}) custom-call(bf16[336,128]{1,0:T(8,128)(2,1)S(1)} %add_convert_fusion.refs_0_, bf16[336,128]{1,0:T(8,128)(2,1)S(1)} %collective-permute-done.12.refs_1_, bf16[336,128]{1,0:T(8,128)(2,1)S(1)} %collective-permute-done.13.refs_2_, bf16[336,128]{1,0:T(8,128)(2,1)S(1)} %collective-permute-done.14.refs_3_), custom_call_target="tpu_custom_call" | custom-call | flops 1000000 | bytes 1500000 | tf_op jit(solution)/shard_map/finish/pallas_call | solution.py:1032
  (12 shorter events, 0.2 us)
Async XLA Ops:
  0.6 5.3 %copy-start = (bf16[512]{0:T(512)(128)(2,1)S(1)}, bf16[512]{0:T(512)(128)(2,1)}, u32[]{:S(2)}) copy-start(bf16[512]{0:T(512)(128)(2,1)} %param.15) | copy-start | bytes 3076
  0.6 5.3 %collective-permute-start = (s32[1,5,16,128]{3,2,1,0:T(8,128)}, s32[1,5,16,128]{3,2,1,0:T(8,128)S(1)}, u32[]{:S(2)}, u32[]{:S(2)}) collective-permute-start(s32[1,5,16,128]{3,2,1,0:T(8,128)} %got_hbm.1), channel_id=1, source_target_pairs={{0,1},{1,0},{2,3},{3,2},{4,5},{5,4},{6,7},{7,6},{8,9},{9,8},{10,11... | collective-permute-start | bytes 122888 | tf_op jit(solution)/shard_map/ppermute | solution.py:693
  5.8 3.7 %collective-permute-start.1 = (bf16[16,128]{1,0:T(8,128)(2,1)S(1)}, bf16[16,128]{1,0:T(8,128)(2,1)S(1)}, u32[]{:S(2)}, u32[]{:S(2)}) collective-permute-start(bf16[16,128]{1,0:T(8,128)(2,1)S(1)} %get-tuple-element.51), channel_id=1, source_target_pairs={{0,1},{1,0},{2,3},{3,2},{4,5},{5,4},{6,7},{7,6},{8,9},{9,8},{10,11... | collective-permute-start | bytes 12296 | tf_op jit(solution)/shard_map/ppermute | solution.py:693
  9.5 6.4 %collective-permute-start.6 = (bf16[1,272,128]{2,1,0:T(8,128)(2,1)S(1)}, bf16[1,272,128]{2,1,0:T(8,128)(2,1)S(1)}, u32[]{:S(2)}, u32[]{:S(2)}) collective-permute-start(bf16[1,272,128]{2,1,0:T(8,128)(2,1)S(1)} %bitcast_dynamic-update-slice_fusion.payload_ref), channel_id=1, source_target_pairs={{0,16},{2,18},{4,20},{6,22},{8,24},{10,26},{12,28},{14,30},{16,0},... | collective-permute-start | bytes 208904 | tf_op jit(solution)/shard_map/ppermute | solution.py:693
  15.7 1.9 %collective-permute-start.2 = (bf16[2,336,128]{2,1,0:T(8,128)(2,1)S(1)}, bf16[2,336,128]{2,1,0:T(8,128)(2,1)S(1)}, u32[]{:S(2)}, u32[]{:S(2)}) collective-permute-start(bf16[2,336,128]{2,1,0:T(8,128)(2,1)S(1)} %get-tuple-element.60), channel_id=1, source_target_pairs={{0,2},{2,0},{4,6},{6,4},{8,10},{10,8},{12,14},{14,12},{16,18},{18,... | collective-permute-start | bytes 516104 | tf_op jit(solution)/shard_map/ppermute | solution.py:693
  15.9 6.1 %collective-permute-start.8 = (bf16[2,272,128]{2,1,0:T(8,128)(2,1)S(1)}, bf16[2,272,128]{2,1,0:T(8,128)(2,1)S(1)}, u32[]{:S(2)}, u32[]{:S(2)}) collective-permute-start(bf16[2,272,128]{2,1,0:T(8,128)(2,1)S(1)} %slice.28), channel_id=1, source_target_pairs={{0,8},{2,10},{4,12},{6,14},{8,0},{10,2},{12,4},{14,6},{16,24},{18,... | collective-permute-start | bytes 417800 | tf_op jit(solution)/shard_map/ppermute | solution.py:693
  17.6 5.3 %collective-permute-start.3 = (bf16[336,128]{1,0:T(8,128)(2,1)S(1)}, bf16[336,128]{1,0:T(8,128)(2,1)S(1)}, u32[]{:S(2)}, u32[]{:S(2)}) collective-permute-start(bf16[336,128]{1,0:T(8,128)(2,1)S(1)} %fusion.2), channel_id=1, source_target_pairs={{0,4},{2,6},{4,0},{6,2},{8,12},{10,14},{12,8},{14,10},{16,20},{18,... | collective-permute-start | bytes 258056 | tf_op jit(solution)/shard_map/ppermute | solution.py:693
  19.2 6.1 %collective-permute-start.7 = (bf16[2,272,128]{2,1,0:T(8,128)(2,1)S(1)}, bf16[2,272,128]{2,1,0:T(8,128)(2,1)S(1)}, u32[]{:S(2)}, u32[]{:S(2)}) collective-permute-start(bf16[2,272,128]{2,1,0:T(8,128)(2,1)S(1)} %slice.28), channel_id=1, source_target_pairs={{0,4},{2,6},{4,0},{6,2},{8,12},{10,14},{12,8},{14,10},{16,20},{18,... | collective-permute-start | bytes 417800 | tf_op jit(solution)/shard_map/ppermute | solution.py:693
  22.9 4.6 %collective-permute-start.4 = (bf16[336,128]{1,0:T(8,128)(2,1)S(1)}, bf16[336,128]{1,0:T(8,128)(2,1)S(1)}, u32[]{:S(2)}, u32[]{:S(2)}) collective-permute-start(bf16[336,128]{1,0:T(8,128)(2,1)S(1)} %fusion), channel_id=1, source_target_pairs={{0,8},{2,10},{4,12},{6,14},{8,0},{10,2},{12,4},{14,6},{16,24},{18,... | collective-permute-start | bytes 258056 | tf_op jit(solution)/shard_map/ppermute | solution.py:693
  25.4 7.5 %collective-permute-start.10 = (bf16[6,272,128]{2,1,0:T(8,128)(2,1)S(1)}, bf16[6,272,128]{2,1,0:T(8,128)(2,1)S(1)}, u32[]{:S(2)}, u32[]{:S(2)}) collective-permute-start(bf16[6,272,128]{2,1,0:T(8,128)(2,1)S(1)} %slice.29), channel_id=1, source_target_pairs={{0,2},{2,0},{4,6},{6,4},{8,10},{10,8},{12,14},{14,12},{16,18},{18,... | collective-permute-start | bytes 1253384 | tf_op jit(solution)/shard_map/ppermute | solution.py:693
  25.4 6.1 %collective-permute-start.9 = (bf16[2,272,128]{2,1,0:T(8,128)(2,1)S(1)}, bf16[2,272,128]{2,1,0:T(8,128)(2,1)S(1)}, u32[]{:S(2)}, u32[]{:S(2)}) collective-permute-start(bf16[2,272,128]{2,1,0:T(8,128)(2,1)S(1)} %collective-permute-done.8), channel_id=1, source_target_pairs={{0,4},{2,6},{4,0},{6,2},{8,12},{10,14},{12,8},{14,10},{16,20},{18,... | collective-permute-start | bytes 417800 | tf_op jit(solution)/shard_map/ppermute | solution.py:693
  27.5 8.9 %collective-permute-start.5 = (bf16[336,128]{1,0:T(8,128)(2,1)S(1)}, bf16[336,128]{1,0:T(8,128)(2,1)S(1)}, u32[]{:S(2)}, u32[]{:S(2)}) collective-permute-start(bf16[336,128]{1,0:T(8,128)(2,1)S(1)} %add_convert_fusion.1), channel_id=1, source_target_pairs={{0,16},{2,18},{4,20},{6,22},{8,24},{10,26},{12,28},{14,30},{16,0},... | collective-permute-start | bytes 258056 | tf_op jit(solution)/shard_map/ppermute | solution.py:693
  31.5 1.4 %collective-permute-start.11 = (bf16[2,272,128]{2,1,0:T(8,128)(2,1)S(1)}, bf16[2,272,128]{2,1,0:T(8,128)(2,1)S(1)}, u32[]{:S(2)}, u32[]{:S(2)}) collective-permute-start(bf16[2,272,128]{2,1,0:T(8,128)(2,1)S(1)} %collective-permute-done.9), channel_id=1, source_target_pairs={{0,2},{2,0},{4,6},{6,4},{8,10},{10,8},{12,14},{14,12},{16,18},{18,... | collective-permute-start | bytes 417800 | tf_op jit(solution)/shard_map/ppermute | solution.py:693
  36.5 4.6 %collective-permute-start.13 = (bf16[336,128]{1,0:T(8,128)(2,1)S(1)}, bf16[336,128]{1,0:T(8,128)(2,1)S(1)}, u32[]{:S(2)}, u32[]{:S(2)}) collective-permute-start(bf16[336,128]{1,0:T(8,128)(2,1)S(1)} %add_convert_fusion.refs_0_), channel_id=1, source_target_pairs={{0,4},{2,6},{4,0},{6,2},{8,12},{10,14},{12,8},{14,10},{16,20},{18,... | collective-permute-start | bytes 258056 | tf_op jit(solution)/shard_map/ppermute | solution.py:693
  41.1 2.5 %collective-permute-start.14 = (bf16[336,128]{1,0:T(8,128)(2,1)S(1)}, bf16[336,128]{1,0:T(8,128)(2,1)S(1)}, u32[]{:S(2)}, u32[]{:S(2)}) collective-permute-start(bf16[336,128]{1,0:T(8,128)(2,1)S(1)} %collective-permute-done.13.refs_2_), channel_id=1, source_target_pairs={{0,2},{2,0},{4,6},{6,4},{8,10},{10,8},{12,14},{14,12},{16,18},{18,... | collective-permute-start | bytes 258056 | tf_op jit(solution)/shard_map/ppermute | solution.py:693
  41.1 2.5 %collective-permute-start.12 = (bf16[336,128]{1,0:T(8,128)(2,1)S(1)}, bf16[336,128]{1,0:T(8,128)(2,1)S(1)}, u32[]{:S(2)}, u32[]{:S(2)}) collective-permute-start(bf16[336,128]{1,0:T(8,128)(2,1)S(1)} %add_convert_fusion.refs_0_), channel_id=1, source_target_pairs={{0,2},{2,0},{4,6},{6,4},{8,10},{10,8},{12,14},{14,12},{16,18},{18,... | collective-permute-start | bytes 258056 | tf_op jit(solution)/shard_map/ppermute | solution.py:693

commit v10 on v9

--- a/solution.py
+++ b/solution.py
@@ -175,6 +175,9 @@
         (second_w_hbm, second_w_ref),
         (third_w_hbm, third_w_ref),
         (fourth_w_hbm, fourth_w_ref),
+    )
+    pairs = pairs[:-1] + tuple(
+        (fourth_w_hbm.at[pl.ds(tap, 1)], fourth_w_ref.at[pl.ds(tap, 1)]) for tap in range(9)
     )
     copies = [
         pltpu.make_async_copy(source, target, sems.at[k])
@@ -314,17 +317,24 @@
         )
 
 
-def delta_columns(ref, weight_ref, row_parity, col_parity, rows, phases):
+def delta_columns(ref, rows, phases):
+    columns = {}
+    for row_step in range(2):
+        for col_step in range(2):
+            cells = ref[:, pl.ds(row_step, rows), pl.ds(col_step, phases)]
+            cells = cells.reshape(-1, cells.shape[-1])
+            columns[row_step, col_step] = cells.T.astype(jnp.bfloat16)
+    return columns
+
+
+def column_parts(columns, weight_ref, row_parity, col_parity, rows, phases):
     taps = (((1, 0),), ((2, 0), (0, 1)))
     total = None
     for row_tap, row_step in taps[row_parity]:
         for col_tap, col_step in taps[col_parity]:
-            cells = ref[:, pl.ds(row_step, rows), pl.ds(col_step, phases)]
-            lead = cells.shape[:-1]
-            columns = cells.reshape(-1, cells.shape[-1]).T.astype(jnp.bfloat16)
-            part = dot_nn(weight_ref[3 * row_tap + col_tap], columns)
+            part = dot_nn(weight_ref[3 * row_tap + col_tap], columns[row_step, col_step])
             total = part if total is None else total + part
-    return total.T.reshape(*lead, total.shape[0])
+    return total.T.reshape(-1, rows, phases, BLOCK, total.shape[0])
 
 
 def put_label(ref, inner, label_ref, place, bands):
@@ -419,9 +429,10 @@
     delta = rounded(logit_grad * head * slope)
     last_row_zero(fourth_delta_ref)
     fill_delta(fourth_delta_ref, delta.reshape(samples, rows, phases, BLOCK, delta.shape[-1]))
+    parts = fourth_parts(fourth_delta_ref, rows, phases)
     for row_parity in range(2):
         for col_parity in range(2):
-            part = fourth_parts(fourth_delta_ref, row_parity, col_parity, rows, phases)
+            part = parts(row_parity, col_parity, rows, phases)
             part = rounded(part * third_slope_ref[:, :, row_parity, :, col_parity])
             for row in range(rows):
                 third_delta_ref[:, 2 * row + row_parity, col_parity] = part[:, row, 0]
@@ -497,7 +508,7 @@
         batch,
         bands,
         fourth_w_ref,
-        lambda ref, *where: delta_parts(ref, fourth_wt_ref, *where),
+        lambda ref, *_: functools.partial(delta_parts, ref, fourth_wt_ref),
         head_ref,
         fourth_taps_ref,
         label_ref,
@@ -536,7 +547,7 @@
         bands,
         third_w_ref,
         fourth_w_ref,
-        lambda ref, *where: delta_parts(ref, fourth_wt_ref, *where),
+        lambda ref, *_: functools.partial(delta_parts, ref, fourth_wt_ref),
         head_ref,
         fourth_taps_ref,
         second_ref,
@@ -582,7 +593,9 @@
         bands,
         third_w_ref,
         fourth_w_ref,
-        lambda ref, *where: delta_columns(ref, fourth_w_ref, *where),
+        lambda ref, *size: functools.partial(
+            column_parts, delta_columns(ref, *size), fourth_w_ref
+        ),
         head_ref,
         fourth_taps_ref,
         second_map_ref,
@@ -594,18 +607,20 @@
     fill_delta(third_ref, third_delta_ref[...])
     last_row_zero(third_ref)
     last_row_zero(second_ref)
+    columns = delta_columns(third_ref, rows, phases)
     for row_parity in range(2):
         for col_parity in range(2):
-            part = delta_columns(third_ref, third_w_ref, row_parity, col_parity, rows, phases)
+            part = column_parts(columns, third_w_ref, row_parity, col_parity, rows, phases)
             for row in range(rows):
                 for phase in range(phases):
                     at = (slice(None), 2 * row + row_parity, 2 * phase + col_parity)
                     second_ref[at] = rounded(part[:, row, phase] * second_slope_ref[at])
     rows, phases = 2 * rows, 2 * phases
     second_ref[:, :, phases] = shift_block(second_ref[:, :, 0], -1)
+    columns = delta_columns(second_ref, rows, phases)
     for row_parity in range(2):
         for col_parity in range(2):
-            part = delta_columns(second_ref, second_w_ref, row_parity, col_parity, rows, phases)
+            part = column_parts(columns, second_w_ref, row_parity, col_parity, rows, phases)
             for row in range(rows):
                 for phase in range(phases):
                     at = (slice(None), 2 * row + row_parity, 2 * phase + col_parity)
@@ -731,12 +746,13 @@
             near = put(near, beside, quarter + beside_count)
             beside_count = count
     total = added(mine, after(mine_beside, weights))
-    beside = swapped(after(near[beside_count:quarter], total), "dp", 2)
+    beside = swapped(after(near[beside_count:quarter], theirs), "dp", 2)
     early = swapped(near[: quarter + beside_count], "dp", 1)
     bit = 4
     while 2 * bit < samples:
-        total = added(total, swapped(total, "dp", bit))
+        other = swapped(total, "dp", bit)
         beside = after(beside, total)
+        total = added(total, after(other, beside))
         bit *= 2
     near = put(near, beside, quarter + beside_count)
     last = swapped(beside, "dp", 1)
@@ -830,7 +846,7 @@
             pltpu.VMEM(lift_weight.shape, bf16),
             pltpu.VMEM(first_w.shape, bf16),
             bits_scratch,
-            pltpu.SemaphoreType.DMA((7,)),
+            pltpu.SemaphoreType.DMA((15,)),
         ],
         compiler_params=grant(24),
         cost_estimate=cost(100_000_000, 10_000_000),

time: 45 us -> 44.3 us (0.984)
  waiting for transfers between devices: 8.71 us -> 7.77 us
  starting transfers between devices: 16 us -> 16.5 us
    ppermute x15, waiting for transfers between devices: 8.71 us -> 7.77 us  [swapped(): lax.ppermute(value, axis, [(i, i ^ bit) for i in range(lax.axis_size(axis...]
  transfers between devices with their start and end apart: 15 -> 15, of which waited for: 8 -> 6; matrix products, arithmetic and copies ran while one was open for 1% -> 1% of each run, Pallas kernels for 40% -> 40%
where the time goes in v10:
time: 44.3 us; the launch traced here: 44.2 us
  Pallas kernels  18.8 us (42%)
  starting transfers between devices  16.5 us (37%)
  waiting for transfers between devices  7.77 us (18%)
  between operations  0.83 us (2%)
    ppermute x15, starting transfers between devices, swapped(): lax.ppermute(value, axis, [(i, i ^ bit) for i in range(lax.axis_size(axis...  16.5 us
    ppermute x15, waiting for transfers between devices, swapped(): lax.ppermute(value, axis, [(i, i ^ bit) for i in range(lax.axis_size(axis...  7.77 us
    pallas_call x1, Pallas kernels, local(): pl.pallas_call(functools.partial(far_kernel, samples, bands), out_shape=f...  3.56 us
    pallas_call x1, Pallas kernels, local(): local_call(payload, *deep_weights, *maps)  3.49 us
    pallas_call x1, Pallas kernels, local(): pl.pallas_call(functools.partial(early_kernel, pieces, lift_all - 128), o...  2.72 us
    pallas_call x1, Pallas kernels, local(): pl.pallas_call(fourth_grad_alone_kernel, out_shape=shaped((9, three, four...  2.5 us
    pallas_call x1, Pallas kernels, local(): pl.pallas_call(own_kernel, out_shape=(own_cells, own_cells, shaped((16, t...  2.13 us
    pallas_call x1, Pallas kernels, local(): pl.pallas_call(third_grad_kernel, out_shape=grad_shape, in_specs=[vmem] *...  1.96 us
  transfers between devices with their start and end apart: 15, of which 6 were waited for; matrix products, arithmetic and copies ran while one was open for 1% of the time, Pallas kernels for 40%

profile of v10, /device:TPU:0, one launch (start us, length us, event | category | flops | bytes accessed | tf_op | source)
XLA Modules:
  0.0 44.2 jit_solution(11459287450700321364)
XLA Ops:
  0.6 0.0 copy-start
  0.6 3.0 %collective-permute-start = (s32[1,5,16,128]{3,2,1,0:T(8,128)}, s32[1,5,16,128]{3,2,1,0:T(8,128)S(1)}, u32[]{:S(2)}, u32[]{:S(2)}) collective-permute-start(s32[1,5,16,128]{3,2,1,0:T(8,128)} %got_hbm.1), channel_id=1, source_target_pairs={{0,1},{1,0},{2,3},{3,2},{4,5},{5,4},{6,7},{7,6},{8,9},{9,8},{10,11... | collective-permute-start | bytes 122888 | tf_op jit(solution)/shard_map/ppermute | solution.py:708
  3.6 2.1 %own_band.1 = (bf16[512,512]{1,0:T(8,128)(2,1)S(1)}, bf16[512,512]{1,0:T(8,128)(2,1)S(1)}, bf16[16,128]{1,0:T(8,128)(2,1)S(1)}, bf16[128,256]{1,0:T(8,128)(2,1)S...) custom-call(s32[1,5,16,128]{3,2,1,0:T(8,128)} %got_hbm.1, ...), custom_call_target="tpu_custom_call" | custom-call | flops 100000000 | bytes 10000000 | tf_op jit(solution)/shard_map/own_band/pallas_call | solution.py:829
  5.8 0.1 collective-permute-start.1
  5.9 0.0 copy-done
  5.9 0.0 collective-permute-done.refs_0_
  5.9 2.7 %early.1 = (bf16[1024,512]{1,0:T(8,128)(2,1)S(1)}, bf16[1088,512]{1,0:T(8,128)(2,1)S(1)}, bf16[272,128]{1,0:T(8,128)(2,1)S(1)}, f32[1,9,2,5,2,8,64]{6,5,4,3,2,1,...) custom-call(s32[1,5,16,128]{3,2,1,0:T(8,128)S(1)} %collective-permute-done.refs_0_, ...), custom_call_target="tpu_custom_call" | custom-call | flops 150000000 | bytes 4000000 | tf_op jit(solution)/shard_map/early/pallas_call | solution.py:856
  8.6 0.8 %collective-permute-done.1 = bf16[16,128]{1,0:T(8,128)(2,1)S(1)} collective-permute-done((bf16[16,128]{1,0:T(8,128)(2,1)S(1)}, bf16[16,128]{1,0:T(8,128)(2,1)S(1)}, u32[]{:S(2)}, u32[]{:S(2)}) %collective-permute-start.1) | collective-permute-done | bytes 4128 | tf_op jit(solution)/shard_map/ppermute | solution.py:708
  9.5 2.6 %collective-permute-start.5 = (bf16[1,272,128]{2,1,0:T(8,128)(2,1)S(1)}, bf16[1,272,128]{2,1,0:T(8,128)(2,1)S(1)}, u32[]{:S(2)}, u32[]{:S(2)}) collective-permute-start(bf16[1,272,128]{2,1,0:T(8,128)(2,1)S(1)} %bitcast_dynamic-update-slice_fusion.payload_ref), channel_id=1, source_target_pairs={{0,16},{2,18},{4,20},{6,22},{8,24},{10,26},{12,28},{14,30},{16,0},... | collective-permute-start | bytes 208904 | tf_op jit(solution)/shard_map/ppermute | solution.py:708
  12.1 3.5 %local.1 = (bf16[2,336,128]{2,1,0:T(8,128)(2,1)S(1)}, bf16[2,336,128]{2,1,0:T(8,128)(2,1)S(1)}) custom-call(bf16[1,272,128]{2,1,0:T(8,128)(2,1)S(1)} %bitcast_dynamic-update-slice_fusion.payload_ref, bf16[9,128,256]{2,1,0:T(8,128)(2,1)S(1)} %get-tuple-element.53.third_w_ref, bf16[9,256,512]{2,1,0:T(8,128)(2,1)S(1)} %get-tuple-element.62.fourth_w_ref.weight_ref, ...), custom_call_target="tpu_custom_call" | custom-call | flops 300000000 | bytes 9000000 | tf_op jit(solution)/shard_map/local/pallas_call | solution.py:932
  15.6 0.1 collective-permute-start.2
  15.6 0.1 dynamic_update_slice.20
  15.7 0.0 collective-permute-done.5
  15.8 1.6 %collective-permute-start.6 = (bf16[2,272,128]{2,1,0:T(8,128)(2,1)S(1)}, bf16[2,272,128]{2,1,0:T(8,128)(2,1)S(1)}, u32[]{:S(2)}, u32[]{:S(2)}) collective-permute-start(bf16[2,272,128]{2,1,0:T(8,128)(2,1)S(1)} %slice.28), channel_id=1, source_target_pairs={{0,8},{2,10},{4,12},{6,14},{8,0},{10,2},{12,4},{14,6},{16,24},{18,... | collective-permute-start | bytes 417800 | tf_op jit(solution)/shard_map/ppermute | solution.py:708
  17.4 0.0 collective-permute-done.2
  17.4 1.6 %collective-permute-start.3 = (bf16[336,128]{1,0:T(8,128)(2,1)S(1)}, bf16[336,128]{1,0:T(8,128)(2,1)S(1)}, u32[]{:S(2)}, u32[]{:S(2)}) collective-permute-start(bf16[336,128]{1,0:T(8,128)(2,1)S(1)} %fusion.2), channel_id=1, source_target_pairs={{0,4},{2,6},{4,0},{6,2},{8,12},{10,14},{12,8},{14,10},{16,20},{18,... | collective-permute-start | bytes 258056 | tf_op jit(solution)/shard_map/ppermute | solution.py:708
  19.0 0.5 %collective-permute-start.9 = (bf16[2,272,128]{2,1,0:T(8,128)(2,1)S(1)}, bf16[2,272,128]{2,1,0:T(8,128)(2,1)S(1)}, u32[]{:S(2)}, u32[]{:S(2)}) collective-permute-start(bf16[2,272,128]{2,1,0:T(8,128)(2,1)S(1)} %slice.28), channel_id=1, source_target_pairs={{0,4},{2,6},{4,0},{6,2},{8,12},{10,14},{12,8},{14,10},{16,20},{18,... | collective-permute-start | bytes 417800 | tf_op jit(solution)/shard_map/ppermute | solution.py:708
  19.5 0.7 %transpose.1.fourth_wt_ref = bf16[9,512,256]{2,1,0:T(8,128)(2,1)S(1)} custom-call(bf16[9,256,512]{2,1,0:T(8,128)(2,1)S(1)} %get-tuple-element.62.fourth_w_ref.weight_ref), custom_call_target="tpu_custom_call" | custom-call | flops 10000000 | bytes 5000000 | tf_op jit(solution)/shard_map/transpose/pallas_call | solution.py:933
  20.2 1.7 %collective-permute-done.6 = bf16[2,272,128]{2,1,0:T(8,128)(2,1)S(1)} collective-permute-done((bf16[2,272,128]{2,1,0:T(8,128)(2,1)S(1)}, bf16[2,272,128]{2,1,0:T(8,128)(2,1)S(1)}, u32[]{:S(2)}, u32[]{:S(2)}) %collective-permute-start.6) | collective-permute-done | bytes 139296 | tf_op jit(solution)/shard_map/ppermute | solution.py:708
  21.9 1.5 %collective-permute-start.7 = (bf16[2,272,128]{2,1,0:T(8,128)(2,1)S(1)}, bf16[2,272,128]{2,1,0:T(8,128)(2,1)S(1)}, u32[]{:S(2)}, u32[]{:S(2)}) collective-permute-start(bf16[2,272,128]{2,1,0:T(8,128)(2,1)S(1)} %collective-permute-done.6), channel_id=1, source_target_pairs={{0,4},{2,6},{4,0},{6,2},{8,12},{10,14},{12,8},{14,10},{16,20},{18,... | collective-permute-start | bytes 417800 | tf_op jit(solution)/shard_map/ppermute | solution.py:708
  23.4 0.0 collective-permute-done.3
  23.5 1.6 %collective-permute-start.4 = (bf16[336,128]{1,0:T(8,128)(2,1)S(1)}, bf16[336,128]{1,0:T(8,128)(2,1)S(1)}, u32[]{:S(2)}, u32[]{:S(2)}) collective-permute-start(bf16[336,128]{1,0:T(8,128)(2,1)S(1)} %fusion), channel_id=1, source_target_pairs={{0,8},{2,10},{4,12},{6,14},{8,0},{10,2},{12,4},{14,6},{16,24},{18,... | collective-permute-start | bytes 258056 | tf_op jit(solution)/shard_map/ppermute | solution.py:708
  25.1 0.6 %collective-permute-done.9 = bf16[2,272,128]{2,1,0:T(8,128)(2,1)S(1)} collective-permute-done((bf16[2,272,128]{2,1,0:T(8,128)(2,1)S(1)}, bf16[2,272,128]{2,1,0:T(8,128)(2,1)S(1)}, u32[]{:S(2)}, u32[]{:S(2)}) %collective-permute-start.9) | collective-permute-done | bytes 139296 | tf_op jit(solution)/shard_map/ppermute | solution.py:708
  25.8 0.1 collective-permute-start.10
  25.9 2.2 %collective-permute-done.7 = bf16[2,272,128]{2,1,0:T(8,128)(2,1)S(1)} collective-permute-done((bf16[2,272,128]{2,1,0:T(8,128)(2,1)S(1)}, bf16[2,272,128]{2,1,0:T(8,128)(2,1)S(1)}, u32[]{:S(2)}, u32[]{:S(2)}) %collective-permute-start.7) | collective-permute-done | bytes 139296 | tf_op jit(solution)/shard_map/ppermute | solution.py:708
  28.1 0.0 collective-permute-start.11
  28.1 0.0 collective-permute-done.4
  28.2 1.7 %collective-permute-start.8 = (bf16[336,128]{1,0:T(8,128)(2,1)S(1)}, bf16[336,128]{1,0:T(8,128)(2,1)S(1)}, u32[]{:S(2)}, u32[]{:S(2)}) collective-permute-start(bf16[336,128]{1,0:T(8,128)(2,1)S(1)} %add_convert_fusion.1), channel_id=1, source_target_pairs={{0,16},{2,18},{4,20},{6,22},{8,24},{10,26},{12,28},{14,30},{16,0},... | collective-permute-start | bytes 258056 | tf_op jit(solution)/shard_map/ppermute | solution.py:708
  29.8 0.6 %near.1 = (bf16[512,1152]{1,0:T(8,128)(2,1)S(1)}, f32[8,4,2,8,256]{4,3,2,1,0:T(8,128)S(1)}, f32[8,4,2,8,256]{4,3,2,1,0:T(8,128)S(1)}) custom-call(bf16[8,272,128]{2,1,0:T(8,128)(2,1)S(1)} %constant_dynamic-update-slice_fusion.near_ref, bf16[9,128,256]{2,1,0:T(8,128)(2,1)S(1)} %get-tuple-element.53.third_w_ref), custom_call_target="tpu_custom_call" | custom-call | flops 300000000 | bytes 4000000 | tf_op jit(solution)/shard_map/near/pallas_call | solution.py:956
  30.4 0.0 collective-permute-done.11.last_ref
  30.4 0.0 collective-permute-done.10.far_ref
  30.4 3.6 %deep.1 = (bf16[256,2304]{1,0:T(8,128)(2,1)S(1)}, bf16[256,512]{1,0:T(8,128)(2,1)S(1)}, f32[1,512]{1,0:T(1,128)}, bf16[1024,1152]{1,0:T(8,128)(2,1)S(1)}, bf16[1024,256]{1,0:T(8,128)(2,1)S(1)}) custom-call(bf16[8,272,128]{2,1,0:T(8,128)(2,1)S(1)} %constant_dynamic-update-slice_fusion.near_ref, bf16[6,272,128]{2,1,0:T(8,128)(2,1)S(1)} %collective-permute-done.10.far_ref, ...), custom_call_target="tpu_custom_call" | custom-call | flops 1300000000 | bytes 12000000 | tf_op jit(solution)/shard_map/deep/pallas_call | solution.py:966
  34.0 1.9 %collective-permute-done.8 = bf16[336,128]{1,0:T(8,128)(2,1)S(1)} collective-permute-done((bf16[336,128]{1,0:T(8,128)(2,1)S(1)}, bf16[336,128]{1,0:T(8,128)(2,1)S(1)}, u32[]{:S(2)}, u32[]{:S(2)}) %collective-permute-start.8) | collective-permute-done | bytes 86048 | tf_op jit(solution)/shard_map/ppermute | solution.py:708
  35.9 1.6 %collective-permute-start.13 = (bf16[336,128]{1,0:T(8,128)(2,1)S(1)}, bf16[336,128]{1,0:T(8,128)(2,1)S(1)}, u32[]{:S(2)}, u32[]{:S(2)}) collective-permute-start(bf16[336,128]{1,0:T(8,128)(2,1)S(1)} %add_convert_fusion.refs_0_), channel_id=1, source_target_pairs={{0,4},{2,6},{4,0},{6,2},{8,12},{10,14},{12,8},{14,10},{16,20},{18,... | collective-permute-start | bytes 258056 | tf_op jit(solution)/shard_map/ppermute | solution.py:708
  37.5 2.5 %fourth_grad.1 = f32[9,256,512]{2,1,0:T(8,128)} custom-call(bf16[256,2304]{1,0:T(8,128)(2,1)S(1)} %get-tuple-element.76.fourth_taps_ref, bf16[256,512]{1,0:T(8,128)(2,1)S(1)} %get-tuple-element.77.fourth_flat_ref), custom_call_target="tpu_custom_call" | custom-call | flops 600000000 | bytes 6000000 | tf_op jit(solution)/shard_map/fourth_grad/pallas_call | solution.py:1008
  40.0 0.5 %collective-permute-done.13.refs_2_ = bf16[336,128]{1,0:T(8,128)(2,1)S(1)} collective-permute-done((bf16[336,128]{1,0:T(8,128)(2,1)S(1)}, bf16[336,128]{1,0:T(8,128)(2,1)S(1)}, u32[]{:S(2)}, u32[]{:S(2)}) %collective-permute-start.13) | collective-permute-done | bytes 86048 | tf_op jit(solution)/shard_map/ppermute | solution.py:708
  40.5 0.0 collective-permute-start.14
  40.5 0.5 %collective-permute-start.12 = (bf16[336,128]{1,0:T(8,128)(2,1)S(1)}, bf16[336,128]{1,0:T(8,128)(2,1)S(1)}, u32[]{:S(2)}, u32[]{:S(2)}) collective-permute-start(bf16[336,128]{1,0:T(8,128)(2,1)S(1)} %add_convert_fusion.refs_0_), channel_id=1, source_target_pairs={{0,2},{2,0},{4,6},{6,4},{8,10},{10,8},{12,14},{14,12},{16,18},{18,... | collective-permute-start | bytes 258056 | tf_op jit(solution)/shard_map/ppermute | solution.py:708
  41.0 2.0 %third_grad.1 = f32[1152,256]{1,0:T(8,128)} custom-call(bf16[1024,1152]{1,0:T(8,128)(2,1)S(1)} %get-tuple-element.79.taps_ref, bf16[1024,256]{1,0:T(8,128)(2,1)S(1)} %get-tuple-element.80.delta_ref), custom_call_target="tpu_custom_call" | custom-call | flops 600000000 | bytes 4000000 | tf_op jit(solution)/shard_map/third_grad/pallas_call | solution.py:1038
  43.0 0.0 collective-permute-done.14.refs_3_
  43.0 0.0 collective-permute-done.12.refs_1_
  43.0 1.2 %finish.1 = (f32[9,160,64]{2,1,0:T(8,128)}, f32[576,128]{1,0:T(8,128)}) custom-call(bf16[336,128]{1,0:T(8,128)(2,1)S(1)} %add_convert_fusion.refs_0_, bf16[336,128]{1,0:T(8,128)(2,1)S(1)} %collective-permute-done.12.refs_1_, bf16[336,128]{1,0:T(8,128)(2,1)S(1)} %collective-permute-done.13.refs_2_, bf16[336,128]{1,0:T(8,128)(2,1)S(1)} %collective-permute-done.14.refs_3_), custom_call_target="tpu_custom_call" | custom-call | flops 1000000 | bytes 1500000 | tf_op jit(solution)/shard_map/finish/pallas_call | solution.py:1048
  (12 shorter events, 0.2 us)
Async XLA Ops:
  0.6 5.2 %copy-start = (bf16[512]{0:T(512)(128)(2,1)S(1)}, bf16[512]{0:T(512)(128)(2,1)}, u32[]{:S(2)}) copy-start(bf16[512]{0:T(512)(128)(2,1)} %param.15) | copy-start | bytes 3076
  0.6 5.2 %collective-permute-start = (s32[1,5,16,128]{3,2,1,0:T(8,128)}, s32[1,5,16,128]{3,2,1,0:T(8,128)S(1)}, u32[]{:S(2)}, u32[]{:S(2)}) collective-permute-start(s32[1,5,16,128]{3,2,1,0:T(8,128)} %got_hbm.1), channel_id=1, source_target_pairs={{0,1},{1,0},{2,3},{3,2},{4,5},{5,4},{6,7},{7,6},{8,9},{9,8},{10,11... | collective-permute-start | bytes 122888 | tf_op jit(solution)/shard_map/ppermute | solution.py:708
  5.8 3.7 %collective-permute-start.1 = (bf16[16,128]{1,0:T(8,128)(2,1)S(1)}, bf16[16,128]{1,0:T(8,128)(2,1)S(1)}, u32[]{:S(2)}, u32[]{:S(2)}) collective-permute-start(bf16[16,128]{1,0:T(8,128)(2,1)S(1)} %get-tuple-element.52), channel_id=1, source_target_pairs={{0,1},{1,0},{2,3},{3,2},{4,5},{5,4},{6,7},{7,6},{8,9},{9,8},{10,11... | collective-permute-start | bytes 12296 | tf_op jit(solution)/shard_map/ppermute | solution.py:708
  9.5 6.2 %collective-permute-start.5 = (bf16[1,272,128]{2,1,0:T(8,128)(2,1)S(1)}, bf16[1,272,128]{2,1,0:T(8,128)(2,1)S(1)}, u32[]{:S(2)}, u32[]{:S(2)}) collective-permute-start(bf16[1,272,128]{2,1,0:T(8,128)(2,1)S(1)} %bitcast_dynamic-update-slice_fusion.payload_ref), channel_id=1, source_target_pairs={{0,16},{2,18},{4,20},{6,22},{8,24},{10,26},{12,28},{14,30},{16,0},... | collective-permute-start | bytes 208904 | tf_op jit(solution)/shard_map/ppermute | solution.py:708
  15.6 1.9 %collective-permute-start.2 = (bf16[2,336,128]{2,1,0:T(8,128)(2,1)S(1)}, bf16[2,336,128]{2,1,0:T(8,128)(2,1)S(1)}, u32[]{:S(2)}, u32[]{:S(2)}) collective-permute-start(bf16[2,336,128]{2,1,0:T(8,128)(2,1)S(1)} %get-tuple-element.61), channel_id=1, source_target_pairs={{0,2},{2,0},{4,6},{6,4},{8,10},{10,8},{12,14},{14,12},{16,18},{18,... | collective-permute-start | bytes 516104 | tf_op jit(solution)/shard_map/ppermute | solution.py:708
  15.8 6.1 %collective-permute-start.6 = (bf16[2,272,128]{2,1,0:T(8,128)(2,1)S(1)}, bf16[2,272,128]{2,1,0:T(8,128)(2,1)S(1)}, u32[]{:S(2)}, u32[]{:S(2)}) collective-permute-start(bf16[2,272,128]{2,1,0:T(8,128)(2,1)S(1)} %slice.28), channel_id=1, source_target_pairs={{0,8},{2,10},{4,12},{6,14},{8,0},{10,2},{12,4},{14,6},{16,24},{18,... | collective-permute-start | bytes 417800 | tf_op jit(solution)/shard_map/ppermute | solution.py:708
  17.4 6.0 %collective-permute-start.3 = (bf16[336,128]{1,0:T(8,128)(2,1)S(1)}, bf16[336,128]{1,0:T(8,128)(2,1)S(1)}, u32[]{:S(2)}, u32[]{:S(2)}) collective-permute-start(bf16[336,128]{1,0:T(8,128)(2,1)S(1)} %fusion.2), channel_id=1, source_target_pairs={{0,4},{2,6},{4,0},{6,2},{8,12},{10,14},{12,8},{14,10},{16,20},{18,... | collective-permute-start | bytes 258056 | tf_op jit(solution)/shard_map/ppermute | solution.py:708
  19.0 6.7 %collective-permute-start.9 = (bf16[2,272,128]{2,1,0:T(8,128)(2,1)S(1)}, bf16[2,272,128]{2,1,0:T(8,128)(2,1)S(1)}, u32[]{:S(2)}, u32[]{:S(2)}) collective-permute-start(bf16[2,272,128]{2,1,0:T(8,128)(2,1)S(1)} %slice.28), channel_id=1, source_target_pairs={{0,4},{2,6},{4,0},{6,2},{8,12},{10,14},{12,8},{14,10},{16,20},{18,... | collective-permute-start | bytes 417800 | tf_op jit(solution)/shard_map/ppermute | solution.py:708
  21.9 6.2 %collective-permute-start.7 = (bf16[2,272,128]{2,1,0:T(8,128)(2,1)S(1)}, bf16[2,272,128]{2,1,0:T(8,128)(2,1)S(1)}, u32[]{:S(2)}, u32[]{:S(2)}) collective-permute-start(bf16[2,272,128]{2,1,0:T(8,128)(2,1)S(1)} %collective-permute-done.6), channel_id=1, source_target_pairs={{0,4},{2,6},{4,0},{6,2},{8,12},{10,14},{12,8},{14,10},{16,20},{18,... | collective-permute-start | bytes 417800 | tf_op jit(solution)/shard_map/ppermute | solution.py:708
  23.5 4.7 %collective-permute-start.4 = (bf16[336,128]{1,0:T(8,128)(2,1)S(1)}, bf16[336,128]{1,0:T(8,128)(2,1)S(1)}, u32[]{:S(2)}, u32[]{:S(2)}) collective-permute-start(bf16[336,128]{1,0:T(8,128)(2,1)S(1)} %fusion), channel_id=1, source_target_pairs={{0,8},{2,10},{4,12},{6,14},{8,0},{10,2},{12,4},{14,6},{16,24},{18,... | collective-permute-start | bytes 258056 | tf_op jit(solution)/shard_map/ppermute | solution.py:708
  25.8 4.6 %collective-permute-start.10 = (bf16[6,272,128]{2,1,0:T(8,128)(2,1)S(1)}, bf16[6,272,128]{2,1,0:T(8,128)(2,1)S(1)}, u32[]{:S(2)}, u32[]{:S(2)}) collective-permute-start(bf16[6,272,128]{2,1,0:T(8,128)(2,1)S(1)} %slice.29), channel_id=1, source_target_pairs={{0,2},{2,0},{4,6},{6,4},{8,10},{10,8},{12,14},{14,12},{16,18},{18,... | collective-permute-start | bytes 1253384 | tf_op jit(solution)/shard_map/ppermute | solution.py:708
  28.1 2.3 %collective-permute-start.11 = (bf16[2,272,128]{2,1,0:T(8,128)(2,1)S(1)}, bf16[2,272,128]{2,1,0:T(8,128)(2,1)S(1)}, u32[]{:S(2)}, u32[]{:S(2)}) collective-permute-start(bf16[2,272,128]{2,1,0:T(8,128)(2,1)S(1)} %collective-permute-done.7), channel_id=1, source_target_pairs={{0,2},{2,0},{4,6},{6,4},{8,10},{10,8},{12,14},{14,12},{16,18},{18,... | collective-permute-start | bytes 417800 | tf_op jit(solution)/shard_map/ppermute | solution.py:708
  28.2 7.8 %collective-permute-start.8 = (bf16[336,128]{1,0:T(8,128)(2,1)S(1)}, bf16[336,128]{1,0:T(8,128)(2,1)S(1)}, u32[]{:S(2)}, u32[]{:S(2)}) collective-permute-start(bf16[336,128]{1,0:T(8,128)(2,1)S(1)} %add_convert_fusion.1), channel_id=1, source_target_pairs={{0,16},{2,18},{4,20},{6,22},{8,24},{10,26},{12,28},{14,30},{16,0},... | collective-permute-start | bytes 258056 | tf_op jit(solution)/shard_map/ppermute | solution.py:708
  35.9 4.6 %collective-permute-start.13 = (bf16[336,128]{1,0:T(8,128)(2,1)S(1)}, bf16[336,128]{1,0:T(8,128)(2,1)S(1)}, u32[]{:S(2)}, u32[]{:S(2)}) collective-permute-start(bf16[336,128]{1,0:T(8,128)(2,1)S(1)} %add_convert_fusion.refs_0_), channel_id=1, source_target_pairs={{0,4},{2,6},{4,0},{6,2},{8,12},{10,14},{12,8},{14,10},{16,20},{18,... | collective-permute-start | bytes 258056 | tf_op jit(solution)/shard_map/ppermute | solution.py:708
  40.5 2.5 %collective-permute-start.14 = (bf16[336,128]{1,0:T(8,128)(2,1)S(1)}, bf16[336,128]{1,0:T(8,128)(2,1)S(1)}, u32[]{:S(2)}, u32[]{:S(2)}) collective-permute-start(bf16[336,128]{1,0:T(8,128)(2,1)S(1)} %collective-permute-done.13.refs_2_), channel_id=1, source_target_pairs={{0,2},{2,0},{4,6},{6,4},{8,10},{10,8},{12,14},{14,12},{16,18},{18,... | collective-permute-start | bytes 258056 | tf_op jit(solution)/shard_map/ppermute | solution.py:708
  40.5 2.5 %collective-permute-start.12 = (bf16[336,128]{1,0:T(8,128)(2,1)S(1)}, bf16[336,128]{1,0:T(8,128)(2,1)S(1)}, u32[]{:S(2)}, u32[]{:S(2)}) collective-permute-start(bf16[336,128]{1,0:T(8,128)(2,1)S(1)} %add_convert_fusion.refs_0_), channel_id=1, source_target_pairs={{0,2},{2,0},{4,6},{6,4},{8,10},{10,8},{12,14},{14,12},{16,18},{18,... | collective-permute-start | bytes 258056 | tf_op jit(solution)/shard_map/ppermute | solution.py:708

commit v11 on v10

--- a/solution.py
+++ b/solution.py
@@ -654,8 +654,20 @@
     ref[...] = jnp.where(first, 0.0, ref[...]) + value
 
 
-def third_grad_kernel(taps_ref, delta_ref, out_ref):
-    out_ref[...] = dot_tn(delta_ref[...], taps_ref[...]).T
+def third_grad_kernel(taps_ref, delta_ref, out_hbm, grad_ref, sems):
+    depth = grad_ref.shape[1]
+    delta = delta_ref[...].T
+    copies = []
+    for row_tap in range(3):
+        part = dot_nn(delta, taps_ref[:, pl.ds(3 * row_tap * depth, 3 * depth)])
+        grad_ref[pl.ds(3 * row_tap, 3)] = part.T.reshape(3, depth, part.shape[0])
+        rows = pl.ds(3 * row_tap, 3)
+        copies.append(
+            pltpu.make_async_copy(grad_ref.at[rows], out_hbm.at[rows], sems.at[row_tap])
+        )
+        copies[-1].start()
+    for copy in copies:
+        copy.wait()
 
 
 def fourth_grad_alone_kernel(fourth_taps_ref, fourth_flat_ref, out_hbm, grad_ref, sems):
@@ -682,7 +694,7 @@
 
 def finish_kernel(*refs):
     got_refs = refs[:4]
-    temporal_ref, middle_ref, flat_ref = refs[4:]
+    temporal_hbm, middle_hbm, temporal_ref, middle_ref, flat_ref, sems = refs[4:]
     me = lax.axis_index("dp") % 4
     share = got_refs[0].shape[0]
     for slot in range(4):
@@ -690,6 +702,8 @@
         flat_ref[pl.ds(at, share)] = got_refs[slot][...].astype(jnp.float32)
     depth = temporal_ref.shape[2]
     middle_ref[...] = flat_ref[pl.ds(12 * depth, 9 * depth)]
+    copies = [pltpu.make_async_copy(middle_ref, middle_hbm, sems.at[3])]
+    copies[0].start()
     rest = temporal_ref.shape[1] - 128
     for tap in range(3):
         parts = [flat_ref[pl.ds((4 * tap + piece) * depth, depth)].T for piece in range(4)]
@@ -698,6 +712,13 @@
             temporal_ref[3 * tap + col_tap, pl.ds(128, rest)] = parts[3][
                 col_tap * rest : col_tap * rest + rest
             ]
+        rows = pl.ds(3 * tap, 3)
+        copies.append(
+            pltpu.make_async_copy(temporal_ref.at[rows], temporal_hbm.at[rows], sems.at[tap])
+        )
+        copies[-1].start()
+    for copy in copies:
+        copy.wait()
 
 
 def cost(flops, size):
@@ -1037,9 +1058,13 @@
     if small:
         deeper_grad = pl.pallas_call(
             third_grad_kernel,
-            out_shape=grad_shape,
+            out_shape=shaped((9, two, three), f32),
             in_specs=[vmem] * 2,
-            out_specs=vmem,
+            out_specs=pl.BlockSpec(memory_space=pl.ANY),
+            scratch_shapes=[
+                pltpu.VMEM((9, two, three), f32),
+                pltpu.SemaphoreType.DMA((3,)),
+            ],
             compiler_params=grant(24),
             cost_estimate=cost(600_000_000, 4_000_000),
             name="third_grad",
@@ -1049,8 +1074,13 @@
         finish_kernel,
         out_shape=(shaped((9, lift_all, one), f32), shaped((9 * one, two), f32)),
         in_specs=[vmem] * 4,
-        out_specs=(vmem, vmem),
-        scratch_shapes=[pltpu.VMEM((21 * one, two), f32)],
+        out_specs=(pl.BlockSpec(memory_space=pl.ANY),) * 2,
+        scratch_shapes=[
+            pltpu.VMEM((9, lift_all, one), f32),
+            pltpu.VMEM((9 * one, two), f32),
+            pltpu.VMEM((21 * one, two), f32),
+            pltpu.SemaphoreType.DMA((4,)),
+        ],
         compiler_params=grant(16),
         cost_estimate=cost(1_000_000, 1_500_000),
         name="finish",

time: 44.3 us -> 44.2 us (level)
  no operation moved by 1% of the time
where the time goes in v11:
time: 44.2 us; the launch traced here: 44 us
  Pallas kernels  18.6 us (42%)
  starting transfers between devices  16.5 us (37%)
  waiting for transfers between devices  7.77 us (18%)
  between operations  0.85 us (2%)
    ppermute x15, starting transfers between devices, swapped(): lax.ppermute(value, axis, [(i, i ^ bit) for i in range(lax.axis_size(axis...  16.5 us
    ppermute x15, waiting for transfers between devices, swapped(): lax.ppermute(value, axis, [(i, i ^ bit) for i in range(lax.axis_size(axis...  7.77 us
    pallas_call x1, Pallas kernels, local(): pl.pallas_call(functools.partial(far_kernel, samples, bands), out_shape=f...  3.56 us
    pallas_call x1, Pallas kernels, local(): local_call(payload, *deep_weights, *maps)  3.49 us
    pallas_call x1, Pallas kernels, local(): pl.pallas_call(functools.partial(early_kernel, pieces, lift_all - 128), o...  2.72 us
    pallas_call x1, Pallas kernels, local(): pl.pallas_call(fourth_grad_alone_kernel, out_shape=shaped((9, three, four...  2.5 us
    pallas_call x1, Pallas kernels, local(): pl.pallas_call(own_kernel, out_shape=(own_cells, own_cells, shaped((16, t...  2.13 us
    pallas_call x1, Pallas kernels, local(): pl.pallas_call(third_grad_kernel, out_shape=shaped((9, two, three), f32),...  1.88 us
  transfers between devices with their start and end apart: 15, of which 6 were waited for; matrix products, arithmetic and copies ran while one was open for 1% of the time, Pallas kernels for 40%

profile of v11, /device:TPU:0, one launch (start us, length us, event | category | flops | bytes accessed | tf_op | source)
XLA Modules:
  0.0 44.0 jit_solution(11152252324478817355)
XLA Ops:
  0.6 0.0 copy-start
  0.6 3.0 %collective-permute-start = (s32[1,5,16,128]{3,2,1,0:T(8,128)}, s32[1,5,16,128]{3,2,1,0:T(8,128)S(1)}, u32[]{:S(2)}, u32[]{:S(2)}) collective-permute-start(s32[1,5,16,128]{3,2,1,0:T(8,128)} %got_hbm.1), channel_id=1, source_target_pairs={{0,1},{1,0},{2,3},{3,2},{4,5},{5,4},{6,7},{7,6},{8,9},{9,8},{10,11... | collective-permute-start | bytes 122888 | tf_op jit(solution)/shard_map/ppermute | solution.py:729
  3.6 2.1 %own_band.1 = (bf16[512,512]{1,0:T(8,128)(2,1)S(1)}, bf16[512,512]{1,0:T(8,128)(2,1)S(1)}, bf16[16,128]{1,0:T(8,128)(2,1)S(1)}, bf16[128,256]{1,0:T(8,128)(2,1)S...) custom-call(s32[1,5,16,128]{3,2,1,0:T(8,128)} %got_hbm.1, ...), custom_call_target="tpu_custom_call" | custom-call | flops 100000000 | bytes 10000000 | tf_op jit(solution)/shard_map/own_band/pallas_call | solution.py:850
  5.8 0.1 collective-permute-start.1
  5.9 0.0 copy-done
  5.9 0.0 collective-permute-done.refs_0_
  5.9 2.7 %early.1 = (bf16[1024,512]{1,0:T(8,128)(2,1)S(1)}, bf16[1088,512]{1,0:T(8,128)(2,1)S(1)}, bf16[272,128]{1,0:T(8,128)(2,1)S(1)}, f32[1,9,2,5,2,8,64]{6,5,4,3,2,1,...) custom-call(s32[1,5,16,128]{3,2,1,0:T(8,128)S(1)} %collective-permute-done.refs_0_, ...), custom_call_target="tpu_custom_call" | custom-call | flops 150000000 | bytes 4000000 | tf_op jit(solution)/shard_map/early/pallas_call | solution.py:877
  8.6 0.8 %collective-permute-done.1 = bf16[16,128]{1,0:T(8,128)(2,1)S(1)} collective-permute-done((bf16[16,128]{1,0:T(8,128)(2,1)S(1)}, bf16[16,128]{1,0:T(8,128)(2,1)S(1)}, u32[]{:S(2)}, u32[]{:S(2)}) %collective-permute-start.1) | collective-permute-done | bytes 4128 | tf_op jit(solution)/shard_map/ppermute | solution.py:729
  9.5 2.6 %collective-permute-start.5 = (bf16[1,272,128]{2,1,0:T(8,128)(2,1)S(1)}, bf16[1,272,128]{2,1,0:T(8,128)(2,1)S(1)}, u32[]{:S(2)}, u32[]{:S(2)}) collective-permute-start(bf16[1,272,128]{2,1,0:T(8,128)(2,1)S(1)} %bitcast_dynamic-update-slice_fusion.payload_ref), channel_id=1, source_target_pairs={{0,16},{2,18},{4,20},{6,22},{8,24},{10,26},{12,28},{14,30},{16,0},... | collective-permute-start | bytes 208904 | tf_op jit(solution)/shard_map/ppermute | solution.py:729
  12.1 3.5 %local.1 = (bf16[2,336,128]{2,1,0:T(8,128)(2,1)S(1)}, bf16[2,336,128]{2,1,0:T(8,128)(2,1)S(1)}) custom-call(bf16[1,272,128]{2,1,0:T(8,128)(2,1)S(1)} %bitcast_dynamic-update-slice_fusion.payload_ref, bf16[9,128,256]{2,1,0:T(8,128)(2,1)S(1)} %get-tuple-element.53.third_w_ref, bf16[9,256,512]{2,1,0:T(8,128)(2,1)S(1)} %get-tuple-element.62.fourth_w_ref.weight_ref, ...), custom_call_target="tpu_custom_call" | custom-call | flops 300000000 | bytes 9000000 | tf_op jit(solution)/shard_map/local/pallas_call | solution.py:953
  15.6 0.1 collective-permute-start.2
  15.6 0.1 dynamic_update_slice.20
  15.7 0.0 collective-permute-done.5
  15.8 1.6 %collective-permute-start.6 = (bf16[2,272,128]{2,1,0:T(8,128)(2,1)S(1)}, bf16[2,272,128]{2,1,0:T(8,128)(2,1)S(1)}, u32[]{:S(2)}, u32[]{:S(2)}) collective-permute-start(bf16[2,272,128]{2,1,0:T(8,128)(2,1)S(1)} %slice.28), channel_id=1, source_target_pairs={{0,8},{2,10},{4,12},{6,14},{8,0},{10,2},{12,4},{14,6},{16,24},{18,... | collective-permute-start | bytes 417800 | tf_op jit(solution)/shard_map/ppermute | solution.py:729
  17.4 0.0 collective-permute-done.2
  17.4 1.6 %collective-permute-start.3 = (bf16[336,128]{1,0:T(8,128)(2,1)S(1)}, bf16[336,128]{1,0:T(8,128)(2,1)S(1)}, u32[]{:S(2)}, u32[]{:S(2)}) collective-permute-start(bf16[336,128]{1,0:T(8,128)(2,1)S(1)} %fusion.2), channel_id=1, source_target_pairs={{0,4},{2,6},{4,0},{6,2},{8,12},{10,14},{12,8},{14,10},{16,20},{18,... | collective-permute-start | bytes 258056 | tf_op jit(solution)/shard_map/ppermute | solution.py:729
  19.0 0.5 %collective-permute-start.9 = (bf16[2,272,128]{2,1,0:T(8,128)(2,1)S(1)}, bf16[2,272,128]{2,1,0:T(8,128)(2,1)S(1)}, u32[]{:S(2)}, u32[]{:S(2)}) collective-permute-start(bf16[2,272,128]{2,1,0:T(8,128)(2,1)S(1)} %slice.28), channel_id=1, source_target_pairs={{0,4},{2,6},{4,0},{6,2},{8,12},{10,14},{12,8},{14,10},{16,20},{18,... | collective-permute-start | bytes 417800 | tf_op jit(solution)/shard_map/ppermute | solution.py:729
  19.5 0.7 %transpose.1.fourth_wt_ref = bf16[9,512,256]{2,1,0:T(8,128)(2,1)S(1)} custom-call(bf16[9,256,512]{2,1,0:T(8,128)(2,1)S(1)} %get-tuple-element.62.fourth_w_ref.weight_ref), custom_call_target="tpu_custom_call" | custom-call | flops 10000000 | bytes 5000000 | tf_op jit(solution)/shard_map/transpose/pallas_call | solution.py:954
  20.2 1.7 %collective-permute-done.6 = bf16[2,272,128]{2,1,0:T(8,128)(2,1)S(1)} collective-permute-done((bf16[2,272,128]{2,1,0:T(8,128)(2,1)S(1)}, bf16[2,272,128]{2,1,0:T(8,128)(2,1)S(1)}, u32[]{:S(2)}, u32[]{:S(2)}) %collective-permute-start.6) | collective-permute-done | bytes 139296 | tf_op jit(solution)/shard_map/ppermute | solution.py:729
  21.9 1.5 %collective-permute-start.7 = (bf16[2,272,128]{2,1,0:T(8,128)(2,1)S(1)}, bf16[2,272,128]{2,1,0:T(8,128)(2,1)S(1)}, u32[]{:S(2)}, u32[]{:S(2)}) collective-permute-start(bf16[2,272,128]{2,1,0:T(8,128)(2,1)S(1)} %collective-permute-done.6), channel_id=1, source_target_pairs={{0,4},{2,6},{4,0},{6,2},{8,12},{10,14},{12,8},{14,10},{16,20},{18,... | collective-permute-start | bytes 417800 | tf_op jit(solution)/shard_map/ppermute | solution.py:729
  23.4 0.0 collective-permute-done.3
  23.5 1.6 %collective-permute-start.4 = (bf16[336,128]{1,0:T(8,128)(2,1)S(1)}, bf16[336,128]{1,0:T(8,128)(2,1)S(1)}, u32[]{:S(2)}, u32[]{:S(2)}) collective-permute-start(bf16[336,128]{1,0:T(8,128)(2,1)S(1)} %fusion), channel_id=1, source_target_pairs={{0,8},{2,10},{4,12},{6,14},{8,0},{10,2},{12,4},{14,6},{16,24},{18,... | collective-permute-start | bytes 258056 | tf_op jit(solution)/shard_map/ppermute | solution.py:729
  25.1 0.6 %collective-permute-done.9 = bf16[2,272,128]{2,1,0:T(8,128)(2,1)S(1)} collective-permute-done((bf16[2,272,128]{2,1,0:T(8,128)(2,1)S(1)}, bf16[2,272,128]{2,1,0:T(8,128)(2,1)S(1)}, u32[]{:S(2)}, u32[]{:S(2)}) %collective-permute-start.9) | collective-permute-done | bytes 139296 | tf_op jit(solution)/shard_map/ppermute | solution.py:729
  25.8 0.1 collective-permute-start.10
  25.9 2.2 %collective-permute-done.7 = bf16[2,272,128]{2,1,0:T(8,128)(2,1)S(1)} collective-permute-done((bf16[2,272,128]{2,1,0:T(8,128)(2,1)S(1)}, bf16[2,272,128]{2,1,0:T(8,128)(2,1)S(1)}, u32[]{:S(2)}, u32[]{:S(2)}) %collective-permute-start.7) | collective-permute-done | bytes 139296 | tf_op jit(solution)/shard_map/ppermute | solution.py:729
  28.1 0.0 collective-permute-start.11
  28.1 0.0 collective-permute-done.4
  28.2 1.7 %collective-permute-start.8 = (bf16[336,128]{1,0:T(8,128)(2,1)S(1)}, bf16[336,128]{1,0:T(8,128)(2,1)S(1)}, u32[]{:S(2)}, u32[]{:S(2)}) collective-permute-start(bf16[336,128]{1,0:T(8,128)(2,1)S(1)} %add_convert_fusion.1), channel_id=1, source_target_pairs={{0,16},{2,18},{4,20},{6,22},{8,24},{10,26},{12,28},{14,30},{16,0},... | collective-permute-start | bytes 258056 | tf_op jit(solution)/shard_map/ppermute | solution.py:729
  29.8 0.6 %near.1 = (bf16[512,1152]{1,0:T(8,128)(2,1)S(1)}, f32[8,4,2,8,256]{4,3,2,1,0:T(8,128)S(1)}, f32[8,4,2,8,256]{4,3,2,1,0:T(8,128)S(1)}) custom-call(bf16[8,272,128]{2,1,0:T(8,128)(2,1)S(1)} %constant_dynamic-update-slice_fusion.near_ref, bf16[9,128,256]{2,1,0:T(8,128)(2,1)S(1)} %get-tuple-element.53.third_w_ref), custom_call_target="tpu_custom_call" | custom-call | flops 300000000 | bytes 4000000 | tf_op jit(solution)/shard_map/near/pallas_call | solution.py:977
  30.4 0.0 collective-permute-done.11.last_ref
  30.4 0.0 collective-permute-done.10.far_ref
  30.4 3.6 %deep.1 = (bf16[256,2304]{1,0:T(8,128)(2,1)S(1)}, bf16[256,512]{1,0:T(8,128)(2,1)S(1)}, f32[1,512]{1,0:T(1,128)}, bf16[1024,1152]{1,0:T(8,128)(2,1)S(1)}, bf16[1024,256]{1,0:T(8,128)(2,1)S(1)}) custom-call(bf16[8,272,128]{2,1,0:T(8,128)(2,1)S(1)} %constant_dynamic-update-slice_fusion.near_ref, bf16[6,272,128]{2,1,0:T(8,128)(2,1)S(1)} %collective-permute-done.10.far_ref, ...), custom_call_target="tpu_custom_call" | custom-call | flops 1300000000 | bytes 12000000 | tf_op jit(solution)/shard_map/deep/pallas_call | solution.py:987
  34.0 1.9 %collective-permute-done.8 = bf16[336,128]{1,0:T(8,128)(2,1)S(1)} collective-permute-done((bf16[336,128]{1,0:T(8,128)(2,1)S(1)}, bf16[336,128]{1,0:T(8,128)(2,1)S(1)}, u32[]{:S(2)}, u32[]{:S(2)}) %collective-permute-start.8) | collective-permute-done | bytes 86048 | tf_op jit(solution)/shard_map/ppermute | solution.py:729
  35.9 1.6 %collective-permute-start.13 = (bf16[336,128]{1,0:T(8,128)(2,1)S(1)}, bf16[336,128]{1,0:T(8,128)(2,1)S(1)}, u32[]{:S(2)}, u32[]{:S(2)}) collective-permute-start(bf16[336,128]{1,0:T(8,128)(2,1)S(1)} %add_convert_fusion.refs_0_), channel_id=1, source_target_pairs={{0,4},{2,6},{4,0},{6,2},{8,12},{10,14},{12,8},{14,10},{16,20},{18,... | collective-permute-start | bytes 258056 | tf_op jit(solution)/shard_map/ppermute | solution.py:729
  37.5 2.5 %fourth_grad.1 = f32[9,256,512]{2,1,0:T(8,128)} custom-call(bf16[256,2304]{1,0:T(8,128)(2,1)S(1)} %get-tuple-element.76.fourth_taps_ref, bf16[256,512]{1,0:T(8,128)(2,1)S(1)} %get-tuple-element.77.fourth_flat_ref), custom_call_target="tpu_custom_call" | custom-call | flops 600000000 | bytes 6000000 | tf_op jit(solution)/shard_map/fourth_grad/pallas_call | solution.py:1029
  40.0 0.5 %collective-permute-done.13.refs_2_ = bf16[336,128]{1,0:T(8,128)(2,1)S(1)} collective-permute-done((bf16[336,128]{1,0:T(8,128)(2,1)S(1)}, bf16[336,128]{1,0:T(8,128)(2,1)S(1)}, u32[]{:S(2)}, u32[]{:S(2)}) %collective-permute-start.13) | collective-permute-done | bytes 86048 | tf_op jit(solution)/shard_map/ppermute | solution.py:729
  40.5 0.0 collective-permute-start.14
  40.5 0.5 %collective-permute-start.12 = (bf16[336,128]{1,0:T(8,128)(2,1)S(1)}, bf16[336,128]{1,0:T(8,128)(2,1)S(1)}, u32[]{:S(2)}, u32[]{:S(2)}) collective-permute-start(bf16[336,128]{1,0:T(8,128)(2,1)S(1)} %add_convert_fusion.refs_0_), channel_id=1, source_target_pairs={{0,2},{2,0},{4,6},{6,4},{8,10},{10,8},{12,14},{14,12},{16,18},{18,... | collective-permute-start | bytes 258056 | tf_op jit(solution)/shard_map/ppermute | solution.py:729
  41.0 1.9 %third_grad.1 = f32[9,128,256]{2,1,0:T(8,128)} custom-call(bf16[1024,1152]{1,0:T(8,128)(2,1)S(1)} %get-tuple-element.79.taps_ref, bf16[1024,256]{1,0:T(8,128)(2,1)S(1)} %get-tuple-element.80.delta_ref), custom_call_target="tpu_custom_call" | custom-call | flops 600000000 | bytes 4000000 | tf_op jit(solution)/shard_map/third_grad/pallas_call | solution.py:1059
  42.9 0.0 collective-permute-done.14.refs_3_
  42.9 0.0 collective-permute-done.12.refs_1_
  42.9 1.1 %finish.1 = (f32[9,160,64]{2,1,0:T(8,128)}, f32[576,128]{1,0:T(8,128)}) custom-call(bf16[336,128]{1,0:T(8,128)(2,1)S(1)} %add_convert_fusion.refs_0_, bf16[336,128]{1,0:T(8,128)(2,1)S(1)} %collective-permute-done.12.refs_1_, bf16[336,128]{1,0:T(8,128)(2,1)S(1)} %collective-permute-done.13.refs_2_, bf16[336,128]{1,0:T(8,128)(2,1)S(1)} %collective-permute-done.14.refs_3_), custom_call_target="tpu_custom_call" | custom-call | flops 1000000 | bytes 1500000 | tf_op jit(solution)/shard_map/finish/pallas_call | solution.py:1073
  (12 shorter events, 0.2 us)
Async XLA Ops:
  0.6 5.2 %copy-start = (bf16[512]{0:T(512)(128)(2,1)S(1)}, bf16[512]{0:T(512)(128)(2,1)}, u32[]{:S(2)}) copy-start(bf16[512]{0:T(512)(128)(2,1)} %param.15) | copy-start | bytes 3076
  0.6 5.2 %collective-permute-start = (s32[1,5,16,128]{3,2,1,0:T(8,128)}, s32[1,5,16,128]{3,2,1,0:T(8,128)S(1)}, u32[]{:S(2)}, u32[]{:S(2)}) collective-permute-start(s32[1,5,16,128]{3,2,1,0:T(8,128)} %got_hbm.1), channel_id=1, source_target_pairs={{0,1},{1,0},{2,3},{3,2},{4,5},{5,4},{6,7},{7,6},{8,9},{9,8},{10,11... | collective-permute-start | bytes 122888 | tf_op jit(solution)/shard_map/ppermute | solution.py:729
  5.8 3.7 %collective-permute-start.1 = (bf16[16,128]{1,0:T(8,128)(2,1)S(1)}, bf16[16,128]{1,0:T(8,128)(2,1)S(1)}, u32[]{:S(2)}, u32[]{:S(2)}) collective-permute-start(bf16[16,128]{1,0:T(8,128)(2,1)S(1)} %get-tuple-element.52), channel_id=1, source_target_pairs={{0,1},{1,0},{2,3},{3,2},{4,5},{5,4},{6,7},{7,6},{8,9},{9,8},{10,11... | collective-permute-start | bytes 12296 | tf_op jit(solution)/shard_map/ppermute | solution.py:729
  9.5 6.2 %collective-permute-start.5 = (bf16[1,272,128]{2,1,0:T(8,128)(2,1)S(1)}, bf16[1,272,128]{2,1,0:T(8,128)(2,1)S(1)}, u32[]{:S(2)}, u32[]{:S(2)}) collective-permute-start(bf16[1,272,128]{2,1,0:T(8,128)(2,1)S(1)} %bitcast_dynamic-update-slice_fusion.payload_ref), channel_id=1, source_target_pairs={{0,16},{2,18},{4,20},{6,22},{8,24},{10,26},{12,28},{14,30},{16,0},... | collective-permute-start | bytes 208904 | tf_op jit(solution)/shard_map/ppermute | solution.py:729
  15.6 1.9 %collective-permute-start.2 = (bf16[2,336,128]{2,1,0:T(8,128)(2,1)S(1)}, bf16[2,336,128]{2,1,0:T(8,128)(2,1)S(1)}, u32[]{:S(2)}, u32[]{:S(2)}) collective-permute-start(bf16[2,336,128]{2,1,0:T(8,128)(2,1)S(1)} %get-tuple-element.61), channel_id=1, source_target_pairs={{0,2},{2,0},{4,6},{6,4},{8,10},{10,8},{12,14},{14,12},{16,18},{18,... | collective-permute-start | bytes 516104 | tf_op jit(solution)/shard_map/ppermute | solution.py:729
  15.8 6.1 %collective-permute-start.6 = (bf16[2,272,128]{2,1,0:T(8,128)(2,1)S(1)}, bf16[2,272,128]{2,1,0:T(8,128)(2,1)S(1)}, u32[]{:S(2)}, u32[]{:S(2)}) collective-permute-start(bf16[2,272,128]{2,1,0:T(8,128)(2,1)S(1)} %slice.28), channel_id=1, source_target_pairs={{0,8},{2,10},{4,12},{6,14},{8,0},{10,2},{12,4},{14,6},{16,24},{18,... | collective-permute-start | bytes 417800 | tf_op jit(solution)/shard_map/ppermute | solution.py:729
  17.4 6.0 %collective-permute-start.3 = (bf16[336,128]{1,0:T(8,128)(2,1)S(1)}, bf16[336,128]{1,0:T(8,128)(2,1)S(1)}, u32[]{:S(2)}, u32[]{:S(2)}) collective-permute-start(bf16[336,128]{1,0:T(8,128)(2,1)S(1)} %fusion.2), channel_id=1, source_target_pairs={{0,4},{2,6},{4,0},{6,2},{8,12},{10,14},{12,8},{14,10},{16,20},{18,... | collective-permute-start | bytes 258056 | tf_op jit(solution)/shard_map/ppermute | solution.py:729
  19.0 6.7 %collective-permute-start.9 = (bf16[2,272,128]{2,1,0:T(8,128)(2,1)S(1)}, bf16[2,272,128]{2,1,0:T(8,128)(2,1)S(1)}, u32[]{:S(2)}, u32[]{:S(2)}) collective-permute-start(bf16[2,272,128]{2,1,0:T(8,128)(2,1)S(1)} %slice.28), channel_id=1, source_target_pairs={{0,4},{2,6},{4,0},{6,2},{8,12},{10,14},{12,8},{14,10},{16,20},{18,... | collective-permute-start | bytes 417800 | tf_op jit(solution)/shard_map/ppermute | solution.py:729
  21.9 6.2 %collective-permute-start.7 = (bf16[2,272,128]{2,1,0:T(8,128)(2,1)S(1)}, bf16[2,272,128]{2,1,0:T(8,128)(2,1)S(1)}, u32[]{:S(2)}, u32[]{:S(2)}) collective-permute-start(bf16[2,272,128]{2,1,0:T(8,128)(2,1)S(1)} %collective-permute-done.6), channel_id=1, source_target_pairs={{0,4},{2,6},{4,0},{6,2},{8,12},{10,14},{12,8},{14,10},{16,20},{18,... | collective-permute-start | bytes 417800 | tf_op jit(solution)/shard_map/ppermute | solution.py:729
  23.5 4.7 %collective-permute-start.4 = (bf16[336,128]{1,0:T(8,128)(2,1)S(1)}, bf16[336,128]{1,0:T(8,128)(2,1)S(1)}, u32[]{:S(2)}, u32[]{:S(2)}) collective-permute-start(bf16[336,128]{1,0:T(8,128)(2,1)S(1)} %fusion), channel_id=1, source_target_pairs={{0,8},{2,10},{4,12},{6,14},{8,0},{10,2},{12,4},{14,6},{16,24},{18,... | collective-permute-start | bytes 258056 | tf_op jit(solution)/shard_map/ppermute | solution.py:729
  25.8 4.6 %collective-permute-start.10 = (bf16[6,272,128]{2,1,0:T(8,128)(2,1)S(1)}, bf16[6,272,128]{2,1,0:T(8,128)(2,1)S(1)}, u32[]{:S(2)}, u32[]{:S(2)}) collective-permute-start(bf16[6,272,128]{2,1,0:T(8,128)(2,1)S(1)} %slice.29), channel_id=1, source_target_pairs={{0,2},{2,0},{4,6},{6,4},{8,10},{10,8},{12,14},{14,12},{16,18},{18,... | collective-permute-start | bytes 1253384 | tf_op jit(solution)/shard_map/ppermute | solution.py:729
  28.1 2.3 %collective-permute-start.11 = (bf16[2,272,128]{2,1,0:T(8,128)(2,1)S(1)}, bf16[2,272,128]{2,1,0:T(8,128)(2,1)S(1)}, u32[]{:S(2)}, u32[]{:S(2)}) collective-permute-start(bf16[2,272,128]{2,1,0:T(8,128)(2,1)S(1)} %collective-permute-done.7), channel_id=1, source_target_pairs={{0,2},{2,0},{4,6},{6,4},{8,10},{10,8},{12,14},{14,12},{16,18},{18,... | collective-permute-start | bytes 417800 | tf_op jit(solution)/shard_map/ppermute | solution.py:729
  28.2 7.8 %collective-permute-start.8 = (bf16[336,128]{1,0:T(8,128)(2,1)S(1)}, bf16[336,128]{1,0:T(8,128)(2,1)S(1)}, u32[]{:S(2)}, u32[]{:S(2)}) collective-permute-start(bf16[336,128]{1,0:T(8,128)(2,1)S(1)} %add_convert_fusion.1), channel_id=1, source_target_pairs={{0,16},{2,18},{4,20},{6,22},{8,24},{10,26},{12,28},{14,30},{16,0},... | collective-permute-start | bytes 258056 | tf_op jit(solution)/shard_map/ppermute | solution.py:729
  35.9 4.6 %collective-permute-start.13 = (bf16[336,128]{1,0:T(8,128)(2,1)S(1)}, bf16[336,128]{1,0:T(8,128)(2,1)S(1)}, u32[]{:S(2)}, u32[]{:S(2)}) collective-permute-start(bf16[336,128]{1,0:T(8,128)(2,1)S(1)} %add_convert_fusion.refs_0_), channel_id=1, source_target_pairs={{0,4},{2,6},{4,0},{6,2},{8,12},{10,14},{12,8},{14,10},{16,20},{18,... | collective-permute-start | bytes 258056 | tf_op jit(solution)/shard_map/ppermute | solution.py:729
  40.5 2.4 %collective-permute-start.14 = (bf16[336,128]{1,0:T(8,128)(2,1)S(1)}, bf16[336,128]{1,0:T(8,128)(2,1)S(1)}, u32[]{:S(2)}, u32[]{:S(2)}) collective-permute-start(bf16[336,128]{1,0:T(8,128)(2,1)S(1)} %collective-permute-done.13.refs_2_), channel_id=1, source_target_pairs={{0,2},{2,0},{4,6},{6,4},{8,10},{10,8},{12,14},{14,12},{16,18},{18,... | collective-permute-start | bytes 258056 | tf_op jit(solution)/shard_map/ppermute | solution.py:729
  40.5 2.4 %collective-permute-start.12 = (bf16[336,128]{1,0:T(8,128)(2,1)S(1)}, bf16[336,128]{1,0:T(8,128)(2,1)S(1)}, u32[]{:S(2)}, u32[]{:S(2)}) collective-permute-start(bf16[336,128]{1,0:T(8,128)(2,1)S(1)} %add_convert_fusion.refs_0_), channel_id=1, source_target_pairs={{0,2},{2,0},{4,6},{6,4},{8,10},{10,8},{12,14},{14,12},{16,18},{18,... | collective-permute-start | bytes 258056 | tf_op jit(solution)/shard_map/ppermute | solution.py:729

commit v12 on v11

--- a/solution.py
+++ b/solution.py
@@ -1020,8 +1020,24 @@
             name="deep",
         )(near, far, last, *deep_weights, fourth_wt, head)
 
+    if small:
+        deeper_grad = pl.pallas_call(
+            third_grad_kernel,
+            out_shape=shaped((9, two, three), f32),
+            in_specs=[vmem] * 2,
+            out_specs=pl.BlockSpec(memory_space=pl.ANY),
+            scratch_shapes=[
+                pltpu.VMEM((9, two, three), f32),
+                pltpu.SemaphoreType.DMA((3,)),
+            ],
+            compiler_params=grant(24),
+            cost_estimate=cost(600_000_000, 4_000_000),
+            name="third_grad",
+        )(*thirds)
     if bit < samples:
-        other, fourth_flat = lax.optimization_barrier((swapped(total, "dp", bit), fourth_flat))
+        other, fourth_flat, deeper_grad = lax.optimization_barrier(
+            (swapped(total, "dp", bit), fourth_flat, deeper_grad)
+        )
         total = added(total, other)
     beside = swapped(total, "dp", 2)
     core = swapped(total, "dp", 1)
@@ -1055,21 +1071,6 @@
         )(fourth_taps, fourth_flat)
     beside, deepest_grad = lax.optimization_barrier((beside, deepest_grad))
     across = swapped(beside, "dp", 1)
-    if small:
-        deeper_grad = pl.pallas_call(
-            third_grad_kernel,
-            out_shape=shaped((9, two, three), f32),
-            in_specs=[vmem] * 2,
-            out_specs=pl.BlockSpec(memory_space=pl.ANY),
-            scratch_shapes=[
-                pltpu.VMEM((9, two, three), f32),
-                pltpu.SemaphoreType.DMA((3,)),
-            ],
-            compiler_params=grant(24),
-            cost_estimate=cost(600_000_000, 4_000_000),
-            name="third_grad",
-        )(*thirds)
-    across, deeper_grad = lax.optimization_barrier((across, deeper_grad))
     temporal_grad, middle_grad = pl.pallas_call(
         finish_kernel,
         out_shape=(shaped((9, lift_all, one), f32), shaped((9 * one, two), f32)),

time: 44.2 us -> 43.1 us (0.975)
  waiting for transfers between devices: 7.77 us -> 7.01 us
    ppermute x15, waiting for transfers between devices: 7.77 us -> 7.01 us  [swapped(): lax.ppermute(value, axis, [(i, i ^ bit) for i in range(lax.axis_size(axis...]
  transfers between devices with their start and end apart: 15 -> 15, of which waited for: 6 -> 6; matrix products, arithmetic and copies ran while one was open for 1% -> 1% of each run, Pallas kernels for 40% -> 41%
where the time goes in v12:
time: 43.1 us; the launch traced here: 42.9 us
  Pallas kernels  18.6 us (43%)
  starting transfers between devices  16.1 us (37%)
  waiting for transfers between devices  7.01 us (16%)
  between operations  0.84 us (2%)
    ppermute x15, starting transfers between devices, swapped(): lax.ppermute(value, axis, [(i, i ^ bit) for i in range(lax.axis_size(axis...  16.1 us
    ppermute x15, waiting for transfers between devices, swapped(): lax.ppermute(value, axis, [(i, i ^ bit) for i in range(lax.axis_size(axis...  7.01 us
    pallas_call x1, Pallas kernels, local(): pl.pallas_call(functools.partial(far_kernel, samples, bands), out_shape=f...  3.55 us
    pallas_call x1, Pallas kernels, local(): local_call(payload, *deep_weights, *maps)  3.49 us
    pallas_call x1, Pallas kernels, local(): pl.pallas_call(functools.partial(early_kernel, pieces, lift_all - 128), o...  2.72 us
    pallas_call x1, Pallas kernels, local(): pl.pallas_call(fourth_grad_alone_kernel, out_shape=shaped((9, three, four...  2.5 us
    pallas_call x1, Pallas kernels, local(): pl.pallas_call(own_kernel, out_shape=(own_cells, own_cells, shaped((16, t...  2.13 us
    pallas_call x1, Pallas kernels, local(): pl.pallas_call(third_grad_kernel, out_shape=shaped((9, two, three), f32),...  1.9 us
  transfers between devices with their start and end apart: 15, of which 6 were waited for; matrix products, arithmetic and copies ran while one was open for 1% of the time, Pallas kernels for 41%

profile of v12, /device:TPU:0, one launch (start us, length us, event | category | flops | bytes accessed | tf_op | source)
XLA Modules:
  0.0 42.9 jit_solution(15683526651048611938)
XLA Ops:
  0.6 0.0 copy-start
  0.6 3.0 %collective-permute-start = (s32[1,5,16,128]{3,2,1,0:T(8,128)}, s32[1,5,16,128]{3,2,1,0:T(8,128)S(1)}, u32[]{:S(2)}, u32[]{:S(2)}) collective-permute-start(s32[1,5,16,128]{3,2,1,0:T(8,128)} %got_hbm.1), channel_id=1, source_target_pairs={{0,1},{1,0},{2,3},{3,2},{4,5},{5,4},{6,7},{7,6},{8,9},{9,8},{10,11... | collective-permute-start | bytes 122888 | tf_op jit(solution)/shard_map/ppermute | solution.py:729
  3.6 2.1 %own_band.1 = (bf16[512,512]{1,0:T(8,128)(2,1)S(1)}, bf16[512,512]{1,0:T(8,128)(2,1)S(1)}, bf16[16,128]{1,0:T(8,128)(2,1)S(1)}, bf16[128,256]{1,0:T(8,128)(2,1)S...) custom-call(s32[1,5,16,128]{3,2,1,0:T(8,128)} %got_hbm.1, ...), custom_call_target="tpu_custom_call" | custom-call | flops 100000000 | bytes 10000000 | tf_op jit(solution)/shard_map/own_band/pallas_call | solution.py:850
  5.8 0.1 collective-permute-start.1
  5.9 0.0 copy-done
  5.9 0.0 collective-permute-done.refs_0_
  5.9 2.7 %early.1 = (bf16[1024,512]{1,0:T(8,128)(2,1)S(1)}, bf16[1088,512]{1,0:T(8,128)(2,1)S(1)}, bf16[272,128]{1,0:T(8,128)(2,1)S(1)}, f32[1,9,2,5,2,8,64]{6,5,4,3,2,1,...) custom-call(s32[1,5,16,128]{3,2,1,0:T(8,128)S(1)} %collective-permute-done.refs_0_, ...), custom_call_target="tpu_custom_call" | custom-call | flops 150000000 | bytes 4000000 | tf_op jit(solution)/shard_map/early/pallas_call | solution.py:877
  8.6 0.8 %collective-permute-done.1 = bf16[16,128]{1,0:T(8,128)(2,1)S(1)} collective-permute-done((bf16[16,128]{1,0:T(8,128)(2,1)S(1)}, bf16[16,128]{1,0:T(8,128)(2,1)S(1)}, u32[]{:S(2)}, u32[]{:S(2)}) %collective-permute-start.1) | collective-permute-done | bytes 4128 | tf_op jit(solution)/shard_map/ppermute | solution.py:729
  9.5 2.6 %collective-permute-start.5 = (bf16[1,272,128]{2,1,0:T(8,128)(2,1)S(1)}, bf16[1,272,128]{2,1,0:T(8,128)(2,1)S(1)}, u32[]{:S(2)}, u32[]{:S(2)}) collective-permute-start(bf16[1,272,128]{2,1,0:T(8,128)(2,1)S(1)} %bitcast_dynamic-update-slice_fusion.payload_ref), channel_id=1, source_target_pairs={{0,16},{2,18},{4,20},{6,22},{8,24},{10,26},{12,28},{14,30},{16,0},... | collective-permute-start | bytes 208904 | tf_op jit(solution)/shard_map/ppermute | solution.py:729
  12.1 3.5 %local.1 = (bf16[2,336,128]{2,1,0:T(8,128)(2,1)S(1)}, bf16[2,336,128]{2,1,0:T(8,128)(2,1)S(1)}) custom-call(bf16[1,272,128]{2,1,0:T(8,128)(2,1)S(1)} %bitcast_dynamic-update-slice_fusion.payload_ref, bf16[9,128,256]{2,1,0:T(8,128)(2,1)S(1)} %get-tuple-element.52.third_w_ref, bf16[9,256,512]{2,1,0:T(8,128)(2,1)S(1)} %get-tuple-element.61.fourth_w_ref.weight_ref, ...), custom_call_target="tpu_custom_call" | custom-call | flops 300000000 | bytes 9000000 | tf_op jit(solution)/shard_map/local/pallas_call | solution.py:953
  15.6 0.1 collective-permute-start.2
  15.6 0.1 dynamic_update_slice.20
  15.7 0.0 collective-permute-done.5
  15.8 1.6 %collective-permute-start.6 = (bf16[2,272,128]{2,1,0:T(8,128)(2,1)S(1)}, bf16[2,272,128]{2,1,0:T(8,128)(2,1)S(1)}, u32[]{:S(2)}, u32[]{:S(2)}) collective-permute-start(bf16[2,272,128]{2,1,0:T(8,128)(2,1)S(1)} %slice.28), channel_id=1, source_target_pairs={{0,8},{2,10},{4,12},{6,14},{8,0},{10,2},{12,4},{14,6},{16,24},{18,... | collective-permute-start | bytes 417800 | tf_op jit(solution)/shard_map/ppermute | solution.py:729
  17.4 0.0 collective-permute-done.2
  17.4 1.6 %collective-permute-start.3 = (bf16[336,128]{1,0:T(8,128)(2,1)S(1)}, bf16[336,128]{1,0:T(8,128)(2,1)S(1)}, u32[]{:S(2)}, u32[]{:S(2)}) collective-permute-start(bf16[336,128]{1,0:T(8,128)(2,1)S(1)} %fusion.2), channel_id=1, source_target_pairs={{0,4},{2,6},{4,0},{6,2},{8,12},{10,14},{12,8},{14,10},{16,20},{18,... | collective-permute-start | bytes 258056 | tf_op jit(solution)/shard_map/ppermute | solution.py:729
  19.0 0.5 %collective-permute-start.9 = (bf16[2,272,128]{2,1,0:T(8,128)(2,1)S(1)}, bf16[2,272,128]{2,1,0:T(8,128)(2,1)S(1)}, u32[]{:S(2)}, u32[]{:S(2)}) collective-permute-start(bf16[2,272,128]{2,1,0:T(8,128)(2,1)S(1)} %slice.28), channel_id=1, source_target_pairs={{0,4},{2,6},{4,0},{6,2},{8,12},{10,14},{12,8},{14,10},{16,20},{18,... | collective-permute-start | bytes 417800 | tf_op jit(solution)/shard_map/ppermute | solution.py:729
  19.5 0.7 %transpose.1.fourth_wt_ref = bf16[9,512,256]{2,1,0:T(8,128)(2,1)S(1)} custom-call(bf16[9,256,512]{2,1,0:T(8,128)(2,1)S(1)} %get-tuple-element.61.fourth_w_ref.weight_ref), custom_call_target="tpu_custom_call" | custom-call | flops 10000000 | bytes 5000000 | tf_op jit(solution)/shard_map/transpose/pallas_call | solution.py:954
  20.2 1.7 %collective-permute-done.6 = bf16[2,272,128]{2,1,0:T(8,128)(2,1)S(1)} collective-permute-done((bf16[2,272,128]{2,1,0:T(8,128)(2,1)S(1)}, bf16[2,272,128]{2,1,0:T(8,128)(2,1)S(1)}, u32[]{:S(2)}, u32[]{:S(2)}) %collective-permute-start.6) | collective-permute-done | bytes 139296 | tf_op jit(solution)/shard_map/ppermute | solution.py:729
  21.9 1.5 %collective-permute-start.7 = (bf16[2,272,128]{2,1,0:T(8,128)(2,1)S(1)}, bf16[2,272,128]{2,1,0:T(8,128)(2,1)S(1)}, u32[]{:S(2)}, u32[]{:S(2)}) collective-permute-start(bf16[2,272,128]{2,1,0:T(8,128)(2,1)S(1)} %collective-permute-done.6), channel_id=1, source_target_pairs={{0,4},{2,6},{4,0},{6,2},{8,12},{10,14},{12,8},{14,10},{16,20},{18,... | collective-permute-start | bytes 417800 | tf_op jit(solution)/shard_map/ppermute | solution.py:729
  23.4 0.0 collective-permute-done.3
  23.5 1.6 %collective-permute-start.4 = (bf16[336,128]{1,0:T(8,128)(2,1)S(1)}, bf16[336,128]{1,0:T(8,128)(2,1)S(1)}, u32[]{:S(2)}, u32[]{:S(2)}) collective-permute-start(bf16[336,128]{1,0:T(8,128)(2,1)S(1)} %fusion), channel_id=1, source_target_pairs={{0,8},{2,10},{4,12},{6,14},{8,0},{10,2},{12,4},{14,6},{16,24},{18,... | collective-permute-start | bytes 258056 | tf_op jit(solution)/shard_map/ppermute | solution.py:729
  25.1 0.6 %collective-permute-done.9 = bf16[2,272,128]{2,1,0:T(8,128)(2,1)S(1)} collective-permute-done((bf16[2,272,128]{2,1,0:T(8,128)(2,1)S(1)}, bf16[2,272,128]{2,1,0:T(8,128)(2,1)S(1)}, u32[]{:S(2)}, u32[]{:S(2)}) %collective-permute-start.9) | collective-permute-done | bytes 139296 | tf_op jit(solution)/shard_map/ppermute | solution.py:729
  25.8 0.1 collective-permute-start.10
  25.9 2.2 %collective-permute-done.7 = bf16[2,272,128]{2,1,0:T(8,128)(2,1)S(1)} collective-permute-done((bf16[2,272,128]{2,1,0:T(8,128)(2,1)S(1)}, bf16[2,272,128]{2,1,0:T(8,128)(2,1)S(1)}, u32[]{:S(2)}, u32[]{:S(2)}) %collective-permute-start.7) | collective-permute-done | bytes 139296 | tf_op jit(solution)/shard_map/ppermute | solution.py:729
  28.1 0.0 collective-permute-start.11
  28.1 0.0 collective-permute-done.4
  28.2 1.7 %collective-permute-start.8 = (bf16[336,128]{1,0:T(8,128)(2,1)S(1)}, bf16[336,128]{1,0:T(8,128)(2,1)S(1)}, u32[]{:S(2)}, u32[]{:S(2)}) collective-permute-start(bf16[336,128]{1,0:T(8,128)(2,1)S(1)} %add_convert_fusion.1), channel_id=1, source_target_pairs={{0,16},{2,18},{4,20},{6,22},{8,24},{10,26},{12,28},{14,30},{16,0},... | collective-permute-start | bytes 258056 | tf_op jit(solution)/shard_map/ppermute | solution.py:729
  29.8 0.6 %near.1 = (bf16[512,1152]{1,0:T(8,128)(2,1)S(1)}, f32[8,4,2,8,256]{4,3,2,1,0:T(8,128)S(1)}, f32[8,4,2,8,256]{4,3,2,1,0:T(8,128)S(1)}) custom-call(bf16[8,272,128]{2,1,0:T(8,128)(2,1)S(1)} %constant_dynamic-update-slice_fusion.near_ref, bf16[9,128,256]{2,1,0:T(8,128)(2,1)S(1)} %get-tuple-element.52.third_w_ref), custom_call_target="tpu_custom_call" | custom-call | flops 300000000 | bytes 4000000 | tf_op jit(solution)/shard_map/near/pallas_call | solution.py:977
  30.4 0.0 collective-permute-done.11.last_ref
  30.4 0.0 collective-permute-done.10.far_ref
  30.4 3.6 %deep.1 = (bf16[256,2304]{1,0:T(8,128)(2,1)S(1)}, bf16[256,512]{1,0:T(8,128)(2,1)S(1)}, f32[1,512]{1,0:T(1,128)}, bf16[1024,1152]{1,0:T(8,128)(2,1)S(1)}, bf16[1024,256]{1,0:T(8,128)(2,1)S(1)}) custom-call(bf16[8,272,128]{2,1,0:T(8,128)(2,1)S(1)} %constant_dynamic-update-slice_fusion.near_ref, bf16[6,272,128]{2,1,0:T(8,128)(2,1)S(1)} %collective-permute-done.10.far_ref, ...), custom_call_target="tpu_custom_call" | custom-call | flops 1300000000 | bytes 12000000 | tf_op jit(solution)/shard_map/deep/pallas_call | solution.py:987
  34.0 1.9 %third_grad.1 = f32[9,128,256]{2,1,0:T(8,128)} custom-call(bf16[1024,1152]{1,0:T(8,128)(2,1)S(1)} %get-tuple-element.74.taps_ref, bf16[1024,256]{1,0:T(8,128)(2,1)S(1)} %get-tuple-element.75.delta_ref), custom_call_target="tpu_custom_call" | custom-call | flops 600000000 | bytes 4000000 | tf_op jit(solution)/shard_map/third_grad/pallas_call | solution.py:1024
  35.9 0.0 collective-permute-done.8
  35.9 1.6 %collective-permute-start.13 = (bf16[336,128]{1,0:T(8,128)(2,1)S(1)}, bf16[336,128]{1,0:T(8,128)(2,1)S(1)}, u32[]{:S(2)}, u32[]{:S(2)}) collective-permute-start(bf16[336,128]{1,0:T(8,128)(2,1)S(1)} %add_convert_fusion.refs_0_), channel_id=1, source_target_pairs={{0,4},{2,6},{4,0},{6,2},{8,12},{10,14},{12,8},{14,10},{16,20},{18,... | collective-permute-start | bytes 258056 | tf_op jit(solution)/shard_map/ppermute | solution.py:729
  37.5 0.0 collective-permute-start.12
  37.5 2.5 %fourth_grad.1 = f32[9,256,512]{2,1,0:T(8,128)} custom-call(bf16[256,2304]{1,0:T(8,128)(2,1)S(1)} %get-tuple-element.77.fourth_taps_ref, bf16[256,512]{1,0:T(8,128)(2,1)S(1)} %get-tuple-element.78.fourth_flat_ref), custom_call_target="tpu_custom_call" | custom-call | flops 600000000 | bytes 6000000 | tf_op jit(solution)/shard_map/fourth_grad/pallas_call | solution.py:1045
  40.0 0.5 %collective-permute-done.13.refs_2_ = bf16[336,128]{1,0:T(8,128)(2,1)S(1)} collective-permute-done((bf16[336,128]{1,0:T(8,128)(2,1)S(1)}, bf16[336,128]{1,0:T(8,128)(2,1)S(1)}, u32[]{:S(2)}, u32[]{:S(2)}) %collective-permute-start.13) | collective-permute-done | bytes 86048 | tf_op jit(solution)/shard_map/ppermute | solution.py:729
  40.5 0.1 collective-permute-start.14
  40.6 0.0 collective-permute-done.12.refs_1_
  40.6 1.1 %collective-permute-done.14.refs_3_ = bf16[336,128]{1,0:T(8,128)(2,1)S(1)} collective-permute-done((bf16[336,128]{1,0:T(8,128)(2,1)S(1)}, bf16[336,128]{1,0:T(8,128)(2,1)S(1)}, u32[]{:S(2)}, u32[]{:S(2)}) %collective-permute-start.14) | collective-permute-done | bytes 86048 | tf_op jit(solution)/shard_map/ppermute | solution.py:729
  41.8 1.1 %finish.1 = (f32[9,160,64]{2,1,0:T(8,128)}, f32[576,128]{1,0:T(8,128)}) custom-call(bf16[336,128]{1,0:T(8,128)(2,1)S(1)} %add_convert_fusion.refs_0_, bf16[336,128]{1,0:T(8,128)(2,1)S(1)} %collective-permute-done.12.refs_1_, bf16[336,128]{1,0:T(8,128)(2,1)S(1)} %collective-permute-done.13.refs_2_, bf16[336,128]{1,0:T(8,128)(2,1)S(1)} %collective-permute-done.14.refs_3_), custom_call_target="tpu_custom_call" | custom-call | flops 1000000 | bytes 1500000 | tf_op jit(solution)/shard_map/finish/pallas_call | solution.py:1074
  (12 shorter events, 0.2 us)
Async XLA Ops:
  0.6 5.2 %copy-start = (bf16[512]{0:T(512)(128)(2,1)S(1)}, bf16[512]{0:T(512)(128)(2,1)}, u32[]{:S(2)}) copy-start(bf16[512]{0:T(512)(128)(2,1)} %param.15) | copy-start | bytes 3076
  0.6 5.2 %collective-permute-start = (s32[1,5,16,128]{3,2,1,0:T(8,128)}, s32[1,5,16,128]{3,2,1,0:T(8,128)S(1)}, u32[]{:S(2)}, u32[]{:S(2)}) collective-permute-start(s32[1,5,16,128]{3,2,1,0:T(8,128)} %got_hbm.1), channel_id=1, source_target_pairs={{0,1},{1,0},{2,3},{3,2},{4,5},{5,4},{6,7},{7,6},{8,9},{9,8},{10,11... | collective-permute-start | bytes 122888 | tf_op jit(solution)/shard_map/ppermute | solution.py:729
  5.8 3.7 %collective-permute-start.1 = (bf16[16,128]{1,0:T(8,128)(2,1)S(1)}, bf16[16,128]{1,0:T(8,128)(2,1)S(1)}, u32[]{:S(2)}, u32[]{:S(2)}) collective-permute-start(bf16[16,128]{1,0:T(8,128)(2,1)S(1)} %get-tuple-element.51), channel_id=1, source_target_pairs={{0,1},{1,0},{2,3},{3,2},{4,5},{5,4},{6,7},{7,6},{8,9},{9,8},{10,11... | collective-permute-start | bytes 12296 | tf_op jit(solution)/shard_map/ppermute | solution.py:729
  9.5 6.2 %collective-permute-start.5 = (bf16[1,272,128]{2,1,0:T(8,128)(2,1)S(1)}, bf16[1,272,128]{2,1,0:T(8,128)(2,1)S(1)}, u32[]{:S(2)}, u32[]{:S(2)}) collective-permute-start(bf16[1,272,128]{2,1,0:T(8,128)(2,1)S(1)} %bitcast_dynamic-update-slice_fusion.payload_ref), channel_id=1, source_target_pairs={{0,16},{2,18},{4,20},{6,22},{8,24},{10,26},{12,28},{14,30},{16,0},... | collective-permute-start | bytes 208904 | tf_op jit(solution)/shard_map/ppermute | solution.py:729
  15.6 1.9 %collective-permute-start.2 = (bf16[2,336,128]{2,1,0:T(8,128)(2,1)S(1)}, bf16[2,336,128]{2,1,0:T(8,128)(2,1)S(1)}, u32[]{:S(2)}, u32[]{:S(2)}) collective-permute-start(bf16[2,336,128]{2,1,0:T(8,128)(2,1)S(1)} %get-tuple-element.60), channel_id=1, source_target_pairs={{0,2},{2,0},{4,6},{6,4},{8,10},{10,8},{12,14},{14,12},{16,18},{18,... | collective-permute-start | bytes 516104 | tf_op jit(solution)/shard_map/ppermute | solution.py:729
  15.8 6.1 %collective-permute-start.6 = (bf16[2,272,128]{2,1,0:T(8,128)(2,1)S(1)}, bf16[2,272,128]{2,1,0:T(8,128)(2,1)S(1)}, u32[]{:S(2)}, u32[]{:S(2)}) collective-permute-start(bf16[2,272,128]{2,1,0:T(8,128)(2,1)S(1)} %slice.28), channel_id=1, source_target_pairs={{0,8},{2,10},{4,12},{6,14},{8,0},{10,2},{12,4},{14,6},{16,24},{18,... | collective-permute-start | bytes 417800 | tf_op jit(solution)/shard_map/ppermute | solution.py:729
  17.4 6.0 %collective-permute-start.3 = (bf16[336,128]{1,0:T(8,128)(2,1)S(1)}, bf16[336,128]{1,0:T(8,128)(2,1)S(1)}, u32[]{:S(2)}, u32[]{:S(2)}) collective-permute-start(bf16[336,128]{1,0:T(8,128)(2,1)S(1)} %fusion.2), channel_id=1, source_target_pairs={{0,4},{2,6},{4,0},{6,2},{8,12},{10,14},{12,8},{14,10},{16,20},{18,... | collective-permute-start | bytes 258056 | tf_op jit(solution)/shard_map/ppermute | solution.py:729
  19.0 6.7 %collective-permute-start.9 = (bf16[2,272,128]{2,1,0:T(8,128)(2,1)S(1)}, bf16[2,272,128]{2,1,0:T(8,128)(2,1)S(1)}, u32[]{:S(2)}, u32[]{:S(2)}) collective-permute-start(bf16[2,272,128]{2,1,0:T(8,128)(2,1)S(1)} %slice.28), channel_id=1, source_target_pairs={{0,4},{2,6},{4,0},{6,2},{8,12},{10,14},{12,8},{14,10},{16,20},{18,... | collective-permute-start | bytes 417800 | tf_op jit(solution)/shard_map/ppermute | solution.py:729
  21.9 6.2 %collective-permute-start.7 = (bf16[2,272,128]{2,1,0:T(8,128)(2,1)S(1)}, bf16[2,272,128]{2,1,0:T(8,128)(2,1)S(1)}, u32[]{:S(2)}, u32[]{:S(2)}) collective-permute-start(bf16[2,272,128]{2,1,0:T(8,128)(2,1)S(1)} %collective-permute-done.6), channel_id=1, source_target_pairs={{0,4},{2,6},{4,0},{6,2},{8,12},{10,14},{12,8},{14,10},{16,20},{18,... | collective-permute-start | bytes 417800 | tf_op jit(solution)/shard_map/ppermute | solution.py:729
  23.5 4.7 %collective-permute-start.4 = (bf16[336,128]{1,0:T(8,128)(2,1)S(1)}, bf16[336,128]{1,0:T(8,128)(2,1)S(1)}, u32[]{:S(2)}, u32[]{:S(2)}) collective-permute-start(bf16[336,128]{1,0:T(8,128)(2,1)S(1)} %fusion), channel_id=1, source_target_pairs={{0,8},{2,10},{4,12},{6,14},{8,0},{10,2},{12,4},{14,6},{16,24},{18,... | collective-permute-start | bytes 258056 | tf_op jit(solution)/shard_map/ppermute | solution.py:729
  25.8 4.6 %collective-permute-start.10 = (bf16[6,272,128]{2,1,0:T(8,128)(2,1)S(1)}, bf16[6,272,128]{2,1,0:T(8,128)(2,1)S(1)}, u32[]{:S(2)}, u32[]{:S(2)}) collective-permute-start(bf16[6,272,128]{2,1,0:T(8,128)(2,1)S(1)} %slice.29), channel_id=1, source_target_pairs={{0,2},{2,0},{4,6},{6,4},{8,10},{10,8},{12,14},{14,12},{16,18},{18,... | collective-permute-start | bytes 1253384 | tf_op jit(solution)/shard_map/ppermute | solution.py:729
  28.1 2.3 %collective-permute-start.11 = (bf16[2,272,128]{2,1,0:T(8,128)(2,1)S(1)}, bf16[2,272,128]{2,1,0:T(8,128)(2,1)S(1)}, u32[]{:S(2)}, u32[]{:S(2)}) collective-permute-start(bf16[2,272,128]{2,1,0:T(8,128)(2,1)S(1)} %collective-permute-done.7), channel_id=1, source_target_pairs={{0,2},{2,0},{4,6},{6,4},{8,10},{10,8},{12,14},{14,12},{16,18},{18,... | collective-permute-start | bytes 417800 | tf_op jit(solution)/shard_map/ppermute | solution.py:729
  28.2 7.8 %collective-permute-start.8 = (bf16[336,128]{1,0:T(8,128)(2,1)S(1)}, bf16[336,128]{1,0:T(8,128)(2,1)S(1)}, u32[]{:S(2)}, u32[]{:S(2)}) collective-permute-start(bf16[336,128]{1,0:T(8,128)(2,1)S(1)} %add_convert_fusion.1), channel_id=1, source_target_pairs={{0,16},{2,18},{4,20},{6,22},{8,24},{10,26},{12,28},{14,30},{16,0},... | collective-permute-start | bytes 258056 | tf_op jit(solution)/shard_map/ppermute | solution.py:729
  35.9 4.6 %collective-permute-start.13 = (bf16[336,128]{1,0:T(8,128)(2,1)S(1)}, bf16[336,128]{1,0:T(8,128)(2,1)S(1)}, u32[]{:S(2)}, u32[]{:S(2)}) collective-permute-start(bf16[336,128]{1,0:T(8,128)(2,1)S(1)} %add_convert_fusion.refs_0_), channel_id=1, source_target_pairs={{0,4},{2,6},{4,0},{6,2},{8,12},{10,14},{12,8},{14,10},{16,20},{18,... | collective-permute-start | bytes 258056 | tf_op jit(solution)/shard_map/ppermute | solution.py:729
  37.5 3.1 %collective-permute-start.12 = (bf16[336,128]{1,0:T(8,128)(2,1)S(1)}, bf16[336,128]{1,0:T(8,128)(2,1)S(1)}, u32[]{:S(2)}, u32[]{:S(2)}) collective-permute-start(bf16[336,128]{1,0:T(8,128)(2,1)S(1)} %add_convert_fusion.refs_0_), channel_id=1, source_target_pairs={{0,2},{2,0},{4,6},{6,4},{8,10},{10,8},{12,14},{14,12},{16,18},{18,... | collective-permute-start | bytes 258056 | tf_op jit(solution)/shard_map/ppermute | solution.py:729
  40.5 1.3 %collective-permute-start.14 = (bf16[336,128]{1,0:T(8,128)(2,1)S(1)}, bf16[336,128]{1,0:T(8,128)(2,1)S(1)}, u32[]{:S(2)}, u32[]{:S(2)}) collective-permute-start(bf16[336,128]{1,0:T(8,128)(2,1)S(1)} %collective-permute-done.13.refs_2_), channel_id=1, source_target_pairs={{0,2},{2,0},{4,6},{6,4},{8,10},{10,8},{12,14},{14,12},{16,18},{18,... | collective-permute-start | bytes 258056 | tf_op jit(solution)/shard_map/ppermute | solution.py:729
